TPU v7x, 32 devices: a whole 2x2x4 slice. The times are simulated.
32 devices in a mesh: lon: 8 (over y, x, core), lat: 4 (over z).
Axes of the slice: x: 2, y: 2, z: 4, core: 2. Of those that a mesh axis runs over, the one named last changes fastest.
Arguments:
- fields: float32 [8, 64, 16, 1024], P(None, None, 'lat', 'lon'), may hold values from -6 to 6
- courant: float32 [2, 64, 16, 1024], P(None, None, 'lat', 'lon'), may hold values from -0.5 to 0.5
- cos_zenith: float32 [16, 1024], P('lat', 'lon'), may hold values from 0.2 to 1
- albedo: float32 [16, 1024], P('lat', 'lon'), may hold values from 0.05 to 0.5
- extinction: float32 [14], replicated, may hold values from 0.05 to 4
- single_albedo: float32 [14], replicated, may hold values from 0.2 to 0.95
- band_weight: float32 [14], replicated, may hold values from 0.02 to 0.14
- sun_order: int32 [16, 8, 128], P('lat', 'lon'), may hold values from 0 to 127, each once within a row
- sun_count: int32 [16, 8], P('lat', 'lon'), may hold values from 0 to 128, as said below
Outputs:
- new_fields: float32 [8, 64, 16, 1024], P(None, None, 'lat', 'lon')
- heating: float32 [64, 16, 1024], P(None, 'lat', 'lon')
Inputs may be any that keep to these rules, and one draw needn't show every extreme that they name: `sun_count`: for every latitude the counts of tiles t and t + 4 sum to 128.
All inputs are finite; a program needn't handle non-finite values.
Results may differ from a plain program's by a relative error of at most 0.00005.
Values sent between devices are 32-bit elements; how exact they have to be, the bound alone decides.
No kernel may reach another device: no remote copies, remote signals or barrier semaphores. Data moves between devices by JAX's collectives and lax.ppermute only.
A program may use at most 128 MiB of HBM per device.

v0:
```python
import jax
import jax.numpy as jnp
from jax import lax
from jax.sharding import PartitionSpec as P


def padded_2(block, sides, width):
    for axis, dim in sides:
        count = lax.axis_size(axis)
        forward = [(i, i + 1) for i in range(count - 1)]
        forward.append((count - 1, 0))
        backward = [(target, source) for source, target in forward]
        low = lax.ppermute(
            lax.slice_in_dim(block, block.shape[dim] - width, None, axis=dim), axis, forward
        )
        high = lax.ppermute(lax.slice_in_dim(block, 0, width, axis=dim), axis, backward)
        block = jnp.concatenate([low, block, high], axis=dim)
    return block


def flux_div(field, east_num, north_num):
    inner_rows = field[..., 2:-2, :]
    east = (
        east_num[..., 2:-2, 1:-2]
        * (
            7.0 * (inner_rows[..., 1:-2] + inner_rows[..., 2:-1])
            - (inner_rows[..., 0:-3] + inner_rows[..., 3:])
        )
        / 12.0
    )
    div_east = east[..., 1:] - east[..., :-1]
    inner_cols = field[..., 2:-2]
    north = (
        north_num[..., 1:-2, 2:-2]
        * (
            7.0 * (inner_cols[..., 1:-2, :] + inner_cols[..., 2:-1, :])
            - (inner_cols[..., 0:-3, :] + inner_cols[..., 3:, :])
        )
        / 12.0
    )
    div_north = north[..., 1:, :] - north[..., :-1, :]
    return -(div_east + div_north)


def row_mask(rows_padded, width, lat_dev):
    global_row = lax.axis_index("lat") * lat_dev + jnp.arange(rows_padded, dtype=jnp.int32) - width
    inside = (global_row >= 0) & (global_row < lat_dev * lax.axis_size("lat"))
    return inside.astype(jnp.float32)[None, None, :, None]


def optics(water, cosz, extinction, single_albedo):
    levels = water.shape[0]
    tau = (extinction * (4.0 / levels))[None, :, None] * water[:, None, :]
    depth = jnp.cumsum(tau, axis=0)
    mu = cosz[None, None, :]
    s_top = jnp.exp(-(depth - tau) / mu)
    s_bot = jnp.exp(-depth / mu)
    direct = jnp.exp(-tau / mu)
    decay = jnp.exp(-1.66 * tau)
    scat = 0.5 * single_albedo[None, :, None] * (1.0 - decay)
    transmit = decay + scat
    source = 0.5 * single_albedo[None, :, None] * mu * s_top * (1.0 - direct)
    return (scat, transmit, source, s_top, s_bot)


def up_step(carry, layer):
    a_below, b_below = carry
    reflect, transmit, source = layer
    den = 1.0 - reflect * a_below
    a_here = reflect + transmit * transmit * a_below / den
    b_here = transmit * (a_below * source + b_below) / den + source
    return ((a_here, b_here), (a_here, b_here, den, b_below))


def down_step(d_top, layer):
    transmit, reflect, source, den, b_below = layer
    d_bot = (transmit * d_top + reflect * b_below + source) / den
    return (d_bot, d_top)


def blocked(array, block):
    return array.reshape((array.shape[0] // block, block) + array.shape[1:])


def unblock(array):
    return array.reshape((array.shape[0] * array.shape[1],) + array.shape[2:])


def radiate(water, cosz, surface, extinction, single_albedo, band_weight):
    block = 16
    reflect, transmit, source, s_top, s_bot = optics(water, cosz, extinction, single_albedo)
    mu = cosz[None, :]
    a_floor = jnp.broadcast_to(surface[None, :], reflect.shape[1:])
    b_floor = a_floor * mu * s_bot[-1]

    def up_block(carry, layers):
        outputs = []
        for level in reversed(range(block)):
            carry, out = up_step(carry, (layers[0][level], layers[1][level], layers[2][level]))
            outputs.append(out)
        outputs = outputs[::-1]
        return (carry, tuple((jnp.stack([item[n] for item in outputs]) for n in range(4))))

    _, up_out = lax.scan(
        up_block,
        (a_floor, b_floor),
        (blocked(reflect, block), blocked(transmit, block), blocked(source, block)),
        reverse=True,
    )
    a_all, b_all, den_all, b_next = (unblock(item) for item in up_out)

    def down_block(carry, layers):
        tops = []
        for level in range(block):
            carry, top = down_step(carry, tuple((item[level] for item in layers)))
            tops.append(top)
        return (carry, jnp.stack(tops))

    d_floor, d_blocks = lax.scan(
        down_block,
        jnp.zeros_like(a_floor),
        tuple((blocked(item, block) for item in (transmit, reflect, source, den_all, b_next))),
    )
    d_all = unblock(d_blocks)
    net_top = mu[None] * s_top + d_all - (a_all * d_all + b_all)
    net_floor = mu * s_bot[-1] + d_floor - (a_floor * d_floor + b_floor)
    net_bot = jnp.concatenate([net_top[1:], net_floor[None]], axis=0)
    absorbed = net_top - net_bot
    return water.shape[0] * jnp.sum(absorbed * band_weight[None, :, None], axis=1)


def per_device(
    fields,
    courant,
    cos_zenith,
    albedo,
    extinction,
    single_albedo,
    band_weight,
    sun_order,
    sun_count,
):
    nfields, levels, lat_dev, lon_dev = fields.shape
    order = sun_order[:, 0, :]
    onehot = (order[:, :, None] == jnp.arange(lon_dev, dtype=jnp.int32)[None, None, :]).astype(
        jnp.float32
    )
    ranks = jnp.arange(lon_dev, dtype=jnp.int32)[None, None, :]
    water = jax.nn.softplus(fields[1])
    packed = jnp.concatenate([water, cos_zenith[None], albedo[None]], axis=0)
    flat = packed.reshape(levels + 2, lat_dev * lon_dev)
    heat_all = radiate(
        flat[:levels], flat[levels], flat[levels + 1], extinction, single_albedo, band_weight
    )
    sunlit = jnp.einsum(
        "rkc,rk->rc",
        onehot,
        (ranks[0] < sun_count).astype(jnp.float32),
        precision=lax.Precision.HIGHEST,
    )
    heating = heat_all.reshape(levels, lat_dev, lon_dev) * sunlit[None]
    stack = jnp.concatenate([fields, courant], axis=0)
    padded = padded_2(stack, (("lon", 3), ("lat", 2)), 4)
    padded = padded * row_mask(lat_dev + 8, 4, lat_dev)
    east_num = padded[nfields]
    north_num = padded[nfields + 1]
    wider = padded[:nfields, :, 2:-2, 2:-2] + flux_div(padded[:nfields], east_num, north_num)
    wider = wider * row_mask(lat_dev + 4, 2, lat_dev)
    section = wider[:, :, 2:-2, 2:-2]
    second = flux_div(wider, east_num[:, 2:-2, 2:-2], north_num[:, 2:-2, 2:-2])
    advanced = 0.5 * (fields + section + second)
    new_fields = jnp.concatenate([advanced[:1] + 0.5 * heating[None], advanced[1:]], axis=0)
    return (new_fields, heating)


def solution(mesh):
    in_specs = (
        P(None, None, "lat", "lon"),
        P(None, None, "lat", "lon"),
        P("lat", "lon"),
        P("lat", "lon"),
        P(),
        P(),
        P(),
        P("lat", "lon", None),
        P("lat", "lon"),
    )
    out_specs = (P(None, None, "lat", "lon"), P(None, "lat", "lon"))
    return jax.shard_map(
        per_device, mesh=mesh, in_specs=in_specs, out_specs=out_specs, check_vma=False
    )
```

profile of v0, /device:TPU:0, one launch (start us, length us, event | category | flops | bytes accessed | tf_op | source)
XLA Modules:
  0.0 326.1 jit_solution(16014951552930345391)
XLA Ops:
  2.0 1.9 fusion.150
  3.9 2.4 copy.16
  7.9 2.9 collective-permute-start.1
  13.8 3.4 %fusion.100 = (f32[4,16,14,512]{3,2,1,0:T(8,128)S(1)}, f32[4,16,14,512]{3,2,1,0:T(8,128)}, f32[4,16,14,512]{3,2,1,0:T(8,128)}) fusion(f32[14]{0:T(128)S(1)} %get-tuple-element.429, f32[4,16,512]{2,1,0:T(8,128)S(1)} %compare_select_fusion, f32[14]{0:T(128)S(1)} %get-tuple-element.430, f32[512]{0:T(512)S(1)} %bitcast.1227, ...), kind=kLoop, calls=%fused_computation.357 | loop fusion | flops 5963776 | bytes 7501936 | tf_op jit(solution)/shard_map/mul | solution.py:60
  23.6 24.1 %while.37 = (s32[]{:T(128)}, f32[14,512]{1,0:T(8,128)S(1)}, f32[14,512]{1,0:T(8,128)S(1)}, f32[4,16,14,512]{3,2,1,0:T(8,128)}, f32[4,16,14,512]{3,2,1,0:T(8,128)...) while((s32[]{:T(128)}, f32[14,512]{1,0:T(8,128)S(1)}, ...), condition=%wide.region_2.3_spmd, body=%wide.region_1.2_spmd.sunk | while | flops 1505294 | bytes 10752637 | solution.py:104
  49.8 100.8 %while.38 = (s32[]{:T(128)}, f32[14,512]{1,0:T(8,128)S(1)}, f32[4,16,14,512]{3,2,1,0:T(8,128)}, f32[4,16,14,512]{3,2,1,0:T(8,128)}, f32[4,16,14,512]{3,2,1,0:T(8...) while((s32[]{:T(128)}, f32[14,512]{1,0:T(8,128)S(1)}, ...), condition=%wide.region_4.5_spmd.clone, body=%wide.region_3.4_spmd.clone.sunk | while | flops 587793 | bytes 5128668 | solution.py:119
  72.3 1.9 bitcast_dynamic-update-slice_fusion.10
  97.5 1.9 bitcast_dynamic-update-slice_fusion.10
  147.9 1.9 bitcast_dynamic-update-slice_fusion.10
  150.6 4.5 %fusion.113 = f32[63,14,512]{2,1,0:T(8,128)S(1)} fusion(f32[64,14,512]{2,1,0:T(8,128)} %bitcast.109, f32[64,14,512]{2,1,0:T(8,128)} %bitcast.108, f32[64,14,512]{2,1,0:T(8,128)} %get-tuple-element.427, f32[64,14,512]{2,1,0:T(8,128)} %bitcast.1221, f32[512]{0:T(512)S(1)} %bitcast.1229), kind=kLoop, calls=%fused_computation.377 | loop fusion | flops 3161088 | bytes 9033728 | tf_op jit(solution)/shard_map/sub | solution.py:125
  156.7 2.4 copy.18
  159.1 2.5 copy.19
  161.6 5.5 %pad_maximum_fusion = f32[10,64,4,136]{3,2,1,0:T(4,128)} fusion(f32[10,64,4,4]{3,2,1,0:T(4,128)} %copy.19, f32[10,64,4,128]{3,2,1,0:T(4,128)S(1)} %constant_dynamic-update-slice_fusion.80, f32[10,64,4,4]{3,2,1,0:T(4,128)} %copy.18), kind=kLoop, calls=%fused_computation.350 | loop fusion | flops 696320 | bytes 2785280 | tf_op jit(solution)/shard_map/concatenate | solution.py:17
  167.1 2.3 collective-permute-start.2
  169.4 2.0 collective-permute-start.3
  171.5 4.1 %multiply_reduce_fusion = f32[4,16,512]{2,1,0:T(8,128)S(1)} fusion(f32[4,16,14,512]{3,2,1,0:T(8,128)S(1)} %bitcast.1222, f32[4,16,14,512]{3,2,1,0:T(8,128)} %get-tuple-element.250, f32[4,16,14,512]{3,2,1,0:T(8,128)} %get-tuple-element.249, f32[4,16,14,512]{3,2,1,0:T(8,128)S(1)} %copy-done.3, f32[14]{0:T(128)S(1)} %copy-done.13, f32[512]{0:T(512)S(1)} %bitcast.1230, ...), kind=kLoop, calls=%fused_computation.375 | loop fusion | flops 5472256 | bytes 9439344 | tf_op jit(solution)/shard_map/reduce_sum | solution.py:129
  177.4 52.2 %collective-permute-done.2 = f32[10,64,4,136]{3,2,1,0:T(4,128)} collective-permute-done((f32[10,64,4,136]{3,2,1,0:T(4,128)}, f32[10,64,4,136]{3,2,1,0:T(4,128)}, u32[]{:S(2)}, u32[]{:S(2)}) %collective-permute-start.2) | collective-permute-done | bytes 1392672 | tf_op jit(solution)/shard_map/ppermute | solution.py:13
  229.6 53.8 %collective-permute-done.3 = f32[10,64,4,136]{3,2,1,0:T(4,128)} collective-permute-done((f32[10,64,4,136]{3,2,1,0:T(4,128)}, f32[10,64,4,136]{3,2,1,0:T(4,128)}, u32[]{:S(2)}, u32[]{:S(2)}) %collective-permute-start.3) | collective-permute-done | bytes 1392672 | tf_op jit(solution)/shard_map/ppermute | solution.py:16
  283.4 7.3 %maximum_multiply_fusion = f32[10,64,12,136]{3,2,1,0:T(8,128)S(1)} fusion(f32[10,64,4,136]{3,2,1,0:T(4,128)} %collective-permute-done.3, f32[10,64,4,4]{3,2,1,0:T(4,128)} %copy.19, f32[10,64,4,128]{3,2,1,0:T(4,128)S(1)} %constant_dynamic-update-slice_fusion.80, f32[10,64,4,4]{3,2,1,0:T(4,128)} %copy.18, f32[10,64,4,136]{3,2,1,0:T(4,128)} %collective-permute-done.2, ...), kind=kLoop, calls=%fused_computation.325 | loop fusion | flops 5222400 | bytes 8355888 | tf_op jit(solution)/shard_map/mul | solution.py:164
  292.5 4.7 %fusion.90 = f32[8,64,8,133]{3,2,1,0:T(8,128)} fusion(f32[10,64,12,136]{3,2,1,0:T(8,128)S(1)} %maximum_multiply_fusion, f32[64,8,133]{2,1,0:T(8,128)S(1)} %slice.1074), kind=kLoop, calls=%fused_computation.341 | loop fusion | flops 3268608 | bytes 11167744 | tf_op jit(solution)/shard_map/div | solution.py:24
  297.3 10.8 %fusion.82 = f32[8,64,9,132]{3,2,1,0:T(8,128)} fusion(f32[10,64,12,136]{3,2,1,0:T(8,128)S(1)} %maximum_multiply_fusion, f32[64,9,132]{2,1,0:T(8,128)S(1)} %slice.1082), kind=kLoop, calls=%fused_computation.329 | loop fusion | flops 3649536 | bytes 12469248 | tf_op jit(solution)/shard_map/div | solution.py:34
  308.0 9.5 %fusion.87 = f32[8,64,8,132]{3,2,1,0:T(8,128)S(1)} fusion(f32[8,64,9,132]{3,2,1,0:T(8,128)} %fusion.82, f32[8,64,8,133]{3,2,1,0:T(8,128)} %fusion.90, f32[10,64,12,136]{3,2,1,0:T(8,128)S(1)} %maximum_multiply_fusion, f32[8]{0:T(128)S(1)} %and_convert_fusion), kind=kLoop, calls=%fused_computation.336 | loop fusion | flops 3244032 | bytes 12976160 | tf_op jit(solution)/shard_map/mul | solution.py:168
  317.5 3.7 %fusion.111 = f32[8,64,4,129]{3,2,1,0:T(4,128)S(1)} fusion(f32[8,64,8,132]{3,2,1,0:T(8,128)S(1)} %fusion.87, f32[64,4,129]{2,1,0:T(4,128)S(1)} %slice.1090), kind=kLoop, calls=%fused_computation.371 | loop fusion | flops 1585152 | bytes 5415936 | tf_op jit(solution)/shard_map/div | solution.py:24
  321.2 2.2 fusion.107
  (350 shorter events, 139.9 us)
Async XLA Ops:
  0.6 1.4 copy-start.10
  3.9 8.0 %copy-start.14 = (f32[14]{0:T(128)S(1)}, f32[14]{0:T(128)}, u32[]{:S(2)}) copy-start(f32[14]{0:T(128)} %param.18) | copy-start | bytes 172
  3.9 8.0 %copy-start.15 = (f32[14]{0:T(128)S(1)}, f32[14]{0:T(128)}, u32[]{:S(2)}) copy-start(f32[14]{0:T(128)} %param.17) | copy-start | bytes 172
  6.3 150.4 %collective-permute-start = (f32[10,64,4,4]{1,3,2,0:T(4,128)}, f32[10,64,4,4]{1,3,2,0:T(4,128)}, u32[]{:S(2)}, u32[]{:S(2)}) collective-permute-start(f32[10,64,4,4]{1,3,2,0:T(4,128)} %copy.16), channel_id=1, source_target_pairs={{0,4},{4,8},{8,12},{12,16},{16,20},{20,24},{24,28},{28,0},{1,5},{5... | collective-permute-start | bytes 122888 | tf_op jit(solution)/shard_map/ppermute | solution.py:13
  7.9 151.3 %collective-permute-start.1 = (f32[10,64,4,4]{1,3,2,0:T(4,128)}, f32[10,64,4,4]{1,3,2,0:T(4,128)}, u32[]{:S(2)}, u32[]{:S(2)}) collective-permute-start(f32[10,64,4,4]{1,3,2,0:T(4,128)} %copy.17), channel_id=1, source_target_pairs={{4,0},{8,4},{12,8},{16,12},{20,16},{24,20},{28,24},{0,28},{5,1},{9... | collective-permute-start | bytes 122888 | tf_op jit(solution)/shard_map/ppermute | solution.py:16
  11.9 1.9 copy-start.6
  12.0 1.8 copy-start.11
  12.0 1.8 copy-start.12
  13.7 3.4 %copy-start.1 = (f32[64,14,512]{2,1,0:T(8,128)}, f32[64,14,512]{2,1,0:T(8,128)S(1)}, u32[]{:S(2)}) copy-start(f32[64,14,512]{2,1,0:T(8,128)S(1)} %get-tuple-element.428) | copy-start | bytes 5505028
  47.7 2.1 copy-start
  49.8 100.8 %copy-start.2 = (f32[64,14,512]{2,1,0:T(8,128)S(1)}, f32[64,14,512]{2,1,0:T(8,128)}, u32[]{:S(2)}) copy-start(f32[64,14,512]{2,1,0:T(8,128)} %copy-done.1) | copy-start | bytes 5505028
  161.6 9.9 %copy-start.3 = (f32[4,16,14,512]{3,2,1,0:T(8,128)S(1)}, f32[4,16,14,512]{3,2,1,0:T(8,128)}, u32[]{:S(2)}) copy-start(f32[4,16,14,512]{3,2,1,0:T(8,128)} %get-tuple-element.248) | copy-start | bytes 5505028
  161.6 9.9 %copy-start.4 = (f32[64,14,512]{2,1,0:T(8,128)S(1)}, f32[64,14,512]{2,1,0:T(8,128)}, u32[]{:S(2)}) copy-start(f32[64,14,512]{2,1,0:T(8,128)} %pad_maximum_fusion.1) | copy-start | bytes 5505028
  161.6 9.9 %copy-start.7 = (f32[4,16,512]{2,1,0:T(8,128)S(1)}, f32[4,16,512]{2,1,0:T(8,128)}, u32[]{:S(2)}) copy-start(f32[4,16,512]{2,1,0:T(8,128)} %copy-done.6) | copy-start | bytes 393220
  161.6 9.9 %copy-start.13 = (f32[14]{0:T(128)S(1)}, f32[14]{0:T(128)}, u32[]{:S(2)}) copy-start(f32[14]{0:T(128)} %param.19) | copy-start | bytes 172
  167.1 62.5 %collective-permute-start.2 = (f32[10,64,4,136]{3,2,1,0:T(4,128)}, f32[10,64,4,136]{3,2,1,0:T(4,128)}, u32[]{:S(2)}, u32[]{:S(2)}) collective-permute-start(f32[10,64,4,136]{3,2,1,0:T(4,128)} %pad_maximum_fusion), channel_id=1, source_target_pairs={{0,1},{1,2},{2,3},{3,0},{4,5},{5,6},{6,7},{7,4},{8,9},{9,10},{10,1... | collective-permute-start | bytes 4177928 | tf_op jit(solution)/shard_map/ppermute | solution.py:13
  169.4 113.9 %collective-permute-start.3 = (f32[10,64,4,136]{3,2,1,0:T(4,128)}, f32[10,64,4,136]{3,2,1,0:T(4,128)}, u32[]{:S(2)}, u32[]{:S(2)}) collective-permute-start(f32[10,64,4,136]{3,2,1,0:T(4,128)} %pad_maximum_fusion), channel_id=1, source_target_pairs={{1,0},{2,1},{3,2},{0,3},{5,4},{6,5},{7,6},{4,7},{9,8},{10,9},{11,1... | collective-permute-start | bytes 4177928 | tf_op jit(solution)/shard_map/ppermute | solution.py:16
  171.5 4.9 %copy-start.17 = (s32[4,1]{0,1:T(1,128)S(1)}, s32[4,1]{0,1:T(1,128)}, u32[]{:S(2)}) copy-start(s32[4,1]{0,1:T(1,128)} %param.21) | copy-start | bytes 52
  171.5 5.0 %copy-start.16 = (s32[4,1,128]{2,1,0:T(1,128)S(1)}, s32[4,1,128]{2,1,0:T(1,128)}, u32[]{:S(2)}) copy-start(s32[4,1,128]{2,1,0:T(1,128)} %param.20) | copy-start | bytes 6148
  317.5 3.7 %copy-start.8 = (f32[64,5,128]{2,1,0:T(8,128)S(1)}, f32[64,5,128]{2,1,0:T(8,128)}, u32[]{:S(2)}) copy-start(f32[64,5,128]{2,1,0:T(8,128)} %slice.1097) | copy-start | bytes 491524
  321.2 2.2 copy-start.5
  323.5 1.3 copy-start.9
where the time goes:
time: 332 us; the launch traced here: 326 us
  other arithmetic  169 us (51%)
  waiting for transfers between devices  106 us (32%)
  local copies, waits for them, and re-layouts  40.9 us (12%)
  starting transfers between devices  7.7 us (2%)
    while x128, other arithmetic  97 us
    ppermute x2, waiting for transfers between devices, padded_2(): lax.ppermute(lax.slice_in_dim(block, 0, width, axis=dim), axis, backward)  53.8 us
    ppermute x2, waiting for transfers between devices, padded_2(): lax.ppermute(lax.slice_in_dim(block, block.shape[dim] - width, None, axis...  52.2 us
    dynamic_update_slice x12, local copies, waits for them, and re-layouts, radiate(): lax.scan(up_block, (a_floor, b_floor), (blocked(reflect, block), blocked(...  16.4 us
    div x2, other arithmetic, flux_div(): north_num[..., 1:-2, 2:-2]  13 us
    mul x1, other arithmetic, per_device(): wider = wider * row_mask(lat_dev + 4, 2, lat_dev)  9.48 us
    div x2, other arithmetic, flux_div(): east_num[..., 2:-2, 1:-2]  8.41 us
    another operation x5, local copies, waits for them, and re-layouts  8.26 us
  transfers between devices with their start and end apart: 4, of which 2 were waited for; matrix products, arithmetic and copies ran while one was open for 47% of the time, Pallas kernels for 0%

commit v1 on v0

v1 whole, which is shorter than its diff:
```python
import functools
import math

import jax
import jax.numpy as jnp
from jax import lax
from jax.experimental import pallas as pl
from jax.experimental.pallas import tpu as pltpu
from jax.sharding import PartitionSpec as P

GROUPS = ((0, 4), (4, 8))
SUB = 8
LANES = 128
LOG2E = math.log2(math.e)
VMEM = pl.BlockSpec(memory_space=pltpu.VMEM)
SMEM = pl.BlockSpec(memory_space=pltpu.SMEM)
ANY = pl.BlockSpec(memory_space=pl.ANY)
PARAMS = pltpu.CompilerParams(vmem_limit_bytes=24 * 1024 * 1024)


def swaps(block, axis, ring):
    n = lax.axis_size(axis)
    first = [(i, i ^ 1) for i in range(n)]
    second = []
    for i in range(1, n if ring else n - 1, 2):
        second += [(i, (i + 1) % n), ((i + 1) % n, i)]
    return lax.ppermute(block[0], axis, first), lax.ppermute(block[1], axis, second)


def lane_index():
    return lax.broadcasted_iota(jnp.int32, (SUB, LANES), 1)


def is_even(axis):
    return lax.rem(lax.axis_index(axis), 2) == 0


def pack(rows, block, blocks, packed, lane):
    for r, value in enumerate(rows):
        k = r * blocks + block
        packed = jnp.where(lane // 4 == k, pltpu.roll(value, (4 * k + 2) % LANES, 1), packed)
    return packed


def native_rows(ref, index, block, nrows):
    return [ref[index, pl.ds(SUB * nrows * block + r, SUB, stride=nrows), :] for r in range(nrows)]


def put_sends(even, rows, za, zb, index, block):
    span = pl.ds(SUB * block, SUB)
    za[index, span, :] = jnp.where(even, rows[2], rows[0])
    za[index + 1, span, :] = jnp.where(even, rows[3], rows[1])
    zb[index, span, :] = jnp.where(even, rows[0], rows[2])
    zb[index + 1, span, :] = jnp.where(even, rows[1], rows[3])


def pack_kernel(lo, hi, with_courant, fields, courant, za, zb, packed):
    nrows = 4
    blocks = fields.shape[1] // nrows // SUB
    lane = lane_index()
    even = is_even("lat")

    def one(i, _):
        acc = jnp.zeros((SUB, LANES), jnp.float32)
        for b in range(blocks):
            rows = native_rows(fields, lo + i, b, nrows)
            put_sends(even, rows, za, zb, 2 * i, b)
            acc = pack(rows, b, blocks, acc, lane)
        packed[i] = acc
        return 0

    lax.fori_loop(0, hi - lo, one, 0)
    if with_courant:
        acc = jnp.zeros((SUB, LANES), jnp.float32)
        for b in range(blocks):
            acc = pack(native_rows(courant, 0, b, nrows), b, blocks, acc, lane)
            top = courant[1, pl.ds(SUB * nrows * b + nrows - 1, SUB, stride=nrows), :]
            za[2 * (hi - lo), pl.ds(SUB * b, SUB), :] = top
            zb[2 * (hi - lo), pl.ds(SUB * b, SUB), :] = top
        packed[hi - lo] = acc


def seam(own, first, second, c_first, c_second, lon_even, lane):
    west = jnp.where(lon_even, second, first)
    east = jnp.where(lon_even, first, second)
    c_west = pltpu.roll(jnp.where(lon_even, c_second, c_first), LANES - 1, 1)
    q_m1 = pltpu.roll(west, LANES - 1, 1)
    q_0 = pltpu.roll(own, LANES - 2, 1)
    q_1 = pltpu.roll(own, LANES - 3, 1)
    flux = c_west * (7.0 * (q_m1 + q_0) - (west + q_1)) * (1.0 / 12.0)
    place = lane % 4
    return jnp.where(place == 0, flux, jnp.where(place == 1, west, east))


def divergence(q, c_east, c_north, packed, block, blocks, lane):
    north = []
    for r in range(5):
        north.append(
            c_north[r] * (7.0 * (q[r + 1] + q[r + 2]) - (q[r] + q[r + 3])) * (1.0 / 12.0)
        )
    out = []
    zero, low, last = lane == 0, lane < 2, lane == LANES - 1
    for r in range(4):
        k = r * blocks + block
        here = q[r + 2]
        halo = pltpu.roll(packed, (2 * LANES - 4 * k - 2) % LANES, 1)
        edge = pltpu.roll(packed, (2 * LANES - 4 * k - 1) % LANES, 1)
        right = pltpu.roll(jnp.where(zero, halo, here), LANES - 1, 1)
        right_two = pltpu.roll(jnp.where(low, halo, here), LANES - 2, 1)
        left = pltpu.roll(jnp.where(last, halo, here), 1, 1)
        flux = c_east[r] * (7.0 * (here + right) - (left + right_two)) * (1.0 / 12.0)
        flux_west = pltpu.roll(jnp.where(last, edge, flux), 1, 1)
        out.append((flux - flux_west) + (north[r + 1] - north[r]))
    return out


def halo_rows(rows, lat_even, ra, rb, index, block):
    span = pl.ds(SUB * block, SUB)
    a0, a1 = ra[index, span, :], ra[index + 1, span, :]
    b0, b1 = rb[index, span, :], rb[index + 1, span, :]
    south = [jnp.where(lat_even, b0, a0), jnp.where(lat_even, b1, a1)]
    north = [jnp.where(lat_even, a0, b0), jnp.where(lat_even, a1, b1)]
    return south + rows + north


def courant_rows(courant, lat_even, ca, cb, block, nrows):
    span = pl.ds(SUB * block, SUB)
    row = ca.shape[0] - 1
    below = jnp.where(lat_even, cb[row, span, :], ca[row, span, :])
    return native_rows(courant, 0, block, nrows), [below] + native_rows(courant, 1, block, nrows)


def first_kernel(
    lo, hi, fields, courant, own, ra, rb, rl, rr, ca, cb, cl, cr, section, za, zb, packed
):
    nrows = 4
    blocks = fields.shape[1] // nrows // SUB
    lane = lane_index()
    lat_even, lon_even = is_even("lat"), is_even("lon")
    c_row = cl.shape[0] - 1

    def one(i, _):
        halo = seam(own[i], rl[i], rr[i], cl[c_row], cr[c_row], lon_even, lane)
        acc = jnp.zeros((SUB, LANES), jnp.float32)
        for b in range(blocks):
            rows = native_rows(fields, lo + i, b, nrows)
            q = halo_rows(rows, lat_even, ra, rb, 2 * i, b)
            c_east, c_north = courant_rows(courant, lat_even, ca, cb, b, nrows)
            div = divergence(q, c_east, c_north, halo, b, blocks, lane)
            new = [rows[r] - div[r] for r in range(nrows)]
            for r in range(nrows):
                section[nrows * i + r, pl.ds(SUB * b, SUB), :] = new[r]
            put_sends(lat_even, new, za, zb, 2 * i, b)
            acc = pack(new, b, blocks, acc, lane)
        packed[i] = acc
        return 0

    lax.fori_loop(0, hi - lo, one, 0)


def second_kernel(
    lo, hi, fields, courant, section, own, ra, rb, rl, rr, ca, cb, cl, cr, heating, *rest
):
    out, buffer, sems = rest[-3:]
    nrows = 4
    blocks = fields.shape[1] // nrows // SUB
    lane = lane_index()
    lat_even, lon_even = is_even("lat"), is_even("lon")
    c_row = cl.shape[0] - 1

    def copy(i):
        return pltpu.make_async_copy(buffer.at[i], out.at[lo + i], sems.at[i])

    def one(i, _):
        halo = seam(own[i], rl[i], rr[i], cl[c_row], cr[c_row], lon_even, lane)
        for b in range(blocks):
            rows = native_rows(fields, lo + i, b, nrows)
            own_rows = [section[nrows * i + r, pl.ds(SUB * b, SUB), :] for r in range(nrows)]
            s = halo_rows(own_rows, lat_even, ra, rb, 2 * i, b)
            c_east, c_north = courant_rows(courant, lat_even, ca, cb, b, nrows)
            div = divergence(s, c_east, c_north, halo, b, blocks, lane)
            for r in range(nrows):
                buffer[i, pl.ds(SUB * nrows * b + r, SUB, stride=nrows), :] = 0.5 * (
                    (rows[r] + own_rows[r]) - div[r]
                )
        if lo == 0:

            @pl.when(i == 0)
            def _():
                buffer[0] = buffer[0] + 0.5 * heating[...]

        copy(i).start()
        return 0

    lax.fori_loop(0, hi - lo, one, 0)
    for i in range(hi - lo):
        copy(i).wait()


def radiation_kernel(
    fields, cosz, albedo, ext, single, weight, order, count, after, heat, water, depth, save_a, save_b, save_t, save_g
):
    del after
    nrows, _ = cosz.shape
    levels = fields.shape[1] // nrows
    pairs = ext.shape[0] // 2
    x = fields[0]
    wet = jnp.maximum(x, 0.0) + jnp.log1p(jnp.exp(-jnp.abs(x)))
    heat[...] = wet
    total = jnp.zeros((nrows, LANES), jnp.float32)
    depth[0] = jnp.zeros((2 * nrows, LANES), jnp.float32)
    for l in range(levels):
        w = heat[pl.ds(nrows * l, nrows), :]
        total = total + w
        water[l, pl.ds(0, nrows), :] = w
        water[l, pl.ds(nrows, nrows), :] = w
        depth[l + 1, pl.ds(0, nrows), :] = total
        depth[l + 1, pl.ds(nrows, nrows), :] = total

    mu = jnp.concatenate([cosz[...], cosz[...]], axis=0)
    floor_albedo = jnp.concatenate([albedo[...], albedo[...]], axis=0)
    first = lax.broadcasted_iota(jnp.int32, (2 * nrows, LANES), 0) < nrows

    def by_band(ref):
        return [jnp.where(first, ref[2 * p], ref[2 * p + 1]) for p in range(pairs)]

    scale = 4.0 / levels
    inv_mu = 1.0 / mu
    ext_of, half_of, weight_of = by_band(ext), by_band(single), by_band(weight)
    beam = [-(e * scale * LOG2E) * inv_mu for e in ext_of]
    diffuse = [-(1.66 * scale * LOG2E) * e for e in ext_of]
    half = [0.5 * s for s in half_of]
    half_mu = [0.5 * s * mu for s in half_of]

    def up(step, carry):
        l = levels - 1 - step
        a_all, b_all, s_all = carry
        w = water[l]
        above = depth[l]
        new_a, new_b, new_s = [], [], []
        for p in range(pairs):
            a, b, s_bot = a_all[p], b_all[p], s_all[p]
            decay = jnp.exp2(diffuse[p] * w)
            s_top = jnp.exp2(beam[p] * above)
            reflect = half[p] - half[p] * decay
            transmit = decay + reflect
            source = half_mu[p] * (s_top - s_bot)
            den = 1.0 - reflect * a
            inv = pl.reciprocal(den, approx=True)
            inv = inv * (2.0 - den * inv)
            t = transmit * inv
            a_here = reflect + transmit * (t * a)
            b_here = t * (a * source + b) + source
            save_t[l, p] = t
            save_g[l, p] = (reflect * b + source) * inv
            save_a[l, p] = 1.0 - a_here
            save_b[l, p] = mu * s_top - b_here
            new_a.append(a_here)
            new_b.append(b_here)
            new_s.append(s_top)
        return tuple(new_a), tuple(new_b), tuple(new_s)

    s_floor = [jnp.exp2(beam[p] * depth[levels]) for p in range(pairs)]
    a_floor = [floor_albedo for _ in range(pairs)]
    b_floor = [floor_albedo * (mu * s_floor[p]) for p in range(pairs)]
    lax.fori_loop(0, levels, up, (tuple(a_floor), tuple(b_floor), tuple(s_floor)))

    sunlit = []
    column = lax.broadcasted_iota(jnp.int32, (LANES, LANES), 1)
    rank = lax.broadcasted_iota(jnp.int32, (LANES, LANES), 0)
    for r in range(nrows):
        place = jnp.transpose(jnp.broadcast_to(order[pl.ds(r, 1), :], (LANES, LANES)))
        hit = (place == column) & (rank < count[r, 0])
        sunlit.append(jnp.max(jnp.where(hit, 1.0, 0.0), axis=0, keepdims=True))
    gain = float(levels) * jnp.concatenate(sunlit, axis=0)

    def weighted(l, d_all):
        net = jnp.zeros((2 * nrows, LANES), jnp.float32)
        for p in range(pairs):
            net = net + weight_of[p] * (save_b[l, p] + d_all[p] * save_a[l, p])
        return net

    def put(l, absorbed):
        both = absorbed[:nrows] + absorbed[nrows:]
        heat[pl.ds(pl.multiple_of(nrows * l, nrows), nrows), :] = gain * both

    def down(l, carry):
        d_all, net_above = carry
        d_new = tuple(save_t[l - 1, p] * d_all[p] + save_g[l - 1, p] for p in range(pairs))
        net = weighted(l, d_new)
        put(l - 1, net_above - net)
        return d_new, net

    d_top = tuple(jnp.zeros((2 * nrows, LANES), jnp.float32) for _ in range(pairs))
    d_low, net_low = lax.fori_loop(1, levels, down, (d_top, weighted(0, d_top)))
    net = jnp.zeros((2 * nrows, LANES), jnp.float32)
    for p in range(pairs):
        d_floor = save_t[levels - 1, p] * d_low[p] + save_g[levels - 1, p]
        at_floor = (mu * s_floor[p] - b_floor[p]) + d_floor * (1.0 - a_floor[p])
        net = net + weight_of[p] * at_floor
    put(levels - 1, net_low - net)


def shape(*dims):
    return jax.ShapeDtypeStruct(dims, jnp.float32)


def per_device(
    fields, courant, cos_zenith, albedo, extinction, single_albedo, band_weight, sun_order, sun_count
):
    nfields, levels, nrows, ncols = fields.shape
    flat = fields.reshape(nfields, levels * nrows, ncols)
    wind = courant.reshape(2, levels * nrows, ncols)

    sent, got = [], []
    for lo, hi in GROUPS:
        n, extra = hi - lo, int(lo == 0)
        rows = shape(2 * n + extra, levels, ncols)
        za, zb, packed = pl.pallas_call(
            functools.partial(pack_kernel, lo, hi, lo == 0),
            out_shape=(rows, rows, shape(n + extra, SUB, ncols)),
            in_specs=[VMEM, VMEM],
            out_specs=(VMEM, VMEM, VMEM),
            compiler_params=PARAMS,
            name=f"pack_{lo}",
        )(flat, wind)
        sent.append(packed)
        got.append(swaps((za, zb), "lat", False) + swaps((packed, packed), "lon", True))

    sections, sent_two, got_two = [], [], []
    for g, (lo, hi) in enumerate(GROUPS):
        n = hi - lo
        rows = shape(2 * n, levels, ncols)
        section, za, zb, packed = pl.pallas_call(
            functools.partial(first_kernel, lo, hi),
            out_shape=(shape(nrows * n, levels, ncols), rows, rows, shape(n, SUB, ncols)),
            in_specs=[VMEM] * 11,
            out_specs=(VMEM,) * 4,
            compiler_params=PARAMS,
            name=f"first_{lo}",
        )(flat, wind, sent[g], *got[g], *got[0])
        sections.append(section)
        sent_two.append(packed)
        got_two.append(swaps((za, zb), "lat", False) + swaps((packed, packed), "lon", True))

    pairs = extinction.shape[0] // 2
    store = pltpu.VMEM((levels, pairs, 2 * nrows, ncols), jnp.float32)
    heating = pl.pallas_call(
        radiation_kernel,
        out_shape=shape(levels * nrows, ncols),
        grid=(1,),
        in_specs=[
            pl.BlockSpec((1, levels * nrows, ncols), lambda i: (1, 0, 0)),
            VMEM, VMEM, SMEM, SMEM, SMEM, VMEM, SMEM, ANY,
        ],
        out_specs=pl.BlockSpec((levels * nrows, ncols), lambda i: (0, 0)),
        scratch_shapes=[
            pltpu.VMEM((levels, 2 * nrows, ncols), jnp.float32),
            pltpu.VMEM((levels + 1, 2 * nrows, ncols), jnp.float32),
            store, store, store, store,
        ],
        compiler_params=PARAMS,
        cost_estimate=pl.CostEstimate(flops=20_000_000, bytes_accessed=400_000, transcendentals=1_500_000),
        name="radiation",
    )(
        flat, cos_zenith, albedo, extinction, single_albedo, band_weight,
        sun_order.reshape(nrows, ncols), sun_count, sent_two[-1],
    )

    out = None
    for g, (lo, hi) in enumerate(GROUPS):
        n = hi - lo
        args = [flat, wind, sections[g], sent_two[g], *got_two[g], *got[0], heating]
        specs = [VMEM] * len(args)
        aliases = {}
        if out is not None:
            aliases = {len(args): 0}
            args.append(out)
            specs.append(ANY)
        out = pl.pallas_call(
            functools.partial(second_kernel, lo, hi),
            out_shape=shape(nfields, levels * nrows, ncols),
            in_specs=specs,
            out_specs=ANY,
            scratch_shapes=[
                pltpu.VMEM((n, levels * nrows, ncols), jnp.float32),
                pltpu.SemaphoreType.DMA((n,)),
            ],
            input_output_aliases=aliases,
            compiler_params=PARAMS,
            name=f"second_{lo}",
        )(*args)
    return out.reshape(fields.shape), heating.reshape(levels, nrows, ncols)


def solution(mesh):
    in_specs = (
        P(None, None, "lat", "lon"),
        P(None, None, "lat", "lon"),
        P("lat", "lon"),
        P("lat", "lon"),
        P(),
        P(),
        P(),
        P("lat", "lon", None),
        P("lat", "lon"),
    )
    out_specs = (P(None, None, "lat", "lon"), P(None, "lat", "lon"))
    return jax.shard_map(
        per_device, mesh=mesh, in_specs=in_specs, out_specs=out_specs, check_vma=False
    )
```

time: 332 us -> 54.7 us (0.16); the launches traced: 326 us -> 54.3 us
  other arithmetic: 169 us -> 0 us
  waiting for transfers between devices: 106 us -> 7.7 us
  local copies, waits for them, and re-layouts: 40.9 us -> 7.05 us
  Pallas kernels: 0 us -> 17.4 us
  starting transfers between devices: 7.7 us -> 21.4 us
    ppermute x4 -> x16, waiting for transfers between devices: 106 us -> 7.7 us  [the longest x8 5.32 us: swaps(): lax.ppermute(block[1], axis, second)]
    while x128 -> x0, other arithmetic: 97 us -> none
    div x8 -> x0, other arithmetic: 24.8 us -> none  [the longest x2 13 us: flux_div(): north_num[..., 1:-2, 2:-2]]
    mul x9 -> x0, other arithmetic: 22.1 us -> none  [the longest x1 9.48 us: per_device(): wider = wider * row_mask(lat_dev + 4, 2, lat_dev)]
    pallas_call x0 -> x7, Pallas kernels: none -> 17.4 us  [the longest x2 5.73 us: per_device(): pl.pallas_call(functools.partial(second_kernel, lo, hi), out_shape=shape(...]
    dynamic_update_slice x12 -> x0, local copies, waits for them, and re-layouts: 16.4 us -> none  [radiate(): lax.scan(up_block, (a_floor, b_floor), (blocked(reflect, block), blocked(...]
    ppermute x4 -> x16, starting transfers between devices: 7.7 us -> 21.4 us  [the longest x8 12.1 us: swaps(): lax.ppermute(block[0], axis, first)]
    concatenate x3 -> x0, other arithmetic: 8.34 us -> none  [the longest x1 5.51 us: padded_2(): block = jnp.concatenate([low, block, high], axis=dim)]
  transfers between devices with their start and end apart: 4 -> 16, of which waited for: 2 -> 4; matrix products, arithmetic and copies ran while one was open for 47% -> 1% of each run, Pallas kernels for 0% -> 25%
where the time goes in v1:
time: 54.7 us; the launch traced here: 54.3 us
  starting transfers between devices  21.4 us (39%)
  Pallas kernels  17.4 us (32%)
  waiting for transfers between devices  7.7 us (14%)
  local copies, waits for them, and re-layouts  7.05 us (13%)
  between operations  0.81 us (1%)
    ppermute x8, starting transfers between devices, swaps(): lax.ppermute(block[0], axis, first)  12.1 us
    ppermute x8, starting transfers between devices, swaps(): lax.ppermute(block[1], axis, second)  9.28 us
    unnamed x31, local copies, waits for them, and re-layouts  7.05 us
    pallas_call x2, Pallas kernels, per_device(): pl.pallas_call(functools.partial(second_kernel, lo, hi), out_shape=shape(...  5.73 us
    pallas_call x1, Pallas kernels, per_device(): pl.pallas_call(radiation_kernel, out_shape=shape(levels * nrows, ncols),...  5.45 us
    ppermute x8, waiting for transfers between devices, swaps(): lax.ppermute(block[1], axis, second)  5.32 us
    pallas_call x2, Pallas kernels, per_device(): pl.pallas_call(functools.partial(first_kernel, lo, hi), out_shape=(shape(...  5.27 us
    ppermute x8, waiting for transfers between devices, swaps(): lax.ppermute(block[0], axis, first)  2.37 us
  transfers between devices with their start and end apart: 16, of which 4 were waited for; matrix products, arithmetic and copies ran while one was open for 1% of the time, Pallas kernels for 25%

profile of v1, /device:TPU:0, one launch (start us, length us, event | category | flops | bytes accessed | tf_op | source)
XLA Modules:
  0.0 54.3 jit_solution(13872134727841198376)
XLA Ops:
  0.6 1.2 %copy-done = f32[8,64,4,128]{3,2,1,0:T(4,128)S(1)} copy-done((f32[8,64,4,128]{3,2,1,0:T(4,128)S(1)}, f32[8,64,4,128]{3,2,1,0:T(4,128)}, u32[]{:S(2)}) %copy-start) | copy-done | bytes 1048600
  1.9 0.9 %copy-done.2 = f32[2,64,4,128]{3,2,1,0:T(4,128)S(1)} copy-done((f32[2,64,4,128]{3,2,1,0:T(4,128)S(1)}, f32[2,64,4,128]{3,2,1,0:T(4,128)}, u32[]{:S(2)}) %copy-start.2) | copy-done | bytes 262168
  3.3 3.1 %collective-permute-start.4 = (f32[9,64,128]{2,1,0:T(8,128)S(1)}, f32[9,64,128]{2,1,0:T(8,128)S(1)}, u32[]{:S(2)}, u32[]{:S(2)}) collective-permute-start(f32[9,64,128]{2,1,0:T(8,128)S(1)} %get-tuple-element.19), channel_id=1, source_target_pairs={{0,1},{1,0},{2,3},{3,2},{4,5},{5,4},{6,7},{7,6},{8,9},{9,8},{10,11... | collective-permute-start | bytes 884744 | tf_op jit(solution)/shard_map/ppermute | solution.py:27
  7.5 4.4 %collective-permute-start = (f32[8,64,128]{2,1,0:T(8,128)S(1)}, f32[8,64,128]{2,1,0:T(8,128)S(1)}, u32[]{:S(2)}, u32[]{:S(2)}) collective-permute-start(f32[8,64,128]{2,1,0:T(8,128)S(1)} %get-tuple-element.17), channel_id=1, source_target_pairs={{0,1},{1,0},{2,3},{3,2},{4,5},{5,4},{6,7},{7,6},{8,9},{9,8},{10,11... | collective-permute-start | bytes 786440 | tf_op jit(solution)/shard_map/ppermute | solution.py:27
  12.7 1.2 %collective-permute-done.6.cl.rl = f32[5,8,128]{2,1,0:T(8,128)S(1)} collective-permute-done((f32[5,8,128]{2,1,0:T(8,128)S(1)}, f32[5,8,128]{2,1,0:T(8,128)S(1)}, u32[]{:S(2)}, u32[]{:S(2)}) %collective-permute-start.6) | collective-permute-done | bytes 20512 | tf_op jit(solution)/shard_map/ppermute | solution.py:27
  13.9 2.2 %collective-permute-start.7 = (f32[5,8,128]{2,1,0:T(8,128)S(1)}, f32[5,8,128]{2,1,0:T(8,128)S(1)}, u32[]{:S(2)}, u32[]{:S(2)}) collective-permute-start(f32[5,8,128]{2,1,0:T(8,128)S(1)} %get-tuple-element.21.own), channel_id=1, source_target_pairs={{4,8},{8,4},{12,16},{16,12},{20,24},{24,20},{28,0},{0,28},{5,9},{9... | collective-permute-start | bytes 61448 | tf_op jit(solution)/shard_map/ppermute | solution.py:27
  16.1 1.9 %collective-permute-done.7.cr.rr = f32[5,8,128]{2,1,0:T(8,128)S(1)} collective-permute-done((f32[5,8,128]{2,1,0:T(8,128)S(1)}, f32[5,8,128]{2,1,0:T(8,128)S(1)}, u32[]{:S(2)}, u32[]{:S(2)}) %collective-permute-start.7) | collective-permute-done | bytes 20512 | tf_op jit(solution)/shard_map/ppermute | solution.py:27
  18.0 2.2 %collective-permute-start.3 = (f32[4,8,128]{2,1,0:T(8,128)S(1)}, f32[4,8,128]{2,1,0:T(8,128)S(1)}, u32[]{:S(2)}, u32[]{:S(2)}) collective-permute-start(f32[4,8,128]{2,1,0:T(8,128)S(1)} %get-tuple-element.16.own), channel_id=1, source_target_pairs={{4,8},{8,4},{12,16},{16,12},{20,24},{24,20},{28,0},{0,28},{5,9},{9... | collective-permute-start | bytes 49160 | tf_op jit(solution)/shard_map/ppermute | solution.py:27
  20.2 2.6 %first_0.1 = (f32[16,64,128]{2,1,0:T(8,128)S(1)}, f32[8,64,128]{2,1,0:T(8,128)S(1)}, f32[8,64,128]{2,1,0:T(8,128)}, f32[4,8,128]{2,1,0:T(8,128)S(1)}) custom-call(f32[8,256,128]{2,1,0:T(8,128)S(1)} %bitcast.7, f32[2,256,128]{2,1,0:T(8,128)S(1)} %bitcast.14, f32[5,8,128]{2,1,0:T(8,128)S(1)} %get-tuple-element.21.own, ...), custom_call_target="tpu_custom_call" | custom-call | tf_op jit(solution)/shard_map/first_0/pallas_call | solution.py:334
  22.8 1.3 %collective-permute-start.12 = (f32[8,64,128]{2,1,0:T(8,128)S(1)}, f32[8,64,128]{2,1,0:T(8,128)S(1)}, u32[]{:S(2)}, u32[]{:S(2)}) collective-permute-start(f32[8,64,128]{2,1,0:T(8,128)S(1)} %get-tuple-element.28), channel_id=1, source_target_pairs={{0,1},{1,0},{2,3},{3,2},{4,5},{5,4},{6,7},{7,6},{8,9},{9,8},{10,11... | collective-permute-start | bytes 786440 | tf_op jit(solution)/shard_map/ppermute | solution.py:27
  24.1 0.8 %collective-permute-start.13 = (f32[8,64,128]{2,1,0:T(8,128)}, f32[8,64,128]{2,1,0:T(8,128)S(1)}, u32[]{:S(2)}, u32[]{:S(2)}) collective-permute-start(f32[8,64,128]{2,1,0:T(8,128)} %get-tuple-element.29), channel_id=1, source_target_pairs={{1,2},{2,1},{5,6},{6,5},{9,10},{10,9},{13,14},{14,13},{17,18},{18,... | collective-permute-start | bytes 786440 | tf_op jit(solution)/shard_map/ppermute | solution.py:27
  24.9 2.7 %first_4.1 = (f32[16,64,128]{2,1,0:T(8,128)S(1)}, f32[8,64,128]{2,1,0:T(8,128)}, f32[8,64,128]{2,1,0:T(8,128)}, f32[4,8,128]{2,1,0:T(8,128)S(1)}) custom-call(f32[8,256,128]{2,1,0:T(8,128)S(1)} %bitcast.8, f32[2,256,128]{2,1,0:T(8,128)S(1)} %bitcast.15, f32[4,8,128]{2,1,0:T(8,128)S(1)} %get-tuple-element.16.own, f32[8,64,128]{2,1,0:T(8,128)S(1)} %collective-permute-done.ra, ...), custom_call_target="tpu_custom_call" | custom-call | tf_op jit(solution)/shard_map/first_4/pallas_call | solution.py:334
  27.6 3.3 %collective-permute-start.8 = (f32[8,64,128]{2,1,0:T(8,128)}, f32[8,64,128]{2,1,0:T(8,128)S(1)}, u32[]{:S(2)}, u32[]{:S(2)}) collective-permute-start(f32[8,64,128]{2,1,0:T(8,128)} %get-tuple-element.24), channel_id=1, source_target_pairs={{0,1},{1,0},{2,3},{3,2},{4,5},{5,4},{6,7},{7,6},{8,9},{9,8},{10,11... | collective-permute-start | bytes 786440 | tf_op jit(solution)/shard_map/ppermute | solution.py:27
  30.8 1.4 %collective-permute-start.9 = (f32[8,64,128]{2,1,0:T(8,128)}, f32[8,64,128]{2,1,0:T(8,128)}, u32[]{:S(2)}, u32[]{:S(2)}) collective-permute-start(f32[8,64,128]{2,1,0:T(8,128)} %get-tuple-element.25), channel_id=1, source_target_pairs={{1,2},{2,1},{5,6},{6,5},{9,10},{10,9},{13,14},{14,13},{17,18},{18,... | collective-permute-start | bytes 786440 | tf_op jit(solution)/shard_map/ppermute | solution.py:27
  32.2 1.2 %collective-permute-done.14.rl = f32[4,8,128]{2,1,0:T(8,128)S(1)} collective-permute-done((f32[4,8,128]{2,1,0:T(8,128)S(1)}, f32[4,8,128]{2,1,0:T(8,128)S(1)}, u32[]{:S(2)}, u32[]{:S(2)}) %collective-permute-start.14) | collective-permute-done | bytes 16416 | tf_op jit(solution)/shard_map/ppermute | solution.py:27
  34.6 3.4 %collective-permute-done.15.rr = f32[4,8,128]{2,1,0:T(8,128)S(1)} collective-permute-done((f32[4,8,128]{2,1,0:T(8,128)S(1)}, f32[4,8,128]{2,1,0:T(8,128)S(1)}, u32[]{:S(2)}, u32[]{:S(2)}) %collective-permute-start.15) | collective-permute-done | bytes 16416 | tf_op jit(solution)/shard_map/ppermute | solution.py:27
  38.7 0.7 %collective-permute-start.11 = (f32[4,8,128]{2,1,0:T(8,128)S(1)}, f32[4,8,128]{2,1,0:T(8,128)}, u32[]{:S(2)}, u32[]{:S(2)}) collective-permute-start(f32[4,8,128]{2,1,0:T(8,128)S(1)} %get-tuple-element.23.after.own), channel_id=1, source_target_pairs={{4,8},{8,4},{12,16},{16,12},{20,24},{24,20},{28,0},{0,28},{5,9},{9... | collective-permute-start | bytes 49160 | tf_op jit(solution)/shard_map/ppermute | solution.py:27
  39.4 0.7 %copy.12.count = s32[4,1]{1,0:T(4,128)S(1)} copy(s32[4,1]{0,1:T(1,128)} %param.17) | data formatting | bytes 32 | tf_op args[8]
  40.8 0.7 %copy-done.10 = f32[4,128]{1,0:T(4,128)S(1)} copy-done((f32[4,128]{1,0:T(4,128)S(1)}, f32[4,128]{1,0:T(4,128)}, u32[]{:S(2)}) %copy-start.10) | copy-done | bytes 2072
  41.5 0.7 %copy-done.11 = s32[4,1,128]{2,1,0:T(1,128)S(1)} copy-done((s32[4,1,128]{2,1,0:T(1,128)S(1)}, s32[4,1,128]{2,1,0:T(1,128)}, u32[]{:S(2)}) %copy-start.11) | copy-done | bytes 2072
  42.2 5.5 %radiation.1.heating = f32[256,128]{1,0:T(8,128)} custom-call(f32[8,256,128]{2,1,0:T(8,128)S(1)} %bitcast.9, f32[4,128]{1,0:T(4,128)S(1)} %copy-done.9, f32[4,128]{1,0:T(4,128)S(1)} %copy-done.10, f32[14]{0:T(128)S(1)} %copy-done.12, f32[14]{0:T(128)S(1)} %copy-done.13, f32[14]{0:T(128)S(1)} %copy-done.14, s32[4,128]{1,0:T(4,128)S(1)} %bitcast.19, ...), custom_call_target="tpu_custom_call" | custom-call | flops 20000000 | bytes 400000 | tf_op jit(solution)/shard_map/radiation/pallas_call | solution.py:348
  47.7 0.9 %copy-done.4 = f32[256,128]{1,0:T(8,128)S(1)} copy-done((f32[256,128]{1,0:T(8,128)S(1)}, f32[256,128]{1,0:T(8,128)}, u32[]{:S(2)}) %copy-start.4) | copy-done | bytes 131096
  48.6 2.4 %second_0.1.rest_0_ = f32[8,256,128]{2,1,0:T(8,128)} custom-call(f32[8,256,128]{2,1,0:T(8,128)S(1)} %bitcast.10, f32[2,256,128]{2,1,0:T(8,128)S(1)} %bitcast.16, f32[16,64,128]{2,1,0:T(8,128)S(1)} %get-tuple-element.26.section, f32[4,8,128]{2,1,0:T(8,128)S(1)} %get-tuple-element.27.own, f32[8,64,128]{2,1,0:T(8,128)S(1)} %collective-permute-done.12.ra, ...), custom_call_target="tpu_custom_call" | custom-call | tf_op jit(solution)/shard_map/second_0/pallas_call | solution.py:380
  51.0 3.3 %second_4.1 = f32[8,256,128]{2,1,0:T(8,128)} custom-call(f32[8,256,128]{2,1,0:T(8,128)S(1)} %bitcast.11, f32[2,256,128]{2,1,0:T(8,128)S(1)} %bitcast.17, f32[16,64,128]{2,1,0:T(8,128)S(1)} %get-tuple-element.22.section, f32[4,8,128]{2,1,0:T(8,128)S(1)} %get-tuple-element.23.after.own, ...), custom_call_target="tpu_custom_call", output_to_operand_aliasing={{}: (13, {})} | custom-call | tf_op jit(solution)/shard_map/second_4/pallas_call | solution.py:380
  (46 shorter events, 4.9 us)
Async XLA Ops:
  0.6 1.2 %copy-start = (f32[8,64,4,128]{3,2,1,0:T(4,128)S(1)}, f32[8,64,4,128]{3,2,1,0:T(4,128)}, u32[]{:S(2)}) copy-start(f32[8,64,4,128]{3,2,1,0:T(4,128)} %param.9) | copy-start | bytes 3145732
  1.9 0.9 %copy-start.2 = (f32[2,64,4,128]{3,2,1,0:T(4,128)S(1)}, f32[2,64,4,128]{3,2,1,0:T(4,128)}, u32[]{:S(2)}) copy-start(f32[2,64,4,128]{3,2,1,0:T(4,128)} %param.10) | copy-start | bytes 786436
  3.3 14.7 %collective-permute-start.4 = (f32[9,64,128]{2,1,0:T(8,128)S(1)}, f32[9,64,128]{2,1,0:T(8,128)S(1)}, u32[]{:S(2)}, u32[]{:S(2)}) collective-permute-start(f32[9,64,128]{2,1,0:T(8,128)S(1)} %get-tuple-element.19), channel_id=1, source_target_pairs={{0,1},{1,0},{2,3},{3,2},{4,5},{5,4},{6,7},{7,6},{8,9},{9,8},{10,11... | collective-permute-start | bytes 884744 | tf_op jit(solution)/shard_map/ppermute | solution.py:27
  6.4 13.8 %collective-permute-start.5 = (f32[9,64,128]{2,1,0:T(8,128)S(1)}, f32[9,64,128]{2,1,0:T(8,128)S(1)}, u32[]{:S(2)}, u32[]{:S(2)}) collective-permute-start(f32[9,64,128]{2,1,0:T(8,128)S(1)} %get-tuple-element.20), channel_id=1, source_target_pairs={{1,2},{2,1},{5,6},{6,5},{9,10},{10,9},{13,14},{14,13},{17,18},{18,... | collective-permute-start | bytes 884744 | tf_op jit(solution)/shard_map/ppermute | solution.py:27
  7.5 17.4 %collective-permute-start = (f32[8,64,128]{2,1,0:T(8,128)S(1)}, f32[8,64,128]{2,1,0:T(8,128)S(1)}, u32[]{:S(2)}, u32[]{:S(2)}) collective-permute-start(f32[8,64,128]{2,1,0:T(8,128)S(1)} %get-tuple-element.17), channel_id=1, source_target_pairs={{0,1},{1,0},{2,3},{3,2},{4,5},{5,4},{6,7},{7,6},{8,9},{9,8},{10,11... | collective-permute-start | bytes 786440 | tf_op jit(solution)/shard_map/ppermute | solution.py:27
  11.9 12.9 %collective-permute-start.1 = (f32[8,64,128]{2,1,0:T(8,128)S(1)}, f32[8,64,128]{2,1,0:T(8,128)S(1)}, u32[]{:S(2)}, u32[]{:S(2)}) collective-permute-start(f32[8,64,128]{2,1,0:T(8,128)S(1)} %get-tuple-element.18), channel_id=1, source_target_pairs={{1,2},{2,1},{5,6},{6,5},{9,10},{10,9},{13,14},{14,13},{17,18},{18,... | collective-permute-start | bytes 786440 | tf_op jit(solution)/shard_map/ppermute | solution.py:27
  12.6 1.3 %collective-permute-start.6 = (f32[5,8,128]{2,1,0:T(8,128)S(1)}, f32[5,8,128]{2,1,0:T(8,128)S(1)}, u32[]{:S(2)}, u32[]{:S(2)}) collective-permute-start(f32[5,8,128]{2,1,0:T(8,128)S(1)} %get-tuple-element.21.own), channel_id=1, source_target_pairs={{0,4},{4,0},{8,12},{12,8},{16,20},{20,16},{24,28},{28,24},{1,5},{5... | collective-permute-start | bytes 61448 | tf_op jit(solution)/shard_map/ppermute | solution.py:27
  13.9 4.1 %collective-permute-start.7 = (f32[5,8,128]{2,1,0:T(8,128)S(1)}, f32[5,8,128]{2,1,0:T(8,128)S(1)}, u32[]{:S(2)}, u32[]{:S(2)}) collective-permute-start(f32[5,8,128]{2,1,0:T(8,128)S(1)} %get-tuple-element.21.own), channel_id=1, source_target_pairs={{4,8},{8,4},{12,16},{16,12},{20,24},{24,20},{28,0},{0,28},{5,9},{9... | collective-permute-start | bytes 61448 | tf_op jit(solution)/shard_map/ppermute | solution.py:27
  18.0 6.1 %collective-permute-start.2 = (f32[4,8,128]{2,1,0:T(8,128)S(1)}, f32[4,8,128]{2,1,0:T(8,128)S(1)}, u32[]{:S(2)}, u32[]{:S(2)}) collective-permute-start(f32[4,8,128]{2,1,0:T(8,128)S(1)} %get-tuple-element.16.own), channel_id=1, source_target_pairs={{0,4},{4,0},{8,12},{12,8},{16,20},{20,16},{24,28},{28,24},{1,5},{5... | collective-permute-start | bytes 49160 | tf_op jit(solution)/shard_map/ppermute | solution.py:27
  18.0 6.9 %collective-permute-start.3 = (f32[4,8,128]{2,1,0:T(8,128)S(1)}, f32[4,8,128]{2,1,0:T(8,128)S(1)}, u32[]{:S(2)}, u32[]{:S(2)}) collective-permute-start(f32[4,8,128]{2,1,0:T(8,128)S(1)} %get-tuple-element.16.own), channel_id=1, source_target_pairs={{4,8},{8,4},{12,16},{16,12},{20,24},{24,20},{28,0},{0,28},{5,9},{9... | collective-permute-start | bytes 49160 | tf_op jit(solution)/shard_map/ppermute | solution.py:27
  22.8 15.9 %collective-permute-start.12 = (f32[8,64,128]{2,1,0:T(8,128)S(1)}, f32[8,64,128]{2,1,0:T(8,128)S(1)}, u32[]{:S(2)}, u32[]{:S(2)}) collective-permute-start(f32[8,64,128]{2,1,0:T(8,128)S(1)} %get-tuple-element.28), channel_id=1, source_target_pairs={{0,1},{1,0},{2,3},{3,2},{4,5},{5,4},{6,7},{7,6},{8,9},{9,8},{10,11... | collective-permute-start | bytes 786440 | tf_op jit(solution)/shard_map/ppermute | solution.py:27
  24.1 16.1 %copy-start.1 = (f32[8,64,4,128]{3,2,1,0:T(4,128)S(1)}, f32[8,64,4,128]{3,2,1,0:T(4,128)}, u32[]{:S(2)}) copy-start(f32[8,64,4,128]{3,2,1,0:T(4,128)} %param.9) | copy-start | bytes 3145732
  24.1 23.6 %collective-permute-start.13 = (f32[8,64,128]{2,1,0:T(8,128)}, f32[8,64,128]{2,1,0:T(8,128)S(1)}, u32[]{:S(2)}, u32[]{:S(2)}) collective-permute-start(f32[8,64,128]{2,1,0:T(8,128)} %get-tuple-element.29), channel_id=1, source_target_pairs={{1,2},{2,1},{5,6},{6,5},{9,10},{10,9},{13,14},{14,13},{17,18},{18,... | collective-permute-start | bytes 786440 | tf_op jit(solution)/shard_map/ppermute | solution.py:27
  27.6 23.4 %collective-permute-start.8 = (f32[8,64,128]{2,1,0:T(8,128)}, f32[8,64,128]{2,1,0:T(8,128)S(1)}, u32[]{:S(2)}, u32[]{:S(2)}) collective-permute-start(f32[8,64,128]{2,1,0:T(8,128)} %get-tuple-element.24), channel_id=1, source_target_pairs={{0,1},{1,0},{2,3},{3,2},{4,5},{5,4},{6,7},{7,6},{8,9},{9,8},{10,11... | collective-permute-start | bytes 786440 | tf_op jit(solution)/shard_map/ppermute | solution.py:27
  30.8 20.1 %collective-permute-start.9 = (f32[8,64,128]{2,1,0:T(8,128)}, f32[8,64,128]{2,1,0:T(8,128)}, u32[]{:S(2)}, u32[]{:S(2)}) collective-permute-start(f32[8,64,128]{2,1,0:T(8,128)} %get-tuple-element.25), channel_id=1, source_target_pairs={{1,2},{2,1},{5,6},{6,5},{9,10},{10,9},{13,14},{14,13},{17,18},{18,... | collective-permute-start | bytes 786440 | tf_op jit(solution)/shard_map/ppermute | solution.py:27
  32.2 1.2 %collective-permute-start.14 = (f32[4,8,128]{2,1,0:T(8,128)S(1)}, f32[4,8,128]{2,1,0:T(8,128)S(1)}, u32[]{:S(2)}, u32[]{:S(2)}) collective-permute-start(f32[4,8,128]{2,1,0:T(8,128)S(1)} %get-tuple-element.27.own), channel_id=1, source_target_pairs={{0,4},{4,0},{8,12},{12,8},{16,20},{20,16},{24,28},{28,24},{1,5},{5... | collective-permute-start | bytes 49160 | tf_op jit(solution)/shard_map/ppermute | solution.py:27
  34.0 4.1 %collective-permute-start.15 = (f32[4,8,128]{2,1,0:T(8,128)S(1)}, f32[4,8,128]{2,1,0:T(8,128)S(1)}, u32[]{:S(2)}, u32[]{:S(2)}) collective-permute-start(f32[4,8,128]{2,1,0:T(8,128)S(1)} %get-tuple-element.27.own), channel_id=1, source_target_pairs={{4,8},{8,4},{12,16},{16,12},{20,24},{24,20},{28,0},{0,28},{5,9},{9... | collective-permute-start | bytes 49160 | tf_op jit(solution)/shard_map/ppermute | solution.py:27
  38.7 1.5 %copy-start.9 = (f32[4,128]{1,0:T(4,128)S(1)}, f32[4,128]{1,0:T(4,128)}, u32[]{:S(2)}) copy-start(f32[4,128]{1,0:T(4,128)} %cosz.1) | copy-start | bytes 6148
  38.7 12.3 %collective-permute-start.10 = (f32[4,8,128]{2,1,0:T(8,128)S(1)}, f32[4,8,128]{2,1,0:T(8,128)}, u32[]{:S(2)}, u32[]{:S(2)}) collective-permute-start(f32[4,8,128]{2,1,0:T(8,128)S(1)} %get-tuple-element.23.after.own), channel_id=1, source_target_pairs={{0,4},{4,0},{8,12},{12,8},{16,20},{20,16},{24,28},{28,24},{1,5},{5... | collective-permute-start | bytes 49160 | tf_op jit(solution)/shard_map/ppermute | solution.py:27
  38.7 12.3 %collective-permute-start.11 = (f32[4,8,128]{2,1,0:T(8,128)S(1)}, f32[4,8,128]{2,1,0:T(8,128)}, u32[]{:S(2)}, u32[]{:S(2)}) collective-permute-start(f32[4,8,128]{2,1,0:T(8,128)S(1)} %get-tuple-element.23.after.own), channel_id=1, source_target_pairs={{4,8},{8,4},{12,16},{16,12},{20,24},{24,20},{28,0},{0,28},{5,9},{9... | collective-permute-start | bytes 49160 | tf_op jit(solution)/shard_map/ppermute | solution.py:27
  42.2 5.5 %copy-start.3 = (f32[2,64,4,128]{3,2,1,0:T(4,128)S(1)}, f32[2,64,4,128]{3,2,1,0:T(4,128)}, u32[]{:S(2)}) copy-start(f32[2,64,4,128]{3,2,1,0:T(4,128)} %param.10) | copy-start | bytes 786436
  42.2 5.5 %copy-start.6 = (f32[4,8,128]{2,1,0:T(8,128)S(1)}, f32[4,8,128]{2,1,0:T(8,128)}, u32[]{:S(2)}) copy-start(f32[4,8,128]{2,1,0:T(8,128)} %copy-done.5) | copy-start | bytes 49156
  42.2 5.5 %copy-start.8 = (f32[4,8,128]{2,1,0:T(8,128)S(1)}, f32[4,8,128]{2,1,0:T(8,128)}, u32[]{:S(2)}) copy-start(f32[4,8,128]{2,1,0:T(8,128)} %copy-done.7) | copy-start | bytes 49156
  47.6 0.9 %copy-start.4 = (f32[256,128]{1,0:T(8,128)S(1)}, f32[256,128]{1,0:T(8,128)}, u32[]{:S(2)}) copy-start(f32[256,128]{1,0:T(8,128)} %radiation.1.heating) | copy-start | bytes 393220
  (7 other events, 4.6 us)

commit v2 on v1

v2 whole, which is shorter than its diff:
```python
import functools
import math

import jax
import jax.numpy as jnp
from jax import lax
from jax.experimental import pallas as pl
from jax.experimental.pallas import tpu as pltpu
from jax.sharding import PartitionSpec as P

SPLIT = 2
SUB = 8
LANES = 128
LOG2E = math.log2(math.e)
VMEM = pl.BlockSpec(memory_space=pltpu.VMEM)
SMEM = pl.BlockSpec(memory_space=pltpu.SMEM)
ANY = pl.BlockSpec(memory_space=pl.ANY)
PARAMS = pltpu.CompilerParams(vmem_limit_bytes=24 * 1024 * 1024)


def scratch(*dims):
    return pltpu.VMEM(dims, jnp.float32)


def shape(*dims):
    return jax.ShapeDtypeStruct(dims, jnp.float32)


def swaps(first_block, second_block, axis, ring):
    n = lax.axis_size(axis)
    first = [(i, i ^ 1) for i in range(n)]
    second = []
    for i in range(1, n if ring else n - 1, 2):
        second += [(i, (i + 1) % n), ((i + 1) % n, i)]
    return lax.ppermute(first_block, axis, first), lax.ppermute(second_block, axis, second)


def is_even(axis):
    return lax.rem(lax.axis_index(axis), 2) == 0


def native(ref, index, r, nrows):
    levels = ref.shape[1] // nrows
    return ref[index, pl.ds(r, levels, stride=nrows), :]


def tile_of(low, high):
    return jnp.transpose(jnp.concatenate([low, high], axis=0))


def put_lat_sends(even, tiles, pair, nrows, za, zb):
    north = jnp.where(even, 2, 0)
    for k in range(2):
        span = pl.ds(pl.multiple_of((2 * pair + k) * LANES, LANES), LANES)
        za[span, :] = tiles[nrows * pair + north + k]
        zb[span, :] = tiles[nrows * pair + (2 - north) + k]


def put_lon_sends(even, tiles, pair, at, nrows, la, lb):
    for r in range(nrows):
        west = tiles[nrows * pair + r, pl.ds(0, 2), :]
        east = tiles[nrows * pair + r, pl.ds(LANES - 2, 2), :]
        la[pl.ds(at + 2 * r, 2), :] = jnp.where(even, east, west)
        lb[pl.ds(at + 2 * r, 2), :] = jnp.where(even, west, east)


def pack_first(pairs, nrows, fields, courant, tiles, za, zb, nat, nat_late, nat_wind, sems):
    n = 2 * pairs
    copies = [pltpu.make_async_copy(fields.at[i], nat.at[i], sems.at[i]) for i in range(n)]
    wind = pltpu.make_async_copy(courant, nat_wind, sems.at[n])
    late = pltpu.make_async_copy(fields.at[pl.ds(n, nat_late.shape[0])], nat_late, sems.at[n + 1])
    for copy in copies + [wind, late]:
        copy.start()
    even = is_even("lat")
    for p in range(pairs):
        copies[2 * p].wait()
        copies[2 * p + 1].wait()
        for r in range(nrows):
            tiles[nrows * p + r] = tile_of(native(nat, 2 * p, r, nrows), native(nat, 2 * p + 1, r, nrows))
        put_lat_sends(even, tiles, p, nrows, za, zb)
    wind.wait()
    top = native(nat_wind, 1, nrows - 1, nrows) * (1.0 / 12.0)
    top = tile_of(top, top)
    half = LANES // 2
    lane = lax.broadcasted_iota(jnp.int32, (half, LANES), 1)
    top = jnp.where(lane < half, top[:half], top[half:])
    span = pl.ds(2 * pairs * LANES, half)
    za[span, :] = top
    zb[span, :] = top
    late.wait()


def pack_second(pairs, nrows, nat, nat_wind, tiles_first, tiles, za, zb, ce, cn, la, lb):
    lat_even, lon_even = is_even("lat"), is_even("lon")
    for p in range(pairs):
        for r in range(nrows):
            tiles[nrows * p + r] = tile_of(native(nat, 2 * p, r, nrows), native(nat, 2 * p + 1, r, nrows))
        put_lat_sends(lat_even, tiles, p, nrows, za, zb)
    for r in range(nrows):
        east = native(nat_wind, 0, r, nrows) * (1.0 / 12.0)
        north = native(nat_wind, 1, r, nrows) * (1.0 / 12.0)
        ce[r] = tile_of(east, east)
        cn[r] = tile_of(north, north)
    early = tiles_first.shape[0] // nrows
    for p in range(early):
        put_lon_sends(lon_even, tiles_first, p, 2 * nrows * p, nrows, la, lb)
    for p in range(pairs):
        put_lon_sends(lon_even, tiles, p, 2 * nrows * (early + p), nrows, la, lb)
    at = 2 * nrows * (early + pairs)
    for r in range(nrows):
        edge = ce[r, pl.ds(LANES - 1, 1), :]
        la[pl.ds(at + r, 1), :] = edge
        lb[pl.ds(at + r, 1), :] = edge


def put_sides(even, la, lb, west, east):
    rows = la.shape[0]
    a, b = la[...], lb[...]
    west[pl.ds(SUB, rows), :] = jnp.where(even, b, a)
    east[pl.ds(SUB, rows), :] = jnp.where(even, a, b)


def put_edges(q, pair, at, nrows, west, east, edge_w, edge_e):
    for r in range(nrows):
        tile = nrows * pair + r
        edge_w[r, pl.ds(0, SUB), :] = west[pl.ds(at + 2 + 2 * r, SUB), :]
        edge_w[r, pl.ds(SUB, SUB), :] = q[tile, pl.ds(0, SUB), :]
        edge_e[r, pl.ds(0, SUB), :] = q[tile, pl.ds(LANES - SUB, SUB), :]
        edge_e[r, pl.ds(SUB, SUB), :] = east[pl.ds(at + SUB + 2 * r, SUB), :]


def put_wind_edges(ce, at, nrows, west, edge_c):
    for r in range(nrows):
        edge_c[r, pl.ds(0, SUB), :] = west[pl.ds(at + 1 + r, SUB), :]
        edge_c[r, pl.ds(SUB, SUB), :] = ce[r, pl.ds(0, SUB), :]


def put_fluxes(q, pair, nrows, ce, edge_w, edge_e, edge_c, flux):
    def face(c, left, here, right, right_two):
        return c * (7.0 * (here + right) - (left + right_two))

    for r in range(nrows):
        tile = nrows * pair + r
        window = [edge_w[r, pl.ds(k, SUB), :] for k in range(4)]
        flux[r, pl.ds(1, SUB), :] = face(edge_c[r, pl.ds(1, SUB), :], *window)
        for b in range(LANES // SUB):
            at = SUB * b

            def load(shift):
                if at + shift < 0:
                    return edge_w[r, pl.ds(SUB + shift, SUB), :]
                if at + shift + SUB > LANES:
                    return edge_e[r, pl.ds(shift, SUB), :]
                return q[tile, pl.ds(at + shift, SUB), :]

            flux[r, pl.ds(SUB + at, SUB), :] = face(
                ce[r, pl.ds(at, SUB), :], load(-1), load(0), load(1), load(2)
            )


def divergence(q, pair, nrows, b, lat_even, ra, rb, cn, below, flux):
    at = SUB * b
    here = pl.ds(at, SUB)

    def halo(k):
        span = pl.ds(pl.multiple_of((2 * pair + k) * LANES, LANES) + at, SUB)
        a, b_ = ra[span, :], rb[span, :]
        return jnp.where(lat_even, b_, a), jnp.where(lat_even, a, b_)

    (s0, n0), (s1, n1) = halo(0), halo(1)
    own = [q[nrows * pair + r, here, :] for r in range(nrows)]
    rows = [s0, s1] + own + [n0, n1]
    winds = [below[here, :]] + [cn[r, here, :] for r in range(nrows)]
    north = []
    for r in range(nrows + 1):
        north.append(winds[r] * (7.0 * (rows[r + 1] + rows[r + 2]) - (rows[r] + rows[r + 3])))
    div = []
    for r in range(nrows):
        east = flux[r, pl.ds(SUB + at, SUB), :] - flux[r, pl.ds(SUB + at - 1, SUB), :]
        div.append(east + (north[r + 1] - north[r]))
    return own, div


def edge_scratch(nrows, lon_rows):
    return [
        scratch(lon_rows + 2 * SUB, LANES),
        scratch(lon_rows + 2 * SUB, LANES),
        scratch(nrows, 2 * SUB, LANES),
        scratch(nrows, 2 * SUB, LANES),
        scratch(nrows, 2 * SUB, LANES),
        scratch(nrows, LANES + SUB, LANES),
    ]


def first_stage(pairs, done, nrows, is_first, *refs):
    q, ce, cn, ra, rb, la, lb = refs[:7]
    refs = refs[7:]
    lat_even, lon_even = is_even("lat"), is_even("lon")
    if is_first:
        section, za, zb, below, *refs = refs
        half = LANES // 2
        span = pl.ds(2 * pairs * LANES, half)
        a = jnp.where(lat_even, rb[span, :], ra[span, :])
        turned = pltpu.roll(a, half, 1)
        low = lax.broadcasted_iota(jnp.int32, (half, LANES), 1) < half
        below[pl.ds(0, half), :] = jnp.where(low, a, turned)
        below[pl.ds(half, half), :] = jnp.where(low, turned, a)
    else:
        below, earlier, section, za, zb, sa, sb, *refs = refs
    west, east, edge_w, edge_e, edge_c, flux = refs
    put_sides(lon_even, la, lb, west, east)
    put_wind_edges(ce, la.shape[0] - SUB, nrows, west, edge_c)

    def one(p, _):
        put_edges(q, p, 2 * nrows * (done + p), nrows, west, east, edge_w, edge_e)
        put_fluxes(q, p, nrows, ce, edge_w, edge_e, edge_c, flux)
        for b in range(LANES // SUB):
            own, div = divergence(q, p, nrows, b, lat_even, ra, rb, cn, below, flux)
            for r in range(nrows):
                section[nrows * p + r, pl.ds(SUB * b, SUB), :] = own[r] - div[r]
        put_lat_sends(lat_even, section, p, nrows, za, zb)
        return 0

    lax.fori_loop(0, pairs, one, 0)
    if not is_first:
        for p in range(done):
            put_lon_sends(lon_even, earlier, p, 2 * nrows * p, nrows, sa, sb)
        for p in range(pairs):
            put_lon_sends(lon_even, section, p, 2 * nrows * (done + p), nrows, sa, sb)


def second_stage(pairs, done, nrows, is_first, *refs):
    q, s, ce, cn, below, ra, rb, la, lb, sa, sb, heating = refs[:12]
    out, buffer, sems, west, east, edge_w, edge_e, edge_c, flux, wind_w, wind_e = refs[-11:]
    levels = LANES // 2
    lat_even, lon_even = is_even("lat"), is_even("lon")
    put_sides(lon_even, la, lb, wind_w, wind_e)
    put_wind_edges(ce, la.shape[0] - SUB, nrows, wind_w, edge_c)
    put_sides(lon_even, sa, sb, west, east)

    def copy(p):
        return pltpu.make_async_copy(
            buffer.at[pl.ds(2 * p, 2)], out.at[pl.ds(2 * (done + p), 2)], sems.at[p]
        )

    def one(p, _):
        put_edges(s, p, 2 * nrows * (done + p), nrows, west, east, edge_w, edge_e)
        put_fluxes(s, p, nrows, ce, edge_w, edge_e, edge_c, flux)
        parts = [[] for _ in range(nrows)]
        for b in range(LANES // SUB):
            own, div = divergence(s, p, nrows, b, lat_even, ra, rb, cn, below, flux)
            for r in range(nrows):
                old = q[nrows * p + r, pl.ds(SUB * b, SUB), :]
                parts[r].append(0.5 * ((old + own[r]) - div[r]))
        for r in range(nrows):
            turned = jnp.transpose(jnp.concatenate(parts[r], axis=0))
            for h in range(2):
                buffer[2 * p + h, pl.ds(r, levels, stride=nrows), :] = turned[levels * h : levels * (h + 1)]
        if is_first:

            @pl.when(p == 0)
            def _():
                buffer[0] = buffer[0] + 0.5 * heating[...]

        copy(p).start()
        return 0

    lax.fori_loop(0, pairs, one, 0)
    for p in range(pairs):
        copy(p).wait()


def radiation(
    nat, cosz_in, albedo_in, ext_in, single_in, weight_in, order_in, count_in, after, heat,
    water, depth, save_a, save_b, save_t, save_g, cosz, albedo, ext, single, weight, order, count, sems
):
    del after
    copies = []
    for i, (src, dst) in enumerate(
        (
            (cosz_in, cosz), (albedo_in, albedo), (ext_in, ext), (single_in, single),
            (weight_in, weight), (order_in, order), (count_in, count),
        )
    ):
        copies.append(pltpu.make_async_copy(src, dst, sems.at[i]))
        copies[-1].start()
    nrows, _ = cosz.shape
    levels = nat.shape[1] // nrows
    pairs = ext.shape[0] // 2
    x = nat[1]
    heat[...] = jnp.maximum(x, 0.0) + jnp.log1p(jnp.exp(-jnp.abs(x)))
    total = jnp.zeros((nrows, LANES), jnp.float32)
    depth[0] = jnp.zeros((2 * nrows, LANES), jnp.float32)
    for l in range(levels):
        w = heat[pl.ds(nrows * l, nrows), :]
        total = total + w
        water[l, pl.ds(0, nrows), :] = w
        water[l, pl.ds(nrows, nrows), :] = w
        depth[l + 1, pl.ds(0, nrows), :] = total
        depth[l + 1, pl.ds(nrows, nrows), :] = total
    for copy in copies:
        copy.wait()

    mu = jnp.concatenate([cosz[...], cosz[...]], axis=0)
    floor_albedo = jnp.concatenate([albedo[...], albedo[...]], axis=0)
    first = lax.broadcasted_iota(jnp.int32, (2 * nrows, LANES), 0) < nrows

    def by_band(ref):
        return [jnp.where(first, ref[2 * p], ref[2 * p + 1]) for p in range(pairs)]

    scale = 4.0 / levels
    inv_mu = 1.0 / mu
    ext_of, half_of, weight_of = by_band(ext), by_band(single), by_band(weight)
    beam = [-(e * scale * LOG2E) * inv_mu for e in ext_of]
    diffuse = [-(1.66 * scale * LOG2E) * e for e in ext_of]
    half = [0.5 * s for s in half_of]
    strength = [w * mu for w in weight_of]

    def up(step, carry):
        l = levels - 1 - step
        a_all, b_all, s_all = carry
        w = water[l]
        above = depth[l]
        new_a, new_b, new_s = [], [], []
        for p in range(pairs):
            a, b, s_bot = a_all[p], b_all[p], s_all[p]
            decay = jnp.exp2(diffuse[p] * w)
            s_top = strength[p] * jnp.exp2(beam[p] * above)
            reflect = half[p] - half[p] * decay
            transmit = decay + reflect
            source = half[p] * (s_top - s_bot)
            den = 1.0 - reflect * a
            inv = pl.reciprocal(den, approx=True)
            inv = inv * (2.0 - den * inv)
            t = transmit * inv
            a_here = reflect + transmit * (t * a)
            b_here = t * (a * source + b) + source
            save_t[l, p] = t
            save_g[l, p] = (reflect * b + source) * inv
            save_a[l, p] = 1.0 - a_here
            save_b[l, p] = s_top - b_here
            new_a.append(a_here)
            new_b.append(b_here)
            new_s.append(s_top)
        return tuple(new_a), tuple(new_b), tuple(new_s)

    s_floor = [strength[p] * jnp.exp2(beam[p] * depth[levels]) for p in range(pairs)]
    a_floor = [floor_albedo for _ in range(pairs)]
    b_floor = [floor_albedo * s_floor[p] for p in range(pairs)]
    lax.fori_loop(0, levels, up, (tuple(a_floor), tuple(b_floor), tuple(s_floor)))

    sunlit = []
    column = lax.broadcasted_iota(jnp.int32, (LANES, LANES), 1)
    rank = lax.broadcasted_iota(jnp.int32, (LANES, LANES), 0)
    for r in range(nrows):
        place = jnp.transpose(jnp.broadcast_to(order[r], (LANES, LANES)))
        hit = (place == column) & (rank < count[r])
        sunlit.append(jnp.max(jnp.where(hit, 1.0, 0.0), axis=0, keepdims=True))
    gain = float(levels) * jnp.concatenate(sunlit, axis=0)

    def net_flux(l, d_all):
        net = jnp.zeros((2 * nrows, LANES), jnp.float32)
        for p in range(pairs):
            net = net + (save_b[l, p] + d_all[p] * save_a[l, p])
        return net

    def put(l, absorbed):
        both = absorbed[:nrows] + absorbed[nrows:]
        heat[pl.ds(pl.multiple_of(nrows * l, nrows), nrows), :] = gain * both

    def down(l, carry):
        d_all, net_above = carry
        d_new = tuple(save_t[l - 1, p] * d_all[p] + save_g[l - 1, p] for p in range(pairs))
        net = net_flux(l, d_new)
        put(l - 1, net_above - net)
        return d_new, net

    d_top = tuple(jnp.zeros((2 * nrows, LANES), jnp.float32) for _ in range(pairs))
    d_low, net_low = lax.fori_loop(1, levels, down, (d_top, net_flux(0, d_top)))
    net = jnp.zeros((2 * nrows, LANES), jnp.float32)
    for p in range(pairs):
        d_floor = save_t[levels - 1, p] * d_low[p] + save_g[levels - 1, p]
        net = net + ((s_floor[p] - b_floor[p]) + d_floor * (1.0 - a_floor[p]))
    put(levels - 1, net_low - net)


def call(kernel, name, out_shape, specs, out_specs, args, scratches, **kw):
    return pl.pallas_call(
        kernel,
        out_shape=out_shape,
        in_specs=specs,
        out_specs=out_specs,
        scratch_shapes=scratches,
        compiler_params=PARAMS,
        name=name,
        **kw,
    )(*args)


def per_device(
    fields, courant, cos_zenith, albedo, extinction, single_albedo, band_weight, sun_order, sun_count
):
    nfields, levels, nrows, ncols = fields.shape
    flat = fields.reshape(nfields, levels * nrows, ncols)
    wind = courant.reshape(2, levels * nrows, ncols)
    npairs = nfields // 2
    counts = (SPLIT, npairs - SPLIT)
    starts = (0, SPLIT)
    early, late = counts
    lon_rows = 2 * nrows * npairs

    z0 = shape((2 * early) * ncols + ncols // 2, LANES)
    tiles0, za, zb, nat, nat_late, nat_wind = call(
        functools.partial(pack_first, early, nrows),
        "pack_first",
        (
            shape(nrows * early, ncols, LANES), z0, z0,
            shape(2 * early, levels * nrows, ncols), shape(2 * late, levels * nrows, ncols),
            shape(2, levels * nrows, ncols),
        ),
        [ANY, ANY],
        (VMEM,) * 6,
        (flat, wind),
        [pltpu.SemaphoreType.DMA((2 * early + 2,))],
    )
    lat0 = swaps(za, zb, "lat", False)
    z1 = shape(2 * late * ncols, LANES)
    lon = shape(lon_rows + SUB, LANES)
    winds = shape(nrows, ncols, LANES)
    tiles1, za, zb, ce, cn, la, lb = call(
        functools.partial(pack_second, late, nrows),
        "pack_second",
        (shape(nrows * late, ncols, LANES), z1, z1, winds, winds, lon, lon),
        [VMEM] * 3,
        (VMEM,) * 7,
        (nat_late, nat_wind, tiles0),
        [],
    )
    lon_q = swaps(la, lb, "lon", True)
    lat1 = swaps(za, zb, "lat", False)

    edges = edge_scratch(nrows, lon_rows + SUB)
    z0 = shape(2 * early * ncols, LANES)
    section0, za, zb, below = call(
        functools.partial(first_stage, early, 0, nrows, True),
        "first_stage_0",
        (shape(nrows * early, ncols, LANES), z0, z0, shape(ncols, LANES)),
        [VMEM] * 7,
        (VMEM,) * 4,
        (tiles0, ce, cn, *lat0, *lon_q),
        edges,
    )
    lat2 = swaps(za, zb, "lat", False)
    lon = shape(lon_rows, LANES)
    section1, za, zb, la, lb = call(
        functools.partial(first_stage, late, early, nrows, False),
        "first_stage_1",
        (shape(nrows * late, ncols, LANES), z1, z1, lon, lon),
        [VMEM] * 9,
        (VMEM,) * 5,
        (tiles1, ce, cn, *lat1, *lon_q, below, section0),
        edges,
    )
    lat3 = swaps(za, zb, "lat", False)
    lon_s = swaps(la, lb, "lon", True)

    pairs = extinction.shape[0] // 2
    store = scratch(levels, pairs, 2 * nrows, ncols)
    heating = call(
        radiation,
        "radiation",
        shape(levels * nrows, ncols),
        [VMEM] + [ANY] * 8,
        VMEM,
        (
            nat, cos_zenith, albedo, extinction, single_albedo, band_weight, sun_order,
            sun_count.reshape(nrows), la,
        ),
        [
            scratch(levels, 2 * nrows, ncols), scratch(levels + 1, 2 * nrows, ncols),
            store, store, store, store,
            scratch(nrows, ncols), scratch(nrows, ncols),
            pltpu.SMEM(extinction.shape, jnp.float32), pltpu.SMEM(extinction.shape, jnp.float32),
            pltpu.SMEM(extinction.shape, jnp.float32), pltpu.VMEM((nrows, 1, ncols), jnp.int32),
            pltpu.SMEM((nrows,), jnp.int32), pltpu.SemaphoreType.DMA((7,)),
        ],
        cost_estimate=pl.CostEstimate(flops=20_000_000, bytes_accessed=400_000, transcendentals=1_500_000),
    )

    out = None
    for g, (tiles, section, lat) in enumerate(((tiles0, section0, lat2), (tiles1, section1, lat3))):
        args = [tiles, section, ce, cn, below, *lat, *lon_q, *lon_s, heating]
        specs = [VMEM] * len(args)
        aliases = {}
        if out is not None:
            aliases = {len(args): 0}
            args.append(out)
            specs.append(ANY)
        out = call(
            functools.partial(second_stage, counts[g], starts[g], nrows, g == 0),
            f"second_stage_{g}",
            shape(nfields, levels * nrows, ncols),
            specs,
            ANY,
            args,
            [
                scratch(2 * counts[g], levels * nrows, ncols),
                pltpu.SemaphoreType.DMA((counts[g],)),
                *edge_scratch(nrows, lon_rows),
                scratch(lon_rows + 3 * SUB, LANES),
                scratch(lon_rows + 3 * SUB, LANES),
            ],
            input_output_aliases=aliases,
        )
    return out.reshape(fields.shape), heating.reshape(levels, nrows, ncols)


def solution(mesh):
    in_specs = (
        P(None, None, "lat", "lon"),
        P(None, None, "lat", "lon"),
        P("lat", "lon"),
        P("lat", "lon"),
        P(),
        P(),
        P(),
        P("lat", "lon", None),
        P("lat", "lon"),
    )
    out_specs = (P(None, None, "lat", "lon"), P(None, "lat", "lon"))
    return jax.shard_map(
        per_device, mesh=mesh, in_specs=in_specs, out_specs=out_specs, check_vma=False
    )
```

time: 54.7 us -> 40.7 us (0.74)
  Pallas kernels: 17.4 us -> 10.7 us
  local copies, waits for them, and re-layouts: 7.05 us -> 3.75 us
  starting transfers between devices: 21.4 us -> 18.9 us
  waiting for transfers between devices: 7.7 us -> 5.68 us
    pallas_call x7, Pallas kernels: 17.4 us -> 10.7 us  [call(): pl.pallas_call(kernel, out_shape=out_shape, in_specs=specs, out_specs=out...]
    unnamed x31 -> x20, local copies, waits for them, and re-layouts: 7.05 us -> 3.75 us
    ppermute x16 -> x12, starting transfers between devices: 21.4 us -> 18.9 us  [the longest x6 12.4 us: swaps(): lax.ppermute(first_block, axis, first)]
    ppermute x16 -> x12, waiting for transfers between devices: 7.7 us -> 5.68 us  [the longest x6 4.49 us: swaps(): lax.ppermute(second_block, axis, second)]
  transfers between devices with their start and end apart: 16 -> 12, of which waited for: 4 -> 3; matrix products, arithmetic and copies ran while one was open for 1% -> 0% of each run, Pallas kernels for 25% -> 20%
where the time goes in v2:
time: 40.7 us; the launch traced here: 39.9 us
  starting transfers between devices  18.9 us (46%)
  Pallas kernels  10.7 us (26%)
  waiting for transfers between devices  5.68 us (14%)
  local copies, waits for them, and re-layouts  3.75 us (9%)
  between operations  0.84 us (2%)
    ppermute x6, starting transfers between devices, swaps(): lax.ppermute(first_block, axis, first)  12.4 us
    pallas_call x7, Pallas kernels, call(): pl.pallas_call(kernel, out_shape=out_shape, in_specs=specs, out_specs=out...  10.7 us
    ppermute x6, starting transfers between devices, swaps(): lax.ppermute(second_block, axis, second)  6.49 us
    ppermute x6, waiting for transfers between devices, swaps(): lax.ppermute(second_block, axis, second)  4.49 us
    unnamed x20, local copies, waits for them, and re-layouts  3.75 us
    ppermute x6, waiting for transfers between devices, swaps(): lax.ppermute(first_block, axis, first)  1.19 us
  transfers between devices with their start and end apart: 12, of which 3 were waited for; matrix products, arithmetic and copies ran while one was open for 0% of the time, Pallas kernels for 20%

profile of v2, /device:TPU:0, one launch (start us, length us, event | category | flops | bytes accessed | tf_op | source)
XLA Modules:
  0.0 39.9 jit_solution(15294511099772081097)
XLA Ops:
  0.6 1.2 %copy-done = f32[8,64,4,128]{3,2,1,0:T(4,128)S(1)} copy-done((f32[8,64,4,128]{3,2,1,0:T(4,128)S(1)}, f32[8,64,4,128]{3,2,1,0:T(4,128)}, u32[]{:S(2)}) %copy-start) | copy-done | bytes 1048600
  1.9 0.9 %copy-done.2 = f32[2,64,4,128]{3,2,1,0:T(4,128)S(1)} copy-done((f32[2,64,4,128]{3,2,1,0:T(4,128)S(1)}, f32[2,64,4,128]{3,2,1,0:T(4,128)}, u32[]{:S(2)}) %copy-start.2) | copy-done | bytes 262168
  2.8 1.2 %pack_first.1 = (f32[8,128,128]{2,1,0:T(8,128)S(1)}, f32[576,128]{1,0:T(8,128)S(1)}, f32[576,128]{1,0:T(8,128)S(1)}, f32[4,256,128]{2,1,0:T(8,128)S(1)}, f32[4,2...) custom-call(f32[8,256,128]{2,1,0:T(8,128)S(1)} %bitcast.5, f32[2,256,128]{2,1,0:T(8,128)S(1)} %bitcast.7), custom_call_target="tpu_custom_call" | custom-call | tf_op jit(solution)/shard_map/pack_first/pallas_call | solution.py:388
  4.0 3.1 %collective-permute-start.4 = (f32[576,128]{1,0:T(8,128)S(1)}, f32[576,128]{1,0:T(8,128)S(1)}, u32[]{:S(2)}, u32[]{:S(2)}) collective-permute-start(f32[576,128]{1,0:T(8,128)S(1)} %get-tuple-element.34), channel_id=1, source_target_pairs={{0,1},{1,0},{2,3},{3,2},{4,5},{5,4},{6,7},{7,6},{8,9},{9,8},{10,11... | collective-permute-start | bytes 884744 | tf_op jit(solution)/shard_map/ppermute | solution.py:35
  7.1 0.7 %collective-permute-start.5 = (f32[576,128]{1,0:T(8,128)S(1)}, f32[576,128]{1,0:T(8,128)S(1)}, u32[]{:S(2)}, u32[]{:S(2)}) collective-permute-start(f32[576,128]{1,0:T(8,128)S(1)} %get-tuple-element.35), channel_id=1, source_target_pairs={{1,2},{2,1},{5,6},{6,5},{9,10},{10,9},{13,14},{14,13},{17,18},{18,... | collective-permute-start | bytes 884744 | tf_op jit(solution)/shard_map/ppermute | solution.py:35
  7.8 0.4 %pack_second.1 = (f32[8,128,128]{2,1,0:T(8,128)S(1)}, f32[512,128]{1,0:T(8,128)S(1)}, f32[512,128]{1,0:T(8,128)S(1)}, f32[4,128,128]{2,1,0:T(8,128)S(1)}, f32[4,...) custom-call(f32[4,256,128]{2,1,0:T(8,128)S(1)} %get-tuple-element.24.nat, ...), custom_call_target="tpu_custom_call" | custom-call | tf_op jit(solution)/shard_map/pack_second/pallas_call | solution.py:388
  8.2 4.4 %collective-permute-start = (f32[512,128]{1,0:T(8,128)S(1)}, f32[512,128]{1,0:T(8,128)S(1)}, u32[]{:S(2)}, u32[]{:S(2)}) collective-permute-start(f32[512,128]{1,0:T(8,128)S(1)} %get-tuple-element.30), channel_id=1, source_target_pairs={{0,1},{1,0},{2,3},{3,2},{4,5},{5,4},{6,7},{7,6},{8,9},{9,8},{10,11... | collective-permute-start | bytes 786440 | tf_op jit(solution)/shard_map/ppermute | solution.py:35
  12.6 0.7 %collective-permute-start.1 = (f32[512,128]{1,0:T(8,128)S(1)}, f32[512,128]{1,0:T(8,128)S(1)}, u32[]{:S(2)}, u32[]{:S(2)}) collective-permute-start(f32[512,128]{1,0:T(8,128)S(1)} %get-tuple-element.31), channel_id=1, source_target_pairs={{1,2},{2,1},{5,6},{6,5},{9,10},{10,9},{13,14},{14,13},{17,18},{18,... | collective-permute-start | bytes 786440 | tf_op jit(solution)/shard_map/ppermute | solution.py:35
  13.4 1.2 %collective-permute-done.2.refs_5_.refs_7_ = f32[40,128]{1,0:T(8,128)S(1)} collective-permute-done((f32[40,128]{1,0:T(8,128)S(1)}, f32[40,128]{1,0:T(8,128)S(1)}, u32[]{:S(2)}, u32[]{:S(2)}) %collective-permute-start.2) | collective-permute-done | bytes 20512 | tf_op jit(solution)/shard_map/ppermute | solution.py:35
  14.6 2.2 %collective-permute-start.3 = (f32[40,128]{1,0:T(8,128)S(1)}, f32[40,128]{1,0:T(8,128)S(1)}, u32[]{:S(2)}, u32[]{:S(2)}) collective-permute-start(f32[40,128]{1,0:T(8,128)S(1)} %get-tuple-element.33), channel_id=1, source_target_pairs={{4,8},{8,4},{12,16},{16,12},{20,24},{24,20},{28,0},{0,28},{5,9},{9... | collective-permute-start | bytes 61448 | tf_op jit(solution)/shard_map/ppermute | solution.py:35
  16.8 1.9 %collective-permute-done.3.refs_6_.refs_8_ = f32[40,128]{1,0:T(8,128)S(1)} collective-permute-done((f32[40,128]{1,0:T(8,128)S(1)}, f32[40,128]{1,0:T(8,128)S(1)}, u32[]{:S(2)}, u32[]{:S(2)}) %collective-permute-start.3) | collective-permute-done | bytes 20512 | tf_op jit(solution)/shard_map/ppermute | solution.py:35
  18.7 0.5 %first_stage_0.1 = (f32[8,128,128]{2,1,0:T(8,128)S(1)}, f32[512,128]{1,0:T(8,128)S(1)}, f32[512,128]{1,0:T(8,128)S(1)}, f32[128,128]{1,0:T(8,128)S(1)}) custom-call(f32[8,128,128]{2,1,0:T(8,128)S(1)} %get-tuple-element.26.tiles_first.refs_0_, f32[4,128,128]{2,1,0:T(8,128)S(1)} %get-tuple-element.28.refs_1_.refs_2_, ...), custom_call_target="tpu_custom_call" | custom-call | tf_op jit(solution)/shard_map/first_stage_0/pallas_call | solution.py:388
  19.2 1.4 %collective-permute-start.10 = (f32[512,128]{1,0:T(8,128)S(1)}, f32[512,128]{1,0:T(8,128)S(1)}, u32[]{:S(2)}, u32[]{:S(2)}) collective-permute-start(f32[512,128]{1,0:T(8,128)S(1)} %get-tuple-element.44), channel_id=1, source_target_pairs={{0,1},{1,0},{2,3},{3,2},{4,5},{5,4},{6,7},{7,6},{8,9},{9,8},{10,11... | collective-permute-start | bytes 786440 | tf_op jit(solution)/shard_map/ppermute | solution.py:35
  20.6 0.7 %collective-permute-start.11 = (f32[512,128]{1,0:T(8,128)S(1)}, f32[512,128]{1,0:T(8,128)S(1)}, u32[]{:S(2)}, u32[]{:S(2)}) collective-permute-start(f32[512,128]{1,0:T(8,128)S(1)} %get-tuple-element.45), channel_id=1, source_target_pairs={{1,2},{2,1},{5,6},{6,5},{9,10},{10,9},{13,14},{14,13},{17,18},{18,... | collective-permute-start | bytes 786440 | tf_op jit(solution)/shard_map/ppermute | solution.py:35
  21.3 0.5 %first_stage_1.1 = (f32[8,128,128]{2,1,0:T(8,128)S(1)}, f32[512,128]{1,0:T(8,128)S(1)}, f32[512,128]{1,0:T(8,128)S(1)}, f32[32,128]{1,0:T(8,128)S(1)}, f32[32,128]{1,0:T(8,128)S(1)}) custom-call(f32[8,128,128]{2,1,0:T(8,128)S(1)} %get-tuple-element.27.refs_0_, f32[4,128,128]{2,1,0:T(8,128)S(1)} %get-tuple-element.28.refs_1_.refs_2_, ...), custom_call_target="tpu_custom_call" | custom-call | tf_op jit(solution)/shard_map/first_stage_1/pallas_call | solution.py:388
  21.8 3.4 %collective-permute-start.6 = (f32[512,128]{1,0:T(8,128)S(1)}, f32[512,128]{1,0:T(8,128)S(1)}, u32[]{:S(2)}, u32[]{:S(2)}) collective-permute-start(f32[512,128]{1,0:T(8,128)S(1)} %get-tuple-element.39), channel_id=1, source_target_pairs={{0,1},{1,0},{2,3},{3,2},{4,5},{5,4},{6,7},{7,6},{8,9},{9,8},{10,11... | collective-permute-start | bytes 786440 | tf_op jit(solution)/shard_map/ppermute | solution.py:35
  25.2 0.7 %collective-permute-start.7 = (f32[512,128]{1,0:T(8,128)S(1)}, f32[512,128]{1,0:T(8,128)S(1)}, u32[]{:S(2)}, u32[]{:S(2)}) collective-permute-start(f32[512,128]{1,0:T(8,128)S(1)} %get-tuple-element.40), channel_id=1, source_target_pairs={{1,2},{2,1},{5,6},{6,5},{9,10},{10,9},{13,14},{14,13},{17,18},{18,... | collective-permute-start | bytes 786440 | tf_op jit(solution)/shard_map/ppermute | solution.py:35
  25.8 1.6 %collective-permute-start.9 = (f32[32,128]{1,0:T(8,128)S(1)}, f32[32,128]{1,0:T(8,128)S(1)}, u32[]{:S(2)}, u32[]{:S(2)}) collective-permute-start(f32[32,128]{1,0:T(8,128)S(1)} %get-tuple-element.42), channel_id=1, source_target_pairs={{4,8},{8,4},{12,16},{16,12},{20,24},{24,20},{28,0},{0,28},{5,9},{9... | collective-permute-start | bytes 49160 | tf_op jit(solution)/shard_map/ppermute | solution.py:35
  27.5 2.6 %collective-permute-done.9.refs_10_ = f32[32,128]{1,0:T(8,128)S(1)} collective-permute-done((f32[32,128]{1,0:T(8,128)S(1)}, f32[32,128]{1,0:T(8,128)S(1)}, u32[]{:S(2)}, u32[]{:S(2)}) %collective-permute-start.9) | collective-permute-done | bytes 16416 | tf_op jit(solution)/shard_map/ppermute | solution.py:35
  30.1 0.6 %copy-done.4 = f32[4,128]{1,0:T(4,128)S(1)} copy-done((f32[4,128]{1,0:T(4,128)S(1)}, f32[4,128]{1,0:T(4,128)}, u32[]{:S(2)}) %copy-start.4) | copy-done | bytes 2072
  30.8 5.3 %radiation.1.refs_11_ = f32[256,128]{1,0:T(8,128)} custom-call(f32[4,256,128]{2,1,0:T(8,128)S(1)} %get-tuple-element.43.nat, f32[4,128]{1,0:T(4,128)S(1)} %copy-done.3, f32[4,128]{1,0:T(4,128)S(1)} %copy-done.4, f32[14]{0:T(128)S(1)} %copy-done.6, f32[14]{0:T(128)S(1)} %copy-done.7, f32[14]{0:T(128)S(1)} %copy-done.8, s32[4,1,128]{2,1,0:T(1,128)S(1)} %copy-done.5, ...), custom_call_target="tpu_custom_call" | custom-call | flops 20000000 | bytes 400000 | tf_op jit(solution)/shard_map/radiation/pallas_call | solution.py:388
  36.1 0.9 %copy-done.1 = f32[256,128]{1,0:T(8,128)S(1)} copy-done((f32[256,128]{1,0:T(8,128)S(1)}, f32[256,128]{1,0:T(8,128)}, u32[]{:S(2)}) %copy-start.1) | copy-done | bytes 131096
  37.0 1.4 %second_stage_0.1.refs_12_ = f32[8,256,128]{2,1,0:T(8,128)} custom-call(f32[8,128,128]{2,1,0:T(8,128)S(1)} %get-tuple-element.26.tiles_first.refs_0_, f32[8,128,128]{2,1,0:T(8,128)S(1)} %get-tuple-element.37.refs_8_.refs_1_, f32[4,128,128]{2,1,0:T(8,128)S(1)} %get-tuple-element.28.refs_1_.refs_2_, f32[4,128,128]{2,1,0:T(8,128)S(1)} %get-tuple-element.29.refs_2_.refs_3_, ...), custom_call_target="tpu_custom_call" | custom-call | tf_op jit(solution)/shard_map/second_stage_0/pallas_call | solution.py:388
  38.4 1.4 %second_stage_1.1 = f32[8,256,128]{2,1,0:T(8,128)} custom-call(f32[8,128,128]{2,1,0:T(8,128)S(1)} %get-tuple-element.27.refs_0_, f32[8,128,128]{2,1,0:T(8,128)S(1)} %get-tuple-element.38.refs_1_, f32[4,128,128]{2,1,0:T(8,128)S(1)} %get-tuple-element.28.refs_1_.refs_2_, ...), custom_call_target="tpu_custom_call", output_to_operand_aliasing={{}: (12, {})} | custom-call | tf_op jit(solution)/shard_map/second_stage_1/pallas_call | solution.py:388
  (27 shorter events, 0.2 us)
Async XLA Ops:
  0.6 1.2 %copy-start = (f32[8,64,4,128]{3,2,1,0:T(4,128)S(1)}, f32[8,64,4,128]{3,2,1,0:T(4,128)}, u32[]{:S(2)}) copy-start(f32[8,64,4,128]{3,2,1,0:T(4,128)} %param.9) | copy-start | bytes 3145732
  1.9 0.9 %copy-start.2 = (f32[2,64,4,128]{3,2,1,0:T(4,128)S(1)}, f32[2,64,4,128]{3,2,1,0:T(4,128)}, u32[]{:S(2)}) copy-start(f32[2,64,4,128]{3,2,1,0:T(4,128)} %param.10) | copy-start | bytes 786436
  4.0 14.7 %collective-permute-start.4 = (f32[576,128]{1,0:T(8,128)S(1)}, f32[576,128]{1,0:T(8,128)S(1)}, u32[]{:S(2)}, u32[]{:S(2)}) collective-permute-start(f32[576,128]{1,0:T(8,128)S(1)} %get-tuple-element.34), channel_id=1, source_target_pairs={{0,1},{1,0},{2,3},{3,2},{4,5},{5,4},{6,7},{7,6},{8,9},{9,8},{10,11... | collective-permute-start | bytes 884744 | tf_op jit(solution)/shard_map/ppermute | solution.py:35
  7.1 11.6 %collective-permute-start.5 = (f32[576,128]{1,0:T(8,128)S(1)}, f32[576,128]{1,0:T(8,128)S(1)}, u32[]{:S(2)}, u32[]{:S(2)}) collective-permute-start(f32[576,128]{1,0:T(8,128)S(1)} %get-tuple-element.35), channel_id=1, source_target_pairs={{1,2},{2,1},{5,6},{6,5},{9,10},{10,9},{13,14},{14,13},{17,18},{18,... | collective-permute-start | bytes 884744 | tf_op jit(solution)/shard_map/ppermute | solution.py:35
  8.2 13.1 %collective-permute-start = (f32[512,128]{1,0:T(8,128)S(1)}, f32[512,128]{1,0:T(8,128)S(1)}, u32[]{:S(2)}, u32[]{:S(2)}) collective-permute-start(f32[512,128]{1,0:T(8,128)S(1)} %get-tuple-element.30), channel_id=1, source_target_pairs={{0,1},{1,0},{2,3},{3,2},{4,5},{5,4},{6,7},{7,6},{8,9},{9,8},{10,11... | collective-permute-start | bytes 786440 | tf_op jit(solution)/shard_map/ppermute | solution.py:35
  12.6 8.6 %collective-permute-start.1 = (f32[512,128]{1,0:T(8,128)S(1)}, f32[512,128]{1,0:T(8,128)S(1)}, u32[]{:S(2)}, u32[]{:S(2)}) collective-permute-start(f32[512,128]{1,0:T(8,128)S(1)} %get-tuple-element.31), channel_id=1, source_target_pairs={{1,2},{2,1},{5,6},{6,5},{9,10},{10,9},{13,14},{14,13},{17,18},{18,... | collective-permute-start | bytes 786440 | tf_op jit(solution)/shard_map/ppermute | solution.py:35
  13.3 1.3 %collective-permute-start.2 = (f32[40,128]{1,0:T(8,128)S(1)}, f32[40,128]{1,0:T(8,128)S(1)}, u32[]{:S(2)}, u32[]{:S(2)}) collective-permute-start(f32[40,128]{1,0:T(8,128)S(1)} %get-tuple-element.32), channel_id=1, source_target_pairs={{0,4},{4,0},{8,12},{12,8},{16,20},{20,16},{24,28},{28,24},{1,5},{5... | collective-permute-start | bytes 61448 | tf_op jit(solution)/shard_map/ppermute | solution.py:35
  14.6 4.1 %collective-permute-start.3 = (f32[40,128]{1,0:T(8,128)S(1)}, f32[40,128]{1,0:T(8,128)S(1)}, u32[]{:S(2)}, u32[]{:S(2)}) collective-permute-start(f32[40,128]{1,0:T(8,128)S(1)} %get-tuple-element.33), channel_id=1, source_target_pairs={{4,8},{8,4},{12,16},{16,12},{20,24},{24,20},{28,0},{0,28},{5,9},{9... | collective-permute-start | bytes 61448 | tf_op jit(solution)/shard_map/ppermute | solution.py:35
  19.2 16.9 %collective-permute-start.10 = (f32[512,128]{1,0:T(8,128)S(1)}, f32[512,128]{1,0:T(8,128)S(1)}, u32[]{:S(2)}, u32[]{:S(2)}) collective-permute-start(f32[512,128]{1,0:T(8,128)S(1)} %get-tuple-element.44), channel_id=1, source_target_pairs={{0,1},{1,0},{2,3},{3,2},{4,5},{5,4},{6,7},{7,6},{8,9},{9,8},{10,11... | collective-permute-start | bytes 786440 | tf_op jit(solution)/shard_map/ppermute | solution.py:35
  20.6 15.5 %collective-permute-start.11 = (f32[512,128]{1,0:T(8,128)S(1)}, f32[512,128]{1,0:T(8,128)S(1)}, u32[]{:S(2)}, u32[]{:S(2)}) collective-permute-start(f32[512,128]{1,0:T(8,128)S(1)} %get-tuple-element.45), channel_id=1, source_target_pairs={{1,2},{2,1},{5,6},{6,5},{9,10},{10,9},{13,14},{14,13},{17,18},{18,... | collective-permute-start | bytes 786440 | tf_op jit(solution)/shard_map/ppermute | solution.py:35
  21.3 8.8 %copy-start.5 = (s32[4,1,128]{2,1,0:T(1,128)S(1)}, s32[4,1,128]{2,1,0:T(1,128)}, u32[]{:S(2)}) copy-start(s32[4,1,128]{2,1,0:T(1,128)} %order_in.1) | copy-start | bytes 6148
  21.3 8.8 %copy-start.9 = (s32[4,1]{0,1:T(1,128)S(1)}, s32[4,1]{0,1:T(1,128)}, u32[]{:S(2)}) copy-start(s32[4,1]{0,1:T(1,128)} %param.17) | copy-start | bytes 52
  21.8 16.6 %collective-permute-start.6 = (f32[512,128]{1,0:T(8,128)S(1)}, f32[512,128]{1,0:T(8,128)S(1)}, u32[]{:S(2)}, u32[]{:S(2)}) collective-permute-start(f32[512,128]{1,0:T(8,128)S(1)} %get-tuple-element.39), channel_id=1, source_target_pairs={{0,1},{1,0},{2,3},{3,2},{4,5},{5,4},{6,7},{7,6},{8,9},{9,8},{10,11... | collective-permute-start | bytes 786440 | tf_op jit(solution)/shard_map/ppermute | solution.py:35
  25.2 13.3 %collective-permute-start.7 = (f32[512,128]{1,0:T(8,128)S(1)}, f32[512,128]{1,0:T(8,128)S(1)}, u32[]{:S(2)}, u32[]{:S(2)}) collective-permute-start(f32[512,128]{1,0:T(8,128)S(1)} %get-tuple-element.40), channel_id=1, source_target_pairs={{1,2},{2,1},{5,6},{6,5},{9,10},{10,9},{13,14},{14,13},{17,18},{18,... | collective-permute-start | bytes 786440 | tf_op jit(solution)/shard_map/ppermute | solution.py:35
  25.8 4.2 %collective-permute-start.9 = (f32[32,128]{1,0:T(8,128)S(1)}, f32[32,128]{1,0:T(8,128)S(1)}, u32[]{:S(2)}, u32[]{:S(2)}) collective-permute-start(f32[32,128]{1,0:T(8,128)S(1)} %get-tuple-element.42), channel_id=1, source_target_pairs={{4,8},{8,4},{12,16},{16,12},{20,24},{24,20},{28,0},{0,28},{5,9},{9... | collective-permute-start | bytes 49160 | tf_op jit(solution)/shard_map/ppermute | solution.py:35
  30.0 0.7 %copy-start.4 = (f32[4,128]{1,0:T(4,128)S(1)}, f32[4,128]{1,0:T(4,128)}, u32[]{:S(2)}) copy-start(f32[4,128]{1,0:T(4,128)} %albedo_in.1) | copy-start | bytes 6148
  30.0 0.7 %copy-start.3 = (f32[4,128]{1,0:T(4,128)S(1)}, f32[4,128]{1,0:T(4,128)}, u32[]{:S(2)}) copy-start(f32[4,128]{1,0:T(4,128)} %cosz_in.1) | copy-start | bytes 6148
  30.0 6.1 %collective-permute-start.8 = (f32[32,128]{1,0:T(8,128)S(1)}, f32[32,128]{1,0:T(8,128)S(1)}, u32[]{:S(2)}, u32[]{:S(2)}) collective-permute-start(f32[32,128]{1,0:T(8,128)S(1)} %get-tuple-element.41.after), channel_id=1, source_target_pairs={{0,4},{4,0},{8,12},{12,8},{16,20},{20,16},{24,28},{28,24},{1,5},{5... | collective-permute-start | bytes 49160 | tf_op jit(solution)/shard_map/ppermute | solution.py:35
  30.1 0.7 %copy-start.6 = (f32[14]{0:T(128)S(1)}, f32[14]{0:T(128)}, u32[]{:S(2)}) copy-start(f32[14]{0:T(128)} %ext_in.1) | copy-start | bytes 172
  30.1 0.7 %copy-start.7 = (f32[14]{0:T(128)S(1)}, f32[14]{0:T(128)}, u32[]{:S(2)}) copy-start(f32[14]{0:T(128)} %single_in.1) | copy-start | bytes 172
  30.1 0.7 %copy-start.8 = (f32[14]{0:T(128)S(1)}, f32[14]{0:T(128)}, u32[]{:S(2)}) copy-start(f32[14]{0:T(128)} %weight_in.1) | copy-start | bytes 172
  36.1 0.9 %copy-start.1 = (f32[256,128]{1,0:T(8,128)S(1)}, f32[256,128]{1,0:T(8,128)}, u32[]{:S(2)}) copy-start(f32[256,128]{1,0:T(8,128)} %radiation.1.refs_11_) | copy-start | bytes 393220

commit v3 on v2

v3 whole, which is shorter than its diff:
```python
import functools
import math

import jax
import jax.numpy as jnp
from jax import lax
from jax.experimental import pallas as pl
from jax.experimental.pallas import tpu as pltpu
from jax.sharding import PartitionSpec as P

SPLIT = 2
SUB = 8
LANES = 128
LOG2E = math.log2(math.e)
VMEM = pl.BlockSpec(memory_space=pltpu.VMEM)
HBM = pl.BlockSpec(memory_space=pltpu.HBM)
MIB = 1024 * 1024


def scratch(*dims):
    return pltpu.VMEM(dims, jnp.float32)


def shape(*dims):
    return jax.ShapeDtypeStruct(dims, jnp.float32)


def lon_swaps(first_block, second_block):
    n = lax.axis_size("lon")
    first = [(i, i ^ 1) for i in range(n)]
    second = [(i, (i + 1 if i % 2 else i - 1) % n) for i in range(n)]
    return lax.ppermute(first_block, "lon", first), lax.ppermute(second_block, "lon", second)


def lat_swaps(first_block, second_block):
    nlon, nlat = lax.axis_size("lon"), lax.axis_size("lat")
    second = []
    for i in range(nlon):
        for j in range(nlat):
            k = j + 1 if j % 2 else j - 1
            to = i * nlat + k if 0 <= k < nlat else (i ^ 1) * nlat + j
            second.append((i * nlat + j, to))
    got = lax.ppermute(second_block, ("lon", "lat"), second)
    return lax.ppermute(first_block, "lat", [(j, j ^ 1) for j in range(nlat)]), got


def is_even(axis):
    return lax.rem(lax.axis_index(axis), 2) == 0


def sublanes():
    return lax.broadcasted_iota(jnp.int32, (SUB, LANES), 0)


def lanes():
    return lax.broadcasted_iota(jnp.int32, (SUB, LANES), 1)


def half_turn(block):
    return pltpu.roll(block, SUB // 2, 0)


def native(ref, index, r, nrows):
    levels = ref.shape[1] // nrows
    return ref[index, pl.ds(r, levels, stride=nrows), :]


def tile_of(low, high):
    return jnp.transpose(jnp.concatenate([low, high], axis=0))


def put_lat_sends(even, tiles, pair, nrows, za, zb):
    north = jnp.where(even, 2, 0)
    for k in range(2):
        span = pl.ds(pl.multiple_of((2 * pair + k) * LANES, LANES), LANES)
        za[span, :] = tiles[nrows * pair + north + k]
        zb[span, :] = tiles[nrows * pair + (2 - north) + k]


def take_sides(tile):
    head = sublanes() < SUB // 2
    return jnp.where(head, tile[pl.ds(0, SUB), :], tile[pl.ds(LANES - SUB, SUB), :])


def pack_first(pairs, nrows, fields, courant, tiles, za, zb, nat, nat_late, nat_wind, sems):
    n = 2 * pairs
    copies = [pltpu.make_async_copy(fields.at[i], nat.at[i], sems.at[i]) for i in range(n)]
    wind = pltpu.make_async_copy(courant, nat_wind, sems.at[n])
    late = pltpu.make_async_copy(fields.at[pl.ds(n, nat_late.shape[0])], nat_late, sems.at[n + 1])
    for copy in copies + [wind, late]:
        copy.start()
    even = is_even("lat")
    for p in range(pairs):
        copies[2 * p].wait()
        copies[2 * p + 1].wait()
        for r in range(nrows):
            tiles[nrows * p + r] = tile_of(native(nat, 2 * p, r, nrows), native(nat, 2 * p + 1, r, nrows))
        put_lat_sends(even, tiles, p, nrows, za, zb)
    wind.wait()
    top = native(nat_wind, 1, nrows - 1, nrows) * (1.0 / 12.0)
    top = tile_of(top, top)
    half = LANES // 2
    lane = lax.broadcasted_iota(jnp.int32, (half, LANES), 1)
    top = jnp.where(lane < half, top[:half], top[half:])
    span = pl.ds(2 * pairs * LANES, half)
    za[span, :] = top
    zb[span, :] = top
    late.wait()


def pack_middle(pairs, nrows, nat, nat_wind, tiles_first, tiles, ce, cn, la, lb):
    for p in range(pairs):
        for r in range(nrows):
            tiles[nrows * p + r] = tile_of(native(nat, 2 * p, r, nrows), native(nat, 2 * p + 1, r, nrows))
    for r in range(nrows):
        east = native(nat_wind, 0, r, nrows) * (1.0 / 12.0)
        north = native(nat_wind, 1, r, nrows) * (1.0 / 12.0)
        ce[r] = tile_of(east, east)
        cn[r] = tile_of(north, north)
    even = is_even("lon")
    head, low = sublanes() < SUB // 2, lanes() < LANES // 2
    blocks = [take_sides(ref.at[t]) for ref in (tiles_first, tiles) for t in range(ref.shape[0])]
    blocks += [jnp.where(low, take_sides(ce.at[r]), take_sides(cn.at[r])) for r in range(nrows)]
    for i in range(0, len(blocks), 2):
        one, two = blocks[i : i + 2]
        east = jnp.where(head, half_turn(one), two)
        west = jnp.where(head, one, half_turn(two))
        span = pl.ds(SUB * (i // 2), SUB)
        la[span, :] = jnp.where(even, east, west)
        lb[span, :] = jnp.where(even, west, east)


def pack_last(pairs, done, nrows, tiles, la, lb, za, zb, side):
    lat_even, lon_even = is_even("lat"), is_even("lon")
    ntiles = nrows * (done + pairs)
    head, low = sublanes() < SUB // 2, lanes() < LANES // 2
    blocks = []
    for i in range(la.shape[0] // SUB):
        span = pl.ds(SUB * i, SUB)
        a, b = la[span, :], lb[span, :]
        east, west = jnp.where(lon_even, a, b), jnp.where(lon_even, b, a)
        blocks += [jnp.where(head, east, half_turn(west)), jnp.where(head, half_turn(east), west)]
    winds = blocks[ntiles:]
    turned = [pltpu.roll(wind, LANES // 2, 1) for wind in winds]
    blocks[ntiles:] = [jnp.where(low, x, y) for x, y in zip(winds, turned)]
    blocks += [jnp.where(low, y, x) for x, y in zip(winds, turned)]
    for t, value in enumerate(blocks):
        side[pl.ds(SUB * t, SUB), :] = value
    north = jnp.where(lat_even, 2, 0)
    at = 2 * pairs * LANES
    row = sublanes()
    outer = (row < 2) | (row >= SUB - 2)

    def corner(p, first):
        start = pl.multiple_of(SUB * (nrows * p + first), SUB)
        one, two = side[pl.ds(start, SUB), :], side[pl.ds(start + SUB, SUB), :]
        return jnp.where(outer, one, half_turn(two))

    for p in range(done + pairs):
        to = pl.ds(at + SUB * p, SUB)
        za[to, :] = corner(p, north)
        zb[to, :] = corner(p, 2 - north)
    to = pl.ds(at + SUB * (done + pairs), SUB)
    top = side[pl.ds(SUB * (ntiles + 2 * nrows - 1), SUB), :]
    za[to, :] = top
    zb[to, :] = top
    for p in range(pairs):
        put_lat_sends(lat_even, tiles, p, nrows, za, zb)


def put_edges(q, first, side, at, nrows, edge_w, edge_e):
    for r in range(nrows):
        beside = side[pl.ds(pl.multiple_of(SUB * (at + r), SUB), SUB), :]
        edge_w[r, pl.ds(SUB, SUB), :] = beside
        edge_w[r, pl.ds(2 * SUB, SUB), :] = q[first + r, pl.ds(0, SUB), :]
        edge_e[r, pl.ds(0, SUB), :] = q[first + r, pl.ds(LANES - SUB, SUB), :]
        edge_e[r, pl.ds(SUB, SUB), :] = beside


def through(c, before, left, right, after):
    return c * (7.0 * (left + right) - (before + after))


def put_fluxes(q, first, nrows, ce, edge_w, edge_e, edge_c, flux):
    for r in range(nrows):
        window = [edge_w[r, pl.ds(SUB + k, SUB), :] for k in range(4)]
        flux[r, pl.ds(1, SUB), :] = through(edge_c[r, pl.ds(SUB + 1, SUB), :], *window)
        for b in range(LANES // SUB):
            at = SUB * b

            def load(shift):
                if at + shift < 0:
                    return edge_w[r, pl.ds(2 * SUB + shift, SUB), :]
                if at + shift + SUB > LANES:
                    return edge_e[r, pl.ds(shift, SUB), :]
                return q[first + r, pl.ds(at + shift, SUB), :]

            flux[r, pl.ds(SUB + at, SUB), :] = through(
                ce[r, pl.ds(at, SUB), :], load(-1), load(0), load(1), load(2)
            )


def lat_divergence(rows, winds):
    north = [through(winds[r], *rows[r : r + 4]) for r in range(len(winds))]
    return [north[r + 1] - north[r] for r in range(len(winds) - 1)]


def sources():
    at, n = lax.axis_index("lat"), lax.axis_size("lat")
    even = lax.rem(at, 2) == 0
    return (even, jnp.logical_not(even), jnp.logical_and(even, at > 0), jnp.logical_and(jnp.logical_not(even), at < n - 1))


def partners(where, ra, rb, span):
    north_a, south_a, south_b, north_b = where
    a, b = ra[span, :], rb[span, :]
    south = jnp.where(south_a, a, jnp.where(south_b, b, 0.0))
    return south, jnp.where(north_a, a, jnp.where(north_b, b, 0.0))


def divergence(q, pair, nrows, b, where, ra, rb, cn, below, flux):
    at = SUB * b
    here = pl.ds(at, SUB)

    def halo(k):
        start = pl.multiple_of((2 * pair + k) * LANES, LANES) + at
        return partners(where, ra, rb, pl.ds(start, SUB))

    (s0, n0), (s1, n1) = halo(0), halo(1)
    own = [q[nrows * pair + r, here, :] for r in range(nrows)]
    winds = [below[here, :]] + [cn[r, here, :] for r in range(nrows)]
    north = lat_divergence([s0, s1] + own + [n0, n1], winds)
    div = []
    for r in range(nrows):
        east = flux[r, pl.ds(SUB + at, SUB), :] - flux[r, pl.ds(SUB + at - 1, SUB), :]
        div.append(east + north[r])
    return own, div


def put_side_section(at, nrows, where, ra, rb, corner, side, ntiles, edge_w, edge_e, edge_c, edge_d, out):
    head = sublanes() < SUB // 2

    def shifted(w, e, r, k):
        return jnp.where(head, e[r, pl.ds(SUB + k, SUB), :], w[r, pl.ds(SUB + k, SUB), :])

    def beside(t):
        return side[pl.ds(pl.multiple_of(SUB * t, SUB), SUB), :]

    start = pl.multiple_of(corner + SUB * (at // nrows), SUB)
    south, above = partners(where, ra, rb, pl.ds(start, SUB))
    s0, s1 = south, half_turn(south)
    n0, n1 = above, half_turn(above)
    own = [beside(at + r) for r in range(nrows)]
    last = pl.ds(corner + SUB * (ntiles // nrows), SUB)
    winds = [partners(where, ra, rb, last)[0]]
    winds += [beside(ntiles + nrows + r) for r in range(nrows)]
    north = lat_divergence([s0, s1] + own + [n0, n1], winds)
    for r in range(nrows):
        v = [shifted(edge_w, edge_e, r, k) for k in range(-2, 3)]
        east = through(beside(ntiles + r), *v[1:])
        west = through(shifted(edge_c, edge_d, r, -1), *v[:-1])
        new = own[r] - ((east - west) + north[r])
        out[pl.ds(pl.multiple_of(SUB * (at + r), SUB), SUB), :] = new


def edge_scratch(nrows):
    return [scratch(nrows, 3 * SUB, LANES)] * 4 + [scratch(nrows, LANES + SUB, LANES)]


def first_stage_early(pairs, nrows, q, ce, cn, side, ra, rb, section, za, zb, below, *edges):
    edge_w, edge_e, edge_c, edge_d, flux = edges
    lat_even, where = is_even("lat"), sources()
    half = LANES // 2
    a = partners(where, ra, rb, pl.ds(2 * pairs * LANES, half))[0]
    turned = pltpu.roll(a, half, 1)
    low = lax.broadcasted_iota(jnp.int32, (half, LANES), 1) < half
    below[pl.ds(0, half), :] = jnp.where(low, a, turned)
    below[pl.ds(half, half), :] = jnp.where(low, turned, a)
    put_edges(ce, 0, side, side.shape[0] // SUB - 2 * nrows, nrows, edge_c, edge_d)

    def one(p, _):
        put_edges(q, nrows * p, side, nrows * p, nrows, edge_w, edge_e)
        put_fluxes(q, nrows * p, nrows, ce, edge_w, edge_e, edge_c, flux)
        for b in range(LANES // SUB):
            own, div = divergence(q, p, nrows, b, where, ra, rb, cn, below, flux)
            for r in range(nrows):
                section[nrows * p + r, pl.ds(SUB * b, SUB), :] = own[r] - div[r]
        put_lat_sends(lat_even, section, p, nrows, za, zb)
        return 0

    lax.fori_loop(0, pairs, one, 0)


def first_stage_late(
    pairs, done, nrows, q, ce, cn, side, ra, rb, below, q_early, section, za, zb, sides, *edges
):
    edge_w, edge_e, edge_c, edge_d, flux = edges
    lat_even, where = is_even("lat"), sources()
    ntiles = nrows * (done + pairs)
    corner = 2 * pairs * LANES
    put_edges(ce, 0, side, ntiles, nrows, edge_c, edge_d)

    def side_section(at):
        put_side_section(
            at, nrows, where, ra, rb, corner, side, ntiles, edge_w, edge_e, edge_c, edge_d, sides
        )

    def one(p, _):
        at = nrows * (done + p)
        put_edges(q, nrows * p, side, at, nrows, edge_w, edge_e)
        put_fluxes(q, nrows * p, nrows, ce, edge_w, edge_e, edge_c, flux)
        for b in range(LANES // SUB):
            own, div = divergence(q, p, nrows, b, where, ra, rb, cn, below, flux)
            for r in range(nrows):
                section[nrows * p + r, pl.ds(SUB * b, SUB), :] = own[r] - div[r]
        put_lat_sends(lat_even, section, p, nrows, za, zb)
        side_section(at)
        return 0

    def another(p, _):
        put_edges(q_early, nrows * p, side, nrows * p, nrows, edge_w, edge_e)
        side_section(nrows * p)
        return 0

    lax.fori_loop(0, pairs, one, 0)
    lax.fori_loop(0, done, another, 0)


def second_stage(pairs, done, nrows, is_first, *refs):
    q, s, ce, cn, below, ra, rb, side, sides, heating = refs[:10]
    buffer, sems, edge_w, edge_e, edge_c, edge_d, flux = refs[-7:]
    out = refs[11]
    levels = LANES // 2
    where = sources()
    if is_first:
        out, heat_out = refs[10:12]
        heat_copy = pltpu.make_async_copy(heating, heat_out, sems.at[pairs])
        heat_copy.start()
    put_edges(ce, 0, side, side.shape[0] // SUB - 2 * nrows, nrows, edge_c, edge_d)

    def copy(p):
        return pltpu.make_async_copy(
            buffer.at[pl.ds(2 * p, 2)], out.at[pl.ds(2 * (done + p), 2)], sems.at[p]
        )

    def one(p, _):
        put_edges(s, nrows * p, sides, nrows * (done + p), nrows, edge_w, edge_e)
        put_fluxes(s, nrows * p, nrows, ce, edge_w, edge_e, edge_c, flux)
        parts = [[] for _ in range(nrows)]
        for b in range(LANES // SUB):
            own, div = divergence(s, p, nrows, b, where, ra, rb, cn, below, flux)
            for r in range(nrows):
                old = q[nrows * p + r, pl.ds(SUB * b, SUB), :]
                parts[r].append(0.5 * ((old + own[r]) - div[r]))
        for r in range(nrows):
            turned = jnp.transpose(jnp.concatenate(parts[r], axis=0))
            for h in range(2):
                buffer[2 * p + h, pl.ds(r, levels, stride=nrows), :] = turned[levels * h : levels * (h + 1)]
        if is_first:

            @pl.when(p == 0)
            def _():
                buffer[0] = buffer[0] + 0.5 * heating[...]

        copy(p).start()
        return 0

    lax.fori_loop(0, pairs, one, 0)
    for p in range(pairs):
        copy(p).wait()
    if is_first:
        heat_copy.wait()


def radiation(
    nat, cosz_in, albedo_in, ext_in, single_in, weight_in, order_in, count_in, after, heat,
    water, depth, save_a, save_b, save_t, save_g, cosz, albedo, ext, single, weight, order, count, sems
):
    del after
    copies = []
    for i, (src, dst) in enumerate(
        (
            (cosz_in, cosz), (albedo_in, albedo), (ext_in, ext), (single_in, single),
            (weight_in, weight), (order_in, order), (count_in, count),
        )
    ):
        copies.append(pltpu.make_async_copy(src, dst, sems.at[i]))
        copies[-1].start()
    nrows, _ = cosz.shape
    levels = nat.shape[1] // nrows
    pairs = ext.shape[0] // 2
    x = nat[1]
    heat[...] = jnp.maximum(x, 0.0) + jnp.log1p(jnp.exp(-jnp.abs(x)))
    total = jnp.zeros((nrows, LANES), jnp.float32)
    depth[0] = jnp.zeros((2 * nrows, LANES), jnp.float32)
    for l in range(levels):
        w = heat[pl.ds(nrows * l, nrows), :]
        total = total + w
        water[l, pl.ds(0, nrows), :] = w
        water[l, pl.ds(nrows, nrows), :] = w
        depth[l + 1, pl.ds(0, nrows), :] = total
        depth[l + 1, pl.ds(nrows, nrows), :] = total
    for copy in copies:
        copy.wait()

    mu = jnp.concatenate([cosz[...], cosz[...]], axis=0)
    floor_albedo = jnp.concatenate([albedo[...], albedo[...]], axis=0)
    first = lax.broadcasted_iota(jnp.int32, (2 * nrows, LANES), 0) < nrows

    def by_band(ref):
        return [jnp.where(first, ref[2 * p], ref[2 * p + 1]) for p in range(pairs)]

    scale = 4.0 / levels
    inv_mu = 1.0 / mu
    ext_of, half_of, weight_of = by_band(ext), by_band(single), by_band(weight)
    beam = [-(e * scale * LOG2E) * inv_mu for e in ext_of]
    diffuse = [-(1.66 * scale * LOG2E) * e for e in ext_of]
    half = [0.5 * s for s in half_of]
    strength = [w * mu for w in weight_of]

    def up(step, carry):
        l = levels - 1 - step
        a_all, b_all, s_all = carry
        w = water[l]
        above = depth[l]
        new_a, new_b, new_s = [], [], []
        for p in range(pairs):
            a, b, s_bot = a_all[p], b_all[p], s_all[p]
            decay = jnp.exp2(diffuse[p] * w)
            s_top = strength[p] * jnp.exp2(beam[p] * above)
            reflect = half[p] - half[p] * decay
            transmit = decay + reflect
            source = half[p] * (s_top - s_bot)
            den = 1.0 - reflect * a
            inv = pl.reciprocal(den, approx=True)
            inv = inv * (2.0 - den * inv)
            t = transmit * inv
            a_here = reflect + transmit * (t * a)
            b_here = t * (a * source + b) + source
            save_t[l, p] = t
            save_g[l, p] = (reflect * b + source) * inv
            save_a[l, p] = 1.0 - a_here
            save_b[l, p] = s_top - b_here
            new_a.append(a_here)
            new_b.append(b_here)
            new_s.append(s_top)
        return tuple(new_a), tuple(new_b), tuple(new_s)

    s_floor = [strength[p] * jnp.exp2(beam[p] * depth[levels]) for p in range(pairs)]
    a_floor = [floor_albedo for _ in range(pairs)]
    b_floor = [floor_albedo * s_floor[p] for p in range(pairs)]
    lax.fori_loop(0, levels, up, (tuple(a_floor), tuple(b_floor), tuple(s_floor)))

    sunlit = []
    column = lax.broadcasted_iota(jnp.int32, (LANES, LANES), 1)
    rank = lax.broadcasted_iota(jnp.int32, (LANES, LANES), 0)
    for r in range(nrows):
        place = jnp.transpose(jnp.broadcast_to(order[r], (LANES, LANES)))
        hit = (place == column) & (rank < count[r])
        sunlit.append(jnp.max(jnp.where(hit, 1.0, 0.0), axis=0, keepdims=True))
    gain = float(levels) * jnp.concatenate(sunlit, axis=0)

    def net_flux(l, d_all):
        net = jnp.zeros((2 * nrows, LANES), jnp.float32)
        for p in range(pairs):
            net = net + (save_b[l, p] + d_all[p] * save_a[l, p])
        return net

    def put(l, absorbed):
        both = absorbed[:nrows] + absorbed[nrows:]
        heat[pl.ds(pl.multiple_of(nrows * l, nrows), nrows), :] = gain * both

    def down(l, carry):
        d_all, net_above = carry
        d_new = tuple(save_t[l - 1, p] * d_all[p] + save_g[l - 1, p] for p in range(pairs))
        net = net_flux(l, d_new)
        put(l - 1, net_above - net)
        return d_new, net

    d_top = tuple(jnp.zeros((2 * nrows, LANES), jnp.float32) for _ in range(pairs))
    d_low, net_low = lax.fori_loop(1, levels, down, (d_top, net_flux(0, d_top)))
    net = jnp.zeros((2 * nrows, LANES), jnp.float32)
    for p in range(pairs):
        d_floor = save_t[levels - 1, p] * d_low[p] + save_g[levels - 1, p]
        net = net + ((s_floor[p] - b_floor[p]) + d_floor * (1.0 - a_floor[p]))
    put(levels - 1, net_low - net)


def in_hbm(x):
    return pltpu.with_memory_space_constraint(x, pltpu.HBM)


def call(kernel, name, out_shape, specs, out_specs, args, scratches, moved=1000, limit=24, **kw):
    return pl.pallas_call(
        kernel,
        out_shape=out_shape,
        in_specs=specs,
        out_specs=out_specs,
        scratch_shapes=scratches,
        compiler_params=pltpu.CompilerParams(vmem_limit_bytes=limit * MIB),
        name=name,
        cost_estimate=pl.CostEstimate(flops=moved, bytes_accessed=moved, transcendentals=0),
        **kw,
    )(*args)


def per_device(
    fields, courant, cos_zenith, albedo, extinction, single_albedo, band_weight, sun_order, sun_count
):
    nfields, levels, nrows, ncols = fields.shape
    flat = fields.reshape(nfields, levels * nrows, ncols)
    wind = courant.reshape(2, levels * nrows, ncols)
    npairs = nfields // 2
    counts = (SPLIT, npairs - SPLIT)
    starts = (0, SPLIT)
    early, late = counts

    z0 = shape((2 * early) * ncols + ncols // 2, LANES)
    tiles0, za, zb, nat, nat_late, nat_wind = call(
        functools.partial(pack_first, early, nrows),
        "pack_first",
        (
            shape(nrows * early, ncols, LANES), z0, z0,
            shape(2 * early, levels * nrows, ncols), shape(2 * late, levels * nrows, ncols),
            shape(2, levels * nrows, ncols),
        ),
        [HBM, HBM],
        (VMEM,) * 6,
        (in_hbm(flat), in_hbm(wind)),
        [pltpu.SemaphoreType.DMA((2 * early + 2,))],
    )
    lat0 = lat_swaps(za, zb)
    ntiles = nrows * npairs
    winds = shape(nrows, ncols, LANES)
    sides = shape(SUB * (ntiles + 2 * nrows), LANES)
    edge = shape(SUB * (ntiles + nrows) // 2, LANES)
    tiles1, ce, cn, la, lb = call(
        functools.partial(pack_middle, late, nrows),
        "pack_middle",
        (shape(nrows * late, ncols, LANES), winds, winds, edge, edge),
        [VMEM] * 3,
        (VMEM,) * 5,
        (nat_late, nat_wind, tiles0),
        [],
    )
    lon = lon_swaps(la, lb)
    z1 = shape(2 * late * ncols + SUB * (npairs + 1), LANES)
    za, zb, side = call(
        functools.partial(pack_last, late, early, nrows),
        "pack_last",
        (z1, z1, sides),
        [VMEM] * 3,
        (VMEM,) * 3,
        (tiles1, *lon),
        [],
    )
    lat1 = lat_swaps(za, zb)

    edges = edge_scratch(nrows)
    z0 = shape(2 * early * ncols, LANES)
    section0, za, zb, below = call(
        functools.partial(first_stage_early, early, nrows),
        "first_stage_early",
        (shape(nrows * early, ncols, LANES), z0, z0, shape(ncols, LANES)),
        [VMEM] * 6,
        (VMEM,) * 4,
        (tiles0, ce, cn, side, *lat0),
        edges,
        moved=1000_000_000,
    )
    lat2 = lat_swaps(za, zb)
    z1 = shape(2 * late * ncols, LANES)
    section1, za, zb, section_side = call(
        functools.partial(first_stage_late, late, early, nrows),
        "first_stage_late",
        (shape(nrows * late, ncols, LANES), z1, z1, shape(SUB * ntiles, LANES)),
        [VMEM] * 8,
        (VMEM,) * 4,
        (tiles1, ce, cn, side, *lat1, below, tiles0),
        edges,
        moved=12_000_000,
    )
    lat3 = lat_swaps(za, zb)

    pairs = extinction.shape[0] // 2
    store = scratch(levels, pairs, 2 * nrows, ncols)
    heating = call(
        radiation,
        "radiation",
        shape(levels * nrows, ncols),
        [VMEM] + [HBM] * 7 + [VMEM],
        VMEM,
        (
            nat, in_hbm(cos_zenith), in_hbm(albedo), in_hbm(extinction), in_hbm(single_albedo),
            in_hbm(band_weight), in_hbm(sun_order), in_hbm(sun_count.reshape(nrows)), section_side,
        ),
        [
            scratch(levels, 2 * nrows, ncols), scratch(levels + 1, 2 * nrows, ncols),
            store, store, store, store,
            scratch(nrows, ncols), scratch(nrows, ncols),
            pltpu.SMEM(extinction.shape, jnp.float32), pltpu.SMEM(extinction.shape, jnp.float32),
            pltpu.SMEM(extinction.shape, jnp.float32), pltpu.VMEM((nrows, 1, ncols), jnp.int32),
            pltpu.SMEM((nrows,), jnp.int32), pltpu.SemaphoreType.DMA((7,)),
        ],
        moved=16_000_000,
    )

    out = heat_out = None
    for g, (tiles, section, lat) in enumerate(((tiles0, section0, lat2), (tiles1, section1, lat3))):
        args = [tiles, section, ce, cn, below, *lat, side, section_side, heating]
        specs = [VMEM] * len(args)
        results = [shape(nfields, levels * nrows, ncols), shape(levels * nrows, ncols)]
        aliases = {}
        if g:
            aliases = {len(args): 0}
            args.append(out)
            specs.append(HBM)
            results.pop()
        out, *rest = call(
            functools.partial(second_stage, counts[g], starts[g], nrows, g == 0),
            f"second_stage_{g}",
            results,
            specs,
            [HBM] * len(results),
            args,
            [
                scratch(2 * counts[g], levels * nrows, ncols),
                pltpu.SemaphoreType.DMA((counts[g] + 1,)),
                *edges,
            ],
            input_output_aliases=aliases,
        )
        if not g:
            heat_out = rest[0]
    return out.reshape(fields.shape), heat_out.reshape(levels, nrows, ncols)


def solution(mesh):
    in_specs = (
        P(None, None, "lat", "lon"),
        P(None, None, "lat", "lon"),
        P("lat", "lon"),
        P("lat", "lon"),
        P(),
        P(),
        P(),
        P("lat", "lon", None),
        P("lat", "lon"),
    )
    out_specs = (P(None, None, "lat", "lon"), P(None, "lat", "lon"))
    return jax.shard_map(
        per_device, mesh=mesh, in_specs=in_specs, out_specs=out_specs, check_vma=False
    )
```

time: 40.7 us -> 32.9 us (0.81); the launches traced: 39.9 us -> 32.7 us
  starting transfers between devices: 18.9 us -> 12.5 us
  local copies, waits for them, and re-layouts: 3.75 us -> 0 us
  waiting for transfers between devices: 5.68 us -> 8.89 us
    ppermute x12 -> x10, starting transfers between devices: 18.9 us -> 12.5 us  [the longest x4 9.75 us: lat_swaps(): lax.ppermute(first_block, 'lat', [(j, j ^ 1) for j in range(nlat)])]
    unnamed x20 -> x0, local copies, waits for them, and re-layouts: 3.75 us -> none
    ppermute x12 -> x10, waiting for transfers between devices: 5.68 us -> 8.89 us  [the longest x4 6.56 us: lat_swaps(): lax.ppermute(first_block, 'lat', [(j, j ^ 1) for j in range(nlat)])]
    pallas_call x7 -> x8, Pallas kernels: 10.7 us -> 10.7 us  [call(): pl.pallas_call(kernel, out_shape=out_shape, in_specs=specs, out_specs=out...]
  transfers between devices with their start and end apart: 12 -> 10, of which waited for: 3 -> 3; matrix products, arithmetic and copies ran while one was open for 0% -> 0% of each run, Pallas kernels for 20% -> 24%
where the time goes in v3:
time: 32.9 us; the launch traced here: 32.7 us
  starting transfers between devices  12.5 us (38%)
  Pallas kernels  10.7 us (33%)
  waiting for transfers between devices  8.89 us (27%)
  between operations  0.7 us (2%)
    pallas_call x8, Pallas kernels, call(): pl.pallas_call(kernel, out_shape=out_shape, in_specs=specs, out_specs=out...  10.7 us
    ppermute x4, starting transfers between devices, lat_swaps(): lax.ppermute(first_block, 'lat', [(j, j ^ 1) for j in range(nlat)])  9.75 us
    ppermute x4, waiting for transfers between devices, lat_swaps(): lax.ppermute(first_block, 'lat', [(j, j ^ 1) for j in range(nlat)])  6.56 us
    ppermute x1, waiting for transfers between devices, lon_swaps(): lax.ppermute(second_block, 'lon', second)  2.31 us
    ppermute x1, starting transfers between devices, lon_swaps(): lax.ppermute(second_block, 'lon', second)  2.13 us
  transfers between devices with their start and end apart: 10, of which 3 were waited for; matrix products, arithmetic and copies ran while one was open for 0% of the time, Pallas kernels for 24%

profile of v3, /device:TPU:0, one launch (start us, length us, event | category | flops | bytes accessed | tf_op | source)
XLA Modules:
  0.0 32.7 jit_solution(11982498040685906416)
XLA Ops:
  0.6 1.5 %pack_first.1 = (f32[8,128,128]{2,1,0:T(8,128)S(1)}, f32[576,128]{1,0:T(8,128)S(1)}, f32[576,128]{1,0:T(8,128)S(1)}, f32[4,256,128]{2,1,0:T(8,128)S(1)}, f32[4,2...) custom-call(f32[8,256,128]{2,1,0:T(8,128)} %bitcast.6, f32[2,256,128]{2,1,0:T(8,128)} %bitcast.7), custom_call_target="tpu_custom_call" | custom-call | flops 1000 | bytes 1000 | tf_op jit(solution)/shard_map/pack_first/pallas_call | solution.py:494
  2.1 3.1 %collective-permute-start.4 = (f32[576,128]{1,0:T(8,128)S(1)}, f32[576,128]{1,0:T(8,128)S(1)}, u32[]{:S(2)}, u32[]{:S(2)}) collective-permute-start(f32[576,128]{1,0:T(8,128)S(1)} %get-tuple-element.37), channel_id=1, source_target_pairs={{0,1},{1,0},{2,3},{3,2},{4,5},{5,4},{6,7},{7,6},{8,9},{9,8},{10,11... | collective-permute-start | bytes 884744 | tf_op jit(solution)/shard_map/ppermute | solution.py:44
  5.2 0.0 collective-permute-start.5
  5.2 0.3 %pack_middle.1 = (f32[8,128,128]{2,1,0:T(8,128)S(1)}, f32[4,128,128]{2,1,0:T(8,128)S(1)}, f32[4,128,128]{2,1,0:T(8,128)S(1)}, f32[80,128]{1,0:T(8,128)S(1)}, f32[80,128]{1,0:T(8,128)S(1)}) custom-call(f32[4,256,128]{2,1,0:T(8,128)S(1)} %get-tuple-element.26.nat, f32[2,256,128]{2,1,0:T(8,128)S(1)} %get-tuple-element.27.nat_wind, ...), custom_call_target="tpu_custom_call" | custom-call | flops 1000 | bytes 1000 | tf_op jit(solution)/shard_map/pack_middle/pallas_call | solution.py:494
  5.5 0.6 %collective-permute-start = (f32[80,128]{1,0:T(8,128)S(1)}, f32[80,128]{1,0:T(8,128)S(1)}, u32[]{:S(2)}, u32[]{:S(2)}) collective-permute-start(f32[80,128]{1,0:T(8,128)S(1)} %get-tuple-element.32), channel_id=1, source_target_pairs={{0,4},{4,0},{8,12},{12,8},{16,20},{20,16},{24,28},{28,24},{1,5},{5... | collective-permute-start | bytes 122888 | tf_op jit(solution)/shard_map/ppermute | solution.py:32
  6.1 2.1 %collective-permute-start.1 = (f32[80,128]{1,0:T(8,128)S(1)}, f32[80,128]{1,0:T(8,128)S(1)}, u32[]{:S(2)}, u32[]{:S(2)}) collective-permute-start(f32[80,128]{1,0:T(8,128)S(1)} %get-tuple-element.33), channel_id=1, source_target_pairs={{0,28},{4,8},{8,4},{12,16},{16,12},{20,24},{24,20},{28,0},{1,29},{... | collective-permute-start | bytes 122888 | tf_op jit(solution)/shard_map/ppermute | solution.py:32
  8.2 0.0 collective-permute-done.la
  8.2 2.3 %collective-permute-done.1.lb = f32[80,128]{1,0:T(8,128)S(1)} collective-permute-done((f32[80,128]{1,0:T(8,128)S(1)}, f32[80,128]{1,0:T(8,128)S(1)}, u32[]{:S(2)}, u32[]{:S(2)}) %collective-permute-start.1) | collective-permute-done | bytes 40992 | tf_op jit(solution)/shard_map/ppermute | solution.py:32
  10.6 0.1 pack_last.1
  10.6 2.6 %collective-permute-start.2 = (f32[552,128]{1,0:T(8,128)S(1)}, f32[552,128]{1,0:T(8,128)S(1)}, u32[]{:S(2)}, u32[]{:S(2)}) collective-permute-start(f32[552,128]{1,0:T(8,128)S(1)} %get-tuple-element.35), channel_id=1, source_target_pairs={{0,1},{1,0},{2,3},{3,2},{4,5},{5,4},{6,7},{7,6},{8,9},{9,8},{10,11... | collective-permute-start | bytes 847880 | tf_op jit(solution)/shard_map/ppermute | solution.py:44
  13.3 0.0 collective-permute-start.3
  13.3 0.0 collective-permute-done.4.ra
  13.3 0.0 collective-permute-done.5.rb
  13.3 0.5 %first_stage_early.1 = (f32[8,128,128]{2,1,0:T(8,128)S(1)}, f32[512,128]{1,0:T(8,128)S(1)}, f32[512,128]{1,0:T(8,128)S(1)}, f32[128,128]{1,0:T(8,128)S(1)}) custom-call(f32[8,128,128]{2,1,0:T(8,128)S(1)} %get-tuple-element.28.tiles_first.q.q_early.refs_0_, f32[4,128,128]{2,1,0:T(8,128)S(1)} %get-tuple-element.30.ce.refs_2_, ...), custom_call_target="tpu_custom_call" | custom-call | flops 1000000000 | bytes 1000000000 | tf_op jit(solution)/shard_map/first_stage_early/pallas_call | solution.py:494
  13.8 1.8 %collective-permute-start.8 = (f32[512,128]{1,0:T(8,128)S(1)}, f32[512,128]{1,0:T(8,128)S(1)}, u32[]{:S(2)}, u32[]{:S(2)}) collective-permute-start(f32[512,128]{1,0:T(8,128)S(1)} %get-tuple-element.46), channel_id=1, source_target_pairs={{0,1},{1,0},{2,3},{3,2},{4,5},{5,4},{6,7},{7,6},{8,9},{9,8},{10,11... | collective-permute-start | bytes 786440 | tf_op jit(solution)/shard_map/ppermute | solution.py:44
  15.7 5.2 %collective-permute-done.2.ra = f32[552,128]{1,0:T(8,128)S(1)} collective-permute-done((f32[552,128]{1,0:T(8,128)S(1)}, f32[552,128]{1,0:T(8,128)S(1)}, u32[]{:S(2)}, u32[]{:S(2)}) %collective-permute-start.2) | collective-permute-done | bytes 282656 | tf_op jit(solution)/shard_map/ppermute | solution.py:44
  20.9 0.5 %first_stage_late.1 = (f32[8,128,128]{2,1,0:T(8,128)S(1)}, f32[512,128]{1,0:T(8,128)S(1)}, f32[512,128]{1,0:T(8,128)S(1)}, f32[128,128]{1,0:T(8,128)S(1)}) custom-call(f32[8,128,128]{2,1,0:T(8,128)S(1)} %get-tuple-element.29.tiles.q.refs_0_, f32[4,128,128]{2,1,0:T(8,128)S(1)} %get-tuple-element.30.ce.refs_2_, ...), custom_call_target="tpu_custom_call" | custom-call | flops 12000000 | bytes 12000000 | tf_op jit(solution)/shard_map/first_stage_late/pallas_call | solution.py:494
  21.4 2.2 %collective-permute-start.6 = (f32[512,128]{1,0:T(8,128)S(1)}, f32[512,128]{1,0:T(8,128)S(1)}, u32[]{:S(2)}, u32[]{:S(2)}) collective-permute-start(f32[512,128]{1,0:T(8,128)S(1)} %get-tuple-element.41), channel_id=1, source_target_pairs={{0,1},{1,0},{2,3},{3,2},{4,5},{5,4},{6,7},{7,6},{8,9},{9,8},{10,11... | collective-permute-start | bytes 786440 | tf_op jit(solution)/shard_map/ppermute | solution.py:44
  23.6 0.0 collective-permute-start.7
  23.6 5.0 %radiation.1.refs_9_ = f32[256,128]{1,0:T(8,128)S(1)} custom-call(f32[4,256,128]{2,1,0:T(8,128)S(1)} %get-tuple-element.44.nat, f32[4,128]{1,0:T(4,128)} %cosz_in.1, f32[4,128]{1,0:T(4,128)} %albedo_in.1, f32[14]{0:T(128)} %ext_in.1, f32[14]{0:T(128)} %single_in.1, f32[14]{0:T(128)} %weight_in.1, s32[4,1,128]{2,1,0:T(1,128)} %order_in.1, s32[4]{0:T(128)} %bitcast.8, ...), custom_call_target="tpu_custom_call" | custom-call | flops 16000000 | bytes 16000000 | tf_op jit(solution)/shard_map/radiation/pallas_call | solution.py:494
  28.6 0.0 collective-permute-done.9.refs_6_
  28.6 1.4 %second_stage_0.1 = (f32[8,256,128]{2,1,0:T(8,128)}, f32[256,128]{1,0:T(8,128)}) custom-call(f32[8,128,128]{2,1,0:T(8,128)S(1)} %get-tuple-element.28.tiles_first.q.q_early.refs_0_, f32[8,128,128]{2,1,0:T(8,128)S(1)} %get-tuple-element.45.refs_1_, f32[4,128,128]{2,1,0:T(8,128)S(1)} %get-tuple-element.30.ce.refs_2_, ...), custom_call_target="tpu_custom_call" | custom-call | flops 1000 | bytes 1000 | tf_op jit(solution)/shard_map/second_stage_0/pallas_call | solution.py:494
  30.0 1.4 %collective-permute-done.6.refs_5_ = f32[512,128]{1,0:T(8,128)S(1)} collective-permute-done((f32[512,128]{1,0:T(8,128)S(1)}, f32[512,128]{1,0:T(8,128)S(1)}, u32[]{:S(2)}, u32[]{:S(2)}) %collective-permute-start.6) | collective-permute-done | bytes 262176 | tf_op jit(solution)/shard_map/ppermute | solution.py:44
  31.4 1.4 %second_stage_1.1 = f32[8,256,128]{2,1,0:T(8,128)} custom-call(f32[8,128,128]{2,1,0:T(8,128)S(1)} %get-tuple-element.29.tiles.q.refs_0_, f32[8,128,128]{2,1,0:T(8,128)S(1)} %get-tuple-element.40.refs_1_, f32[4,128,128]{2,1,0:T(8,128)S(1)} %get-tuple-element.30.ce.refs_2_, ...), custom_call_target="tpu_custom_call", output_to_operand_aliasing={{}: (10, {})} | custom-call | flops 1000 | bytes 1000 | tf_op jit(solution)/shard_map/second_stage_1/pallas_call | solution.py:494
  (4 shorter events, 0.0 us)
Async XLA Ops:
  2.1 11.2 %collective-permute-start.4 = (f32[576,128]{1,0:T(8,128)S(1)}, f32[576,128]{1,0:T(8,128)S(1)}, u32[]{:S(2)}, u32[]{:S(2)}) collective-permute-start(f32[576,128]{1,0:T(8,128)S(1)} %get-tuple-element.37), channel_id=1, source_target_pairs={{0,1},{1,0},{2,3},{3,2},{4,5},{5,4},{6,7},{7,6},{8,9},{9,8},{10,11... | collective-permute-start | bytes 884744 | tf_op jit(solution)/shard_map/ppermute | solution.py:44
  5.2 8.1 %collective-permute-start.5 = (f32[576,128]{1,0:T(8,128)S(1)}, f32[576,128]{1,0:T(8,128)S(1)}, u32[]{:S(2)}, u32[]{:S(2)}) collective-permute-start(f32[576,128]{1,0:T(8,128)S(1)} %get-tuple-element.38), channel_id=1, source_target_pairs={{0,4},{1,2},{2,1},{3,7},{4,0},{5,6},{6,5},{7,3},{8,12},{9,10},{10,... | collective-permute-start | bytes 884744 | tf_op jit(solution)/shard_map/ppermute | solution.py:43
  5.5 2.7 %collective-permute-start = (f32[80,128]{1,0:T(8,128)S(1)}, f32[80,128]{1,0:T(8,128)S(1)}, u32[]{:S(2)}, u32[]{:S(2)}) collective-permute-start(f32[80,128]{1,0:T(8,128)S(1)} %get-tuple-element.32), channel_id=1, source_target_pairs={{0,4},{4,0},{8,12},{12,8},{16,20},{20,16},{24,28},{28,24},{1,5},{5... | collective-permute-start | bytes 122888 | tf_op jit(solution)/shard_map/ppermute | solution.py:32
  6.1 4.4 %collective-permute-start.1 = (f32[80,128]{1,0:T(8,128)S(1)}, f32[80,128]{1,0:T(8,128)S(1)}, u32[]{:S(2)}, u32[]{:S(2)}) collective-permute-start(f32[80,128]{1,0:T(8,128)S(1)} %get-tuple-element.33), channel_id=1, source_target_pairs={{0,28},{4,8},{8,4},{12,16},{16,12},{20,24},{24,20},{28,0},{1,29},{... | collective-permute-start | bytes 122888 | tf_op jit(solution)/shard_map/ppermute | solution.py:32
  10.6 10.2 %collective-permute-start.2 = (f32[552,128]{1,0:T(8,128)S(1)}, f32[552,128]{1,0:T(8,128)S(1)}, u32[]{:S(2)}, u32[]{:S(2)}) collective-permute-start(f32[552,128]{1,0:T(8,128)S(1)} %get-tuple-element.35), channel_id=1, source_target_pairs={{0,1},{1,0},{2,3},{3,2},{4,5},{5,4},{6,7},{7,6},{8,9},{9,8},{10,11... | collective-permute-start | bytes 847880 | tf_op jit(solution)/shard_map/ppermute | solution.py:44
  13.3 7.6 %collective-permute-start.3 = (f32[552,128]{1,0:T(8,128)S(1)}, f32[552,128]{1,0:T(8,128)S(1)}, u32[]{:S(2)}, u32[]{:S(2)}) collective-permute-start(f32[552,128]{1,0:T(8,128)S(1)} %get-tuple-element.36), channel_id=1, source_target_pairs={{0,4},{1,2},{2,1},{3,7},{4,0},{5,6},{6,5},{7,3},{8,12},{9,10},{10,... | collective-permute-start | bytes 847880 | tf_op jit(solution)/shard_map/ppermute | solution.py:43
  13.8 14.7 %collective-permute-start.8 = (f32[512,128]{1,0:T(8,128)S(1)}, f32[512,128]{1,0:T(8,128)S(1)}, u32[]{:S(2)}, u32[]{:S(2)}) collective-permute-start(f32[512,128]{1,0:T(8,128)S(1)} %get-tuple-element.46), channel_id=1, source_target_pairs={{0,1},{1,0},{2,3},{3,2},{4,5},{5,4},{6,7},{7,6},{8,9},{9,8},{10,11... | collective-permute-start | bytes 786440 | tf_op jit(solution)/shard_map/ppermute | solution.py:44
  15.7 12.9 %collective-permute-start.9 = (f32[512,128]{1,0:T(8,128)S(1)}, f32[512,128]{1,0:T(8,128)S(1)}, u32[]{:S(2)}, u32[]{:S(2)}) collective-permute-start(f32[512,128]{1,0:T(8,128)S(1)} %get-tuple-element.47), channel_id=1, source_target_pairs={{0,4},{1,2},{2,1},{3,7},{4,0},{5,6},{6,5},{7,3},{8,12},{9,10},{10,... | collective-permute-start | bytes 786440 | tf_op jit(solution)/shard_map/ppermute | solution.py:43
  21.4 10.0 %collective-permute-start.6 = (f32[512,128]{1,0:T(8,128)S(1)}, f32[512,128]{1,0:T(8,128)S(1)}, u32[]{:S(2)}, u32[]{:S(2)}) collective-permute-start(f32[512,128]{1,0:T(8,128)S(1)} %get-tuple-element.41), channel_id=1, source_target_pairs={{0,1},{1,0},{2,3},{3,2},{4,5},{5,4},{6,7},{7,6},{8,9},{9,8},{10,11... | collective-permute-start | bytes 786440 | tf_op jit(solution)/shard_map/ppermute | solution.py:44
  23.6 7.8 %collective-permute-start.7 = (f32[512,128]{1,0:T(8,128)S(1)}, f32[512,128]{1,0:T(8,128)S(1)}, u32[]{:S(2)}, u32[]{:S(2)}) collective-permute-start(f32[512,128]{1,0:T(8,128)S(1)} %get-tuple-element.42), channel_id=1, source_target_pairs={{0,4},{1,2},{2,1},{3,7},{4,0},{5,6},{6,5},{7,3},{8,12},{9,10},{10,... | collective-permute-start | bytes 786440 | tf_op jit(solution)/shard_map/ppermute | solution.py:43

commit v4 on v3

--- a/solution.py
+++ b/solution.py
@@ -9,6 +9,7 @@
 from jax.sharding import PartitionSpec as P
 
 SPLIT = 2
+MOVED = 1
 SUB = 8
 LANES = 128
 LOG2E = math.log2(math.e)
@@ -86,8 +87,11 @@
     n = 2 * pairs
     copies = [pltpu.make_async_copy(fields.at[i], nat.at[i], sems.at[i]) for i in range(n)]
     wind = pltpu.make_async_copy(courant, nat_wind, sems.at[n])
-    late = pltpu.make_async_copy(fields.at[pl.ds(n, nat_late.shape[0])], nat_late, sems.at[n + 1])
-    for copy in copies + [wind, late]:
+    late = [
+        pltpu.make_async_copy(fields.at[pl.ds(n + i, 2)], nat_late.at[pl.ds(i, 2)], sems.at[n + 1 + i // 2])
+        for i in range(0, nat_late.shape[0], 2)
+    ]
+    for copy in copies + [wind] + late:
         copy.start()
     even = is_even("lat")
     for p in range(pairs):
@@ -102,10 +106,19 @@
     half = LANES // 2
     lane = lax.broadcasted_iota(jnp.int32, (half, LANES), 1)
     top = jnp.where(lane < half, top[:half], top[half:])
-    span = pl.ds(2 * pairs * LANES, half)
+    span = pl.ds((2 * pairs + MOVED) * LANES, half)
     za[span, :] = top
     zb[span, :] = top
-    late.wait()
+    for copy in late:
+        copy.wait()
+    for i in range(MOVED):
+        p, k = divmod(i, 2)
+        low, high = (
+            tile_of(native(nat_late, 2 * p, r, nrows), native(nat_late, 2 * p + 1, r, nrows)) for r in (k, k + 2)
+        )
+        span = pl.ds((2 * pairs + i) * LANES, LANES)
+        za[span, :] = jnp.where(even, high, low)
+        zb[span, :] = jnp.where(even, low, high)
 
 
 def pack_middle(pairs, nrows, nat, nat_wind, tiles_first, tiles, ce, cn, la, lb):
@@ -147,7 +160,7 @@
     for t, value in enumerate(blocks):
         side[pl.ds(SUB * t, SUB), :] = value
     north = jnp.where(lat_even, 2, 0)
-    at = 2 * pairs * LANES
+    at = (2 * pairs - MOVED) * LANES
     row = sublanes()
     outer = (row < 2) | (row >= SUB - 2)
 
@@ -164,8 +177,11 @@
     top = side[pl.ds(SUB * (ntiles + 2 * nrows - 1), SUB), :]
     za[to, :] = top
     zb[to, :] = top
-    for p in range(pairs):
-        put_lat_sends(lat_even, tiles, p, nrows, za, zb)
+    for i in range(MOVED, 2 * pairs):
+        p, k = divmod(i, 2)
+        span = pl.ds((i - MOVED) * LANES, LANES)
+        za[span, :] = tiles[nrows * p + north + k]
+        zb[span, :] = tiles[nrows * p + (2 - north) + k]
 
 
 def put_edges(q, first, side, at, nrows, edge_w, edge_e):
@@ -218,15 +234,10 @@
     return south, jnp.where(north_a, a, jnp.where(north_b, b, 0.0))
 
 
-def divergence(q, pair, nrows, b, where, ra, rb, cn, below, flux):
+def divergence(q, pair, nrows, b, halo, cn, below, flux):
     at = SUB * b
     here = pl.ds(at, SUB)
-
-    def halo(k):
-        start = pl.multiple_of((2 * pair + k) * LANES, LANES) + at
-        return partners(where, ra, rb, pl.ds(start, SUB))
-
-    (s0, n0), (s1, n1) = halo(0), halo(1)
+    (s0, n0), (s1, n1) = halo(0, at), halo(1, at)
     own = [q[nrows * pair + r, here, :] for r in range(nrows)]
     winds = [below[here, :]] + [cn[r, here, :] for r in range(nrows)]
     north = lat_divergence([s0, s1] + own + [n0, n1], winds)
@@ -271,7 +282,7 @@
     edge_w, edge_e, edge_c, edge_d, flux = edges
     lat_even, where = is_even("lat"), sources()
     half = LANES // 2
-    a = partners(where, ra, rb, pl.ds(2 * pairs * LANES, half))[0]
+    a = partners(where, ra, rb, pl.ds((2 * pairs + MOVED) * LANES, half))[0]
     turned = pltpu.roll(a, half, 1)
     low = lax.broadcasted_iota(jnp.int32, (half, LANES), 1) < half
     below[pl.ds(0, half), :] = jnp.where(low, a, turned)
@@ -279,10 +290,14 @@
     put_edges(ce, 0, side, side.shape[0] // SUB - 2 * nrows, nrows, edge_c, edge_d)
 
     def one(p, _):
+        def halo(k, shift):
+            start = pl.multiple_of((2 * p + k) * LANES, LANES)
+            return partners(where, ra, rb, pl.ds(start + shift, SUB))
+
         put_edges(q, nrows * p, side, nrows * p, nrows, edge_w, edge_e)
         put_fluxes(q, nrows * p, nrows, ce, edge_w, edge_e, edge_c, flux)
         for b in range(LANES // SUB):
-            own, div = divergence(q, p, nrows, b, where, ra, rb, cn, below, flux)
+            own, div = divergence(q, p, nrows, b, halo, cn, below, flux)
             for r in range(nrows):
                 section[nrows * p + r, pl.ds(SUB * b, SUB), :] = own[r] - div[r]
         put_lat_sends(lat_even, section, p, nrows, za, zb)
@@ -292,12 +307,12 @@
 
 
 def first_stage_late(
-    pairs, done, nrows, q, ce, cn, side, ra, rb, below, q_early, section, za, zb, sides, *edges
+    pairs, done, nrows, q, ce, cn, side, ra, rb, ra_first, rb_first, below, q_early, section, za, zb, sides, *edges
 ):
     edge_w, edge_e, edge_c, edge_d, flux = edges
     lat_even, where = is_even("lat"), sources()
     ntiles = nrows * (done + pairs)
-    corner = 2 * pairs * LANES
+    corner = (2 * pairs - MOVED) * LANES
     put_edges(ce, 0, side, ntiles, nrows, edge_c, edge_d)
 
     def side_section(at):
@@ -305,24 +320,30 @@
             at, nrows, where, ra, rb, corner, side, ntiles, edge_w, edge_e, edge_c, edge_d, sides
         )
 
-    def one(p, _):
+    def one(p):
+        def halo(k, shift):
+            i = 2 * p + k
+            if i < MOVED:
+                return partners(where, ra_first, rb_first, pl.ds((2 * done + i) * LANES + shift, SUB))
+            return partners(where, ra, rb, pl.ds((i - MOVED) * LANES + shift, SUB))
+
         at = nrows * (done + p)
         put_edges(q, nrows * p, side, at, nrows, edge_w, edge_e)
         put_fluxes(q, nrows * p, nrows, ce, edge_w, edge_e, edge_c, flux)
         for b in range(LANES // SUB):
-            own, div = divergence(q, p, nrows, b, where, ra, rb, cn, below, flux)
+            own, div = divergence(q, p, nrows, b, halo, cn, below, flux)
             for r in range(nrows):
                 section[nrows * p + r, pl.ds(SUB * b, SUB), :] = own[r] - div[r]
         put_lat_sends(lat_even, section, p, nrows, za, zb)
         side_section(at)
-        return 0
 
     def another(p, _):
         put_edges(q_early, nrows * p, side, nrows * p, nrows, edge_w, edge_e)
         side_section(nrows * p)
         return 0
 
-    lax.fori_loop(0, pairs, one, 0)
+    for p in range(pairs):
+        one(p)
     lax.fori_loop(0, done, another, 0)
 
 
@@ -344,11 +365,15 @@
         )
 
     def one(p, _):
+        def halo(k, shift):
+            start = pl.multiple_of((2 * p + k) * LANES, LANES)
+            return partners(where, ra, rb, pl.ds(start + shift, SUB))
+
         put_edges(s, nrows * p, sides, nrows * (done + p), nrows, edge_w, edge_e)
         put_fluxes(s, nrows * p, nrows, ce, edge_w, edge_e, edge_c, flux)
         parts = [[] for _ in range(nrows)]
         for b in range(LANES // SUB):
-            own, div = divergence(s, p, nrows, b, where, ra, rb, cn, below, flux)
+            own, div = divergence(s, p, nrows, b, halo, cn, below, flux)
             for r in range(nrows):
                 old = q[nrows * p + r, pl.ds(SUB * b, SUB), :]
                 parts[r].append(0.5 * ((old + own[r]) - div[r]))
@@ -515,7 +540,7 @@
     starts = (0, SPLIT)
     early, late = counts
 
-    z0 = shape((2 * early) * ncols + ncols // 2, LANES)
+    z0 = shape((2 * early + MOVED) * ncols + ncols // 2, LANES)
     tiles0, za, zb, nat, nat_late, nat_wind = call(
         functools.partial(pack_first, early, nrows),
         "pack_first",
@@ -527,7 +552,7 @@
         [HBM, HBM],
         (VMEM,) * 6,
         (in_hbm(flat), in_hbm(wind)),
-        [pltpu.SemaphoreType.DMA((2 * early + 2,))],
+        [pltpu.SemaphoreType.DMA((2 * early + 1 + late,))],
     )
     lat0 = lat_swaps(za, zb)
     ntiles = nrows * npairs
@@ -544,7 +569,7 @@
         [],
     )
     lon = lon_swaps(la, lb)
-    z1 = shape(2 * late * ncols + SUB * (npairs + 1), LANES)
+    z1 = shape((2 * late - MOVED) * ncols + SUB * (npairs + 1), LANES)
     za, zb, side = call(
         functools.partial(pack_last, late, early, nrows),
         "pack_last",
@@ -574,9 +599,9 @@
         functools.partial(first_stage_late, late, early, nrows),
         "first_stage_late",
         (shape(nrows * late, ncols, LANES), z1, z1, shape(SUB * ntiles, LANES)),
-        [VMEM] * 8,
+        [VMEM] * 10,
         (VMEM,) * 4,
-        (tiles1, ce, cn, side, *lat1, below, tiles0),
+        (tiles1, ce, cn, side, *lat1, *lat0, below, tiles0),
         edges,
         moved=12_000_000,
     )

time: 32.9 us -> 31.6 us (0.960)
  waiting for transfers between devices: 8.89 us -> 5.33 us
  starting transfers between devices: 12.5 us -> 14.6 us
    ppermute x4, waiting for transfers between devices: 6.56 us -> 3 us  [lat_swaps(): lax.ppermute(first_block, 'lat', [(j, j ^ 1) for j in range(nlat)])]
    ppermute x4, starting transfers between devices: 9.75 us -> 11.8 us  [lat_swaps(): lax.ppermute(first_block, 'lat', [(j, j ^ 1) for j in range(nlat)])]
  transfers between devices with their start and end apart: 10 -> 10, of which waited for: 3 -> 4; matrix products, arithmetic and copies ran while one was open for 0% -> 0% of each run, Pallas kernels for 24% -> 25%
where the time goes in v4:
time: 31.6 us; the launch traced here: 31.4 us
  starting transfers between devices  14.6 us (46%)
  Pallas kernels  10.8 us (34%)
  waiting for transfers between devices  5.33 us (17%)
  between operations  0.7 us (2%)
    ppermute x4, starting transfers between devices, lat_swaps(): lax.ppermute(first_block, 'lat', [(j, j ^ 1) for j in range(nlat)])  11.8 us
    pallas_call x8, Pallas kernels, call(): pl.pallas_call(kernel, out_shape=out_shape, in_specs=specs, out_specs=out...  10.8 us
    ppermute x4, waiting for transfers between devices, lat_swaps(): lax.ppermute(first_block, 'lat', [(j, j ^ 1) for j in range(nlat)])  3 us
    ppermute x1, waiting for transfers between devices, lon_swaps(): lax.ppermute(second_block, 'lon', second)  2.31 us
    ppermute x1, starting transfers between devices, lon_swaps(): lax.ppermute(second_block, 'lon', second)  2.13 us
  transfers between devices with their start and end apart: 10, of which 4 were waited for; matrix products, arithmetic and copies ran while one was open for 0% of the time, Pallas kernels for 25%

profile of v4, /device:TPU:0, one launch (start us, length us, event | category | flops | bytes accessed | tf_op | source)
XLA Modules:
  0.0 31.4 jit_solution(13525025710068591070)
XLA Ops:
  0.6 1.6 %pack_first.1 = (f32[8,128,128]{2,1,0:T(8,128)S(1)}, f32[704,128]{1,0:T(8,128)S(1)}, f32[704,128]{1,0:T(8,128)S(1)}, f32[4,256,128]{2,1,0:T(8,128)S(1)}, f32[4,2...) custom-call(f32[8,256,128]{2,1,0:T(8,128)} %bitcast.6, f32[2,256,128]{2,1,0:T(8,128)} %bitcast.7), custom_call_target="tpu_custom_call" | custom-call | flops 1000 | bytes 1000 | tf_op jit(solution)/shard_map/pack_first/pallas_call | solution.py:519
  2.2 3.1 %collective-permute-start.4 = (f32[704,128]{1,0:T(8,128)S(1)}, f32[704,128]{1,0:T(8,128)S(1)}, u32[]{:S(2)}, u32[]{:S(2)}) collective-permute-start(f32[704,128]{1,0:T(8,128)S(1)} %get-tuple-element.37), channel_id=1, source_target_pairs={{0,1},{1,0},{2,3},{3,2},{4,5},{5,4},{6,7},{7,6},{8,9},{9,8},{10,11... | collective-permute-start | bytes 1081352 | tf_op jit(solution)/shard_map/ppermute | solution.py:45
  5.3 0.0 collective-permute-start.5
  5.3 0.3 %pack_middle.1 = (f32[8,128,128]{2,1,0:T(8,128)S(1)}, f32[4,128,128]{2,1,0:T(8,128)S(1)}, f32[4,128,128]{2,1,0:T(8,128)S(1)}, f32[80,128]{1,0:T(8,128)S(1)}, f32[80,128]{1,0:T(8,128)S(1)}) custom-call(f32[4,256,128]{2,1,0:T(8,128)S(1)} %get-tuple-element.26.nat, f32[2,256,128]{2,1,0:T(8,128)S(1)} %get-tuple-element.27.nat_wind, ...), custom_call_target="tpu_custom_call" | custom-call | flops 1000 | bytes 1000 | tf_op jit(solution)/shard_map/pack_middle/pallas_call | solution.py:519
  5.6 0.6 %collective-permute-start = (f32[80,128]{1,0:T(8,128)S(1)}, f32[80,128]{1,0:T(8,128)S(1)}, u32[]{:S(2)}, u32[]{:S(2)}) collective-permute-start(f32[80,128]{1,0:T(8,128)S(1)} %get-tuple-element.32), channel_id=1, source_target_pairs={{0,4},{4,0},{8,12},{12,8},{16,20},{20,16},{24,28},{28,24},{1,5},{5... | collective-permute-start | bytes 122888 | tf_op jit(solution)/shard_map/ppermute | solution.py:33
  6.2 2.1 %collective-permute-start.1 = (f32[80,128]{1,0:T(8,128)S(1)}, f32[80,128]{1,0:T(8,128)S(1)}, u32[]{:S(2)}, u32[]{:S(2)}) collective-permute-start(f32[80,128]{1,0:T(8,128)S(1)} %get-tuple-element.33), channel_id=1, source_target_pairs={{0,28},{4,8},{8,4},{12,16},{16,12},{20,24},{24,20},{28,0},{1,29},{... | collective-permute-start | bytes 122888 | tf_op jit(solution)/shard_map/ppermute | solution.py:33
  8.4 0.0 collective-permute-done.la
  8.4 2.3 %collective-permute-done.1.lb = f32[80,128]{1,0:T(8,128)S(1)} collective-permute-done((f32[80,128]{1,0:T(8,128)S(1)}, f32[80,128]{1,0:T(8,128)S(1)}, u32[]{:S(2)}, u32[]{:S(2)}) %collective-permute-start.1) | collective-permute-done | bytes 40992 | tf_op jit(solution)/shard_map/ppermute | solution.py:33
  10.7 0.1 pack_last.1
  10.8 2.6 %collective-permute-start.2 = (f32[424,128]{1,0:T(8,128)S(1)}, f32[424,128]{1,0:T(8,128)S(1)}, u32[]{:S(2)}, u32[]{:S(2)}) collective-permute-start(f32[424,128]{1,0:T(8,128)S(1)} %get-tuple-element.35), channel_id=1, source_target_pairs={{0,1},{1,0},{2,3},{3,2},{4,5},{5,4},{6,7},{7,6},{8,9},{9,8},{10,11... | collective-permute-start | bytes 651272 | tf_op jit(solution)/shard_map/ppermute | solution.py:45
  13.4 0.3 %collective-permute-done.4.ra.ra_first = f32[704,128]{1,0:T(8,128)S(1)} collective-permute-done((f32[704,128]{1,0:T(8,128)S(1)}, f32[704,128]{1,0:T(8,128)S(1)}, u32[]{:S(2)}, u32[]{:S(2)}) %collective-permute-start.4) | collective-permute-done | bytes 360480 | tf_op jit(solution)/shard_map/ppermute | solution.py:45
  13.7 0.0 collective-permute-done.5.rb.rb_first
  13.7 0.5 %first_stage_early.1 = (f32[8,128,128]{2,1,0:T(8,128)S(1)}, f32[512,128]{1,0:T(8,128)S(1)}, f32[512,128]{1,0:T(8,128)S(1)}, f32[128,128]{1,0:T(8,128)S(1)}) custom-call(f32[8,128,128]{2,1,0:T(8,128)S(1)} %get-tuple-element.28.tiles_first.q.q_early.refs_0_, f32[4,128,128]{2,1,0:T(8,128)S(1)} %get-tuple-element.30.ce.refs_2_, ...), custom_call_target="tpu_custom_call" | custom-call | flops 1000000000 | bytes 1000000000 | tf_op jit(solution)/shard_map/first_stage_early/pallas_call | solution.py:519
  14.3 3.7 %collective-permute-start.8 = (f32[512,128]{1,0:T(8,128)S(1)}, f32[512,128]{1,0:T(8,128)S(1)}, u32[]{:S(2)}, u32[]{:S(2)}) collective-permute-start(f32[512,128]{1,0:T(8,128)S(1)} %get-tuple-element.46), channel_id=1, source_target_pairs={{0,1},{1,0},{2,3},{3,2},{4,5},{5,4},{6,7},{7,6},{8,9},{9,8},{10,11... | collective-permute-start | bytes 786440 | tf_op jit(solution)/shard_map/ppermute | solution.py:45
  17.9 0.0 collective-permute-start.9
  17.9 1.6 %collective-permute-done.2.ra = f32[424,128]{1,0:T(8,128)S(1)} collective-permute-done((f32[424,128]{1,0:T(8,128)S(1)}, f32[424,128]{1,0:T(8,128)S(1)}, u32[]{:S(2)}, u32[]{:S(2)}) %collective-permute-start.2) | collective-permute-done | bytes 217120 | tf_op jit(solution)/shard_map/ppermute | solution.py:45
  19.5 0.6 %first_stage_late.1 = (f32[8,128,128]{2,1,0:T(8,128)S(1)}, f32[512,128]{1,0:T(8,128)S(1)}, f32[512,128]{1,0:T(8,128)S(1)}, f32[128,128]{1,0:T(8,128)S(1)}) custom-call(f32[8,128,128]{2,1,0:T(8,128)S(1)} %get-tuple-element.29.tiles.q.refs_0_, f32[4,128,128]{2,1,0:T(8,128)S(1)} %get-tuple-element.30.ce.refs_2_, ...), custom_call_target="tpu_custom_call" | custom-call | flops 12000000 | bytes 12000000 | tf_op jit(solution)/shard_map/first_stage_late/pallas_call | solution.py:519
  20.1 2.5 %collective-permute-start.6 = (f32[512,128]{1,0:T(8,128)S(1)}, f32[512,128]{1,0:T(8,128)S(1)}, u32[]{:S(2)}, u32[]{:S(2)}) collective-permute-start(f32[512,128]{1,0:T(8,128)S(1)} %get-tuple-element.41), channel_id=1, source_target_pairs={{0,1},{1,0},{2,3},{3,2},{4,5},{5,4},{6,7},{7,6},{8,9},{9,8},{10,11... | collective-permute-start | bytes 786440 | tf_op jit(solution)/shard_map/ppermute | solution.py:45
  22.6 5.0 %radiation.1.refs_9_ = f32[256,128]{1,0:T(8,128)S(1)} custom-call(f32[4,256,128]{2,1,0:T(8,128)S(1)} %get-tuple-element.44.nat, f32[4,128]{1,0:T(4,128)} %cosz_in.1, f32[4,128]{1,0:T(4,128)} %albedo_in.1, f32[14]{0:T(128)} %ext_in.1, f32[14]{0:T(128)} %single_in.1, f32[14]{0:T(128)} %weight_in.1, s32[4,1,128]{2,1,0:T(1,128)} %order_in.1, s32[4]{0:T(128)} %bitcast.8, ...), custom_call_target="tpu_custom_call" | custom-call | flops 16000000 | bytes 16000000 | tf_op jit(solution)/shard_map/radiation/pallas_call | solution.py:519
  27.6 0.0 collective-permute-done.8.refs_5_
  27.6 1.4 %second_stage_0.1 = (f32[8,256,128]{2,1,0:T(8,128)}, f32[256,128]{1,0:T(8,128)}) custom-call(f32[8,128,128]{2,1,0:T(8,128)S(1)} %get-tuple-element.28.tiles_first.q.q_early.refs_0_, f32[8,128,128]{2,1,0:T(8,128)S(1)} %get-tuple-element.45.refs_1_, f32[4,128,128]{2,1,0:T(8,128)S(1)} %get-tuple-element.30.ce.refs_2_, ...), custom_call_target="tpu_custom_call" | custom-call | flops 1000 | bytes 1000 | tf_op jit(solution)/shard_map/second_stage_0/pallas_call | solution.py:519
  29.0 1.0 %collective-permute-done.6.refs_5_ = f32[512,128]{1,0:T(8,128)S(1)} collective-permute-done((f32[512,128]{1,0:T(8,128)S(1)}, f32[512,128]{1,0:T(8,128)S(1)}, u32[]{:S(2)}, u32[]{:S(2)}) %collective-permute-start.6) | collective-permute-done | bytes 262176 | tf_op jit(solution)/shard_map/ppermute | solution.py:45
  30.0 0.0 collective-permute-done.7.refs_6_
  30.0 1.4 %second_stage_1.1 = f32[8,256,128]{2,1,0:T(8,128)} custom-call(f32[8,128,128]{2,1,0:T(8,128)S(1)} %get-tuple-element.29.tiles.q.refs_0_, f32[8,128,128]{2,1,0:T(8,128)S(1)} %get-tuple-element.40.refs_1_, f32[4,128,128]{2,1,0:T(8,128)S(1)} %get-tuple-element.30.ce.refs_2_, ...), custom_call_target="tpu_custom_call", output_to_operand_aliasing={{}: (10, {})} | custom-call | flops 1000 | bytes 1000 | tf_op jit(solution)/shard_map/second_stage_1/pallas_call | solution.py:519
  (4 shorter events, 0.0 us)
Async XLA Ops:
  2.2 11.5 %collective-permute-start.4 = (f32[704,128]{1,0:T(8,128)S(1)}, f32[704,128]{1,0:T(8,128)S(1)}, u32[]{:S(2)}, u32[]{:S(2)}) collective-permute-start(f32[704,128]{1,0:T(8,128)S(1)} %get-tuple-element.37), channel_id=1, source_target_pairs={{0,1},{1,0},{2,3},{3,2},{4,5},{5,4},{6,7},{7,6},{8,9},{9,8},{10,11... | collective-permute-start | bytes 1081352 | tf_op jit(solution)/shard_map/ppermute | solution.py:45
  5.3 8.4 %collective-permute-start.5 = (f32[704,128]{1,0:T(8,128)S(1)}, f32[704,128]{1,0:T(8,128)S(1)}, u32[]{:S(2)}, u32[]{:S(2)}) collective-permute-start(f32[704,128]{1,0:T(8,128)S(1)} %get-tuple-element.38), channel_id=1, source_target_pairs={{0,4},{1,2},{2,1},{3,7},{4,0},{5,6},{6,5},{7,3},{8,12},{9,10},{10,... | collective-permute-start | bytes 1081352 | tf_op jit(solution)/shard_map/ppermute | solution.py:44
  5.6 2.7 %collective-permute-start = (f32[80,128]{1,0:T(8,128)S(1)}, f32[80,128]{1,0:T(8,128)S(1)}, u32[]{:S(2)}, u32[]{:S(2)}) collective-permute-start(f32[80,128]{1,0:T(8,128)S(1)} %get-tuple-element.32), channel_id=1, source_target_pairs={{0,4},{4,0},{8,12},{12,8},{16,20},{20,16},{24,28},{28,24},{1,5},{5... | collective-permute-start | bytes 122888 | tf_op jit(solution)/shard_map/ppermute | solution.py:33
  6.2 4.4 %collective-permute-start.1 = (f32[80,128]{1,0:T(8,128)S(1)}, f32[80,128]{1,0:T(8,128)S(1)}, u32[]{:S(2)}, u32[]{:S(2)}) collective-permute-start(f32[80,128]{1,0:T(8,128)S(1)} %get-tuple-element.33), channel_id=1, source_target_pairs={{0,28},{4,8},{8,4},{12,16},{16,12},{20,24},{24,20},{28,0},{1,29},{... | collective-permute-start | bytes 122888 | tf_op jit(solution)/shard_map/ppermute | solution.py:33
  10.8 8.8 %collective-permute-start.2 = (f32[424,128]{1,0:T(8,128)S(1)}, f32[424,128]{1,0:T(8,128)S(1)}, u32[]{:S(2)}, u32[]{:S(2)}) collective-permute-start(f32[424,128]{1,0:T(8,128)S(1)} %get-tuple-element.35), channel_id=1, source_target_pairs={{0,1},{1,0},{2,3},{3,2},{4,5},{5,4},{6,7},{7,6},{8,9},{9,8},{10,11... | collective-permute-start | bytes 651272 | tf_op jit(solution)/shard_map/ppermute | solution.py:45
  13.4 6.2 %collective-permute-start.3 = (f32[424,128]{1,0:T(8,128)S(1)}, f32[424,128]{1,0:T(8,128)S(1)}, u32[]{:S(2)}, u32[]{:S(2)}) collective-permute-start(f32[424,128]{1,0:T(8,128)S(1)} %get-tuple-element.36), channel_id=1, source_target_pairs={{0,4},{1,2},{2,1},{3,7},{4,0},{5,6},{6,5},{7,3},{8,12},{9,10},{10,... | collective-permute-start | bytes 651272 | tf_op jit(solution)/shard_map/ppermute | solution.py:44
  14.3 13.3 %collective-permute-start.8 = (f32[512,128]{1,0:T(8,128)S(1)}, f32[512,128]{1,0:T(8,128)S(1)}, u32[]{:S(2)}, u32[]{:S(2)}) collective-permute-start(f32[512,128]{1,0:T(8,128)S(1)} %get-tuple-element.46), channel_id=1, source_target_pairs={{0,1},{1,0},{2,3},{3,2},{4,5},{5,4},{6,7},{7,6},{8,9},{9,8},{10,11... | collective-permute-start | bytes 786440 | tf_op jit(solution)/shard_map/ppermute | solution.py:45
  17.9 9.7 %collective-permute-start.9 = (f32[512,128]{1,0:T(8,128)S(1)}, f32[512,128]{1,0:T(8,128)S(1)}, u32[]{:S(2)}, u32[]{:S(2)}) collective-permute-start(f32[512,128]{1,0:T(8,128)S(1)} %get-tuple-element.47), channel_id=1, source_target_pairs={{0,4},{1,2},{2,1},{3,7},{4,0},{5,6},{6,5},{7,3},{8,12},{9,10},{10,... | collective-permute-start | bytes 786440 | tf_op jit(solution)/shard_map/ppermute | solution.py:44
  20.1 9.9 %collective-permute-start.6 = (f32[512,128]{1,0:T(8,128)S(1)}, f32[512,128]{1,0:T(8,128)S(1)}, u32[]{:S(2)}, u32[]{:S(2)}) collective-permute-start(f32[512,128]{1,0:T(8,128)S(1)} %get-tuple-element.41), channel_id=1, source_target_pairs={{0,1},{1,0},{2,3},{3,2},{4,5},{5,4},{6,7},{7,6},{8,9},{9,8},{10,11... | collective-permute-start | bytes 786440 | tf_op jit(solution)/shard_map/ppermute | solution.py:45
  22.6 7.4 %collective-permute-start.7 = (f32[512,128]{1,0:T(8,128)S(1)}, f32[512,128]{1,0:T(8,128)S(1)}, u32[]{:S(2)}, u32[]{:S(2)}) collective-permute-start(f32[512,128]{1,0:T(8,128)S(1)} %get-tuple-element.42), channel_id=1, source_target_pairs={{0,4},{1,2},{2,1},{3,7},{4,0},{5,6},{6,5},{7,3},{8,12},{9,10},{10,... | collective-permute-start | bytes 786440 | tf_op jit(solution)/shard_map/ppermute | solution.py:44

commit v5 on v4

--- a/solution.py
+++ b/solution.py
@@ -347,29 +347,33 @@
     lax.fori_loop(0, done, another, 0)
 
 
-def second_stage(pairs, done, nrows, is_first, *refs):
-    q, s, ce, cn, below, ra, rb, side, sides, heating = refs[:10]
-    buffer, sems, edge_w, edge_e, edge_c, edge_d, flux = refs[-7:]
-    out = refs[11]
+def put_rows(buffer, pair, rows, nrows):
     levels = LANES // 2
+    for r in range(nrows):
+        turned = jnp.transpose(jnp.concatenate(rows[r], axis=0))
+        for h in range(2):
+            buffer[2 * pair + h, pl.ds(r, levels, stride=nrows), :] = turned[levels * h : levels * (h + 1)]
+
+
+def second_stage_early(
+    pairs, later, nrows, q, s, ce, cn, below, ra, rb, side, sides, heating, q_late, s_late,
+    out, heat_out, part, buffer, sems, *edges
+):
+    edge_w, edge_e, edge_c, edge_d, flux = edges
     where = sources()
-    if is_first:
-        out, heat_out = refs[10:12]
-        heat_copy = pltpu.make_async_copy(heating, heat_out, sems.at[pairs])
-        heat_copy.start()
+    heat_copy = pltpu.make_async_copy(heating, heat_out, sems.at[pairs])
+    heat_copy.start()
     put_edges(ce, 0, side, side.shape[0] // SUB - 2 * nrows, nrows, edge_c, edge_d)
 
     def copy(p):
-        return pltpu.make_async_copy(
-            buffer.at[pl.ds(2 * p, 2)], out.at[pl.ds(2 * (done + p), 2)], sems.at[p]
-        )
+        return pltpu.make_async_copy(buffer.at[pl.ds(2 * p, 2)], out.at[pl.ds(2 * p, 2)], sems.at[p])
 
     def one(p, _):
         def halo(k, shift):
             start = pl.multiple_of((2 * p + k) * LANES, LANES)
             return partners(where, ra, rb, pl.ds(start + shift, SUB))
 
-        put_edges(s, nrows * p, sides, nrows * (done + p), nrows, edge_w, edge_e)
+        put_edges(s, nrows * p, sides, nrows * p, nrows, edge_w, edge_e)
         put_fluxes(s, nrows * p, nrows, ce, edge_w, edge_e, edge_c, flux)
         parts = [[] for _ in range(nrows)]
         for b in range(LANES // SUB):
@@ -377,24 +381,75 @@
             for r in range(nrows):
                 old = q[nrows * p + r, pl.ds(SUB * b, SUB), :]
                 parts[r].append(0.5 * ((old + own[r]) - div[r]))
-        for r in range(nrows):
-            turned = jnp.transpose(jnp.concatenate(parts[r], axis=0))
-            for h in range(2):
-                buffer[2 * p + h, pl.ds(r, levels, stride=nrows), :] = turned[levels * h : levels * (h + 1)]
-        if is_first:
-
-            @pl.when(p == 0)
-            def _():
-                buffer[0] = buffer[0] + 0.5 * heating[...]
-
+        put_rows(buffer, p, parts, nrows)
+
+        @pl.when(p == 0)
+        def _():
+            buffer[0] = buffer[0] + 0.5 * heating[...]
+
+        copy(p).start()
+        return 0
+
+    def another(p, _):
+        put_edges(s_late, nrows * p, sides, nrows * (pairs + p), nrows, edge_w, edge_e)
+        put_fluxes(s_late, nrows * p, nrows, ce, edge_w, edge_e, edge_c, flux)
+        for b in range(LANES // SUB):
+            here = pl.ds(SUB * b, SUB)
+            s0, s1, s2, s3 = own = [s_late[nrows * p + r, here, :] for r in range(nrows)]
+            c = [below[here, :]] + [cn[r, here, :] for r in range(nrows)]
+            north = [
+                c[0] * (7.0 * s0 - s1),
+                c[1] * (7.0 * (s0 + s1) - s2),
+                through(c[2], *own),
+                c[3] * (7.0 * (s2 + s3) - s1),
+                c[4] * (7.0 * s3 - s2),
+            ]
+            for r in range(nrows):
+                east = flux[r, pl.ds(SUB * (b + 1), SUB), :] - flux[r, pl.ds(SUB * (b + 1) - 1, SUB), :]
+                old = q_late[nrows * p + r, here, :]
+                part[nrows * p + r, here, :] = 0.5 * ((old + own[r]) - (east + (north[r + 1] - north[r])))
+        return 0
+
+    lax.fori_loop(0, pairs, one, 0)
+    lax.fori_loop(0, later, another, 0)
+    for p in range(pairs):
+        copy(p).wait()
+    heat_copy.wait()
+
+
+def second_stage_late(pairs, done, nrows, part, cn, below, ra, rb, before, out, buffer, sems):
+    del before
+    where = sources()
+
+    def copy(p):
+        return pltpu.make_async_copy(
+            buffer.at[pl.ds(2 * p, 2)], out.at[pl.ds(2 * (done + p), 2)], sems.at[p]
+        )
+
+    def one(p, _):
+        rows = [[] for _ in range(nrows)]
+        for b in range(LANES // SUB):
+            here = pl.ds(SUB * b, SUB)
+
+            def halo(k):
+                start = pl.multiple_of((2 * p + k) * LANES, LANES) + SUB * b
+                return partners(where, ra, rb, pl.ds(start, SUB))
+
+            (south_two, north_one), (south_one, north_two) = halo(0), halo(1)
+            low = 0.5 * cn[0, here, :] * south_one
+            high = 0.5 * cn[2, here, :] * north_one
+            bottom = 0.5 * below[here, :] * (7.0 * south_one - south_two)
+            top = 0.5 * cn[3, here, :] * (7.0 * north_one - north_two)
+            p0, p1, p2, p3 = (part[nrows * p + r, here, :] for r in range(nrows))
+            for r, value in enumerate((p0 + (low + bottom), p1 - low, p2 + high, p3 - (top + high))):
+                rows[r].append(value)
+        put_rows(buffer, p, rows, nrows)
         copy(p).start()
         return 0
 
     lax.fori_loop(0, pairs, one, 0)
     for p in range(pairs):
         copy(p).wait()
-    if is_first:
-        heat_copy.wait()
 
 
 def radiation(
@@ -536,9 +591,7 @@
     flat = fields.reshape(nfields, levels * nrows, ncols)
     wind = courant.reshape(2, levels * nrows, ncols)
     npairs = nfields // 2
-    counts = (SPLIT, npairs - SPLIT)
-    starts = (0, SPLIT)
-    early, late = counts
+    early, late = SPLIT, npairs - SPLIT
 
     z0 = shape((2 * early + MOVED) * ncols + ncols // 2, LANES)
     tiles0, za, zb, nat, nat_late, nat_wind = call(
@@ -630,33 +683,26 @@
         moved=16_000_000,
     )
 
-    out = heat_out = None
-    for g, (tiles, section, lat) in enumerate(((tiles0, section0, lat2), (tiles1, section1, lat3))):
-        args = [tiles, section, ce, cn, below, *lat, side, section_side, heating]
-        specs = [VMEM] * len(args)
-        results = [shape(nfields, levels * nrows, ncols), shape(levels * nrows, ncols)]
-        aliases = {}
-        if g:
-            aliases = {len(args): 0}
-            args.append(out)
-            specs.append(HBM)
-            results.pop()
-        out, *rest = call(
-            functools.partial(second_stage, counts[g], starts[g], nrows, g == 0),
-            f"second_stage_{g}",
-            results,
-            specs,
-            [HBM] * len(results),
-            args,
-            [
-                scratch(2 * counts[g], levels * nrows, ncols),
-                pltpu.SemaphoreType.DMA((counts[g] + 1,)),
-                *edges,
-            ],
-            input_output_aliases=aliases,
-        )
-        if not g:
-            heat_out = rest[0]
+    full = shape(nfields, levels * nrows, ncols)
+    out, heat_out, part = call(
+        functools.partial(second_stage_early, early, late, nrows),
+        "second_stage_early",
+        (full, shape(levels * nrows, ncols), shape(nrows * late, ncols, LANES)),
+        [VMEM] * 12,
+        (HBM, HBM, VMEM),
+        (tiles0, section0, ce, cn, below, *lat2, side, section_side, heating, tiles1, section1),
+        [scratch(2 * early, levels * nrows, ncols), pltpu.SemaphoreType.DMA((early + 1,)), *edges],
+    )
+    out = call(
+        functools.partial(second_stage_late, late, early, nrows),
+        "second_stage_late",
+        full,
+        [VMEM] * 5 + [HBM],
+        HBM,
+        (part, cn, below, *lat3, out),
+        [scratch(2 * late, levels * nrows, ncols), pltpu.SemaphoreType.DMA((late,))],
+        input_output_aliases={5: 0},
+    )
     return out.reshape(fields.shape), heat_out.reshape(levels, nrows, ncols)
 
 

time: 31.6 us -> 31.2 us (0.987)
  Pallas kernels: 10.8 us -> 10.3 us
    pallas_call x8, Pallas kernels: 10.8 us -> 10.3 us  [call(): pl.pallas_call(kernel, out_shape=out_shape, in_specs=specs, out_specs=out...]
where the time goes in v5:
time: 31.2 us; the launch traced here: 31.1 us
  starting transfers between devices  14.6 us (47%)
  Pallas kernels  10.3 us (33%)
  waiting for transfers between devices  5.5 us (18%)
  between operations  0.7 us (2%)
    ppermute x4, starting transfers between devices, lat_swaps(): lax.ppermute(first_block, 'lat', [(j, j ^ 1) for j in range(nlat)])  11.8 us
    pallas_call x8, Pallas kernels, call(): pl.pallas_call(kernel, out_shape=out_shape, in_specs=specs, out_specs=out...  10.3 us
    ppermute x4, waiting for transfers between devices, lat_swaps(): lax.ppermute(first_block, 'lat', [(j, j ^ 1) for j in range(nlat)])  3.17 us
    ppermute x1, waiting for transfers between devices, lon_swaps(): lax.ppermute(second_block, 'lon', second)  2.31 us
    ppermute x1, starting transfers between devices, lon_swaps(): lax.ppermute(second_block, 'lon', second)  2.13 us
  transfers between devices with their start and end apart: 10, of which 4 were waited for; matrix products, arithmetic and copies ran while one was open for 0% of the time, Pallas kernels for 25%

profile of v5, /device:TPU:0, one launch (start us, length us, event | category | flops | bytes accessed | tf_op | source)
XLA Modules:
  0.0 31.1 jit_solution(18352935583700448517)
XLA Ops:
  0.6 1.6 %pack_first.1 = (f32[8,128,128]{2,1,0:T(8,128)S(1)}, f32[704,128]{1,0:T(8,128)S(1)}, f32[704,128]{1,0:T(8,128)S(1)}, f32[4,256,128]{2,1,0:T(8,128)S(1)}, f32[4,2...) custom-call(f32[8,256,128]{2,1,0:T(8,128)} %bitcast.5, f32[2,256,128]{2,1,0:T(8,128)} %bitcast.7), custom_call_target="tpu_custom_call" | custom-call | flops 1000 | bytes 1000 | tf_op jit(solution)/shard_map/pack_first/pallas_call | solution.py:574
  2.2 3.1 %collective-permute-start.2 = (f32[704,128]{1,0:T(8,128)S(1)}, f32[704,128]{1,0:T(8,128)S(1)}, u32[]{:S(2)}, u32[]{:S(2)}) collective-permute-start(f32[704,128]{1,0:T(8,128)S(1)} %get-tuple-element.36), channel_id=1, source_target_pairs={{0,1},{1,0},{2,3},{3,2},{4,5},{5,4},{6,7},{7,6},{8,9},{9,8},{10,11... | collective-permute-start | bytes 1081352 | tf_op jit(solution)/shard_map/ppermute | solution.py:45
  5.3 0.0 collective-permute-start.3
  5.3 0.3 %pack_middle.1 = (f32[8,128,128]{2,1,0:T(8,128)S(1)}, f32[4,128,128]{2,1,0:T(8,128)S(1)}, f32[4,128,128]{2,1,0:T(8,128)S(1)}, f32[80,128]{1,0:T(8,128)S(1)}, f32[80,128]{1,0:T(8,128)S(1)}) custom-call(f32[4,256,128]{2,1,0:T(8,128)S(1)} %get-tuple-element.28.nat, f32[2,256,128]{2,1,0:T(8,128)S(1)} %get-tuple-element.29.nat_wind, ...), custom_call_target="tpu_custom_call" | custom-call | flops 1000 | bytes 1000 | tf_op jit(solution)/shard_map/pack_middle/pallas_call | solution.py:574
  5.6 0.6 %collective-permute-start = (f32[80,128]{1,0:T(8,128)S(1)}, f32[80,128]{1,0:T(8,128)S(1)}, u32[]{:S(2)}, u32[]{:S(2)}) collective-permute-start(f32[80,128]{1,0:T(8,128)S(1)} %get-tuple-element.33), channel_id=1, source_target_pairs={{0,4},{4,0},{8,12},{12,8},{16,20},{20,16},{24,28},{28,24},{1,5},{5... | collective-permute-start | bytes 122888 | tf_op jit(solution)/shard_map/ppermute | solution.py:33
  6.2 2.1 %collective-permute-start.1 = (f32[80,128]{1,0:T(8,128)S(1)}, f32[80,128]{1,0:T(8,128)S(1)}, u32[]{:S(2)}, u32[]{:S(2)}) collective-permute-start(f32[80,128]{1,0:T(8,128)S(1)} %get-tuple-element.34), channel_id=1, source_target_pairs={{0,28},{4,8},{8,4},{12,16},{16,12},{20,24},{24,20},{28,0},{1,29},{... | collective-permute-start | bytes 122888 | tf_op jit(solution)/shard_map/ppermute | solution.py:33
  8.4 0.0 collective-permute-done.la
  8.4 2.3 %collective-permute-done.1.lb = f32[80,128]{1,0:T(8,128)S(1)} collective-permute-done((f32[80,128]{1,0:T(8,128)S(1)}, f32[80,128]{1,0:T(8,128)S(1)}, u32[]{:S(2)}, u32[]{:S(2)}) %collective-permute-start.1) | collective-permute-done | bytes 40992 | tf_op jit(solution)/shard_map/ppermute | solution.py:33
  10.7 0.1 pack_last.1
  10.8 2.6 %collective-permute-start.6 = (f32[424,128]{1,0:T(8,128)S(1)}, f32[424,128]{1,0:T(8,128)S(1)}, u32[]{:S(2)}, u32[]{:S(2)}) collective-permute-start(f32[424,128]{1,0:T(8,128)S(1)} %get-tuple-element.42), channel_id=1, source_target_pairs={{0,1},{1,0},{2,3},{3,2},{4,5},{5,4},{6,7},{7,6},{8,9},{9,8},{10,11... | collective-permute-start | bytes 651272 | tf_op jit(solution)/shard_map/ppermute | solution.py:45
  13.4 0.3 %collective-permute-done.2.ra.ra_first = f32[704,128]{1,0:T(8,128)S(1)} collective-permute-done((f32[704,128]{1,0:T(8,128)S(1)}, f32[704,128]{1,0:T(8,128)S(1)}, u32[]{:S(2)}, u32[]{:S(2)}) %collective-permute-start.2) | collective-permute-done | bytes 360480 | tf_op jit(solution)/shard_map/ppermute | solution.py:45
  13.7 0.0 collective-permute-done.3.rb.rb_first
  13.7 0.5 %first_stage_early.1 = (f32[8,128,128]{2,1,0:T(8,128)S(1)}, f32[512,128]{1,0:T(8,128)S(1)}, f32[512,128]{1,0:T(8,128)S(1)}, f32[128,128]{1,0:T(8,128)S(1)}) custom-call(f32[8,128,128]{2,1,0:T(8,128)S(1)} %get-tuple-element.27.tiles_first.q.q_early, f32[4,128,128]{2,1,0:T(8,128)S(1)} %get-tuple-element.30.ce, f32[4,128,128]{2,1,0:T(8,128)S(1)} %get-tuple-element.31.cn, ...), custom_call_target="tpu_custom_call" | custom-call | flops 1000000000 | bytes 1000000000 | tf_op jit(solution)/shard_map/first_stage_early/pallas_call | solution.py:574
  14.2 3.7 %collective-permute-start.4 = (f32[512,128]{1,0:T(8,128)S(1)}, f32[512,128]{1,0:T(8,128)S(1)}, u32[]{:S(2)}, u32[]{:S(2)}) collective-permute-start(f32[512,128]{1,0:T(8,128)S(1)} %get-tuple-element.40), channel_id=1, source_target_pairs={{0,1},{1,0},{2,3},{3,2},{4,5},{5,4},{6,7},{7,6},{8,9},{9,8},{10,11... | collective-permute-start | bytes 786440 | tf_op jit(solution)/shard_map/ppermute | solution.py:45
  17.9 0.0 collective-permute-start.5
  17.9 1.7 %collective-permute-done.6.ra = f32[424,128]{1,0:T(8,128)S(1)} collective-permute-done((f32[424,128]{1,0:T(8,128)S(1)}, f32[424,128]{1,0:T(8,128)S(1)}, u32[]{:S(2)}, u32[]{:S(2)}) %collective-permute-start.6) | collective-permute-done | bytes 217120 | tf_op jit(solution)/shard_map/ppermute | solution.py:45
  19.5 0.5 %first_stage_late.1 = (f32[8,128,128]{2,1,0:T(8,128)S(1)}, f32[512,128]{1,0:T(8,128)S(1)}, f32[512,128]{1,0:T(8,128)S(1)}, f32[128,128]{1,0:T(8,128)S(1)}) custom-call(f32[8,128,128]{2,1,0:T(8,128)S(1)} %get-tuple-element.32.tiles.q.q_late, f32[4,128,128]{2,1,0:T(8,128)S(1)} %get-tuple-element.30.ce, f32[4,128,128]{2,1,0:T(8,128)S(1)} %get-tuple-element.31.cn, ...), custom_call_target="tpu_custom_call" | custom-call | flops 12000000 | bytes 12000000 | tf_op jit(solution)/shard_map/first_stage_late/pallas_call | solution.py:574
  20.0 2.5 %collective-permute-start.8 = (f32[512,128]{1,0:T(8,128)S(1)}, f32[512,128]{1,0:T(8,128)S(1)}, u32[]{:S(2)}, u32[]{:S(2)}) collective-permute-start(f32[512,128]{1,0:T(8,128)S(1)} %get-tuple-element.48), channel_id=1, source_target_pairs={{0,1},{1,0},{2,3},{3,2},{4,5},{5,4},{6,7},{7,6},{8,9},{9,8},{10,11... | collective-permute-start | bytes 786440 | tf_op jit(solution)/shard_map/ppermute | solution.py:45
  22.5 5.0 %radiation.1.heating = f32[256,128]{1,0:T(8,128)S(1)} custom-call(f32[4,256,128]{2,1,0:T(8,128)S(1)} %get-tuple-element.45.nat, f32[4,128]{1,0:T(4,128)} %cosz_in.1, f32[4,128]{1,0:T(4,128)} %albedo_in.1, f32[14]{0:T(128)} %ext_in.1, f32[14]{0:T(128)} %single_in.1, f32[14]{0:T(128)} %weight_in.1, s32[4,1,128]{2,1,0:T(1,128)} %order_in.1, s32[4]{0:T(128)} %bitcast.8, ...), custom_call_target="tpu_custom_call" | custom-call | flops 16000000 | bytes 16000000 | tf_op jit(solution)/shard_map/radiation/pallas_call | solution.py:574
  27.5 0.0 collective-permute-done.4.ra
  27.5 1.4 %second_stage_early.1 = (f32[8,256,128]{2,1,0:T(8,128)}, f32[256,128]{1,0:T(8,128)}, f32[8,128,128]{2,1,0:T(8,128)S(1)}) custom-call(f32[8,128,128]{2,1,0:T(8,128)S(1)} %get-tuple-element.27.tiles_first.q.q_early, f32[8,128,128]{2,1,0:T(8,128)S(1)} %get-tuple-element.38.s, f32[4,128,128]{2,1,0:T(8,128)S(1)} %get-tuple-element.30.ce, ...), custom_call_target="tpu_custom_call" | custom-call | flops 1000 | bytes 1000 | tf_op jit(solution)/shard_map/second_stage_early/pallas_call | solution.py:574
  28.9 1.1 %collective-permute-done.8.ra = f32[512,128]{1,0:T(8,128)S(1)} collective-permute-done((f32[512,128]{1,0:T(8,128)S(1)}, f32[512,128]{1,0:T(8,128)S(1)}, u32[]{:S(2)}, u32[]{:S(2)}) %collective-permute-start.8) | collective-permute-done | bytes 262176 | tf_op jit(solution)/shard_map/ppermute | solution.py:45
  30.0 0.0 collective-permute-done.9.rb
  30.0 1.0 %second_stage_late.1 = f32[8,256,128]{2,1,0:T(8,128)} custom-call(f32[8,128,128]{2,1,0:T(8,128)S(1)} %get-tuple-element.47.part, f32[4,128,128]{2,1,0:T(8,128)S(1)} %get-tuple-element.31.cn, f32[128,128]{1,0:T(8,128)S(1)} %get-tuple-element.39.below, f32[512,128]{1,0:T(8,128)S(1)} %collective-permute-done.8.ra, ...), custom_call_target="tpu_custom_call", output_to_operand_aliasing={{}: (5, {})} | custom-call | flops 1000 | bytes 1000 | tf_op jit(solution)/shard_map/second_stage_late/pallas_call | solution.py:574
  (4 shorter events, 0.0 us)
Async XLA Ops:
  2.2 11.5 %collective-permute-start.2 = (f32[704,128]{1,0:T(8,128)S(1)}, f32[704,128]{1,0:T(8,128)S(1)}, u32[]{:S(2)}, u32[]{:S(2)}) collective-permute-start(f32[704,128]{1,0:T(8,128)S(1)} %get-tuple-element.36), channel_id=1, source_target_pairs={{0,1},{1,0},{2,3},{3,2},{4,5},{5,4},{6,7},{7,6},{8,9},{9,8},{10,11... | collective-permute-start | bytes 1081352 | tf_op jit(solution)/shard_map/ppermute | solution.py:45
  5.3 8.4 %collective-permute-start.3 = (f32[704,128]{1,0:T(8,128)S(1)}, f32[704,128]{1,0:T(8,128)S(1)}, u32[]{:S(2)}, u32[]{:S(2)}) collective-permute-start(f32[704,128]{1,0:T(8,128)S(1)} %get-tuple-element.37), channel_id=1, source_target_pairs={{0,4},{1,2},{2,1},{3,7},{4,0},{5,6},{6,5},{7,3},{8,12},{9,10},{10,... | collective-permute-start | bytes 1081352 | tf_op jit(solution)/shard_map/ppermute | solution.py:44
  5.6 2.7 %collective-permute-start = (f32[80,128]{1,0:T(8,128)S(1)}, f32[80,128]{1,0:T(8,128)S(1)}, u32[]{:S(2)}, u32[]{:S(2)}) collective-permute-start(f32[80,128]{1,0:T(8,128)S(1)} %get-tuple-element.33), channel_id=1, source_target_pairs={{0,4},{4,0},{8,12},{12,8},{16,20},{20,16},{24,28},{28,24},{1,5},{5... | collective-permute-start | bytes 122888 | tf_op jit(solution)/shard_map/ppermute | solution.py:33
  6.2 4.4 %collective-permute-start.1 = (f32[80,128]{1,0:T(8,128)S(1)}, f32[80,128]{1,0:T(8,128)S(1)}, u32[]{:S(2)}, u32[]{:S(2)}) collective-permute-start(f32[80,128]{1,0:T(8,128)S(1)} %get-tuple-element.34), channel_id=1, source_target_pairs={{0,28},{4,8},{8,4},{12,16},{16,12},{20,24},{24,20},{28,0},{1,29},{... | collective-permute-start | bytes 122888 | tf_op jit(solution)/shard_map/ppermute | solution.py:33
  10.8 8.8 %collective-permute-start.6 = (f32[424,128]{1,0:T(8,128)S(1)}, f32[424,128]{1,0:T(8,128)S(1)}, u32[]{:S(2)}, u32[]{:S(2)}) collective-permute-start(f32[424,128]{1,0:T(8,128)S(1)} %get-tuple-element.42), channel_id=1, source_target_pairs={{0,1},{1,0},{2,3},{3,2},{4,5},{5,4},{6,7},{7,6},{8,9},{9,8},{10,11... | collective-permute-start | bytes 651272 | tf_op jit(solution)/shard_map/ppermute | solution.py:45
  13.4 6.2 %collective-permute-start.7 = (f32[424,128]{1,0:T(8,128)S(1)}, f32[424,128]{1,0:T(8,128)S(1)}, u32[]{:S(2)}, u32[]{:S(2)}) collective-permute-start(f32[424,128]{1,0:T(8,128)S(1)} %get-tuple-element.43), channel_id=1, source_target_pairs={{0,4},{1,2},{2,1},{3,7},{4,0},{5,6},{6,5},{7,3},{8,12},{9,10},{10,... | collective-permute-start | bytes 651272 | tf_op jit(solution)/shard_map/ppermute | solution.py:44
  14.2 13.3 %collective-permute-start.4 = (f32[512,128]{1,0:T(8,128)S(1)}, f32[512,128]{1,0:T(8,128)S(1)}, u32[]{:S(2)}, u32[]{:S(2)}) collective-permute-start(f32[512,128]{1,0:T(8,128)S(1)} %get-tuple-element.40), channel_id=1, source_target_pairs={{0,1},{1,0},{2,3},{3,2},{4,5},{5,4},{6,7},{7,6},{8,9},{9,8},{10,11... | collective-permute-start | bytes 786440 | tf_op jit(solution)/shard_map/ppermute | solution.py:45
  17.9 9.7 %collective-permute-start.5 = (f32[512,128]{1,0:T(8,128)S(1)}, f32[512,128]{1,0:T(8,128)S(1)}, u32[]{:S(2)}, u32[]{:S(2)}) collective-permute-start(f32[512,128]{1,0:T(8,128)S(1)} %get-tuple-element.41), channel_id=1, source_target_pairs={{0,4},{1,2},{2,1},{3,7},{4,0},{5,6},{6,5},{7,3},{8,12},{9,10},{10,... | collective-permute-start | bytes 786440 | tf_op jit(solution)/shard_map/ppermute | solution.py:44
  20.0 10.0 %collective-permute-start.8 = (f32[512,128]{1,0:T(8,128)S(1)}, f32[512,128]{1,0:T(8,128)S(1)}, u32[]{:S(2)}, u32[]{:S(2)}) collective-permute-start(f32[512,128]{1,0:T(8,128)S(1)} %get-tuple-element.48), channel_id=1, source_target_pairs={{0,1},{1,0},{2,3},{3,2},{4,5},{5,4},{6,7},{7,6},{8,9},{9,8},{10,11... | collective-permute-start | bytes 786440 | tf_op jit(solution)/shard_map/ppermute | solution.py:45
  22.5 7.5 %collective-permute-start.9 = (f32[512,128]{1,0:T(8,128)S(1)}, f32[512,128]{1,0:T(8,128)S(1)}, u32[]{:S(2)}, u32[]{:S(2)}) collective-permute-start(f32[512,128]{1,0:T(8,128)S(1)} %get-tuple-element.49), channel_id=1, source_target_pairs={{0,4},{1,2},{2,1},{3,7},{4,0},{5,6},{6,5},{7,3},{8,12},{9,10},{10,... | collective-permute-start | bytes 786440 | tf_op jit(solution)/shard_map/ppermute | solution.py:44

commit v6 on v5

--- a/solution.py
+++ b/solution.py
@@ -9,7 +9,7 @@
 from jax.sharding import PartitionSpec as P
 
 SPLIT = 2
-MOVED = 1
+MOVED = 0
 SUB = 8
 LANES = 128
 LOG2E = math.log2(math.e)
@@ -121,7 +121,8 @@
         zb[span, :] = jnp.where(even, low, high)
 
 
-def pack_middle(pairs, nrows, nat, nat_wind, tiles_first, tiles, ce, cn, la, lb):
+def pack_middle(pairs, nrows, nat, nat_wind, tiles_first, tiles, ce, cn, la, lb, za, zb):
+    up = jnp.where(is_even("lat"), 2, 0)
     for p in range(pairs):
         for r in range(nrows):
             tiles[nrows * p + r] = tile_of(native(nat, 2 * p, r, nrows), native(nat, 2 * p + 1, r, nrows))
@@ -130,6 +131,11 @@
         north = native(nat_wind, 1, r, nrows) * (1.0 / 12.0)
         ce[r] = tile_of(east, east)
         cn[r] = tile_of(north, north)
+    for i in range(MOVED, 2 * pairs):
+        p, k = divmod(i, 2)
+        span = pl.ds((i - MOVED) * LANES, LANES)
+        za[span, :] = tiles[nrows * p + up + k]
+        zb[span, :] = tiles[nrows * p + (2 - up) + k]
     even = is_even("lon")
     head, low = sublanes() < SUB // 2, lanes() < LANES // 2
     blocks = [take_sides(ref.at[t]) for ref in (tiles_first, tiles) for t in range(ref.shape[0])]
@@ -143,9 +149,8 @@
         lb[span, :] = jnp.where(even, west, east)
 
 
-def pack_last(pairs, done, nrows, tiles, la, lb, za, zb, side):
-    lat_even, lon_even = is_even("lat"), is_even("lon")
-    ntiles = nrows * (done + pairs)
+def put_side(la, lb, ntiles, side):
+    lon_even = is_even("lon")
     head, low = sublanes() < SUB // 2, lanes() < LANES // 2
     blocks = []
     for i in range(la.shape[0] // SUB):
@@ -159,29 +164,27 @@
     blocks += [jnp.where(low, y, x) for x, y in zip(winds, turned)]
     for t, value in enumerate(blocks):
         side[pl.ds(SUB * t, SUB), :] = value
-    north = jnp.where(lat_even, 2, 0)
-    at = (2 * pairs - MOVED) * LANES
+
+
+def put_corners(lat_even, ntiles, nrows, at, side, za, zb):
     row = sublanes()
     outer = (row < 2) | (row >= SUB - 2)
+    north = jnp.where(lat_even, 2, 0)
 
     def corner(p, first):
         start = pl.multiple_of(SUB * (nrows * p + first), SUB)
         one, two = side[pl.ds(start, SUB), :], side[pl.ds(start + SUB, SUB), :]
         return jnp.where(outer, one, half_turn(two))
 
-    for p in range(done + pairs):
+    npairs = ntiles // nrows
+    for p in range(npairs):
         to = pl.ds(at + SUB * p, SUB)
         za[to, :] = corner(p, north)
         zb[to, :] = corner(p, 2 - north)
-    to = pl.ds(at + SUB * (done + pairs), SUB)
+    to = pl.ds(at + SUB * npairs, SUB)
     top = side[pl.ds(SUB * (ntiles + 2 * nrows - 1), SUB), :]
     za[to, :] = top
     zb[to, :] = top
-    for i in range(MOVED, 2 * pairs):
-        p, k = divmod(i, 2)
-        span = pl.ds((i - MOVED) * LANES, LANES)
-        za[span, :] = tiles[nrows * p + north + k]
-        zb[span, :] = tiles[nrows * p + (2 - north) + k]
 
 
 def put_edges(q, first, side, at, nrows, edge_w, edge_e):
@@ -278,7 +281,7 @@
     return [scratch(nrows, 3 * SUB, LANES)] * 4 + [scratch(nrows, LANES + SUB, LANES)]
 
 
-def first_stage_early(pairs, nrows, q, ce, cn, side, ra, rb, section, za, zb, below, *edges):
+def first_stage_early(pairs, ntiles, nrows, q, ce, cn, la, lb, ra, rb, section, za, zb, below, side, *edges):
     edge_w, edge_e, edge_c, edge_d, flux = edges
     lat_even, where = is_even("lat"), sources()
     half = LANES // 2
@@ -287,6 +290,8 @@
     low = lax.broadcasted_iota(jnp.int32, (half, LANES), 1) < half
     below[pl.ds(0, half), :] = jnp.where(low, a, turned)
     below[pl.ds(half, half), :] = jnp.where(low, turned, a)
+    put_side(la, lb, ntiles, side)
+    put_corners(lat_even, ntiles, nrows, 2 * pairs * LANES, side, za, zb)
     put_edges(ce, 0, side, side.shape[0] // SUB - 2 * nrows, nrows, edge_c, edge_d)
 
     def one(p, _):
@@ -307,44 +312,26 @@
 
 
 def first_stage_late(
-    pairs, done, nrows, q, ce, cn, side, ra, rb, ra_first, rb_first, below, q_early, section, za, zb, sides, *edges
+    pairs, done, nrows, q, ce, cn, side, ra, rb, ra_first, rb_first, below, section, za, zb, *edges
 ):
     edge_w, edge_e, edge_c, edge_d, flux = edges
     lat_even, where = is_even("lat"), sources()
-    ntiles = nrows * (done + pairs)
-    corner = (2 * pairs - MOVED) * LANES
-    put_edges(ce, 0, side, ntiles, nrows, edge_c, edge_d)
-
-    def side_section(at):
-        put_side_section(
-            at, nrows, where, ra, rb, corner, side, ntiles, edge_w, edge_e, edge_c, edge_d, sides
-        )
-
-    def one(p):
+    put_edges(ce, 0, side, side.shape[0] // SUB - 2 * nrows, nrows, edge_c, edge_d)
+    for p in range(pairs):
+
         def halo(k, shift):
             i = 2 * p + k
             if i < MOVED:
                 return partners(where, ra_first, rb_first, pl.ds((2 * done + i) * LANES + shift, SUB))
             return partners(where, ra, rb, pl.ds((i - MOVED) * LANES + shift, SUB))
 
-        at = nrows * (done + p)
-        put_edges(q, nrows * p, side, at, nrows, edge_w, edge_e)
+        put_edges(q, nrows * p, side, nrows * (done + p), nrows, edge_w, edge_e)
         put_fluxes(q, nrows * p, nrows, ce, edge_w, edge_e, edge_c, flux)
         for b in range(LANES // SUB):
             own, div = divergence(q, p, nrows, b, halo, cn, below, flux)
             for r in range(nrows):
                 section[nrows * p + r, pl.ds(SUB * b, SUB), :] = own[r] - div[r]
         put_lat_sends(lat_even, section, p, nrows, za, zb)
-        side_section(at)
-
-    def another(p, _):
-        put_edges(q_early, nrows * p, side, nrows * p, nrows, edge_w, edge_e)
-        side_section(nrows * p)
-        return 0
-
-    for p in range(pairs):
-        one(p)
-    lax.fori_loop(0, done, another, 0)
 
 
 def put_rows(buffer, pair, rows, nrows):
@@ -356,14 +343,27 @@
 
 
 def second_stage_early(
-    pairs, later, nrows, q, s, ce, cn, below, ra, rb, side, sides, heating, q_late, s_late,
-    out, heat_out, part, buffer, sems, *edges
+    pairs, later, nrows, q, s, ce, cn, below, ra, rb, side, heating, q_late, s_late,
+    out, heat_out, part, buffer, sems, sides, *edges
 ):
     edge_w, edge_e, edge_c, edge_d, flux = edges
     where = sources()
     heat_copy = pltpu.make_async_copy(heating, heat_out, sems.at[pairs])
     heat_copy.start()
     put_edges(ce, 0, side, side.shape[0] // SUB - 2 * nrows, nrows, edge_c, edge_d)
+
+    ntiles = nrows * (pairs + later)
+    for ref, first, n in ((q, 0, pairs), (q_late, pairs, later)):
+
+        def beside(p, _):
+            at = nrows * (first + p)
+            put_edges(ref, nrows * p, side, at, nrows, edge_w, edge_e)
+            put_side_section(
+                at, nrows, where, ra, rb, 2 * pairs * LANES, side, ntiles, edge_w, edge_e, edge_c, edge_d, sides
+            )
+            return 0
+
+        lax.fori_loop(0, n, beside, 0)
 
     def copy(p):
         return pltpu.make_async_copy(buffer.at[pl.ds(2 * p, 2)], out.at[pl.ds(2 * p, 2)], sems.at[p])
@@ -612,49 +612,40 @@
     winds = shape(nrows, ncols, LANES)
     sides = shape(SUB * (ntiles + 2 * nrows), LANES)
     edge = shape(SUB * (ntiles + nrows) // 2, LANES)
-    tiles1, ce, cn, la, lb = call(
+    z1 = shape((2 * late - MOVED) * ncols, LANES)
+    tiles1, ce, cn, la, lb, za, zb = call(
         functools.partial(pack_middle, late, nrows),
         "pack_middle",
-        (shape(nrows * late, ncols, LANES), winds, winds, edge, edge),
+        (shape(nrows * late, ncols, LANES), winds, winds, edge, edge, z1, z1),
         [VMEM] * 3,
-        (VMEM,) * 5,
+        (VMEM,) * 7,
         (nat_late, nat_wind, tiles0),
         [],
     )
+    lat1 = lat_swaps(za, zb)
     lon = lon_swaps(la, lb)
-    z1 = shape((2 * late - MOVED) * ncols + SUB * (npairs + 1), LANES)
-    za, zb, side = call(
-        functools.partial(pack_last, late, early, nrows),
-        "pack_last",
-        (z1, z1, sides),
-        [VMEM] * 3,
-        (VMEM,) * 3,
-        (tiles1, *lon),
-        [],
-    )
-    lat1 = lat_swaps(za, zb)
 
     edges = edge_scratch(nrows)
-    z0 = shape(2 * early * ncols, LANES)
-    section0, za, zb, below = call(
-        functools.partial(first_stage_early, early, nrows),
+    z0 = shape(2 * early * ncols + SUB * (npairs + 1), LANES)
+    section0, za, zb, below, side = call(
+        functools.partial(first_stage_early, early, ntiles, nrows),
         "first_stage_early",
-        (shape(nrows * early, ncols, LANES), z0, z0, shape(ncols, LANES)),
-        [VMEM] * 6,
-        (VMEM,) * 4,
-        (tiles0, ce, cn, side, *lat0),
+        (shape(nrows * early, ncols, LANES), z0, z0, shape(ncols, LANES), sides),
+        [VMEM] * 7,
+        (VMEM,) * 5,
+        (tiles0, ce, cn, *lon, *lat0),
         edges,
         moved=1000_000_000,
     )
     lat2 = lat_swaps(za, zb)
     z1 = shape(2 * late * ncols, LANES)
-    section1, za, zb, section_side = call(
+    section1, za, zb = call(
         functools.partial(first_stage_late, late, early, nrows),
         "first_stage_late",
-        (shape(nrows * late, ncols, LANES), z1, z1, shape(SUB * ntiles, LANES)),
-        [VMEM] * 10,
-        (VMEM,) * 4,
-        (tiles1, ce, cn, side, *lat1, *lat0, below, tiles0),
+        (shape(nrows * late, ncols, LANES), z1, z1),
+        [VMEM] * 9,
+        (VMEM,) * 3,
+        (tiles1, ce, cn, side, *lat1, *lat0, below),
         edges,
         moved=12_000_000,
     )
@@ -670,7 +661,7 @@
         VMEM,
         (
             nat, in_hbm(cos_zenith), in_hbm(albedo), in_hbm(extinction), in_hbm(single_albedo),
-            in_hbm(band_weight), in_hbm(sun_order), in_hbm(sun_count.reshape(nrows)), section_side,
+            in_hbm(band_weight), in_hbm(sun_order), in_hbm(sun_count.reshape(nrows)), section1,
         ),
         [
             scratch(levels, 2 * nrows, ncols), scratch(levels + 1, 2 * nrows, ncols),
@@ -688,10 +679,15 @@
         functools.partial(second_stage_early, early, late, nrows),
         "second_stage_early",
         (full, shape(levels * nrows, ncols), shape(nrows * late, ncols, LANES)),
-        [VMEM] * 12,
+        [VMEM] * 11,
         (HBM, HBM, VMEM),
-        (tiles0, section0, ce, cn, below, *lat2, side, section_side, heating, tiles1, section1),
-        [scratch(2 * early, levels * nrows, ncols), pltpu.SemaphoreType.DMA((early + 1,)), *edges],
+        (tiles0, section0, ce, cn, below, *lat2, side, heating, tiles1, section1),
+        [
+            scratch(2 * early, levels * nrows, ncols),
+            pltpu.SemaphoreType.DMA((early + 1,)),
+            scratch(SUB * ntiles, LANES),
+            *edges,
+        ],
     )
     out = call(
         functools.partial(second_stage_late, late, early, nrows),

time: 31.2 us -> 30.7 us (0.984)
  starting transfers between devices: 14.6 us -> 14.1 us
    ppermute x4, waiting for transfers between devices: 3.17 us -> 1.95 us  [lat_swaps(): lax.ppermute(first_block, 'lat', [(j, j ^ 1) for j in range(nlat)])]
    ppermute x1, waiting for transfers between devices: 0.01 us -> 1.08 us  [lon_swaps(): lax.ppermute(first_block, 'lon', first)]
    ppermute x4, starting transfers between devices: 11.8 us -> 11.4 us  [lat_swaps(): lax.ppermute(first_block, 'lat', [(j, j ^ 1) for j in range(nlat)])]
    pallas_call x8 -> x7, Pallas kernels: 10.3 us -> 10.5 us  [call(): pl.pallas_call(kernel, out_shape=out_shape, in_specs=specs, out_specs=out...]
  transfers between devices with their start and end apart: 10 -> 10, of which waited for: 4 -> 4; matrix products, arithmetic and copies ran while one was open for 0% -> 0% of each run, Pallas kernels for 25% -> 26%
where the time goes in v6:
time: 30.7 us; the launch traced here: 30.5 us
  starting transfers between devices  14.1 us (46%)
  Pallas kernels  10.5 us (34%)
  waiting for transfers between devices  5.33 us (17%)
  between operations  0.69 us (2%)
    ppermute x4, starting transfers between devices, lat_swaps(): lax.ppermute(first_block, 'lat', [(j, j ^ 1) for j in range(nlat)])  11.4 us
    pallas_call x7, Pallas kernels, call(): pl.pallas_call(kernel, out_shape=out_shape, in_specs=specs, out_specs=out...  10.5 us
    ppermute x1, waiting for transfers between devices, lon_swaps(): lax.ppermute(second_block, 'lon', second)  2.29 us
    ppermute x1, starting transfers between devices, lon_swaps(): lax.ppermute(second_block, 'lon', second)  2.19 us
    ppermute x4, waiting for transfers between devices, lat_swaps(): lax.ppermute(first_block, 'lat', [(j, j ^ 1) for j in range(nlat)])  1.95 us
    ppermute x1, waiting for transfers between devices, lon_swaps(): lax.ppermute(first_block, 'lon', first)  1.08 us
  transfers between devices with their start and end apart: 10, of which 4 were waited for; matrix products, arithmetic and copies ran while one was open for 0% of the time, Pallas kernels for 26%

profile of v6, /device:TPU:0, one launch (start us, length us, event | category | flops | bytes accessed | tf_op | source)
XLA Modules:
  0.0 30.5 jit_solution(7293837256544636671)
XLA Ops:
  0.6 1.5 %pack_first.1 = (f32[8,128,128]{2,1,0:T(8,128)S(1)}, f32[576,128]{1,0:T(8,128)S(1)}, f32[576,128]{1,0:T(8,128)S(1)}, f32[4,256,128]{2,1,0:T(8,128)S(1)}, f32[4,2...) custom-call(f32[8,256,128]{2,1,0:T(8,128)} %bitcast.5, f32[2,256,128]{2,1,0:T(8,128)} %bitcast.7), custom_call_target="tpu_custom_call" | custom-call | flops 1000 | bytes 1000 | tf_op jit(solution)/shard_map/pack_first/pallas_call | solution.py:574
  2.1 3.1 %collective-permute-start.2 = (f32[576,128]{1,0:T(8,128)S(1)}, f32[576,128]{1,0:T(8,128)S(1)}, u32[]{:S(2)}, u32[]{:S(2)}) collective-permute-start(f32[576,128]{1,0:T(8,128)S(1)} %get-tuple-element.33), channel_id=1, source_target_pairs={{0,1},{1,0},{2,3},{3,2},{4,5},{5,4},{6,7},{7,6},{8,9},{9,8},{10,11... | collective-permute-start | bytes 884744 | tf_op jit(solution)/shard_map/ppermute | solution.py:45
  5.2 0.0 collective-permute-start.3
  5.2 0.4 %pack_middle.1 = (f32[8,128,128]{2,1,0:T(8,128)S(1)}, f32[4,128,128]{2,1,0:T(8,128)S(1)}, f32[4,128,128]{2,1,0:T(8,128)S(1)}, f32[80,128]{1,0:T(8,128)S(1)}, f32...) custom-call(f32[4,256,128]{2,1,0:T(8,128)S(1)} %get-tuple-element.27.nat, ...), custom_call_target="tpu_custom_call" | custom-call | flops 1000 | bytes 1000 | tf_op jit(solution)/shard_map/pack_middle/pallas_call | solution.py:574
  5.6 3.2 %collective-permute-start.6 = (f32[512,128]{1,0:T(8,128)S(1)}, f32[512,128]{1,0:T(8,128)S(1)}, u32[]{:S(2)}, u32[]{:S(2)}) collective-permute-start(f32[512,128]{1,0:T(8,128)S(1)} %get-tuple-element.42), channel_id=1, source_target_pairs={{0,1},{1,0},{2,3},{3,2},{4,5},{5,4},{6,7},{7,6},{8,9},{9,8},{10,11... | collective-permute-start | bytes 786440 | tf_op jit(solution)/shard_map/ppermute | solution.py:45
  8.8 0.0 collective-permute-start.7
  8.8 0.5 %collective-permute-start = (f32[80,128]{1,0:T(8,128)S(1)}, f32[80,128]{1,0:T(8,128)S(1)}, u32[]{:S(2)}, u32[]{:S(2)}) collective-permute-start(f32[80,128]{1,0:T(8,128)S(1)} %get-tuple-element.31), channel_id=1, source_target_pairs={{0,4},{4,0},{8,12},{12,8},{16,20},{20,16},{24,28},{28,24},{1,5},{5... | collective-permute-start | bytes 122888 | tf_op jit(solution)/shard_map/ppermute | solution.py:33
  9.3 1.1 %collective-permute-done.la = f32[80,128]{1,0:T(8,128)S(1)} collective-permute-done((f32[80,128]{1,0:T(8,128)S(1)}, f32[80,128]{1,0:T(8,128)S(1)}, u32[]{:S(2)}, u32[]{:S(2)}) %collective-permute-start) | collective-permute-done | bytes 40992 | tf_op jit(solution)/shard_map/ppermute | solution.py:33
  10.4 2.2 %collective-permute-start.1 = (f32[80,128]{1,0:T(8,128)S(1)}, f32[80,128]{1,0:T(8,128)S(1)}, u32[]{:S(2)}, u32[]{:S(2)}) collective-permute-start(f32[80,128]{1,0:T(8,128)S(1)} %get-tuple-element.32), channel_id=1, source_target_pairs={{0,28},{4,8},{8,4},{12,16},{16,12},{20,24},{24,20},{28,0},{1,29},{... | collective-permute-start | bytes 122888 | tf_op jit(solution)/shard_map/ppermute | solution.py:33
  12.6 2.3 %collective-permute-done.1.lb = f32[80,128]{1,0:T(8,128)S(1)} collective-permute-done((f32[80,128]{1,0:T(8,128)S(1)}, f32[80,128]{1,0:T(8,128)S(1)}, u32[]{:S(2)}, u32[]{:S(2)}) %collective-permute-start.1) | collective-permute-done | bytes 40992 | tf_op jit(solution)/shard_map/ppermute | solution.py:33
  14.9 0.0 collective-permute-done.2.ra.ra_first
  14.9 0.0 collective-permute-done.3.rb.rb_first
  14.9 0.6 %first_stage_early.1 = (f32[8,128,128]{2,1,0:T(8,128)S(1)}, f32[552,128]{1,0:T(8,128)S(1)}, f32[552,128]{1,0:T(8,128)S(1)}, f32[128,128]{1,0:T(8,128)S(1)}, f32[192,128]{1,0:T(8,128)S(1)}) custom-call(f32[8,128,128]{2,1,0:T(8,128)S(1)} %get-tuple-element.26.tiles_first.q, f32[4,128,128]{2,1,0:T(8,128)S(1)} %get-tuple-element.29.ce, ...), custom_call_target="tpu_custom_call" | custom-call | flops 1000000000 | bytes 1000000000 | tf_op jit(solution)/shard_map/first_stage_early/pallas_call | solution.py:574
  15.4 1.4 %collective-permute-start.4 = (f32[552,128]{1,0:T(8,128)S(1)}, f32[552,128]{1,0:T(8,128)S(1)}, u32[]{:S(2)}, u32[]{:S(2)}) collective-permute-start(f32[552,128]{1,0:T(8,128)S(1)} %get-tuple-element.37), channel_id=1, source_target_pairs={{0,1},{1,0},{2,3},{3,2},{4,5},{5,4},{6,7},{7,6},{8,9},{9,8},{10,11... | collective-permute-start | bytes 847880 | tf_op jit(solution)/shard_map/ppermute | solution.py:45
  16.8 0.0 collective-permute-start.5
  16.9 1.4 %collective-permute-done.6.ra = f32[512,128]{1,0:T(8,128)S(1)} collective-permute-done((f32[512,128]{1,0:T(8,128)S(1)}, f32[512,128]{1,0:T(8,128)S(1)}, u32[]{:S(2)}, u32[]{:S(2)}) %collective-permute-start.6) | collective-permute-done | bytes 262176 | tf_op jit(solution)/shard_map/ppermute | solution.py:45
  18.2 0.5 %first_stage_late.1 = (f32[8,128,128]{2,1,0:T(8,128)S(1)}, f32[512,128]{1,0:T(8,128)S(1)}, f32[512,128]{1,0:T(8,128)S(1)}) custom-call(f32[8,128,128]{2,1,0:T(8,128)S(1)} %get-tuple-element.41.q.q_late, f32[4,128,128]{2,1,0:T(8,128)S(1)} %get-tuple-element.29.ce, f32[4,128,128]{2,1,0:T(8,128)S(1)} %get-tuple-element.30.cn, ...), custom_call_target="tpu_custom_call" | custom-call | flops 12000000 | bytes 12000000 | tf_op jit(solution)/shard_map/first_stage_late/pallas_call | solution.py:574
  18.7 3.7 %collective-permute-start.8 = (f32[512,128]{1,0:T(8,128)S(1)}, f32[512,128]{1,0:T(8,128)S(1)}, u32[]{:S(2)}, u32[]{:S(2)}) collective-permute-start(f32[512,128]{1,0:T(8,128)S(1)} %get-tuple-element.46), channel_id=1, source_target_pairs={{0,1},{1,0},{2,3},{3,2},{4,5},{5,4},{6,7},{7,6},{8,9},{9,8},{10,11... | collective-permute-start | bytes 786440 | tf_op jit(solution)/shard_map/ppermute | solution.py:45
  22.4 0.0 collective-permute-start.9
  22.4 5.0 %radiation.1.heating = f32[256,128]{1,0:T(8,128)S(1)} custom-call(f32[4,256,128]{2,1,0:T(8,128)S(1)} %get-tuple-element.40.nat, f32[4,128]{1,0:T(4,128)} %cosz_in.1, f32[4,128]{1,0:T(4,128)} %albedo_in.1, f32[14]{0:T(128)} %ext_in.1, f32[14]{0:T(128)} %single_in.1, f32[14]{0:T(128)} %weight_in.1, s32[4,1,128]{2,1,0:T(1,128)} %order_in.1, s32[4]{0:T(128)} %bitcast.8, ...), custom_call_target="tpu_custom_call" | custom-call | flops 16000000 | bytes 16000000 | tf_op jit(solution)/shard_map/radiation/pallas_call | solution.py:574
  27.4 1.6 %second_stage_early.1 = (f32[8,256,128]{2,1,0:T(8,128)}, f32[256,128]{1,0:T(8,128)}, f32[8,128,128]{2,1,0:T(8,128)S(1)}) custom-call(f32[8,128,128]{2,1,0:T(8,128)S(1)} %get-tuple-element.26.tiles_first.q, f32[8,128,128]{2,1,0:T(8,128)S(1)} %get-tuple-element.35.s, f32[4,128,128]{2,1,0:T(8,128)S(1)} %get-tuple-element.29.ce, ...), custom_call_target="tpu_custom_call" | custom-call | flops 1000 | bytes 1000 | tf_op jit(solution)/shard_map/second_stage_early/pallas_call | solution.py:574
  28.9 0.6 %collective-permute-done.8.ra = f32[512,128]{1,0:T(8,128)S(1)} collective-permute-done((f32[512,128]{1,0:T(8,128)S(1)}, f32[512,128]{1,0:T(8,128)S(1)}, u32[]{:S(2)}, u32[]{:S(2)}) %collective-permute-start.8) | collective-permute-done | bytes 262176 | tf_op jit(solution)/shard_map/ppermute | solution.py:45
  29.5 0.0 collective-permute-done.9.rb
  29.5 1.0 %second_stage_late.1 = f32[8,256,128]{2,1,0:T(8,128)} custom-call(f32[8,128,128]{2,1,0:T(8,128)S(1)} %get-tuple-element.45.part, f32[4,128,128]{2,1,0:T(8,128)S(1)} %get-tuple-element.30.cn, f32[128,128]{1,0:T(8,128)S(1)} %get-tuple-element.36.below, f32[512,128]{1,0:T(8,128)S(1)} %collective-permute-done.8.ra, ...), custom_call_target="tpu_custom_call", output_to_operand_aliasing={{}: (5, {})} | custom-call | flops 1000 | bytes 1000 | tf_op jit(solution)/shard_map/second_stage_late/pallas_call | solution.py:574
  (3 shorter events, 0.0 us)
Async XLA Ops:
  2.1 12.8 %collective-permute-start.2 = (f32[576,128]{1,0:T(8,128)S(1)}, f32[576,128]{1,0:T(8,128)S(1)}, u32[]{:S(2)}, u32[]{:S(2)}) collective-permute-start(f32[576,128]{1,0:T(8,128)S(1)} %get-tuple-element.33), channel_id=1, source_target_pairs={{0,1},{1,0},{2,3},{3,2},{4,5},{5,4},{6,7},{7,6},{8,9},{9,8},{10,11... | collective-permute-start | bytes 884744 | tf_op jit(solution)/shard_map/ppermute | solution.py:45
  5.2 9.7 %collective-permute-start.3 = (f32[576,128]{1,0:T(8,128)S(1)}, f32[576,128]{1,0:T(8,128)S(1)}, u32[]{:S(2)}, u32[]{:S(2)}) collective-permute-start(f32[576,128]{1,0:T(8,128)S(1)} %get-tuple-element.34), channel_id=1, source_target_pairs={{0,4},{1,2},{2,1},{3,7},{4,0},{5,6},{6,5},{7,3},{8,12},{9,10},{10,... | collective-permute-start | bytes 884744 | tf_op jit(solution)/shard_map/ppermute | solution.py:44
  5.6 12.6 %collective-permute-start.6 = (f32[512,128]{1,0:T(8,128)S(1)}, f32[512,128]{1,0:T(8,128)S(1)}, u32[]{:S(2)}, u32[]{:S(2)}) collective-permute-start(f32[512,128]{1,0:T(8,128)S(1)} %get-tuple-element.42), channel_id=1, source_target_pairs={{0,1},{1,0},{2,3},{3,2},{4,5},{5,4},{6,7},{7,6},{8,9},{9,8},{10,11... | collective-permute-start | bytes 786440 | tf_op jit(solution)/shard_map/ppermute | solution.py:45
  8.8 9.4 %collective-permute-start.7 = (f32[512,128]{1,0:T(8,128)S(1)}, f32[512,128]{1,0:T(8,128)S(1)}, u32[]{:S(2)}, u32[]{:S(2)}) collective-permute-start(f32[512,128]{1,0:T(8,128)S(1)} %get-tuple-element.43), channel_id=1, source_target_pairs={{0,4},{1,2},{2,1},{3,7},{4,0},{5,6},{6,5},{7,3},{8,12},{9,10},{10,... | collective-permute-start | bytes 786440 | tf_op jit(solution)/shard_map/ppermute | solution.py:44
  8.8 1.6 %collective-permute-start = (f32[80,128]{1,0:T(8,128)S(1)}, f32[80,128]{1,0:T(8,128)S(1)}, u32[]{:S(2)}, u32[]{:S(2)}) collective-permute-start(f32[80,128]{1,0:T(8,128)S(1)} %get-tuple-element.31), channel_id=1, source_target_pairs={{0,4},{4,0},{8,12},{12,8},{16,20},{20,16},{24,28},{28,24},{1,5},{5... | collective-permute-start | bytes 122888 | tf_op jit(solution)/shard_map/ppermute | solution.py:33
  10.4 4.5 %collective-permute-start.1 = (f32[80,128]{1,0:T(8,128)S(1)}, f32[80,128]{1,0:T(8,128)S(1)}, u32[]{:S(2)}, u32[]{:S(2)}) collective-permute-start(f32[80,128]{1,0:T(8,128)S(1)} %get-tuple-element.32), channel_id=1, source_target_pairs={{0,28},{4,8},{8,4},{12,16},{16,12},{20,24},{24,20},{28,0},{1,29},{... | collective-permute-start | bytes 122888 | tf_op jit(solution)/shard_map/ppermute | solution.py:33
  15.4 11.9 %collective-permute-start.4 = (f32[552,128]{1,0:T(8,128)S(1)}, f32[552,128]{1,0:T(8,128)S(1)}, u32[]{:S(2)}, u32[]{:S(2)}) collective-permute-start(f32[552,128]{1,0:T(8,128)S(1)} %get-tuple-element.37), channel_id=1, source_target_pairs={{0,1},{1,0},{2,3},{3,2},{4,5},{5,4},{6,7},{7,6},{8,9},{9,8},{10,11... | collective-permute-start | bytes 847880 | tf_op jit(solution)/shard_map/ppermute | solution.py:45
  16.8 10.5 %collective-permute-start.5 = (f32[552,128]{1,0:T(8,128)S(1)}, f32[552,128]{1,0:T(8,128)S(1)}, u32[]{:S(2)}, u32[]{:S(2)}) collective-permute-start(f32[552,128]{1,0:T(8,128)S(1)} %get-tuple-element.38), channel_id=1, source_target_pairs={{0,4},{1,2},{2,1},{3,7},{4,0},{5,6},{6,5},{7,3},{8,12},{9,10},{10,... | collective-permute-start | bytes 847880 | tf_op jit(solution)/shard_map/ppermute | solution.py:44
  18.7 10.8 %collective-permute-start.8 = (f32[512,128]{1,0:T(8,128)S(1)}, f32[512,128]{1,0:T(8,128)S(1)}, u32[]{:S(2)}, u32[]{:S(2)}) collective-permute-start(f32[512,128]{1,0:T(8,128)S(1)} %get-tuple-element.46), channel_id=1, source_target_pairs={{0,1},{1,0},{2,3},{3,2},{4,5},{5,4},{6,7},{7,6},{8,9},{9,8},{10,11... | collective-permute-start | bytes 786440 | tf_op jit(solution)/shard_map/ppermute | solution.py:45
  22.4 7.1 %collective-permute-start.9 = (f32[512,128]{1,0:T(8,128)S(1)}, f32[512,128]{1,0:T(8,128)S(1)}, u32[]{:S(2)}, u32[]{:S(2)}) collective-permute-start(f32[512,128]{1,0:T(8,128)S(1)} %get-tuple-element.47), channel_id=1, source_target_pairs={{0,4},{1,2},{2,1},{3,7},{4,0},{5,6},{6,5},{7,3},{8,12},{9,10},{10,... | collective-permute-start | bytes 786440 | tf_op jit(solution)/shard_map/ppermute | solution.py:44

commit v7 on v6

--- a/solution.py
+++ b/solution.py
@@ -9,7 +9,6 @@
 from jax.sharding import PartitionSpec as P
 
 SPLIT = 2
-MOVED = 0
 SUB = 8
 LANES = 128
 LOG2E = math.log2(math.e)
@@ -85,40 +84,32 @@
 
 def pack_first(pairs, nrows, fields, courant, tiles, za, zb, nat, nat_late, nat_wind, sems):
     n = 2 * pairs
-    copies = [pltpu.make_async_copy(fields.at[i], nat.at[i], sems.at[i]) for i in range(n)]
-    wind = pltpu.make_async_copy(courant, nat_wind, sems.at[n])
-    late = [
-        pltpu.make_async_copy(fields.at[pl.ds(n + i, 2)], nat_late.at[pl.ds(i, 2)], sems.at[n + 1 + i // 2])
-        for i in range(0, nat_late.shape[0], 2)
-    ]
-    for copy in copies + [wind] + late:
+    first = pltpu.make_async_copy(fields.at[pl.ds(0, n)], nat, sems.at[0])
+    wind = pltpu.make_async_copy(courant, nat_wind, sems.at[1])
+    late = pltpu.make_async_copy(fields.at[pl.ds(n, nat_late.shape[0])], nat_late, sems.at[2])
+    for copy in (first, wind, late):
         copy.start()
-    even = is_even("lat")
-    for p in range(pairs):
-        copies[2 * p].wait()
-        copies[2 * p + 1].wait()
-        for r in range(nrows):
-            tiles[nrows * p + r] = tile_of(native(nat, 2 * p, r, nrows), native(nat, 2 * p + 1, r, nrows))
-        put_lat_sends(even, tiles, p, nrows, za, zb)
+    first.wait()
     wind.wait()
-    top = native(nat_wind, 1, nrows - 1, nrows) * (1.0 / 12.0)
-    top = tile_of(top, top)
     half = LANES // 2
     lane = lax.broadcasted_iota(jnp.int32, (half, LANES), 1)
-    top = jnp.where(lane < half, top[:half], top[half:])
-    span = pl.ds((2 * pairs + MOVED) * LANES, half)
-    za[span, :] = top
-    zb[span, :] = top
-    for copy in late:
-        copy.wait()
-    for i in range(MOVED):
-        p, k = divmod(i, 2)
-        low, high = (
-            tile_of(native(nat_late, 2 * p, r, nrows), native(nat_late, 2 * p + 1, r, nrows)) for r in (k, k + 2)
-        )
-        span = pl.ds((2 * pairs + i) * LANES, LANES)
-        za[span, :] = jnp.where(even, high, low)
-        zb[span, :] = jnp.where(even, low, high)
+
+    def body(up, down):
+        for p in range(pairs):
+            for r in range(nrows):
+                tile = tile_of(native(nat, 2 * p, r, nrows), native(nat, 2 * p + 1, r, nrows))
+                tiles[nrows * p + r] = tile
+                (up if r >= 2 else down)[pl.ds((2 * p + r % 2) * LANES, LANES), :] = tile
+        top = native(nat_wind, 1, nrows - 1, nrows) * (1.0 / 12.0)
+        top = tile_of(top, top)
+        top = jnp.where(lane < half, top[:half], top[half:])
+        for ref in (up, down):
+            ref[pl.ds(2 * pairs * LANES, half), :] = top
+
+    even = is_even("lat")
+    pl.when(even)(lambda: body(za, zb))
+    pl.when(jnp.logical_not(even))(lambda: body(zb, za))
+    late.wait()
 
 
 def pack_middle(pairs, nrows, nat, nat_wind, tiles_first, tiles, ce, cn, la, lb, za, zb):
@@ -131,9 +122,9 @@
         north = native(nat_wind, 1, r, nrows) * (1.0 / 12.0)
         ce[r] = tile_of(east, east)
         cn[r] = tile_of(north, north)
-    for i in range(MOVED, 2 * pairs):
+    for i in range(2 * pairs):
         p, k = divmod(i, 2)
-        span = pl.ds((i - MOVED) * LANES, LANES)
+        span = pl.ds(i * LANES, LANES)
         za[span, :] = tiles[nrows * p + up + k]
         zb[span, :] = tiles[nrows * p + (2 - up) + k]
     even = is_even("lon")
@@ -285,7 +276,7 @@
     edge_w, edge_e, edge_c, edge_d, flux = edges
     lat_even, where = is_even("lat"), sources()
     half = LANES // 2
-    a = partners(where, ra, rb, pl.ds((2 * pairs + MOVED) * LANES, half))[0]
+    a = partners(where, ra, rb, pl.ds(2 * pairs * LANES, half))[0]
     turned = pltpu.roll(a, half, 1)
     low = lax.broadcasted_iota(jnp.int32, (half, LANES), 1) < half
     below[pl.ds(0, half), :] = jnp.where(low, a, turned)
@@ -312,7 +303,7 @@
 
 
 def first_stage_late(
-    pairs, done, nrows, q, ce, cn, side, ra, rb, ra_first, rb_first, below, section, za, zb, *edges
+    pairs, done, nrows, q, ce, cn, side, ra, rb, below, section, za, zb, *edges
 ):
     edge_w, edge_e, edge_c, edge_d, flux = edges
     lat_even, where = is_even("lat"), sources()
@@ -320,10 +311,7 @@
     for p in range(pairs):
 
         def halo(k, shift):
-            i = 2 * p + k
-            if i < MOVED:
-                return partners(where, ra_first, rb_first, pl.ds((2 * done + i) * LANES + shift, SUB))
-            return partners(where, ra, rb, pl.ds((i - MOVED) * LANES + shift, SUB))
+            return partners(where, ra, rb, pl.ds((2 * p + k) * LANES + shift, SUB))
 
         put_edges(q, nrows * p, side, nrows * (done + p), nrows, edge_w, edge_e)
         put_fluxes(q, nrows * p, nrows, ce, edge_w, edge_e, edge_c, flux)
@@ -426,13 +414,13 @@
             buffer.at[pl.ds(2 * p, 2)], out.at[pl.ds(2 * (done + p), 2)], sems.at[p]
         )
 
-    def one(p, _):
+    def one(p):
         rows = [[] for _ in range(nrows)]
         for b in range(LANES // SUB):
             here = pl.ds(SUB * b, SUB)
 
             def halo(k):
-                start = pl.multiple_of((2 * p + k) * LANES, LANES) + SUB * b
+                start = (2 * p + k) * LANES + SUB * b
                 return partners(where, ra, rb, pl.ds(start, SUB))
 
             (south_two, north_one), (south_one, north_two) = halo(0), halo(1)
@@ -445,9 +433,9 @@
                 rows[r].append(value)
         put_rows(buffer, p, rows, nrows)
         copy(p).start()
-        return 0
-
-    lax.fori_loop(0, pairs, one, 0)
+
+    for p in range(pairs):
+        one(p)
     for p in range(pairs):
         copy(p).wait()
 
@@ -593,7 +581,7 @@
     npairs = nfields // 2
     early, late = SPLIT, npairs - SPLIT
 
-    z0 = shape((2 * early + MOVED) * ncols + ncols // 2, LANES)
+    z0 = shape(2 * early * ncols + ncols // 2, LANES)
     tiles0, za, zb, nat, nat_late, nat_wind = call(
         functools.partial(pack_first, early, nrows),
         "pack_first",
@@ -605,14 +593,14 @@
         [HBM, HBM],
         (VMEM,) * 6,
         (in_hbm(flat), in_hbm(wind)),
-        [pltpu.SemaphoreType.DMA((2 * early + 1 + late,))],
+        [pltpu.SemaphoreType.DMA((3,))],
     )
     lat0 = lat_swaps(za, zb)
     ntiles = nrows * npairs
     winds = shape(nrows, ncols, LANES)
     sides = shape(SUB * (ntiles + 2 * nrows), LANES)
     edge = shape(SUB * (ntiles + nrows) // 2, LANES)
-    z1 = shape((2 * late - MOVED) * ncols, LANES)
+    z1 = shape(2 * late * ncols, LANES)
     tiles1, ce, cn, la, lb, za, zb = call(
         functools.partial(pack_middle, late, nrows),
         "pack_middle",
@@ -643,9 +631,9 @@
         functools.partial(first_stage_late, late, early, nrows),
         "first_stage_late",
         (shape(nrows * late, ncols, LANES), z1, z1),
-        [VMEM] * 9,
+        [VMEM] * 7,
         (VMEM,) * 3,
-        (tiles1, ce, cn, side, *lat1, *lat0, below),
+        (tiles1, ce, cn, side, *lat1, below),
         edges,
         moved=12_000_000,
     )

time: 30.7 us -> 30.6 us (level)
  no operation moved by 1% of the time
where the time goes in v7:
time: 30.6 us; the launch traced here: 30.4 us
  starting transfers between devices  14.1 us (46%)
  Pallas kernels  10.3 us (34%)
  waiting for transfers between devices  5.34 us (17%)
  between operations  0.69 us (2%)
    ppermute x4, starting transfers between devices, lat_swaps(): lax.ppermute(first_block, 'lat', [(j, j ^ 1) for j in range(nlat)])  11.4 us
    pallas_call x7, Pallas kernels, call(): pl.pallas_call(kernel, out_shape=out_shape, in_specs=specs, out_specs=out...  10.3 us
    ppermute x1, waiting for transfers between devices, lon_swaps(): lax.ppermute(second_block, 'lon', second)  2.29 us
    ppermute x1, starting transfers between devices, lon_swaps(): lax.ppermute(second_block, 'lon', second)  2.19 us
    ppermute x4, waiting for transfers between devices, lat_swaps(): lax.ppermute(first_block, 'lat', [(j, j ^ 1) for j in range(nlat)])  1.96 us
    ppermute x1, waiting for transfers between devices, lon_swaps(): lax.ppermute(first_block, 'lon', first)  1.08 us
  transfers between devices with their start and end apart: 10, of which 4 were waited for; matrix products, arithmetic and copies ran while one was open for 0% of the time, Pallas kernels for 26%

profile of v7, /device:TPU:0, one launch (start us, length us, event | category | flops | bytes accessed | tf_op | source)
XLA Modules:
  0.0 30.4 jit_solution(4930928632964439248)
XLA Ops:
  0.6 1.4 %pack_first.1 = (f32[8,128,128]{2,1,0:T(8,128)S(1)}, f32[576,128]{1,0:T(8,128)S(1)}, f32[576,128]{1,0:T(8,128)S(1)}, f32[4,256,128]{2,1,0:T(8,128)S(1)}, f32[4,2...) custom-call(f32[8,256,128]{2,1,0:T(8,128)} %bitcast.5, f32[2,256,128]{2,1,0:T(8,128)} %bitcast.7), custom_call_target="tpu_custom_call" | custom-call | flops 1000 | bytes 1000 | tf_op jit(solution)/shard_map/pack_first/pallas_call | solution.py:562
  2.0 3.1 %collective-permute-start.2 = (f32[576,128]{1,0:T(8,128)S(1)}, f32[576,128]{1,0:T(8,128)S(1)}, u32[]{:S(2)}, u32[]{:S(2)}) collective-permute-start(f32[576,128]{1,0:T(8,128)S(1)} %get-tuple-element.33), channel_id=1, source_target_pairs={{0,1},{1,0},{2,3},{3,2},{4,5},{5,4},{6,7},{7,6},{8,9},{9,8},{10,11... | collective-permute-start | bytes 884744 | tf_op jit(solution)/shard_map/ppermute | solution.py:44
  5.1 0.0 collective-permute-start.3
  5.1 0.4 %pack_middle.1 = (f32[8,128,128]{2,1,0:T(8,128)S(1)}, f32[4,128,128]{2,1,0:T(8,128)S(1)}, f32[4,128,128]{2,1,0:T(8,128)S(1)}, f32[80,128]{1,0:T(8,128)S(1)}, f32...) custom-call(f32[4,256,128]{2,1,0:T(8,128)S(1)} %get-tuple-element.27.nat, ...), custom_call_target="tpu_custom_call" | custom-call | flops 1000 | bytes 1000 | tf_op jit(solution)/shard_map/pack_middle/pallas_call | solution.py:562
  5.5 3.2 %collective-permute-start.6 = (f32[512,128]{1,0:T(8,128)S(1)}, f32[512,128]{1,0:T(8,128)S(1)}, u32[]{:S(2)}, u32[]{:S(2)}) collective-permute-start(f32[512,128]{1,0:T(8,128)S(1)} %get-tuple-element.42), channel_id=1, source_target_pairs={{0,1},{1,0},{2,3},{3,2},{4,5},{5,4},{6,7},{7,6},{8,9},{9,8},{10,11... | collective-permute-start | bytes 786440 | tf_op jit(solution)/shard_map/ppermute | solution.py:44
  8.7 0.0 collective-permute-start.7
  8.7 0.5 %collective-permute-start = (f32[80,128]{1,0:T(8,128)S(1)}, f32[80,128]{1,0:T(8,128)S(1)}, u32[]{:S(2)}, u32[]{:S(2)}) collective-permute-start(f32[80,128]{1,0:T(8,128)S(1)} %get-tuple-element.31), channel_id=1, source_target_pairs={{0,4},{4,0},{8,12},{12,8},{16,20},{20,16},{24,28},{28,24},{1,5},{5... | collective-permute-start | bytes 122888 | tf_op jit(solution)/shard_map/ppermute | solution.py:32
  9.2 1.1 %collective-permute-done.la = f32[80,128]{1,0:T(8,128)S(1)} collective-permute-done((f32[80,128]{1,0:T(8,128)S(1)}, f32[80,128]{1,0:T(8,128)S(1)}, u32[]{:S(2)}, u32[]{:S(2)}) %collective-permute-start) | collective-permute-done | bytes 40992 | tf_op jit(solution)/shard_map/ppermute | solution.py:32
  10.3 2.2 %collective-permute-start.1 = (f32[80,128]{1,0:T(8,128)S(1)}, f32[80,128]{1,0:T(8,128)S(1)}, u32[]{:S(2)}, u32[]{:S(2)}) collective-permute-start(f32[80,128]{1,0:T(8,128)S(1)} %get-tuple-element.32), channel_id=1, source_target_pairs={{0,28},{4,8},{8,4},{12,16},{16,12},{20,24},{24,20},{28,0},{1,29},{... | collective-permute-start | bytes 122888 | tf_op jit(solution)/shard_map/ppermute | solution.py:32
  12.5 2.3 %collective-permute-done.1.lb = f32[80,128]{1,0:T(8,128)S(1)} collective-permute-done((f32[80,128]{1,0:T(8,128)S(1)}, f32[80,128]{1,0:T(8,128)S(1)}, u32[]{:S(2)}, u32[]{:S(2)}) %collective-permute-start.1) | collective-permute-done | bytes 40992 | tf_op jit(solution)/shard_map/ppermute | solution.py:32
  14.8 0.0 collective-permute-done.2.ra
  14.8 0.0 collective-permute-done.3.rb
  14.8 0.5 %first_stage_early.1 = (f32[8,128,128]{2,1,0:T(8,128)S(1)}, f32[552,128]{1,0:T(8,128)S(1)}, f32[552,128]{1,0:T(8,128)S(1)}, f32[128,128]{1,0:T(8,128)S(1)}, f32[192,128]{1,0:T(8,128)S(1)}) custom-call(f32[8,128,128]{2,1,0:T(8,128)S(1)} %get-tuple-element.26.tiles_first.q, f32[4,128,128]{2,1,0:T(8,128)S(1)} %get-tuple-element.29.ce, ...), custom_call_target="tpu_custom_call" | custom-call | flops 1000000000 | bytes 1000000000 | tf_op jit(solution)/shard_map/first_stage_early/pallas_call | solution.py:562
  15.3 1.4 %collective-permute-start.4 = (f32[552,128]{1,0:T(8,128)S(1)}, f32[552,128]{1,0:T(8,128)S(1)}, u32[]{:S(2)}, u32[]{:S(2)}) collective-permute-start(f32[552,128]{1,0:T(8,128)S(1)} %get-tuple-element.37), channel_id=1, source_target_pairs={{0,1},{1,0},{2,3},{3,2},{4,5},{5,4},{6,7},{7,6},{8,9},{9,8},{10,11... | collective-permute-start | bytes 847880 | tf_op jit(solution)/shard_map/ppermute | solution.py:44
  16.7 0.0 collective-permute-start.5
  16.7 1.4 %collective-permute-done.6.ra = f32[512,128]{1,0:T(8,128)S(1)} collective-permute-done((f32[512,128]{1,0:T(8,128)S(1)}, f32[512,128]{1,0:T(8,128)S(1)}, u32[]{:S(2)}, u32[]{:S(2)}) %collective-permute-start.6) | collective-permute-done | bytes 262176 | tf_op jit(solution)/shard_map/ppermute | solution.py:44
  18.1 0.5 %first_stage_late.1 = (f32[8,128,128]{2,1,0:T(8,128)S(1)}, f32[512,128]{1,0:T(8,128)S(1)}, f32[512,128]{1,0:T(8,128)S(1)}) custom-call(f32[8,128,128]{2,1,0:T(8,128)S(1)} %get-tuple-element.41.q.q_late, f32[4,128,128]{2,1,0:T(8,128)S(1)} %get-tuple-element.29.ce, f32[4,128,128]{2,1,0:T(8,128)S(1)} %get-tuple-element.30.cn, ...), custom_call_target="tpu_custom_call" | custom-call | flops 12000000 | bytes 12000000 | tf_op jit(solution)/shard_map/first_stage_late/pallas_call | solution.py:562
  18.6 3.7 %collective-permute-start.8 = (f32[512,128]{1,0:T(8,128)S(1)}, f32[512,128]{1,0:T(8,128)S(1)}, u32[]{:S(2)}, u32[]{:S(2)}) collective-permute-start(f32[512,128]{1,0:T(8,128)S(1)} %get-tuple-element.46), channel_id=1, source_target_pairs={{0,1},{1,0},{2,3},{3,2},{4,5},{5,4},{6,7},{7,6},{8,9},{9,8},{10,11... | collective-permute-start | bytes 786440 | tf_op jit(solution)/shard_map/ppermute | solution.py:44
  22.3 0.0 collective-permute-start.9
  22.3 5.0 %radiation.1.heating = f32[256,128]{1,0:T(8,128)S(1)} custom-call(f32[4,256,128]{2,1,0:T(8,128)S(1)} %get-tuple-element.40.nat, f32[4,128]{1,0:T(4,128)} %cosz_in.1, f32[4,128]{1,0:T(4,128)} %albedo_in.1, f32[14]{0:T(128)} %ext_in.1, f32[14]{0:T(128)} %single_in.1, f32[14]{0:T(128)} %weight_in.1, s32[4,1,128]{2,1,0:T(1,128)} %order_in.1, s32[4]{0:T(128)} %bitcast.8, ...), custom_call_target="tpu_custom_call" | custom-call | flops 16000000 | bytes 16000000 | tf_op jit(solution)/shard_map/radiation/pallas_call | solution.py:562
  27.3 1.6 %second_stage_early.1 = (f32[8,256,128]{2,1,0:T(8,128)}, f32[256,128]{1,0:T(8,128)}, f32[8,128,128]{2,1,0:T(8,128)S(1)}) custom-call(f32[8,128,128]{2,1,0:T(8,128)S(1)} %get-tuple-element.26.tiles_first.q, f32[8,128,128]{2,1,0:T(8,128)S(1)} %get-tuple-element.35.s, f32[4,128,128]{2,1,0:T(8,128)S(1)} %get-tuple-element.29.ce, ...), custom_call_target="tpu_custom_call" | custom-call | flops 1000 | bytes 1000 | tf_op jit(solution)/shard_map/second_stage_early/pallas_call | solution.py:562
  28.8 0.6 %collective-permute-done.8.ra = f32[512,128]{1,0:T(8,128)S(1)} collective-permute-done((f32[512,128]{1,0:T(8,128)S(1)}, f32[512,128]{1,0:T(8,128)S(1)}, u32[]{:S(2)}, u32[]{:S(2)}) %collective-permute-start.8) | collective-permute-done | bytes 262176 | tf_op jit(solution)/shard_map/ppermute | solution.py:44
  29.4 0.0 collective-permute-done.9.rb
  29.4 1.0 %second_stage_late.1 = f32[8,256,128]{2,1,0:T(8,128)} custom-call(f32[8,128,128]{2,1,0:T(8,128)S(1)} %get-tuple-element.45.part, f32[4,128,128]{2,1,0:T(8,128)S(1)} %get-tuple-element.30.cn, f32[128,128]{1,0:T(8,128)S(1)} %get-tuple-element.36.below, f32[512,128]{1,0:T(8,128)S(1)} %collective-permute-done.8.ra, ...), custom_call_target="tpu_custom_call", output_to_operand_aliasing={{}: (5, {})} | custom-call | flops 1000 | bytes 1000 | tf_op jit(solution)/shard_map/second_stage_late/pallas_call | solution.py:562
  (3 shorter events, 0.0 us)
Async XLA Ops:
  2.0 12.8 %collective-permute-start.2 = (f32[576,128]{1,0:T(8,128)S(1)}, f32[576,128]{1,0:T(8,128)S(1)}, u32[]{:S(2)}, u32[]{:S(2)}) collective-permute-start(f32[576,128]{1,0:T(8,128)S(1)} %get-tuple-element.33), channel_id=1, source_target_pairs={{0,1},{1,0},{2,3},{3,2},{4,5},{5,4},{6,7},{7,6},{8,9},{9,8},{10,11... | collective-permute-start | bytes 884744 | tf_op jit(solution)/shard_map/ppermute | solution.py:44
  5.1 9.7 %collective-permute-start.3 = (f32[576,128]{1,0:T(8,128)S(1)}, f32[576,128]{1,0:T(8,128)S(1)}, u32[]{:S(2)}, u32[]{:S(2)}) collective-permute-start(f32[576,128]{1,0:T(8,128)S(1)} %get-tuple-element.34), channel_id=1, source_target_pairs={{0,4},{1,2},{2,1},{3,7},{4,0},{5,6},{6,5},{7,3},{8,12},{9,10},{10,... | collective-permute-start | bytes 884744 | tf_op jit(solution)/shard_map/ppermute | solution.py:43
  5.5 12.6 %collective-permute-start.6 = (f32[512,128]{1,0:T(8,128)S(1)}, f32[512,128]{1,0:T(8,128)S(1)}, u32[]{:S(2)}, u32[]{:S(2)}) collective-permute-start(f32[512,128]{1,0:T(8,128)S(1)} %get-tuple-element.42), channel_id=1, source_target_pairs={{0,1},{1,0},{2,3},{3,2},{4,5},{5,4},{6,7},{7,6},{8,9},{9,8},{10,11... | collective-permute-start | bytes 786440 | tf_op jit(solution)/shard_map/ppermute | solution.py:44
  8.7 9.4 %collective-permute-start.7 = (f32[512,128]{1,0:T(8,128)S(1)}, f32[512,128]{1,0:T(8,128)S(1)}, u32[]{:S(2)}, u32[]{:S(2)}) collective-permute-start(f32[512,128]{1,0:T(8,128)S(1)} %get-tuple-element.43), channel_id=1, source_target_pairs={{0,4},{1,2},{2,1},{3,7},{4,0},{5,6},{6,5},{7,3},{8,12},{9,10},{10,... | collective-permute-start | bytes 786440 | tf_op jit(solution)/shard_map/ppermute | solution.py:43
  8.7 1.6 %collective-permute-start = (f32[80,128]{1,0:T(8,128)S(1)}, f32[80,128]{1,0:T(8,128)S(1)}, u32[]{:S(2)}, u32[]{:S(2)}) collective-permute-start(f32[80,128]{1,0:T(8,128)S(1)} %get-tuple-element.31), channel_id=1, source_target_pairs={{0,4},{4,0},{8,12},{12,8},{16,20},{20,16},{24,28},{28,24},{1,5},{5... | collective-permute-start | bytes 122888 | tf_op jit(solution)/shard_map/ppermute | solution.py:32
  10.3 4.5 %collective-permute-start.1 = (f32[80,128]{1,0:T(8,128)S(1)}, f32[80,128]{1,0:T(8,128)S(1)}, u32[]{:S(2)}, u32[]{:S(2)}) collective-permute-start(f32[80,128]{1,0:T(8,128)S(1)} %get-tuple-element.32), channel_id=1, source_target_pairs={{0,28},{4,8},{8,4},{12,16},{16,12},{20,24},{24,20},{28,0},{1,29},{... | collective-permute-start | bytes 122888 | tf_op jit(solution)/shard_map/ppermute | solution.py:32
  15.3 11.9 %collective-permute-start.4 = (f32[552,128]{1,0:T(8,128)S(1)}, f32[552,128]{1,0:T(8,128)S(1)}, u32[]{:S(2)}, u32[]{:S(2)}) collective-permute-start(f32[552,128]{1,0:T(8,128)S(1)} %get-tuple-element.37), channel_id=1, source_target_pairs={{0,1},{1,0},{2,3},{3,2},{4,5},{5,4},{6,7},{7,6},{8,9},{9,8},{10,11... | collective-permute-start | bytes 847880 | tf_op jit(solution)/shard_map/ppermute | solution.py:44
  16.7 10.5 %collective-permute-start.5 = (f32[552,128]{1,0:T(8,128)S(1)}, f32[552,128]{1,0:T(8,128)S(1)}, u32[]{:S(2)}, u32[]{:S(2)}) collective-permute-start(f32[552,128]{1,0:T(8,128)S(1)} %get-tuple-element.38), channel_id=1, source_target_pairs={{0,4},{1,2},{2,1},{3,7},{4,0},{5,6},{6,5},{7,3},{8,12},{9,10},{10,... | collective-permute-start | bytes 847880 | tf_op jit(solution)/shard_map/ppermute | solution.py:43
  18.6 10.8 %collective-permute-start.8 = (f32[512,128]{1,0:T(8,128)S(1)}, f32[512,128]{1,0:T(8,128)S(1)}, u32[]{:S(2)}, u32[]{:S(2)}) collective-permute-start(f32[512,128]{1,0:T(8,128)S(1)} %get-tuple-element.46), channel_id=1, source_target_pairs={{0,1},{1,0},{2,3},{3,2},{4,5},{5,4},{6,7},{7,6},{8,9},{9,8},{10,11... | collective-permute-start | bytes 786440 | tf_op jit(solution)/shard_map/ppermute | solution.py:44
  22.3 7.1 %collective-permute-start.9 = (f32[512,128]{1,0:T(8,128)S(1)}, f32[512,128]{1,0:T(8,128)S(1)}, u32[]{:S(2)}, u32[]{:S(2)}) collective-permute-start(f32[512,128]{1,0:T(8,128)S(1)} %get-tuple-element.47), channel_id=1, source_target_pairs={{0,4},{1,2},{2,1},{3,7},{4,0},{5,6},{6,5},{7,3},{8,12},{9,10},{10,... | collective-permute-start | bytes 786440 | tf_op jit(solution)/shard_map/ppermute | solution.py:43

commit v8 on v7

--- a/solution.py
+++ b/solution.py
@@ -442,7 +442,7 @@
 
 def radiation(
     nat, cosz_in, albedo_in, ext_in, single_in, weight_in, order_in, count_in, after, heat,
-    water, depth, save_a, save_b, save_t, save_g, cosz, albedo, ext, single, weight, order, count, sems
+    water, depth, save_c, save_d, save_t, save_g, cosz, albedo, ext, single, weight, order, count, sems
 ):
     del after
     copies = []
@@ -480,11 +480,11 @@
 
     scale = 4.0 / levels
     inv_mu = 1.0 / mu
-    ext_of, half_of, weight_of = by_band(ext), by_band(single), by_band(weight)
+    ext_of, single_of, weight_of = by_band(ext), by_band(single), by_band(weight)
     beam = [-(e * scale * LOG2E) * inv_mu for e in ext_of]
     diffuse = [-(1.66 * scale * LOG2E) * e for e in ext_of]
-    half = [0.5 * s for s in half_of]
-    strength = [w * mu for w in weight_of]
+    half = [0.5 * s for s in single_of]
+    strength = [weight_of[p] * mu * (1.0 - single_of[p]) for p in range(pairs)]
 
     def up(step, carry):
         l = levels - 1 - step
@@ -492,26 +492,30 @@
         w = water[l]
         above = depth[l]
         new_a, new_b, new_s = [], [], []
+        known = jnp.zeros((2 * nrows, LANES), jnp.float32)
         for p in range(pairs):
             a, b, s_bot = a_all[p], b_all[p], s_all[p]
             decay = jnp.exp2(diffuse[p] * w)
             s_top = strength[p] * jnp.exp2(beam[p] * above)
-            reflect = half[p] - half[p] * decay
+            lost = 1.0 - decay
+            reflect = half[p] * lost
             transmit = decay + reflect
-            source = half[p] * (s_top - s_bot)
+            taken = s_top - s_bot
+            source = half[p] * taken
             den = 1.0 - reflect * a
             inv = pl.reciprocal(den, approx=True)
             inv = inv * (2.0 - den * inv)
             t = transmit * inv
-            a_here = reflect + transmit * (t * a)
-            b_here = t * (a * source + b) + source
+            ta = t * a
+            g = (reflect * b + source) * inv
             save_t[l, p] = t
-            save_g[l, p] = (reflect * b + source) * inv
-            save_a[l, p] = 1.0 - a_here
-            save_b[l, p] = s_top - b_here
-            new_a.append(a_here)
-            new_b.append(b_here)
+            save_g[l, p] = g
+            save_d[l, p] = lost + lost * ta
+            known = known + (lost * (a * g + b) + taken)
+            new_a.append(reflect + transmit * ta)
+            new_b.append(t * (a * source + b) + source)
             new_s.append(s_top)
+        save_c[l] = known
         return tuple(new_a), tuple(new_b), tuple(new_s)
 
     s_floor = [strength[p] * jnp.exp2(beam[p] * depth[levels]) for p in range(pairs)]
@@ -528,30 +532,16 @@
         sunlit.append(jnp.max(jnp.where(hit, 1.0, 0.0), axis=0, keepdims=True))
     gain = float(levels) * jnp.concatenate(sunlit, axis=0)
 
-    def net_flux(l, d_all):
-        net = jnp.zeros((2 * nrows, LANES), jnp.float32)
+    def down(l, d_all):
+        absorbed = save_c[l]
         for p in range(pairs):
-            net = net + (save_b[l, p] + d_all[p] * save_a[l, p])
-        return net
-
-    def put(l, absorbed):
+            absorbed = absorbed + save_d[l, p] * d_all[p]
         both = absorbed[:nrows] + absorbed[nrows:]
         heat[pl.ds(pl.multiple_of(nrows * l, nrows), nrows), :] = gain * both
-
-    def down(l, carry):
-        d_all, net_above = carry
-        d_new = tuple(save_t[l - 1, p] * d_all[p] + save_g[l - 1, p] for p in range(pairs))
-        net = net_flux(l, d_new)
-        put(l - 1, net_above - net)
-        return d_new, net
+        return tuple(save_t[l, p] * d_all[p] + save_g[l, p] for p in range(pairs))
 
     d_top = tuple(jnp.zeros((2 * nrows, LANES), jnp.float32) for _ in range(pairs))
-    d_low, net_low = lax.fori_loop(1, levels, down, (d_top, net_flux(0, d_top)))
-    net = jnp.zeros((2 * nrows, LANES), jnp.float32)
-    for p in range(pairs):
-        d_floor = save_t[levels - 1, p] * d_low[p] + save_g[levels - 1, p]
-        net = net + ((s_floor[p] - b_floor[p]) + d_floor * (1.0 - a_floor[p]))
-    put(levels - 1, net_low - net)
+    lax.fori_loop(0, levels, down, d_top, unroll=4)
 
 
 def in_hbm(x):
@@ -653,7 +643,7 @@
         ),
         [
             scratch(levels, 2 * nrows, ncols), scratch(levels + 1, 2 * nrows, ncols),
-            store, store, store, store,
+            scratch(levels, 2 * nrows, ncols), store, store, store,
             scratch(nrows, ncols), scratch(nrows, ncols),
             pltpu.SMEM(extinction.shape, jnp.float32), pltpu.SMEM(extinction.shape, jnp.float32),
             pltpu.SMEM(extinction.shape, jnp.float32), pltpu.VMEM((nrows, 1, ncols), jnp.int32),

time: 30.6 us -> 30.6 us (level)
  Pallas kernels: 10.3 us -> 9.81 us
  waiting for transfers between devices: 5.34 us -> 5.8 us
    pallas_call x7, Pallas kernels: 10.3 us -> 9.81 us  [call(): pl.pallas_call(kernel, out_shape=out_shape, in_specs=specs, out_specs=out...]
    ppermute x4, waiting for transfers between devices: 1.96 us -> 2.42 us  [lat_swaps(): lax.ppermute(first_block, 'lat', [(j, j ^ 1) for j in range(nlat)])]
  transfers between devices with their start and end apart: 10 -> 10, of which waited for: 4 -> 4; matrix products, arithmetic and copies ran while one was open for 0% -> 0% of each run, Pallas kernels for 26% -> 25%
where the time goes in v8:
time: 30.6 us; the launch traced here: 30.4 us
  starting transfers between devices  14.1 us (46%)
  Pallas kernels  9.81 us (32%)
  waiting for transfers between devices  5.8 us (19%)
  between operations  0.69 us (2%)
    ppermute x4, starting transfers between devices, lat_swaps(): lax.ppermute(first_block, 'lat', [(j, j ^ 1) for j in range(nlat)])  11.4 us
    pallas_call x7, Pallas kernels, call(): pl.pallas_call(kernel, out_shape=out_shape, in_specs=specs, out_specs=out...  9.81 us
    ppermute x4, waiting for transfers between devices, lat_swaps(): lax.ppermute(first_block, 'lat', [(j, j ^ 1) for j in range(nlat)])  2.42 us
    ppermute x1, waiting for transfers between devices, lon_swaps(): lax.ppermute(second_block, 'lon', second)  2.29 us
    ppermute x1, starting transfers between devices, lon_swaps(): lax.ppermute(second_block, 'lon', second)  2.19 us
    ppermute x1, waiting for transfers between devices, lon_swaps(): lax.ppermute(first_block, 'lon', first)  1.08 us
  transfers between devices with their start and end apart: 10, of which 4 were waited for; matrix products, arithmetic and copies ran while one was open for 0% of the time, Pallas kernels for 25%

profile of v8, /device:TPU:0, one launch (start us, length us, event | category | flops | bytes accessed | tf_op | source)
XLA Modules:
  0.0 30.4 jit_solution(8247674760821631533)
XLA Ops:
  0.6 1.4 %pack_first.1 = (f32[8,128,128]{2,1,0:T(8,128)S(1)}, f32[576,128]{1,0:T(8,128)S(1)}, f32[576,128]{1,0:T(8,128)S(1)}, f32[4,256,128]{2,1,0:T(8,128)S(1)}, f32[4,2...) custom-call(f32[8,256,128]{2,1,0:T(8,128)} %bitcast.5, f32[2,256,128]{2,1,0:T(8,128)} %bitcast.7), custom_call_target="tpu_custom_call" | custom-call | flops 1000 | bytes 1000 | tf_op jit(solution)/shard_map/pack_first/pallas_call | solution.py:552
  2.0 3.1 %collective-permute-start.2 = (f32[576,128]{1,0:T(8,128)S(1)}, f32[576,128]{1,0:T(8,128)S(1)}, u32[]{:S(2)}, u32[]{:S(2)}) collective-permute-start(f32[576,128]{1,0:T(8,128)S(1)} %get-tuple-element.33), channel_id=1, source_target_pairs={{0,1},{1,0},{2,3},{3,2},{4,5},{5,4},{6,7},{7,6},{8,9},{9,8},{10,11... | collective-permute-start | bytes 884744 | tf_op jit(solution)/shard_map/ppermute | solution.py:44
  5.1 0.0 collective-permute-start.3
  5.1 0.4 %pack_middle.1 = (f32[8,128,128]{2,1,0:T(8,128)S(1)}, f32[4,128,128]{2,1,0:T(8,128)S(1)}, f32[4,128,128]{2,1,0:T(8,128)S(1)}, f32[80,128]{1,0:T(8,128)S(1)}, f32...) custom-call(f32[4,256,128]{2,1,0:T(8,128)S(1)} %get-tuple-element.27.nat, ...), custom_call_target="tpu_custom_call" | custom-call | flops 1000 | bytes 1000 | tf_op jit(solution)/shard_map/pack_middle/pallas_call | solution.py:552
  5.5 3.2 %collective-permute-start.6 = (f32[512,128]{1,0:T(8,128)S(1)}, f32[512,128]{1,0:T(8,128)S(1)}, u32[]{:S(2)}, u32[]{:S(2)}) collective-permute-start(f32[512,128]{1,0:T(8,128)S(1)} %get-tuple-element.42), channel_id=1, source_target_pairs={{0,1},{1,0},{2,3},{3,2},{4,5},{5,4},{6,7},{7,6},{8,9},{9,8},{10,11... | collective-permute-start | bytes 786440 | tf_op jit(solution)/shard_map/ppermute | solution.py:44
  8.7 0.0 collective-permute-start.7
  8.7 0.5 %collective-permute-start = (f32[80,128]{1,0:T(8,128)S(1)}, f32[80,128]{1,0:T(8,128)S(1)}, u32[]{:S(2)}, u32[]{:S(2)}) collective-permute-start(f32[80,128]{1,0:T(8,128)S(1)} %get-tuple-element.31), channel_id=1, source_target_pairs={{0,4},{4,0},{8,12},{12,8},{16,20},{20,16},{24,28},{28,24},{1,5},{5... | collective-permute-start | bytes 122888 | tf_op jit(solution)/shard_map/ppermute | solution.py:32
  9.2 1.1 %collective-permute-done.la = f32[80,128]{1,0:T(8,128)S(1)} collective-permute-done((f32[80,128]{1,0:T(8,128)S(1)}, f32[80,128]{1,0:T(8,128)S(1)}, u32[]{:S(2)}, u32[]{:S(2)}) %collective-permute-start) | collective-permute-done | bytes 40992 | tf_op jit(solution)/shard_map/ppermute | solution.py:32
  10.3 2.2 %collective-permute-start.1 = (f32[80,128]{1,0:T(8,128)S(1)}, f32[80,128]{1,0:T(8,128)S(1)}, u32[]{:S(2)}, u32[]{:S(2)}) collective-permute-start(f32[80,128]{1,0:T(8,128)S(1)} %get-tuple-element.32), channel_id=1, source_target_pairs={{0,28},{4,8},{8,4},{12,16},{16,12},{20,24},{24,20},{28,0},{1,29},{... | collective-permute-start | bytes 122888 | tf_op jit(solution)/shard_map/ppermute | solution.py:32
  12.5 2.3 %collective-permute-done.1.lb = f32[80,128]{1,0:T(8,128)S(1)} collective-permute-done((f32[80,128]{1,0:T(8,128)S(1)}, f32[80,128]{1,0:T(8,128)S(1)}, u32[]{:S(2)}, u32[]{:S(2)}) %collective-permute-start.1) | collective-permute-done | bytes 40992 | tf_op jit(solution)/shard_map/ppermute | solution.py:32
  14.8 0.0 collective-permute-done.2.ra
  14.8 0.0 collective-permute-done.3.rb
  14.8 0.5 %first_stage_early.1 = (f32[8,128,128]{2,1,0:T(8,128)S(1)}, f32[552,128]{1,0:T(8,128)S(1)}, f32[552,128]{1,0:T(8,128)S(1)}, f32[128,128]{1,0:T(8,128)S(1)}, f32[192,128]{1,0:T(8,128)S(1)}) custom-call(f32[8,128,128]{2,1,0:T(8,128)S(1)} %get-tuple-element.26.tiles_first.q, f32[4,128,128]{2,1,0:T(8,128)S(1)} %get-tuple-element.29.ce, ...), custom_call_target="tpu_custom_call" | custom-call | flops 1000000000 | bytes 1000000000 | tf_op jit(solution)/shard_map/first_stage_early/pallas_call | solution.py:552
  15.3 1.4 %collective-permute-start.4 = (f32[552,128]{1,0:T(8,128)S(1)}, f32[552,128]{1,0:T(8,128)S(1)}, u32[]{:S(2)}, u32[]{:S(2)}) collective-permute-start(f32[552,128]{1,0:T(8,128)S(1)} %get-tuple-element.37), channel_id=1, source_target_pairs={{0,1},{1,0},{2,3},{3,2},{4,5},{5,4},{6,7},{7,6},{8,9},{9,8},{10,11... | collective-permute-start | bytes 847880 | tf_op jit(solution)/shard_map/ppermute | solution.py:44
  16.7 0.0 collective-permute-start.5
  16.7 1.4 %collective-permute-done.6.ra = f32[512,128]{1,0:T(8,128)S(1)} collective-permute-done((f32[512,128]{1,0:T(8,128)S(1)}, f32[512,128]{1,0:T(8,128)S(1)}, u32[]{:S(2)}, u32[]{:S(2)}) %collective-permute-start.6) | collective-permute-done | bytes 262176 | tf_op jit(solution)/shard_map/ppermute | solution.py:44
  18.1 0.5 %first_stage_late.1 = (f32[8,128,128]{2,1,0:T(8,128)S(1)}, f32[512,128]{1,0:T(8,128)S(1)}, f32[512,128]{1,0:T(8,128)S(1)}) custom-call(f32[8,128,128]{2,1,0:T(8,128)S(1)} %get-tuple-element.41.q.q_late, f32[4,128,128]{2,1,0:T(8,128)S(1)} %get-tuple-element.29.ce, f32[4,128,128]{2,1,0:T(8,128)S(1)} %get-tuple-element.30.cn, ...), custom_call_target="tpu_custom_call" | custom-call | flops 12000000 | bytes 12000000 | tf_op jit(solution)/shard_map/first_stage_late/pallas_call | solution.py:552
  18.6 3.7 %collective-permute-start.8 = (f32[512,128]{1,0:T(8,128)S(1)}, f32[512,128]{1,0:T(8,128)S(1)}, u32[]{:S(2)}, u32[]{:S(2)}) collective-permute-start(f32[512,128]{1,0:T(8,128)S(1)} %get-tuple-element.46), channel_id=1, source_target_pairs={{0,1},{1,0},{2,3},{3,2},{4,5},{5,4},{6,7},{7,6},{8,9},{9,8},{10,11... | collective-permute-start | bytes 786440 | tf_op jit(solution)/shard_map/ppermute | solution.py:44
  22.3 0.0 collective-permute-start.9
  22.3 4.5 %radiation.1.heating = f32[256,128]{1,0:T(8,128)S(1)} custom-call(f32[4,256,128]{2,1,0:T(8,128)S(1)} %get-tuple-element.40.nat, f32[4,128]{1,0:T(4,128)} %cosz_in.1, f32[4,128]{1,0:T(4,128)} %albedo_in.1, f32[14]{0:T(128)} %ext_in.1, f32[14]{0:T(128)} %single_in.1, f32[14]{0:T(128)} %weight_in.1, s32[4,1,128]{2,1,0:T(1,128)} %order_in.1, s32[4]{0:T(128)} %bitcast.8, ...), custom_call_target="tpu_custom_call" | custom-call | flops 16000000 | bytes 16000000 | tf_op jit(solution)/shard_map/radiation/pallas_call | solution.py:552
  26.8 0.0 collective-permute-done.5.rb
  26.8 1.6 %second_stage_early.1 = (f32[8,256,128]{2,1,0:T(8,128)}, f32[256,128]{1,0:T(8,128)}, f32[8,128,128]{2,1,0:T(8,128)S(1)}) custom-call(f32[8,128,128]{2,1,0:T(8,128)S(1)} %get-tuple-element.26.tiles_first.q, f32[8,128,128]{2,1,0:T(8,128)S(1)} %get-tuple-element.35.s, f32[4,128,128]{2,1,0:T(8,128)S(1)} %get-tuple-element.29.ce, ...), custom_call_target="tpu_custom_call" | custom-call | flops 1000 | bytes 1000 | tf_op jit(solution)/shard_map/second_stage_early/pallas_call | solution.py:552
  28.4 1.0 %collective-permute-done.8.ra = f32[512,128]{1,0:T(8,128)S(1)} collective-permute-done((f32[512,128]{1,0:T(8,128)S(1)}, f32[512,128]{1,0:T(8,128)S(1)}, u32[]{:S(2)}, u32[]{:S(2)}) %collective-permute-start.8) | collective-permute-done | bytes 262176 | tf_op jit(solution)/shard_map/ppermute | solution.py:44
  29.4 1.0 %second_stage_late.1 = f32[8,256,128]{2,1,0:T(8,128)} custom-call(f32[8,128,128]{2,1,0:T(8,128)S(1)} %get-tuple-element.45.part, f32[4,128,128]{2,1,0:T(8,128)S(1)} %get-tuple-element.30.cn, f32[128,128]{1,0:T(8,128)S(1)} %get-tuple-element.36.below, f32[512,128]{1,0:T(8,128)S(1)} %collective-permute-done.8.ra, ...), custom_call_target="tpu_custom_call", output_to_operand_aliasing={{}: (5, {})} | custom-call | flops 1000 | bytes 1000 | tf_op jit(solution)/shard_map/second_stage_late/pallas_call | solution.py:552
  (3 shorter events, 0.0 us)
Async XLA Ops:
  2.0 12.8 %collective-permute-start.2 = (f32[576,128]{1,0:T(8,128)S(1)}, f32[576,128]{1,0:T(8,128)S(1)}, u32[]{:S(2)}, u32[]{:S(2)}) collective-permute-start(f32[576,128]{1,0:T(8,128)S(1)} %get-tuple-element.33), channel_id=1, source_target_pairs={{0,1},{1,0},{2,3},{3,2},{4,5},{5,4},{6,7},{7,6},{8,9},{9,8},{10,11... | collective-permute-start | bytes 884744 | tf_op jit(solution)/shard_map/ppermute | solution.py:44
  5.1 9.7 %collective-permute-start.3 = (f32[576,128]{1,0:T(8,128)S(1)}, f32[576,128]{1,0:T(8,128)S(1)}, u32[]{:S(2)}, u32[]{:S(2)}) collective-permute-start(f32[576,128]{1,0:T(8,128)S(1)} %get-tuple-element.34), channel_id=1, source_target_pairs={{0,4},{1,2},{2,1},{3,7},{4,0},{5,6},{6,5},{7,3},{8,12},{9,10},{10,... | collective-permute-start | bytes 884744 | tf_op jit(solution)/shard_map/ppermute | solution.py:43
  5.5 12.6 %collective-permute-start.6 = (f32[512,128]{1,0:T(8,128)S(1)}, f32[512,128]{1,0:T(8,128)S(1)}, u32[]{:S(2)}, u32[]{:S(2)}) collective-permute-start(f32[512,128]{1,0:T(8,128)S(1)} %get-tuple-element.42), channel_id=1, source_target_pairs={{0,1},{1,0},{2,3},{3,2},{4,5},{5,4},{6,7},{7,6},{8,9},{9,8},{10,11... | collective-permute-start | bytes 786440 | tf_op jit(solution)/shard_map/ppermute | solution.py:44
  8.7 9.4 %collective-permute-start.7 = (f32[512,128]{1,0:T(8,128)S(1)}, f32[512,128]{1,0:T(8,128)S(1)}, u32[]{:S(2)}, u32[]{:S(2)}) collective-permute-start(f32[512,128]{1,0:T(8,128)S(1)} %get-tuple-element.43), channel_id=1, source_target_pairs={{0,4},{1,2},{2,1},{3,7},{4,0},{5,6},{6,5},{7,3},{8,12},{9,10},{10,... | collective-permute-start | bytes 786440 | tf_op jit(solution)/shard_map/ppermute | solution.py:43
  8.7 1.6 %collective-permute-start = (f32[80,128]{1,0:T(8,128)S(1)}, f32[80,128]{1,0:T(8,128)S(1)}, u32[]{:S(2)}, u32[]{:S(2)}) collective-permute-start(f32[80,128]{1,0:T(8,128)S(1)} %get-tuple-element.31), channel_id=1, source_target_pairs={{0,4},{4,0},{8,12},{12,8},{16,20},{20,16},{24,28},{28,24},{1,5},{5... | collective-permute-start | bytes 122888 | tf_op jit(solution)/shard_map/ppermute | solution.py:32
  10.3 4.5 %collective-permute-start.1 = (f32[80,128]{1,0:T(8,128)S(1)}, f32[80,128]{1,0:T(8,128)S(1)}, u32[]{:S(2)}, u32[]{:S(2)}) collective-permute-start(f32[80,128]{1,0:T(8,128)S(1)} %get-tuple-element.32), channel_id=1, source_target_pairs={{0,28},{4,8},{8,4},{12,16},{16,12},{20,24},{24,20},{28,0},{1,29},{... | collective-permute-start | bytes 122888 | tf_op jit(solution)/shard_map/ppermute | solution.py:32
  15.3 11.4 %collective-permute-start.4 = (f32[552,128]{1,0:T(8,128)S(1)}, f32[552,128]{1,0:T(8,128)S(1)}, u32[]{:S(2)}, u32[]{:S(2)}) collective-permute-start(f32[552,128]{1,0:T(8,128)S(1)} %get-tuple-element.37), channel_id=1, source_target_pairs={{0,1},{1,0},{2,3},{3,2},{4,5},{5,4},{6,7},{7,6},{8,9},{9,8},{10,11... | collective-permute-start | bytes 847880 | tf_op jit(solution)/shard_map/ppermute | solution.py:44
  16.7 10.0 %collective-permute-start.5 = (f32[552,128]{1,0:T(8,128)S(1)}, f32[552,128]{1,0:T(8,128)S(1)}, u32[]{:S(2)}, u32[]{:S(2)}) collective-permute-start(f32[552,128]{1,0:T(8,128)S(1)} %get-tuple-element.38), channel_id=1, source_target_pairs={{0,4},{1,2},{2,1},{3,7},{4,0},{5,6},{6,5},{7,3},{8,12},{9,10},{10,... | collective-permute-start | bytes 847880 | tf_op jit(solution)/shard_map/ppermute | solution.py:43
  18.6 10.8 %collective-permute-start.8 = (f32[512,128]{1,0:T(8,128)S(1)}, f32[512,128]{1,0:T(8,128)S(1)}, u32[]{:S(2)}, u32[]{:S(2)}) collective-permute-start(f32[512,128]{1,0:T(8,128)S(1)} %get-tuple-element.46), channel_id=1, source_target_pairs={{0,1},{1,0},{2,3},{3,2},{4,5},{5,4},{6,7},{7,6},{8,9},{9,8},{10,11... | collective-permute-start | bytes 786440 | tf_op jit(solution)/shard_map/ppermute | solution.py:44
  22.3 7.1 %collective-permute-start.9 = (f32[512,128]{1,0:T(8,128)S(1)}, f32[512,128]{1,0:T(8,128)S(1)}, u32[]{:S(2)}, u32[]{:S(2)}) collective-permute-start(f32[512,128]{1,0:T(8,128)S(1)} %get-tuple-element.47), channel_id=1, source_target_pairs={{0,4},{1,2},{2,1},{3,7},{4,0},{5,6},{6,5},{7,3},{8,12},{9,10},{10,... | collective-permute-start | bytes 786440 | tf_op jit(solution)/shard_map/ppermute | solution.py:43

commit v9 on v8

--- a/solution.py
+++ b/solution.py
@@ -84,32 +84,39 @@
 
 def pack_first(pairs, nrows, fields, courant, tiles, za, zb, nat, nat_late, nat_wind, sems):
     n = 2 * pairs
-    first = pltpu.make_async_copy(fields.at[pl.ds(0, n)], nat, sems.at[0])
-    wind = pltpu.make_async_copy(courant, nat_wind, sems.at[1])
-    late = pltpu.make_async_copy(fields.at[pl.ds(n, nat_late.shape[0])], nat_late, sems.at[2])
-    for copy in (first, wind, late):
+    first = [
+        pltpu.make_async_copy(fields.at[pl.ds(2 * p, 2)], nat.at[pl.ds(2 * p, 2)], sems.at[p]) for p in range(pairs)
+    ]
+    north = pltpu.make_async_copy(courant.at[pl.ds(1, 1)], nat_wind.at[pl.ds(1, 1)], sems.at[pairs])
+    late = pltpu.make_async_copy(fields.at[pl.ds(n, nat_late.shape[0])], nat_late, sems.at[pairs + 1])
+    east = pltpu.make_async_copy(courant.at[pl.ds(0, 1)], nat_wind.at[pl.ds(0, 1)], sems.at[pairs + 2])
+    for copy in first + [north, late, east]:
         copy.start()
-    first.wait()
-    wind.wait()
     half = LANES // 2
-    lane = lax.broadcasted_iota(jnp.int32, (half, LANES), 1)
-
-    def body(up, down):
-        for p in range(pairs):
-            for r in range(nrows):
-                tile = tile_of(native(nat, 2 * p, r, nrows), native(nat, 2 * p + 1, r, nrows))
-                tiles[nrows * p + r] = tile
-                (up if r >= 2 else down)[pl.ds((2 * p + r % 2) * LANES, LANES), :] = tile
+    even = is_even("lat")
+
+    def body(p, up, down):
+        for r in range(nrows):
+            tile = tile_of(native(nat, 2 * p, r, nrows), native(nat, 2 * p + 1, r, nrows))
+            tiles[nrows * p + r] = tile
+            (up if r >= 2 else down)[pl.ds((2 * p + r % 2) * LANES, LANES), :] = tile
+        if p < pairs - 1:
+            return
+        lane = lax.broadcasted_iota(jnp.int32, (half, LANES), 1)
         top = native(nat_wind, 1, nrows - 1, nrows) * (1.0 / 12.0)
         top = tile_of(top, top)
         top = jnp.where(lane < half, top[:half], top[half:])
         for ref in (up, down):
             ref[pl.ds(2 * pairs * LANES, half), :] = top
 
-    even = is_even("lat")
-    pl.when(even)(lambda: body(za, zb))
-    pl.when(jnp.logical_not(even))(lambda: body(zb, za))
+    for p in range(pairs):
+        first[p].wait()
+        if p == pairs - 1:
+            north.wait()
+        pl.when(even)(functools.partial(body, p, za, zb))
+        pl.when(jnp.logical_not(even))(functools.partial(body, p, zb, za))
     late.wait()
+    east.wait()
 
 
 def pack_middle(pairs, nrows, nat, nat_wind, tiles_first, tiles, ce, cn, la, lb, za, zb):
@@ -583,7 +590,7 @@
         [HBM, HBM],
         (VMEM,) * 6,
         (in_hbm(flat), in_hbm(wind)),
-        [pltpu.SemaphoreType.DMA((3,))],
+        [pltpu.SemaphoreType.DMA((early + 3,))],
     )
     lat0 = lat_swaps(za, zb)
     ntiles = nrows * npairs

time: 30.6 us -> 30.5 us (level)
  no operation moved by 1% of the time
where the time goes in v9:
time: 30.5 us; the launch traced here: 30.3 us
  starting transfers between devices  14.1 us (46%)
  Pallas kernels  9.75 us (32%)
  waiting for transfers between devices  5.8 us (19%)
  between operations  0.69 us (2%)
    ppermute x4, starting transfers between devices, lat_swaps(): lax.ppermute(first_block, 'lat', [(j, j ^ 1) for j in range(nlat)])  11.4 us
    pallas_call x7, Pallas kernels, call(): pl.pallas_call(kernel, out_shape=out_shape, in_specs=specs, out_specs=out...  9.75 us
    ppermute x4, waiting for transfers between devices, lat_swaps(): lax.ppermute(first_block, 'lat', [(j, j ^ 1) for j in range(nlat)])  2.42 us
    ppermute x1, waiting for transfers between devices, lon_swaps(): lax.ppermute(second_block, 'lon', second)  2.29 us
    ppermute x1, starting transfers between devices, lon_swaps(): lax.ppermute(second_block, 'lon', second)  2.19 us
    ppermute x1, waiting for transfers between devices, lon_swaps(): lax.ppermute(first_block, 'lon', first)  1.08 us
  transfers between devices with their start and end apart: 10, of which 4 were waited for; matrix products, arithmetic and copies ran while one was open for 0% of the time, Pallas kernels for 25%

profile of v9, /device:TPU:0, one launch (start us, length us, event | category | flops | bytes accessed | tf_op | source)
XLA Modules:
  0.0 30.3 jit_solution(8499016873898937271)
XLA Ops:
  0.6 1.3 %pack_first.1 = (f32[8,128,128]{2,1,0:T(8,128)S(1)}, f32[576,128]{1,0:T(8,128)S(1)}, f32[576,128]{1,0:T(8,128)S(1)}, f32[4,256,128]{2,1,0:T(8,128)S(1)}, f32[4,2...) custom-call(f32[8,256,128]{2,1,0:T(8,128)} %bitcast.5, f32[2,256,128]{2,1,0:T(8,128)} %bitcast.7), custom_call_target="tpu_custom_call" | custom-call | flops 1000 | bytes 1000 | tf_op jit(solution)/shard_map/pack_first/pallas_call | solution.py:559
  1.9 3.1 %collective-permute-start.2 = (f32[576,128]{1,0:T(8,128)S(1)}, f32[576,128]{1,0:T(8,128)S(1)}, u32[]{:S(2)}, u32[]{:S(2)}) collective-permute-start(f32[576,128]{1,0:T(8,128)S(1)} %get-tuple-element.33), channel_id=1, source_target_pairs={{0,1},{1,0},{2,3},{3,2},{4,5},{5,4},{6,7},{7,6},{8,9},{9,8},{10,11... | collective-permute-start | bytes 884744 | tf_op jit(solution)/shard_map/ppermute | solution.py:44
  5.0 0.0 collective-permute-start.3
  5.0 0.4 %pack_middle.1 = (f32[8,128,128]{2,1,0:T(8,128)S(1)}, f32[4,128,128]{2,1,0:T(8,128)S(1)}, f32[4,128,128]{2,1,0:T(8,128)S(1)}, f32[80,128]{1,0:T(8,128)S(1)}, f32...) custom-call(f32[4,256,128]{2,1,0:T(8,128)S(1)} %get-tuple-element.27.nat, ...), custom_call_target="tpu_custom_call" | custom-call | flops 1000 | bytes 1000 | tf_op jit(solution)/shard_map/pack_middle/pallas_call | solution.py:559
  5.4 3.2 %collective-permute-start.6 = (f32[512,128]{1,0:T(8,128)S(1)}, f32[512,128]{1,0:T(8,128)S(1)}, u32[]{:S(2)}, u32[]{:S(2)}) collective-permute-start(f32[512,128]{1,0:T(8,128)S(1)} %get-tuple-element.42), channel_id=1, source_target_pairs={{0,1},{1,0},{2,3},{3,2},{4,5},{5,4},{6,7},{7,6},{8,9},{9,8},{10,11... | collective-permute-start | bytes 786440 | tf_op jit(solution)/shard_map/ppermute | solution.py:44
  8.6 0.0 collective-permute-start.7
  8.6 0.5 %collective-permute-start = (f32[80,128]{1,0:T(8,128)S(1)}, f32[80,128]{1,0:T(8,128)S(1)}, u32[]{:S(2)}, u32[]{:S(2)}) collective-permute-start(f32[80,128]{1,0:T(8,128)S(1)} %get-tuple-element.31), channel_id=1, source_target_pairs={{0,4},{4,0},{8,12},{12,8},{16,20},{20,16},{24,28},{28,24},{1,5},{5... | collective-permute-start | bytes 122888 | tf_op jit(solution)/shard_map/ppermute | solution.py:32
  9.1 1.1 %collective-permute-done.la = f32[80,128]{1,0:T(8,128)S(1)} collective-permute-done((f32[80,128]{1,0:T(8,128)S(1)}, f32[80,128]{1,0:T(8,128)S(1)}, u32[]{:S(2)}, u32[]{:S(2)}) %collective-permute-start) | collective-permute-done | bytes 40992 | tf_op jit(solution)/shard_map/ppermute | solution.py:32
  10.2 2.2 %collective-permute-start.1 = (f32[80,128]{1,0:T(8,128)S(1)}, f32[80,128]{1,0:T(8,128)S(1)}, u32[]{:S(2)}, u32[]{:S(2)}) collective-permute-start(f32[80,128]{1,0:T(8,128)S(1)} %get-tuple-element.32), channel_id=1, source_target_pairs={{0,28},{4,8},{8,4},{12,16},{16,12},{20,24},{24,20},{28,0},{1,29},{... | collective-permute-start | bytes 122888 | tf_op jit(solution)/shard_map/ppermute | solution.py:32
  12.4 2.3 %collective-permute-done.1.lb = f32[80,128]{1,0:T(8,128)S(1)} collective-permute-done((f32[80,128]{1,0:T(8,128)S(1)}, f32[80,128]{1,0:T(8,128)S(1)}, u32[]{:S(2)}, u32[]{:S(2)}) %collective-permute-start.1) | collective-permute-done | bytes 40992 | tf_op jit(solution)/shard_map/ppermute | solution.py:32
  14.7 0.0 collective-permute-done.2.ra
  14.7 0.0 collective-permute-done.3.rb
  14.7 0.5 %first_stage_early.1 = (f32[8,128,128]{2,1,0:T(8,128)S(1)}, f32[552,128]{1,0:T(8,128)S(1)}, f32[552,128]{1,0:T(8,128)S(1)}, f32[128,128]{1,0:T(8,128)S(1)}, f32[192,128]{1,0:T(8,128)S(1)}) custom-call(f32[8,128,128]{2,1,0:T(8,128)S(1)} %get-tuple-element.26.tiles_first.q, f32[4,128,128]{2,1,0:T(8,128)S(1)} %get-tuple-element.29.ce, ...), custom_call_target="tpu_custom_call" | custom-call | flops 1000000000 | bytes 1000000000 | tf_op jit(solution)/shard_map/first_stage_early/pallas_call | solution.py:559
  15.3 1.4 %collective-permute-start.4 = (f32[552,128]{1,0:T(8,128)S(1)}, f32[552,128]{1,0:T(8,128)S(1)}, u32[]{:S(2)}, u32[]{:S(2)}) collective-permute-start(f32[552,128]{1,0:T(8,128)S(1)} %get-tuple-element.37), channel_id=1, source_target_pairs={{0,1},{1,0},{2,3},{3,2},{4,5},{5,4},{6,7},{7,6},{8,9},{9,8},{10,11... | collective-permute-start | bytes 847880 | tf_op jit(solution)/shard_map/ppermute | solution.py:44
  16.7 0.0 collective-permute-start.5
  16.7 1.4 %collective-permute-done.6.ra = f32[512,128]{1,0:T(8,128)S(1)} collective-permute-done((f32[512,128]{1,0:T(8,128)S(1)}, f32[512,128]{1,0:T(8,128)S(1)}, u32[]{:S(2)}, u32[]{:S(2)}) %collective-permute-start.6) | collective-permute-done | bytes 262176 | tf_op jit(solution)/shard_map/ppermute | solution.py:44
  18.1 0.0 collective-permute-done.7.rb
  18.1 0.5 %first_stage_late.1 = (f32[8,128,128]{2,1,0:T(8,128)S(1)}, f32[512,128]{1,0:T(8,128)S(1)}, f32[512,128]{1,0:T(8,128)S(1)}) custom-call(f32[8,128,128]{2,1,0:T(8,128)S(1)} %get-tuple-element.41.q.q_late, f32[4,128,128]{2,1,0:T(8,128)S(1)} %get-tuple-element.29.ce, f32[4,128,128]{2,1,0:T(8,128)S(1)} %get-tuple-element.30.cn, ...), custom_call_target="tpu_custom_call" | custom-call | flops 12000000 | bytes 12000000 | tf_op jit(solution)/shard_map/first_stage_late/pallas_call | solution.py:559
  18.5 3.7 %collective-permute-start.8 = (f32[512,128]{1,0:T(8,128)S(1)}, f32[512,128]{1,0:T(8,128)S(1)}, u32[]{:S(2)}, u32[]{:S(2)}) collective-permute-start(f32[512,128]{1,0:T(8,128)S(1)} %get-tuple-element.46), channel_id=1, source_target_pairs={{0,1},{1,0},{2,3},{3,2},{4,5},{5,4},{6,7},{7,6},{8,9},{9,8},{10,11... | collective-permute-start | bytes 786440 | tf_op jit(solution)/shard_map/ppermute | solution.py:44
  22.2 4.5 %radiation.1.heating = f32[256,128]{1,0:T(8,128)S(1)} custom-call(f32[4,256,128]{2,1,0:T(8,128)S(1)} %get-tuple-element.40.nat, f32[4,128]{1,0:T(4,128)} %cosz_in.1, f32[4,128]{1,0:T(4,128)} %albedo_in.1, f32[14]{0:T(128)} %ext_in.1, f32[14]{0:T(128)} %single_in.1, f32[14]{0:T(128)} %weight_in.1, s32[4,1,128]{2,1,0:T(1,128)} %order_in.1, s32[4]{0:T(128)} %bitcast.8, ...), custom_call_target="tpu_custom_call" | custom-call | flops 16000000 | bytes 16000000 | tf_op jit(solution)/shard_map/radiation/pallas_call | solution.py:559
  26.7 0.0 collective-permute-done.4.ra
  26.7 1.6 %second_stage_early.1 = (f32[8,256,128]{2,1,0:T(8,128)}, f32[256,128]{1,0:T(8,128)}, f32[8,128,128]{2,1,0:T(8,128)S(1)}) custom-call(f32[8,128,128]{2,1,0:T(8,128)S(1)} %get-tuple-element.26.tiles_first.q, f32[8,128,128]{2,1,0:T(8,128)S(1)} %get-tuple-element.35.s, f32[4,128,128]{2,1,0:T(8,128)S(1)} %get-tuple-element.29.ce, ...), custom_call_target="tpu_custom_call" | custom-call | flops 1000 | bytes 1000 | tf_op jit(solution)/shard_map/second_stage_early/pallas_call | solution.py:559
  28.3 1.0 %collective-permute-done.8.ra = f32[512,128]{1,0:T(8,128)S(1)} collective-permute-done((f32[512,128]{1,0:T(8,128)S(1)}, f32[512,128]{1,0:T(8,128)S(1)}, u32[]{:S(2)}, u32[]{:S(2)}) %collective-permute-start.8) | collective-permute-done | bytes 262176 | tf_op jit(solution)/shard_map/ppermute | solution.py:44
  29.3 1.0 %second_stage_late.1 = f32[8,256,128]{2,1,0:T(8,128)} custom-call(f32[8,128,128]{2,1,0:T(8,128)S(1)} %get-tuple-element.45.part, f32[4,128,128]{2,1,0:T(8,128)S(1)} %get-tuple-element.30.cn, f32[128,128]{1,0:T(8,128)S(1)} %get-tuple-element.36.below, f32[512,128]{1,0:T(8,128)S(1)} %collective-permute-done.8.ra, ...), custom_call_target="tpu_custom_call", output_to_operand_aliasing={{}: (5, {})} | custom-call | flops 1000 | bytes 1000 | tf_op jit(solution)/shard_map/second_stage_late/pallas_call | solution.py:559
  (3 shorter events, 0.0 us)
Async XLA Ops:
  1.9 12.8 %collective-permute-start.2 = (f32[576,128]{1,0:T(8,128)S(1)}, f32[576,128]{1,0:T(8,128)S(1)}, u32[]{:S(2)}, u32[]{:S(2)}) collective-permute-start(f32[576,128]{1,0:T(8,128)S(1)} %get-tuple-element.33), channel_id=1, source_target_pairs={{0,1},{1,0},{2,3},{3,2},{4,5},{5,4},{6,7},{7,6},{8,9},{9,8},{10,11... | collective-permute-start | bytes 884744 | tf_op jit(solution)/shard_map/ppermute | solution.py:44
  5.0 9.7 %collective-permute-start.3 = (f32[576,128]{1,0:T(8,128)S(1)}, f32[576,128]{1,0:T(8,128)S(1)}, u32[]{:S(2)}, u32[]{:S(2)}) collective-permute-start(f32[576,128]{1,0:T(8,128)S(1)} %get-tuple-element.34), channel_id=1, source_target_pairs={{0,4},{1,2},{2,1},{3,7},{4,0},{5,6},{6,5},{7,3},{8,12},{9,10},{10,... | collective-permute-start | bytes 884744 | tf_op jit(solution)/shard_map/ppermute | solution.py:43
  5.4 12.6 %collective-permute-start.6 = (f32[512,128]{1,0:T(8,128)S(1)}, f32[512,128]{1,0:T(8,128)S(1)}, u32[]{:S(2)}, u32[]{:S(2)}) collective-permute-start(f32[512,128]{1,0:T(8,128)S(1)} %get-tuple-element.42), channel_id=1, source_target_pairs={{0,1},{1,0},{2,3},{3,2},{4,5},{5,4},{6,7},{7,6},{8,9},{9,8},{10,11... | collective-permute-start | bytes 786440 | tf_op jit(solution)/shard_map/ppermute | solution.py:44
  8.6 9.4 %collective-permute-start.7 = (f32[512,128]{1,0:T(8,128)S(1)}, f32[512,128]{1,0:T(8,128)S(1)}, u32[]{:S(2)}, u32[]{:S(2)}) collective-permute-start(f32[512,128]{1,0:T(8,128)S(1)} %get-tuple-element.43), channel_id=1, source_target_pairs={{0,4},{1,2},{2,1},{3,7},{4,0},{5,6},{6,5},{7,3},{8,12},{9,10},{10,... | collective-permute-start | bytes 786440 | tf_op jit(solution)/shard_map/ppermute | solution.py:43
  8.6 1.6 %collective-permute-start = (f32[80,128]{1,0:T(8,128)S(1)}, f32[80,128]{1,0:T(8,128)S(1)}, u32[]{:S(2)}, u32[]{:S(2)}) collective-permute-start(f32[80,128]{1,0:T(8,128)S(1)} %get-tuple-element.31), channel_id=1, source_target_pairs={{0,4},{4,0},{8,12},{12,8},{16,20},{20,16},{24,28},{28,24},{1,5},{5... | collective-permute-start | bytes 122888 | tf_op jit(solution)/shard_map/ppermute | solution.py:32
  10.2 4.5 %collective-permute-start.1 = (f32[80,128]{1,0:T(8,128)S(1)}, f32[80,128]{1,0:T(8,128)S(1)}, u32[]{:S(2)}, u32[]{:S(2)}) collective-permute-start(f32[80,128]{1,0:T(8,128)S(1)} %get-tuple-element.32), channel_id=1, source_target_pairs={{0,28},{4,8},{8,4},{12,16},{16,12},{20,24},{24,20},{28,0},{1,29},{... | collective-permute-start | bytes 122888 | tf_op jit(solution)/shard_map/ppermute | solution.py:32
  15.3 11.4 %collective-permute-start.4 = (f32[552,128]{1,0:T(8,128)S(1)}, f32[552,128]{1,0:T(8,128)S(1)}, u32[]{:S(2)}, u32[]{:S(2)}) collective-permute-start(f32[552,128]{1,0:T(8,128)S(1)} %get-tuple-element.37), channel_id=1, source_target_pairs={{0,1},{1,0},{2,3},{3,2},{4,5},{5,4},{6,7},{7,6},{8,9},{9,8},{10,11... | collective-permute-start | bytes 847880 | tf_op jit(solution)/shard_map/ppermute | solution.py:44
  16.7 10.0 %collective-permute-start.5 = (f32[552,128]{1,0:T(8,128)S(1)}, f32[552,128]{1,0:T(8,128)S(1)}, u32[]{:S(2)}, u32[]{:S(2)}) collective-permute-start(f32[552,128]{1,0:T(8,128)S(1)} %get-tuple-element.38), channel_id=1, source_target_pairs={{0,4},{1,2},{2,1},{3,7},{4,0},{5,6},{6,5},{7,3},{8,12},{9,10},{10,... | collective-permute-start | bytes 847880 | tf_op jit(solution)/shard_map/ppermute | solution.py:43
  18.5 10.8 %collective-permute-start.8 = (f32[512,128]{1,0:T(8,128)S(1)}, f32[512,128]{1,0:T(8,128)S(1)}, u32[]{:S(2)}, u32[]{:S(2)}) collective-permute-start(f32[512,128]{1,0:T(8,128)S(1)} %get-tuple-element.46), channel_id=1, source_target_pairs={{0,1},{1,0},{2,3},{3,2},{4,5},{5,4},{6,7},{7,6},{8,9},{9,8},{10,11... | collective-permute-start | bytes 786440 | tf_op jit(solution)/shard_map/ppermute | solution.py:44
  22.2 7.1 %collective-permute-start.9 = (f32[512,128]{1,0:T(8,128)S(1)}, f32[512,128]{1,0:T(8,128)S(1)}, u32[]{:S(2)}, u32[]{:S(2)}) collective-permute-start(f32[512,128]{1,0:T(8,128)S(1)} %get-tuple-element.47), channel_id=1, source_target_pairs={{0,4},{1,2},{2,1},{3,7},{4,0},{5,6},{6,5},{7,3},{8,12},{9,10},{10,... | collective-permute-start | bytes 786440 | tf_op jit(solution)/shard_map/ppermute | solution.py:43

commit v10 on v9

--- a/solution.py
+++ b/solution.py
@@ -326,7 +326,11 @@
             own, div = divergence(q, p, nrows, b, halo, cn, below, flux)
             for r in range(nrows):
                 section[nrows * p + r, pl.ds(SUB * b, SUB), :] = own[r] - div[r]
-        put_lat_sends(lat_even, section, p, nrows, za, zb)
+        up = jnp.where(lat_even, 2, 0)
+        for k in range(2):
+            span = pl.ds((2 * p + k) * LANES, LANES)
+            za[span, :] = jnp.transpose(section[nrows * p + up + k])
+            zb[span, :] = jnp.transpose(section[nrows * p + (2 - up) + k])
 
 
 def put_rows(buffer, pair, rows, nrows):
@@ -339,7 +343,7 @@
 
 def second_stage_early(
     pairs, later, nrows, q, s, ce, cn, below, ra, rb, side, heating, q_late, s_late,
-    out, heat_out, part, buffer, sems, sides, *edges
+    out, heat_out, part, winds, buffer, sems, sides, *edges
 ):
     edge_w, edge_e, edge_c, edge_d, flux = edges
     where = sources()
@@ -388,6 +392,7 @@
     def another(p, _):
         put_edges(s_late, nrows * p, sides, nrows * (pairs + p), nrows, edge_w, edge_e)
         put_fluxes(s_late, nrows * p, nrows, ce, edge_w, edge_e, edge_c, flux)
+        rows = [[] for _ in range(nrows)]
         for b in range(LANES // SUB):
             here = pl.ds(SUB * b, SUB)
             s0, s1, s2, s3 = own = [s_late[nrows * p + r, here, :] for r in range(nrows)]
@@ -402,47 +407,46 @@
             for r in range(nrows):
                 east = flux[r, pl.ds(SUB * (b + 1), SUB), :] - flux[r, pl.ds(SUB * (b + 1) - 1, SUB), :]
                 old = q_late[nrows * p + r, here, :]
-                part[nrows * p + r, here, :] = 0.5 * ((old + own[r]) - (east + (north[r + 1] - north[r])))
+                rows[r].append(0.5 * ((old + own[r]) - (east + (north[r + 1] - north[r]))))
+        put_rows(part, p, rows, nrows)
         return 0
 
     lax.fori_loop(0, pairs, one, 0)
     lax.fori_loop(0, later, another, 0)
+    for i, tile in enumerate((cn[0], cn[2], below[...], cn[3])):
+        winds[i] = 0.5 * jnp.transpose(tile)[: LANES // 2]
     for p in range(pairs):
         copy(p).wait()
     heat_copy.wait()
 
 
-def second_stage_late(pairs, done, nrows, part, cn, below, ra, rb, before, out, buffer, sems):
+def second_stage_late(pairs, done, nrows, part, winds, ra, rb, before, out, buffer, sems):
     del before
     where = sources()
+    levels = LANES // 2
 
     def copy(p):
         return pltpu.make_async_copy(
             buffer.at[pl.ds(2 * p, 2)], out.at[pl.ds(2 * (done + p), 2)], sems.at[p]
         )
 
-    def one(p):
-        rows = [[] for _ in range(nrows)]
-        for b in range(LANES // SUB):
-            here = pl.ds(SUB * b, SUB)
-
-            def halo(k):
-                start = (2 * p + k) * LANES + SUB * b
-                return partners(where, ra, rb, pl.ds(start, SUB))
-
-            (south_two, north_one), (south_one, north_two) = halo(0), halo(1)
-            low = 0.5 * cn[0, here, :] * south_one
-            high = 0.5 * cn[2, here, :] * north_one
-            bottom = 0.5 * below[here, :] * (7.0 * south_one - south_two)
-            top = 0.5 * cn[3, here, :] * (7.0 * north_one - north_two)
-            p0, p1, p2, p3 = (part[nrows * p + r, here, :] for r in range(nrows))
-            for r, value in enumerate((p0 + (low + bottom), p1 - low, p2 + high, p3 - (top + high))):
-                rows[r].append(value)
-        put_rows(buffer, p, rows, nrows)
+    for p in range(pairs):
+        for h in range(2):
+            for b in range(levels // SUB):
+                here = pl.ds(SUB * b, SUB)
+
+                def halo(k):
+                    return partners(where, ra, rb, pl.ds((2 * p + k) * LANES + levels * h + SUB * b, SUB))
+
+                (south_two, north_one), (south_one, north_two) = halo(0), halo(1)
+                low = winds[0, here, :] * south_one
+                high = winds[1, here, :] * north_one
+                bottom = winds[2, here, :] * (7.0 * south_one - south_two)
+                top = winds[3, here, :] * (7.0 * north_one - north_two)
+                for r, more in enumerate((low + bottom, -low, high, -(top + high))):
+                    rows = pl.ds(nrows * SUB * b + r, SUB, stride=nrows)
+                    buffer[2 * p + h, rows, :] = part[2 * p + h, rows, :] + more
         copy(p).start()
-
-    for p in range(pairs):
-        one(p)
     for p in range(pairs):
         copy(p).wait()
 
@@ -660,12 +664,12 @@
     )
 
     full = shape(nfields, levels * nrows, ncols)
-    out, heat_out, part = call(
+    out, heat_out, part, half_winds = call(
         functools.partial(second_stage_early, early, late, nrows),
         "second_stage_early",
-        (full, shape(levels * nrows, ncols), shape(nrows * late, ncols, LANES)),
+        (full, shape(levels * nrows, ncols), shape(2 * late, levels * nrows, ncols), shape(nrows, levels, ncols)),
         [VMEM] * 11,
-        (HBM, HBM, VMEM),
+        (HBM, HBM, VMEM, VMEM),
         (tiles0, section0, ce, cn, below, *lat2, side, heating, tiles1, section1),
         [
             scratch(2 * early, levels * nrows, ncols),
@@ -678,11 +682,11 @@
         functools.partial(second_stage_late, late, early, nrows),
         "second_stage_late",
         full,
-        [VMEM] * 5 + [HBM],
+        [VMEM] * 4 + [HBM],
         HBM,
-        (part, cn, below, *lat3, out),
+        (part, half_winds, *lat3, out),
         [scratch(2 * late, levels * nrows, ncols), pltpu.SemaphoreType.DMA((late,))],
-        input_output_aliases={5: 0},
+        input_output_aliases={4: 0},
     )
     return out.reshape(fields.shape), heat_out.reshape(levels, nrows, ncols)
 

time: 30.5 us -> 30.4 us (level)
  no operation moved by 1% of the time
where the time goes in v10:
time: 30.4 us; the launch traced here: 30.2 us
  starting transfers between devices  14.1 us (46%)
  Pallas kernels  9.82 us (32%)
  waiting for transfers between devices  5.6 us (18%)
  between operations  0.69 us (2%)
    ppermute x4, starting transfers between devices, lat_swaps(): lax.ppermute(first_block, 'lat', [(j, j ^ 1) for j in range(nlat)])  11.4 us
    pallas_call x7, Pallas kernels, call(): pl.pallas_call(kernel, out_shape=out_shape, in_specs=specs, out_specs=out...  9.82 us
    ppermute x1, waiting for transfers between devices, lon_swaps(): lax.ppermute(second_block, 'lon', second)  2.29 us
    ppermute x4, waiting for transfers between devices, lat_swaps(): lax.ppermute(first_block, 'lat', [(j, j ^ 1) for j in range(nlat)])  2.22 us
    ppermute x1, starting transfers between devices, lon_swaps(): lax.ppermute(second_block, 'lon', second)  2.19 us
    ppermute x1, waiting for transfers between devices, lon_swaps(): lax.ppermute(first_block, 'lon', first)  1.08 us
  transfers between devices with their start and end apart: 10, of which 4 were waited for; matrix products, arithmetic and copies ran while one was open for 0% of the time, Pallas kernels for 25%

profile of v10, /device:TPU:0, one launch (start us, length us, event | category | flops | bytes accessed | tf_op | source)
XLA Modules:
  0.0 30.2 jit_solution(15594492863039224050)
XLA Ops:
  0.6 1.3 %pack_first.1 = (f32[8,128,128]{2,1,0:T(8,128)S(1)}, f32[576,128]{1,0:T(8,128)S(1)}, f32[576,128]{1,0:T(8,128)S(1)}, f32[4,256,128]{2,1,0:T(8,128)S(1)}, f32[4,2...) custom-call(f32[8,256,128]{2,1,0:T(8,128)} %bitcast.6, f32[2,256,128]{2,1,0:T(8,128)} %bitcast.7), custom_call_target="tpu_custom_call" | custom-call | flops 1000 | bytes 1000 | tf_op jit(solution)/shard_map/pack_first/pallas_call | solution.py:563
  1.9 3.1 %collective-permute-start.2 = (f32[576,128]{1,0:T(8,128)S(1)}, f32[576,128]{1,0:T(8,128)S(1)}, u32[]{:S(2)}, u32[]{:S(2)}) collective-permute-start(f32[576,128]{1,0:T(8,128)S(1)} %get-tuple-element.34), channel_id=1, source_target_pairs={{0,1},{1,0},{2,3},{3,2},{4,5},{5,4},{6,7},{7,6},{8,9},{9,8},{10,11... | collective-permute-start | bytes 884744 | tf_op jit(solution)/shard_map/ppermute | solution.py:44
  5.0 0.0 collective-permute-start.3
  5.0 0.4 %pack_middle.1 = (f32[8,128,128]{2,1,0:T(8,128)S(1)}, f32[4,128,128]{2,1,0:T(8,128)S(1)}, f32[4,128,128]{2,1,0:T(8,128)S(1)}, f32[80,128]{1,0:T(8,128)S(1)}, f32...) custom-call(f32[4,256,128]{2,1,0:T(8,128)S(1)} %get-tuple-element.28.nat, ...), custom_call_target="tpu_custom_call" | custom-call | flops 1000 | bytes 1000 | tf_op jit(solution)/shard_map/pack_middle/pallas_call | solution.py:563
  5.4 3.2 %collective-permute-start.6 = (f32[512,128]{1,0:T(8,128)S(1)}, f32[512,128]{1,0:T(8,128)S(1)}, u32[]{:S(2)}, u32[]{:S(2)}) collective-permute-start(f32[512,128]{1,0:T(8,128)S(1)} %get-tuple-element.43), channel_id=1, source_target_pairs={{0,1},{1,0},{2,3},{3,2},{4,5},{5,4},{6,7},{7,6},{8,9},{9,8},{10,11... | collective-permute-start | bytes 786440 | tf_op jit(solution)/shard_map/ppermute | solution.py:44
  8.6 0.0 collective-permute-start.7
  8.6 0.5 %collective-permute-start = (f32[80,128]{1,0:T(8,128)S(1)}, f32[80,128]{1,0:T(8,128)S(1)}, u32[]{:S(2)}, u32[]{:S(2)}) collective-permute-start(f32[80,128]{1,0:T(8,128)S(1)} %get-tuple-element.32), channel_id=1, source_target_pairs={{0,4},{4,0},{8,12},{12,8},{16,20},{20,16},{24,28},{28,24},{1,5},{5... | collective-permute-start | bytes 122888 | tf_op jit(solution)/shard_map/ppermute | solution.py:32
  9.1 1.1 %collective-permute-done.la = f32[80,128]{1,0:T(8,128)S(1)} collective-permute-done((f32[80,128]{1,0:T(8,128)S(1)}, f32[80,128]{1,0:T(8,128)S(1)}, u32[]{:S(2)}, u32[]{:S(2)}) %collective-permute-start) | collective-permute-done | bytes 40992 | tf_op jit(solution)/shard_map/ppermute | solution.py:32
  10.2 2.2 %collective-permute-start.1 = (f32[80,128]{1,0:T(8,128)S(1)}, f32[80,128]{1,0:T(8,128)S(1)}, u32[]{:S(2)}, u32[]{:S(2)}) collective-permute-start(f32[80,128]{1,0:T(8,128)S(1)} %get-tuple-element.33), channel_id=1, source_target_pairs={{0,28},{4,8},{8,4},{12,16},{16,12},{20,24},{24,20},{28,0},{1,29},{... | collective-permute-start | bytes 122888 | tf_op jit(solution)/shard_map/ppermute | solution.py:32
  12.4 2.3 %collective-permute-done.1.lb = f32[80,128]{1,0:T(8,128)S(1)} collective-permute-done((f32[80,128]{1,0:T(8,128)S(1)}, f32[80,128]{1,0:T(8,128)S(1)}, u32[]{:S(2)}, u32[]{:S(2)}) %collective-permute-start.1) | collective-permute-done | bytes 40992 | tf_op jit(solution)/shard_map/ppermute | solution.py:32
  14.7 0.6 %first_stage_early.1 = (f32[8,128,128]{2,1,0:T(8,128)S(1)}, f32[552,128]{1,0:T(8,128)S(1)}, f32[552,128]{1,0:T(8,128)S(1)}, f32[128,128]{1,0:T(8,128)S(1)}, f32[192,128]{1,0:T(8,128)S(1)}) custom-call(f32[8,128,128]{2,1,0:T(8,128)S(1)} %get-tuple-element.27.tiles_first.q, f32[4,128,128]{2,1,0:T(8,128)S(1)} %get-tuple-element.30.ce, ...), custom_call_target="tpu_custom_call" | custom-call | flops 1000000000 | bytes 1000000000 | tf_op jit(solution)/shard_map/first_stage_early/pallas_call | solution.py:563
  15.3 1.4 %collective-permute-start.4 = (f32[552,128]{1,0:T(8,128)S(1)}, f32[552,128]{1,0:T(8,128)S(1)}, u32[]{:S(2)}, u32[]{:S(2)}) collective-permute-start(f32[552,128]{1,0:T(8,128)S(1)} %get-tuple-element.38), channel_id=1, source_target_pairs={{0,1},{1,0},{2,3},{3,2},{4,5},{5,4},{6,7},{7,6},{8,9},{9,8},{10,11... | collective-permute-start | bytes 847880 | tf_op jit(solution)/shard_map/ppermute | solution.py:44
  16.7 0.0 collective-permute-start.5
  16.7 1.4 %collective-permute-done.6.ra = f32[512,128]{1,0:T(8,128)S(1)} collective-permute-done((f32[512,128]{1,0:T(8,128)S(1)}, f32[512,128]{1,0:T(8,128)S(1)}, u32[]{:S(2)}, u32[]{:S(2)}) %collective-permute-start.6) | collective-permute-done | bytes 262176 | tf_op jit(solution)/shard_map/ppermute | solution.py:44
  18.1 0.0 collective-permute-done.7.rb
  18.1 0.6 %first_stage_late.1 = (f32[8,128,128]{2,1,0:T(8,128)S(1)}, f32[512,128]{1,0:T(8,128)S(1)}, f32[512,128]{1,0:T(8,128)S(1)}) custom-call(f32[8,128,128]{2,1,0:T(8,128)S(1)} %get-tuple-element.42.q.q_late, f32[4,128,128]{2,1,0:T(8,128)S(1)} %get-tuple-element.30.ce, f32[4,128,128]{2,1,0:T(8,128)S(1)} %get-tuple-element.31.cn, ...), custom_call_target="tpu_custom_call" | custom-call | flops 12000000 | bytes 12000000 | tf_op jit(solution)/shard_map/first_stage_late/pallas_call | solution.py:563
  18.7 3.7 %collective-permute-start.8 = (f32[512,128]{1,0:T(8,128)S(1)}, f32[512,128]{1,0:T(8,128)S(1)}, u32[]{:S(2)}, u32[]{:S(2)}) collective-permute-start(f32[512,128]{1,0:T(8,128)S(1)} %get-tuple-element.48), channel_id=1, source_target_pairs={{0,1},{1,0},{2,3},{3,2},{4,5},{5,4},{6,7},{7,6},{8,9},{9,8},{10,11... | collective-permute-start | bytes 786440 | tf_op jit(solution)/shard_map/ppermute | solution.py:44
  22.4 0.0 collective-permute-start.9
  22.4 4.5 %radiation.1.heating = f32[256,128]{1,0:T(8,128)S(1)} custom-call(f32[4,256,128]{2,1,0:T(8,128)S(1)} %get-tuple-element.41.nat, f32[4,128]{1,0:T(4,128)} %cosz_in.1, f32[4,128]{1,0:T(4,128)} %albedo_in.1, f32[14]{0:T(128)} %ext_in.1, f32[14]{0:T(128)} %single_in.1, f32[14]{0:T(128)} %weight_in.1, s32[4,1,128]{2,1,0:T(1,128)} %order_in.1, s32[4]{0:T(128)} %bitcast.8, ...), custom_call_target="tpu_custom_call" | custom-call | flops 16000000 | bytes 16000000 | tf_op jit(solution)/shard_map/radiation/pallas_call | solution.py:563
  26.9 0.0 collective-permute-done.4.ra
  26.9 0.0 collective-permute-done.5.rb
  26.9 1.5 %second_stage_early.1 = (f32[8,256,128]{2,1,0:T(8,128)}, f32[256,128]{1,0:T(8,128)}, f32[4,256,128]{2,1,0:T(8,128)S(1)}, f32[4,64,128]{2,1,0:T(8,128)S(1)}) custom-call(f32[8,128,128]{2,1,0:T(8,128)S(1)} %get-tuple-element.27.tiles_first.q, f32[8,128,128]{2,1,0:T(8,128)S(1)} %get-tuple-element.36.s, f32[4,128,128]{2,1,0:T(8,128)S(1)} %get-tuple-element.30.ce, ...), custom_call_target="tpu_custom_call" | custom-call | flops 1000 | bytes 1000 | tf_op jit(solution)/shard_map/second_stage_early/pallas_call | solution.py:563
  28.5 0.9 %collective-permute-done.8.ra = f32[512,128]{1,0:T(8,128)S(1)} collective-permute-done((f32[512,128]{1,0:T(8,128)S(1)}, f32[512,128]{1,0:T(8,128)S(1)}, u32[]{:S(2)}, u32[]{:S(2)}) %collective-permute-start.8) | collective-permute-done | bytes 262176 | tf_op jit(solution)/shard_map/ppermute | solution.py:44
  29.3 0.9 %second_stage_late.1 = f32[8,256,128]{2,1,0:T(8,128)} custom-call(f32[4,256,128]{2,1,0:T(8,128)S(1)} %get-tuple-element.46.part, f32[4,64,128]{2,1,0:T(8,128)S(1)} %get-tuple-element.47.winds, f32[512,128]{1,0:T(8,128)S(1)} %collective-permute-done.8.ra, f32[512,128]{1,0:T(8,128)S(1)} %collective-permute-done.9.rb, ...), custom_call_target="tpu_custom_call", output_to_operand_aliasing={{}: (4, {})} | custom-call | flops 1000 | bytes 1000 | tf_op jit(solution)/shard_map/second_stage_late/pallas_call | solution.py:563
  (3 shorter events, 0.0 us)
Async XLA Ops:
  1.9 12.8 %collective-permute-start.2 = (f32[576,128]{1,0:T(8,128)S(1)}, f32[576,128]{1,0:T(8,128)S(1)}, u32[]{:S(2)}, u32[]{:S(2)}) collective-permute-start(f32[576,128]{1,0:T(8,128)S(1)} %get-tuple-element.34), channel_id=1, source_target_pairs={{0,1},{1,0},{2,3},{3,2},{4,5},{5,4},{6,7},{7,6},{8,9},{9,8},{10,11... | collective-permute-start | bytes 884744 | tf_op jit(solution)/shard_map/ppermute | solution.py:44
  5.0 9.7 %collective-permute-start.3 = (f32[576,128]{1,0:T(8,128)S(1)}, f32[576,128]{1,0:T(8,128)S(1)}, u32[]{:S(2)}, u32[]{:S(2)}) collective-permute-start(f32[576,128]{1,0:T(8,128)S(1)} %get-tuple-element.35), channel_id=1, source_target_pairs={{0,4},{1,2},{2,1},{3,7},{4,0},{5,6},{6,5},{7,3},{8,12},{9,10},{10,... | collective-permute-start | bytes 884744 | tf_op jit(solution)/shard_map/ppermute | solution.py:43
  5.4 12.6 %collective-permute-start.6 = (f32[512,128]{1,0:T(8,128)S(1)}, f32[512,128]{1,0:T(8,128)S(1)}, u32[]{:S(2)}, u32[]{:S(2)}) collective-permute-start(f32[512,128]{1,0:T(8,128)S(1)} %get-tuple-element.43), channel_id=1, source_target_pairs={{0,1},{1,0},{2,3},{3,2},{4,5},{5,4},{6,7},{7,6},{8,9},{9,8},{10,11... | collective-permute-start | bytes 786440 | tf_op jit(solution)/shard_map/ppermute | solution.py:44
  8.6 9.4 %collective-permute-start.7 = (f32[512,128]{1,0:T(8,128)S(1)}, f32[512,128]{1,0:T(8,128)S(1)}, u32[]{:S(2)}, u32[]{:S(2)}) collective-permute-start(f32[512,128]{1,0:T(8,128)S(1)} %get-tuple-element.44), channel_id=1, source_target_pairs={{0,4},{1,2},{2,1},{3,7},{4,0},{5,6},{6,5},{7,3},{8,12},{9,10},{10,... | collective-permute-start | bytes 786440 | tf_op jit(solution)/shard_map/ppermute | solution.py:43
  8.6 1.6 %collective-permute-start = (f32[80,128]{1,0:T(8,128)S(1)}, f32[80,128]{1,0:T(8,128)S(1)}, u32[]{:S(2)}, u32[]{:S(2)}) collective-permute-start(f32[80,128]{1,0:T(8,128)S(1)} %get-tuple-element.32), channel_id=1, source_target_pairs={{0,4},{4,0},{8,12},{12,8},{16,20},{20,16},{24,28},{28,24},{1,5},{5... | collective-permute-start | bytes 122888 | tf_op jit(solution)/shard_map/ppermute | solution.py:32
  10.2 4.5 %collective-permute-start.1 = (f32[80,128]{1,0:T(8,128)S(1)}, f32[80,128]{1,0:T(8,128)S(1)}, u32[]{:S(2)}, u32[]{:S(2)}) collective-permute-start(f32[80,128]{1,0:T(8,128)S(1)} %get-tuple-element.33), channel_id=1, source_target_pairs={{0,28},{4,8},{8,4},{12,16},{16,12},{20,24},{24,20},{28,0},{1,29},{... | collective-permute-start | bytes 122888 | tf_op jit(solution)/shard_map/ppermute | solution.py:32
  15.3 11.6 %collective-permute-start.4 = (f32[552,128]{1,0:T(8,128)S(1)}, f32[552,128]{1,0:T(8,128)S(1)}, u32[]{:S(2)}, u32[]{:S(2)}) collective-permute-start(f32[552,128]{1,0:T(8,128)S(1)} %get-tuple-element.38), channel_id=1, source_target_pairs={{0,1},{1,0},{2,3},{3,2},{4,5},{5,4},{6,7},{7,6},{8,9},{9,8},{10,11... | collective-permute-start | bytes 847880 | tf_op jit(solution)/shard_map/ppermute | solution.py:44
  16.7 10.2 %collective-permute-start.5 = (f32[552,128]{1,0:T(8,128)S(1)}, f32[552,128]{1,0:T(8,128)S(1)}, u32[]{:S(2)}, u32[]{:S(2)}) collective-permute-start(f32[552,128]{1,0:T(8,128)S(1)} %get-tuple-element.39), channel_id=1, source_target_pairs={{0,4},{1,2},{2,1},{3,7},{4,0},{5,6},{6,5},{7,3},{8,12},{9,10},{10,... | collective-permute-start | bytes 847880 | tf_op jit(solution)/shard_map/ppermute | solution.py:43
  18.7 10.6 %collective-permute-start.8 = (f32[512,128]{1,0:T(8,128)S(1)}, f32[512,128]{1,0:T(8,128)S(1)}, u32[]{:S(2)}, u32[]{:S(2)}) collective-permute-start(f32[512,128]{1,0:T(8,128)S(1)} %get-tuple-element.48), channel_id=1, source_target_pairs={{0,1},{1,0},{2,3},{3,2},{4,5},{5,4},{6,7},{7,6},{8,9},{9,8},{10,11... | collective-permute-start | bytes 786440 | tf_op jit(solution)/shard_map/ppermute | solution.py:44
  22.4 7.0 %collective-permute-start.9 = (f32[512,128]{1,0:T(8,128)S(1)}, f32[512,128]{1,0:T(8,128)S(1)}, u32[]{:S(2)}, u32[]{:S(2)}) collective-permute-start(f32[512,128]{1,0:T(8,128)S(1)} %get-tuple-element.49), channel_id=1, source_target_pairs={{0,4},{1,2},{2,1},{3,7},{4,0},{5,6},{6,5},{7,3},{8,12},{9,10},{10,... | collective-permute-start | bytes 786440 | tf_op jit(solution)/shard_map/ppermute | solution.py:43

commit v11 on v10

--- a/solution.py
+++ b/solution.py
@@ -422,7 +422,6 @@
 
 def second_stage_late(pairs, done, nrows, part, winds, ra, rb, before, out, buffer, sems):
     del before
-    where = sources()
     levels = LANES // 2
 
     def copy(p):
@@ -430,25 +429,35 @@
             buffer.at[pl.ds(2 * p, 2)], out.at[pl.ds(2 * (done + p), 2)], sems.at[p]
         )
 
-    for p in range(pairs):
-        for h in range(2):
-            for b in range(levels // SUB):
-                here = pl.ds(SUB * b, SUB)
-
-                def halo(k):
-                    return partners(where, ra, rb, pl.ds((2 * p + k) * LANES + levels * h + SUB * b, SUB))
-
-                (south_two, north_one), (south_one, north_two) = halo(0), halo(1)
-                low = winds[0, here, :] * south_one
-                high = winds[1, here, :] * north_one
-                bottom = winds[2, here, :] * (7.0 * south_one - south_two)
-                top = winds[3, here, :] * (7.0 * north_one - north_two)
-                for r, more in enumerate((low + bottom, -low, high, -(top + high))):
-                    rows = pl.ds(nrows * SUB * b + r, SUB, stride=nrows)
-                    buffer[2 * p + h, rows, :] = part[2 * p + h, rows, :] + more
-        copy(p).start()
-    for p in range(pairs):
-        copy(p).wait()
+    def finish(south, north):
+        for p in range(pairs):
+            for h in range(2):
+                for b in range(levels // SUB):
+                    here = pl.ds(SUB * b, SUB)
+                    one, two = (pl.ds((2 * p + k) * LANES + levels * h + SUB * b, SUB) for k in range(2))
+                    more = [None] * nrows
+                    if south is not None:
+                        low = winds[0, here, :] * south[two, :]
+                        more[0] = low + winds[2, here, :] * (7.0 * south[two, :] - south[one, :])
+                        more[1] = -low
+                    if north is not None:
+                        high = winds[1, here, :] * north[one, :]
+                        more[2] = high
+                        more[3] = -(winds[3, here, :] * (7.0 * north[one, :] - north[two, :]) + high)
+                    for r in range(nrows):
+                        rows = pl.ds(nrows * SUB * b + r, SUB, stride=nrows)
+                        value = part[2 * p + h, rows, :]
+                        buffer[2 * p + h, rows, :] = value if more[r] is None else value + more[r]
+            copy(p).start()
+        for p in range(pairs):
+            copy(p).wait()
+
+    at, n = lax.axis_index("lat"), lax.axis_size("lat")
+    even, inner = is_even("lat"), jnp.logical_and(at > 0, at < n - 1)
+    pl.when(at == 0)(lambda: finish(None, ra))
+    pl.when(at == n - 1)(lambda: finish(ra, None))
+    pl.when(jnp.logical_and(inner, even))(lambda: finish(rb, ra))
+    pl.when(jnp.logical_and(inner, jnp.logical_not(even)))(lambda: finish(ra, rb))
 
 
 def radiation(

time: 30.4 us -> 30.4 us (level)
  no operation moved by 1% of the time
where the time goes in v11:
time: 30.4 us; the launch traced here: 30.2 us
  starting transfers between devices  14.1 us (46%)
  Pallas kernels  9.79 us (32%)
  waiting for transfers between devices  5.6 us (18%)
  between operations  0.69 us (2%)
    ppermute x4, starting transfers between devices, lat_swaps(): lax.ppermute(first_block, 'lat', [(j, j ^ 1) for j in range(nlat)])  11.4 us
    pallas_call x7, Pallas kernels, call(): pl.pallas_call(kernel, out_shape=out_shape, in_specs=specs, out_specs=out...  9.79 us
    ppermute x1, waiting for transfers between devices, lon_swaps(): lax.ppermute(second_block, 'lon', second)  2.29 us
    ppermute x4, waiting for transfers between devices, lat_swaps(): lax.ppermute(first_block, 'lat', [(j, j ^ 1) for j in range(nlat)])  2.22 us
    ppermute x1, starting transfers between devices, lon_swaps(): lax.ppermute(second_block, 'lon', second)  2.19 us
    ppermute x1, waiting for transfers between devices, lon_swaps(): lax.ppermute(first_block, 'lon', first)  1.08 us
  transfers between devices with their start and end apart: 10, of which 4 were waited for; matrix products, arithmetic and copies ran while one was open for 0% of the time, Pallas kernels for 25%

profile of v11, /device:TPU:0, one launch (start us, length us, event | category | flops | bytes accessed | tf_op | source)
XLA Modules:
  0.0 30.2 jit_solution(5773421714269094946)
XLA Ops:
  0.6 1.3 %pack_first.1 = (f32[8,128,128]{2,1,0:T(8,128)S(1)}, f32[576,128]{1,0:T(8,128)S(1)}, f32[576,128]{1,0:T(8,128)S(1)}, f32[4,256,128]{2,1,0:T(8,128)S(1)}, f32[4,2...) custom-call(f32[8,256,128]{2,1,0:T(8,128)} %bitcast.6, f32[2,256,128]{2,1,0:T(8,128)} %bitcast.7), custom_call_target="tpu_custom_call" | custom-call | flops 1000 | bytes 1000 | tf_op jit(solution)/shard_map/pack_first/pallas_call | solution.py:572
  1.9 3.1 %collective-permute-start.2 = (f32[576,128]{1,0:T(8,128)S(1)}, f32[576,128]{1,0:T(8,128)S(1)}, u32[]{:S(2)}, u32[]{:S(2)}) collective-permute-start(f32[576,128]{1,0:T(8,128)S(1)} %get-tuple-element.34), channel_id=1, source_target_pairs={{0,1},{1,0},{2,3},{3,2},{4,5},{5,4},{6,7},{7,6},{8,9},{9,8},{10,11... | collective-permute-start | bytes 884744 | tf_op jit(solution)/shard_map/ppermute | solution.py:44
  5.0 0.4 %pack_middle.1 = (f32[8,128,128]{2,1,0:T(8,128)S(1)}, f32[4,128,128]{2,1,0:T(8,128)S(1)}, f32[4,128,128]{2,1,0:T(8,128)S(1)}, f32[80,128]{1,0:T(8,128)S(1)}, f32...) custom-call(f32[4,256,128]{2,1,0:T(8,128)S(1)} %get-tuple-element.28.nat, ...), custom_call_target="tpu_custom_call" | custom-call | flops 1000 | bytes 1000 | tf_op jit(solution)/shard_map/pack_middle/pallas_call | solution.py:572
  5.4 3.2 %collective-permute-start.6 = (f32[512,128]{1,0:T(8,128)S(1)}, f32[512,128]{1,0:T(8,128)S(1)}, u32[]{:S(2)}, u32[]{:S(2)}) collective-permute-start(f32[512,128]{1,0:T(8,128)S(1)} %get-tuple-element.43), channel_id=1, source_target_pairs={{0,1},{1,0},{2,3},{3,2},{4,5},{5,4},{6,7},{7,6},{8,9},{9,8},{10,11... | collective-permute-start | bytes 786440 | tf_op jit(solution)/shard_map/ppermute | solution.py:44
  8.6 0.0 collective-permute-start.7
  8.6 0.5 %collective-permute-start = (f32[80,128]{1,0:T(8,128)S(1)}, f32[80,128]{1,0:T(8,128)S(1)}, u32[]{:S(2)}, u32[]{:S(2)}) collective-permute-start(f32[80,128]{1,0:T(8,128)S(1)} %get-tuple-element.32), channel_id=1, source_target_pairs={{0,4},{4,0},{8,12},{12,8},{16,20},{20,16},{24,28},{28,24},{1,5},{5... | collective-permute-start | bytes 122888 | tf_op jit(solution)/shard_map/ppermute | solution.py:32
  9.1 1.1 %collective-permute-done.la = f32[80,128]{1,0:T(8,128)S(1)} collective-permute-done((f32[80,128]{1,0:T(8,128)S(1)}, f32[80,128]{1,0:T(8,128)S(1)}, u32[]{:S(2)}, u32[]{:S(2)}) %collective-permute-start) | collective-permute-done | bytes 40992 | tf_op jit(solution)/shard_map/ppermute | solution.py:32
  10.2 2.2 %collective-permute-start.1 = (f32[80,128]{1,0:T(8,128)S(1)}, f32[80,128]{1,0:T(8,128)S(1)}, u32[]{:S(2)}, u32[]{:S(2)}) collective-permute-start(f32[80,128]{1,0:T(8,128)S(1)} %get-tuple-element.33), channel_id=1, source_target_pairs={{0,28},{4,8},{8,4},{12,16},{16,12},{20,24},{24,20},{28,0},{1,29},{... | collective-permute-start | bytes 122888 | tf_op jit(solution)/shard_map/ppermute | solution.py:32
  12.4 2.3 %collective-permute-done.1.lb = f32[80,128]{1,0:T(8,128)S(1)} collective-permute-done((f32[80,128]{1,0:T(8,128)S(1)}, f32[80,128]{1,0:T(8,128)S(1)}, u32[]{:S(2)}, u32[]{:S(2)}) %collective-permute-start.1) | collective-permute-done | bytes 40992 | tf_op jit(solution)/shard_map/ppermute | solution.py:32
  14.7 0.0 collective-permute-done.2.ra
  14.7 0.0 collective-permute-done.3.rb
  14.7 0.6 %first_stage_early.1 = (f32[8,128,128]{2,1,0:T(8,128)S(1)}, f32[552,128]{1,0:T(8,128)S(1)}, f32[552,128]{1,0:T(8,128)S(1)}, f32[128,128]{1,0:T(8,128)S(1)}, f32[192,128]{1,0:T(8,128)S(1)}) custom-call(f32[8,128,128]{2,1,0:T(8,128)S(1)} %get-tuple-element.27.tiles_first.q, f32[4,128,128]{2,1,0:T(8,128)S(1)} %get-tuple-element.30.ce, ...), custom_call_target="tpu_custom_call" | custom-call | flops 1000000000 | bytes 1000000000 | tf_op jit(solution)/shard_map/first_stage_early/pallas_call | solution.py:572
  15.3 1.4 %collective-permute-start.4 = (f32[552,128]{1,0:T(8,128)S(1)}, f32[552,128]{1,0:T(8,128)S(1)}, u32[]{:S(2)}, u32[]{:S(2)}) collective-permute-start(f32[552,128]{1,0:T(8,128)S(1)} %get-tuple-element.38), channel_id=1, source_target_pairs={{0,1},{1,0},{2,3},{3,2},{4,5},{5,4},{6,7},{7,6},{8,9},{9,8},{10,11... | collective-permute-start | bytes 847880 | tf_op jit(solution)/shard_map/ppermute | solution.py:44
  16.7 0.0 collective-permute-start.5
  16.7 1.4 %collective-permute-done.6.ra = f32[512,128]{1,0:T(8,128)S(1)} collective-permute-done((f32[512,128]{1,0:T(8,128)S(1)}, f32[512,128]{1,0:T(8,128)S(1)}, u32[]{:S(2)}, u32[]{:S(2)}) %collective-permute-start.6) | collective-permute-done | bytes 262176 | tf_op jit(solution)/shard_map/ppermute | solution.py:44
  18.1 0.0 collective-permute-done.7.rb
  18.1 0.6 %first_stage_late.1 = (f32[8,128,128]{2,1,0:T(8,128)S(1)}, f32[512,128]{1,0:T(8,128)S(1)}, f32[512,128]{1,0:T(8,128)S(1)}) custom-call(f32[8,128,128]{2,1,0:T(8,128)S(1)} %get-tuple-element.42.q.q_late, f32[4,128,128]{2,1,0:T(8,128)S(1)} %get-tuple-element.30.ce, f32[4,128,128]{2,1,0:T(8,128)S(1)} %get-tuple-element.31.cn, ...), custom_call_target="tpu_custom_call" | custom-call | flops 12000000 | bytes 12000000 | tf_op jit(solution)/shard_map/first_stage_late/pallas_call | solution.py:572
  18.7 3.7 %collective-permute-start.8 = (f32[512,128]{1,0:T(8,128)S(1)}, f32[512,128]{1,0:T(8,128)S(1)}, u32[]{:S(2)}, u32[]{:S(2)}) collective-permute-start(f32[512,128]{1,0:T(8,128)S(1)} %get-tuple-element.48), channel_id=1, source_target_pairs={{0,1},{1,0},{2,3},{3,2},{4,5},{5,4},{6,7},{7,6},{8,9},{9,8},{10,11... | collective-permute-start | bytes 786440 | tf_op jit(solution)/shard_map/ppermute | solution.py:44
  22.4 0.0 collective-permute-start.9
  22.4 4.5 %radiation.1.heating = f32[256,128]{1,0:T(8,128)S(1)} custom-call(f32[4,256,128]{2,1,0:T(8,128)S(1)} %get-tuple-element.41.nat, f32[4,128]{1,0:T(4,128)} %cosz_in.1, f32[4,128]{1,0:T(4,128)} %albedo_in.1, f32[14]{0:T(128)} %ext_in.1, f32[14]{0:T(128)} %single_in.1, f32[14]{0:T(128)} %weight_in.1, s32[4,1,128]{2,1,0:T(1,128)} %order_in.1, s32[4]{0:T(128)} %bitcast.8, ...), custom_call_target="tpu_custom_call" | custom-call | flops 16000000 | bytes 16000000 | tf_op jit(solution)/shard_map/radiation/pallas_call | solution.py:572
  26.9 0.0 collective-permute-done.4.ra
  26.9 1.5 %second_stage_early.1 = (f32[8,256,128]{2,1,0:T(8,128)}, f32[256,128]{1,0:T(8,128)}, f32[4,256,128]{2,1,0:T(8,128)S(1)}, f32[4,64,128]{2,1,0:T(8,128)S(1)}) custom-call(f32[8,128,128]{2,1,0:T(8,128)S(1)} %get-tuple-element.27.tiles_first.q, f32[8,128,128]{2,1,0:T(8,128)S(1)} %get-tuple-element.36.s, f32[4,128,128]{2,1,0:T(8,128)S(1)} %get-tuple-element.30.ce, ...), custom_call_target="tpu_custom_call" | custom-call | flops 1000 | bytes 1000 | tf_op jit(solution)/shard_map/second_stage_early/pallas_call | solution.py:572
  28.5 0.9 %collective-permute-done.8.ra = f32[512,128]{1,0:T(8,128)S(1)} collective-permute-done((f32[512,128]{1,0:T(8,128)S(1)}, f32[512,128]{1,0:T(8,128)S(1)}, u32[]{:S(2)}, u32[]{:S(2)}) %collective-permute-start.8) | collective-permute-done | bytes 262176 | tf_op jit(solution)/shard_map/ppermute | solution.py:44
  29.3 0.8 %second_stage_late.1 = f32[8,256,128]{2,1,0:T(8,128)} custom-call(f32[4,256,128]{2,1,0:T(8,128)S(1)} %get-tuple-element.46.part, f32[4,64,128]{2,1,0:T(8,128)S(1)} %get-tuple-element.47.winds, f32[512,128]{1,0:T(8,128)S(1)} %collective-permute-done.8.ra, f32[512,128]{1,0:T(8,128)S(1)} %collective-permute-done.9.rb, ...), custom_call_target="tpu_custom_call", output_to_operand_aliasing={{}: (4, {})} | custom-call | flops 1000 | bytes 1000 | tf_op jit(solution)/shard_map/second_stage_late/pallas_call | solution.py:572
  (3 shorter events, 0.0 us)
Async XLA Ops:
  1.9 12.8 %collective-permute-start.2 = (f32[576,128]{1,0:T(8,128)S(1)}, f32[576,128]{1,0:T(8,128)S(1)}, u32[]{:S(2)}, u32[]{:S(2)}) collective-permute-start(f32[576,128]{1,0:T(8,128)S(1)} %get-tuple-element.34), channel_id=1, source_target_pairs={{0,1},{1,0},{2,3},{3,2},{4,5},{5,4},{6,7},{7,6},{8,9},{9,8},{10,11... | collective-permute-start | bytes 884744 | tf_op jit(solution)/shard_map/ppermute | solution.py:44
  5.0 9.7 %collective-permute-start.3 = (f32[576,128]{1,0:T(8,128)S(1)}, f32[576,128]{1,0:T(8,128)S(1)}, u32[]{:S(2)}, u32[]{:S(2)}) collective-permute-start(f32[576,128]{1,0:T(8,128)S(1)} %get-tuple-element.35), channel_id=1, source_target_pairs={{0,4},{1,2},{2,1},{3,7},{4,0},{5,6},{6,5},{7,3},{8,12},{9,10},{10,... | collective-permute-start | bytes 884744 | tf_op jit(solution)/shard_map/ppermute | solution.py:43
  5.4 12.6 %collective-permute-start.6 = (f32[512,128]{1,0:T(8,128)S(1)}, f32[512,128]{1,0:T(8,128)S(1)}, u32[]{:S(2)}, u32[]{:S(2)}) collective-permute-start(f32[512,128]{1,0:T(8,128)S(1)} %get-tuple-element.43), channel_id=1, source_target_pairs={{0,1},{1,0},{2,3},{3,2},{4,5},{5,4},{6,7},{7,6},{8,9},{9,8},{10,11... | collective-permute-start | bytes 786440 | tf_op jit(solution)/shard_map/ppermute | solution.py:44
  8.6 9.4 %collective-permute-start.7 = (f32[512,128]{1,0:T(8,128)S(1)}, f32[512,128]{1,0:T(8,128)S(1)}, u32[]{:S(2)}, u32[]{:S(2)}) collective-permute-start(f32[512,128]{1,0:T(8,128)S(1)} %get-tuple-element.44), channel_id=1, source_target_pairs={{0,4},{1,2},{2,1},{3,7},{4,0},{5,6},{6,5},{7,3},{8,12},{9,10},{10,... | collective-permute-start | bytes 786440 | tf_op jit(solution)/shard_map/ppermute | solution.py:43
  8.6 1.6 %collective-permute-start = (f32[80,128]{1,0:T(8,128)S(1)}, f32[80,128]{1,0:T(8,128)S(1)}, u32[]{:S(2)}, u32[]{:S(2)}) collective-permute-start(f32[80,128]{1,0:T(8,128)S(1)} %get-tuple-element.32), channel_id=1, source_target_pairs={{0,4},{4,0},{8,12},{12,8},{16,20},{20,16},{24,28},{28,24},{1,5},{5... | collective-permute-start | bytes 122888 | tf_op jit(solution)/shard_map/ppermute | solution.py:32
  10.2 4.5 %collective-permute-start.1 = (f32[80,128]{1,0:T(8,128)S(1)}, f32[80,128]{1,0:T(8,128)S(1)}, u32[]{:S(2)}, u32[]{:S(2)}) collective-permute-start(f32[80,128]{1,0:T(8,128)S(1)} %get-tuple-element.33), channel_id=1, source_target_pairs={{0,28},{4,8},{8,4},{12,16},{16,12},{20,24},{24,20},{28,0},{1,29},{... | collective-permute-start | bytes 122888 | tf_op jit(solution)/shard_map/ppermute | solution.py:32
  15.3 11.6 %collective-permute-start.4 = (f32[552,128]{1,0:T(8,128)S(1)}, f32[552,128]{1,0:T(8,128)S(1)}, u32[]{:S(2)}, u32[]{:S(2)}) collective-permute-start(f32[552,128]{1,0:T(8,128)S(1)} %get-tuple-element.38), channel_id=1, source_target_pairs={{0,1},{1,0},{2,3},{3,2},{4,5},{5,4},{6,7},{7,6},{8,9},{9,8},{10,11... | collective-permute-start | bytes 847880 | tf_op jit(solution)/shard_map/ppermute | solution.py:44
  16.7 10.2 %collective-permute-start.5 = (f32[552,128]{1,0:T(8,128)S(1)}, f32[552,128]{1,0:T(8,128)S(1)}, u32[]{:S(2)}, u32[]{:S(2)}) collective-permute-start(f32[552,128]{1,0:T(8,128)S(1)} %get-tuple-element.39), channel_id=1, source_target_pairs={{0,4},{1,2},{2,1},{3,7},{4,0},{5,6},{6,5},{7,3},{8,12},{9,10},{10,... | collective-permute-start | bytes 847880 | tf_op jit(solution)/shard_map/ppermute | solution.py:43
  18.7 10.6 %collective-permute-start.8 = (f32[512,128]{1,0:T(8,128)S(1)}, f32[512,128]{1,0:T(8,128)S(1)}, u32[]{:S(2)}, u32[]{:S(2)}) collective-permute-start(f32[512,128]{1,0:T(8,128)S(1)} %get-tuple-element.48), channel_id=1, source_target_pairs={{0,1},{1,0},{2,3},{3,2},{4,5},{5,4},{6,7},{7,6},{8,9},{9,8},{10,11... | collective-permute-start | bytes 786440 | tf_op jit(solution)/shard_map/ppermute | solution.py:44
  22.4 7.0 %collective-permute-start.9 = (f32[512,128]{1,0:T(8,128)S(1)}, f32[512,128]{1,0:T(8,128)S(1)}, u32[]{:S(2)}, u32[]{:S(2)}) collective-permute-start(f32[512,128]{1,0:T(8,128)S(1)} %get-tuple-element.49), channel_id=1, source_target_pairs={{0,4},{1,2},{2,1},{3,7},{4,0},{5,6},{6,5},{7,3},{8,12},{9,10},{10,... | collective-permute-start | bytes 786440 | tf_op jit(solution)/shard_map/ppermute | solution.py:43

commit v12 on v11

--- a/solution.py
+++ b/solution.py
@@ -424,10 +424,8 @@
     del before
     levels = LANES // 2
 
-    def copy(p):
-        return pltpu.make_async_copy(
-            buffer.at[pl.ds(2 * p, 2)], out.at[pl.ds(2 * (done + p), 2)], sems.at[p]
-        )
+    def copy(i):
+        return pltpu.make_async_copy(buffer.at[i], out.at[2 * done + i], sems.at[i])
 
     def finish(south, north):
         for p in range(pairs):
@@ -448,9 +446,9 @@
                         rows = pl.ds(nrows * SUB * b + r, SUB, stride=nrows)
                         value = part[2 * p + h, rows, :]
                         buffer[2 * p + h, rows, :] = value if more[r] is None else value + more[r]
-            copy(p).start()
-        for p in range(pairs):
-            copy(p).wait()
+                copy(2 * p + h).start()
+        for i in range(2 * pairs):
+            copy(i).wait()
 
     at, n = lax.axis_index("lat"), lax.axis_size("lat")
     even, inner = is_even("lat"), jnp.logical_and(at > 0, at < n - 1)
@@ -694,7 +692,7 @@
         [VMEM] * 4 + [HBM],
         HBM,
         (part, half_winds, *lat3, out),
-        [scratch(2 * late, levels * nrows, ncols), pltpu.SemaphoreType.DMA((late,))],
+        [scratch(2 * late, levels * nrows, ncols), pltpu.SemaphoreType.DMA((2 * late,))],
         input_output_aliases={4: 0},
     )
     return out.reshape(fields.shape), heat_out.reshape(levels, nrows, ncols)

time: 30.4 us -> 30.4 us (level)
  no operation moved by 1% of the time
where the time goes in v12:
time: 30.4 us; the launch traced here: 30.2 us
  starting transfers between devices  14.1 us (46%)
  Pallas kernels  9.79 us (32%)
  waiting for transfers between devices  5.6 us (18%)
  between operations  0.69 us (2%)
    ppermute x4, starting transfers between devices, lat_swaps(): lax.ppermute(first_block, 'lat', [(j, j ^ 1) for j in range(nlat)])  11.4 us
    pallas_call x7, Pallas kernels, call(): pl.pallas_call(kernel, out_shape=out_shape, in_specs=specs, out_specs=out...  9.79 us
    ppermute x1, waiting for transfers between devices, lon_swaps(): lax.ppermute(second_block, 'lon', second)  2.29 us
    ppermute x4, waiting for transfers between devices, lat_swaps(): lax.ppermute(first_block, 'lat', [(j, j ^ 1) for j in range(nlat)])  2.22 us
    ppermute x1, starting transfers between devices, lon_swaps(): lax.ppermute(second_block, 'lon', second)  2.19 us
    ppermute x1, waiting for transfers between devices, lon_swaps(): lax.ppermute(first_block, 'lon', first)  1.08 us
  transfers between devices with their start and end apart: 10, of which 4 were waited for; matrix products, arithmetic and copies ran while one was open for 0% of the time, Pallas kernels for 25%

profile of v12, /device:TPU:0, one launch (start us, length us, event | category | flops | bytes accessed | tf_op | source)
XLA Modules:
  0.0 30.2 jit_solution(17834095652906216006)
XLA Ops:
  0.6 1.3 %pack_first.1 = (f32[8,128,128]{2,1,0:T(8,128)S(1)}, f32[576,128]{1,0:T(8,128)S(1)}, f32[576,128]{1,0:T(8,128)S(1)}, f32[4,256,128]{2,1,0:T(8,128)S(1)}, f32[4,2...) custom-call(f32[8,256,128]{2,1,0:T(8,128)} %bitcast.6, f32[2,256,128]{2,1,0:T(8,128)} %bitcast.7), custom_call_target="tpu_custom_call" | custom-call | flops 1000 | bytes 1000 | tf_op jit(solution)/shard_map/pack_first/pallas_call | solution.py:570
  1.9 3.1 %collective-permute-start.2 = (f32[576,128]{1,0:T(8,128)S(1)}, f32[576,128]{1,0:T(8,128)S(1)}, u32[]{:S(2)}, u32[]{:S(2)}) collective-permute-start(f32[576,128]{1,0:T(8,128)S(1)} %get-tuple-element.34), channel_id=1, source_target_pairs={{0,1},{1,0},{2,3},{3,2},{4,5},{5,4},{6,7},{7,6},{8,9},{9,8},{10,11... | collective-permute-start | bytes 884744 | tf_op jit(solution)/shard_map/ppermute | solution.py:44
  5.0 0.0 collective-permute-start.3
  5.0 0.4 %pack_middle.1 = (f32[8,128,128]{2,1,0:T(8,128)S(1)}, f32[4,128,128]{2,1,0:T(8,128)S(1)}, f32[4,128,128]{2,1,0:T(8,128)S(1)}, f32[80,128]{1,0:T(8,128)S(1)}, f32...) custom-call(f32[4,256,128]{2,1,0:T(8,128)S(1)} %get-tuple-element.28.nat, ...), custom_call_target="tpu_custom_call" | custom-call | flops 1000 | bytes 1000 | tf_op jit(solution)/shard_map/pack_middle/pallas_call | solution.py:570
  5.4 3.2 %collective-permute-start.6 = (f32[512,128]{1,0:T(8,128)S(1)}, f32[512,128]{1,0:T(8,128)S(1)}, u32[]{:S(2)}, u32[]{:S(2)}) collective-permute-start(f32[512,128]{1,0:T(8,128)S(1)} %get-tuple-element.43), channel_id=1, source_target_pairs={{0,1},{1,0},{2,3},{3,2},{4,5},{5,4},{6,7},{7,6},{8,9},{9,8},{10,11... | collective-permute-start | bytes 786440 | tf_op jit(solution)/shard_map/ppermute | solution.py:44
  8.6 0.0 collective-permute-start.7
  8.6 0.5 %collective-permute-start = (f32[80,128]{1,0:T(8,128)S(1)}, f32[80,128]{1,0:T(8,128)S(1)}, u32[]{:S(2)}, u32[]{:S(2)}) collective-permute-start(f32[80,128]{1,0:T(8,128)S(1)} %get-tuple-element.32), channel_id=1, source_target_pairs={{0,4},{4,0},{8,12},{12,8},{16,20},{20,16},{24,28},{28,24},{1,5},{5... | collective-permute-start | bytes 122888 | tf_op jit(solution)/shard_map/ppermute | solution.py:32
  9.1 1.1 %collective-permute-done.la = f32[80,128]{1,0:T(8,128)S(1)} collective-permute-done((f32[80,128]{1,0:T(8,128)S(1)}, f32[80,128]{1,0:T(8,128)S(1)}, u32[]{:S(2)}, u32[]{:S(2)}) %collective-permute-start) | collective-permute-done | bytes 40992 | tf_op jit(solution)/shard_map/ppermute | solution.py:32
  10.2 2.2 %collective-permute-start.1 = (f32[80,128]{1,0:T(8,128)S(1)}, f32[80,128]{1,0:T(8,128)S(1)}, u32[]{:S(2)}, u32[]{:S(2)}) collective-permute-start(f32[80,128]{1,0:T(8,128)S(1)} %get-tuple-element.33), channel_id=1, source_target_pairs={{0,28},{4,8},{8,4},{12,16},{16,12},{20,24},{24,20},{28,0},{1,29},{... | collective-permute-start | bytes 122888 | tf_op jit(solution)/shard_map/ppermute | solution.py:32
  12.4 2.3 %collective-permute-done.1.lb = f32[80,128]{1,0:T(8,128)S(1)} collective-permute-done((f32[80,128]{1,0:T(8,128)S(1)}, f32[80,128]{1,0:T(8,128)S(1)}, u32[]{:S(2)}, u32[]{:S(2)}) %collective-permute-start.1) | collective-permute-done | bytes 40992 | tf_op jit(solution)/shard_map/ppermute | solution.py:32
  14.7 0.0 collective-permute-done.2.ra
  14.7 0.0 collective-permute-done.3.rb
  14.7 0.6 %first_stage_early.1 = (f32[8,128,128]{2,1,0:T(8,128)S(1)}, f32[552,128]{1,0:T(8,128)S(1)}, f32[552,128]{1,0:T(8,128)S(1)}, f32[128,128]{1,0:T(8,128)S(1)}, f32[192,128]{1,0:T(8,128)S(1)}) custom-call(f32[8,128,128]{2,1,0:T(8,128)S(1)} %get-tuple-element.27.tiles_first.q, f32[4,128,128]{2,1,0:T(8,128)S(1)} %get-tuple-element.30.ce, ...), custom_call_target="tpu_custom_call" | custom-call | flops 1000000000 | bytes 1000000000 | tf_op jit(solution)/shard_map/first_stage_early/pallas_call | solution.py:570
  15.3 1.4 %collective-permute-start.4 = (f32[552,128]{1,0:T(8,128)S(1)}, f32[552,128]{1,0:T(8,128)S(1)}, u32[]{:S(2)}, u32[]{:S(2)}) collective-permute-start(f32[552,128]{1,0:T(8,128)S(1)} %get-tuple-element.38), channel_id=1, source_target_pairs={{0,1},{1,0},{2,3},{3,2},{4,5},{5,4},{6,7},{7,6},{8,9},{9,8},{10,11... | collective-permute-start | bytes 847880 | tf_op jit(solution)/shard_map/ppermute | solution.py:44
  16.7 0.0 collective-permute-start.5
  16.7 1.4 %collective-permute-done.6.ra = f32[512,128]{1,0:T(8,128)S(1)} collective-permute-done((f32[512,128]{1,0:T(8,128)S(1)}, f32[512,128]{1,0:T(8,128)S(1)}, u32[]{:S(2)}, u32[]{:S(2)}) %collective-permute-start.6) | collective-permute-done | bytes 262176 | tf_op jit(solution)/shard_map/ppermute | solution.py:44
  18.1 0.6 %first_stage_late.1 = (f32[8,128,128]{2,1,0:T(8,128)S(1)}, f32[512,128]{1,0:T(8,128)S(1)}, f32[512,128]{1,0:T(8,128)S(1)}) custom-call(f32[8,128,128]{2,1,0:T(8,128)S(1)} %get-tuple-element.42.q.q_late, f32[4,128,128]{2,1,0:T(8,128)S(1)} %get-tuple-element.30.ce, f32[4,128,128]{2,1,0:T(8,128)S(1)} %get-tuple-element.31.cn, ...), custom_call_target="tpu_custom_call" | custom-call | flops 12000000 | bytes 12000000 | tf_op jit(solution)/shard_map/first_stage_late/pallas_call | solution.py:570
  18.7 3.7 %collective-permute-start.8 = (f32[512,128]{1,0:T(8,128)S(1)}, f32[512,128]{1,0:T(8,128)S(1)}, u32[]{:S(2)}, u32[]{:S(2)}) collective-permute-start(f32[512,128]{1,0:T(8,128)S(1)} %get-tuple-element.48), channel_id=1, source_target_pairs={{0,1},{1,0},{2,3},{3,2},{4,5},{5,4},{6,7},{7,6},{8,9},{9,8},{10,11... | collective-permute-start | bytes 786440 | tf_op jit(solution)/shard_map/ppermute | solution.py:44
  22.4 4.5 %radiation.1.heating = f32[256,128]{1,0:T(8,128)S(1)} custom-call(f32[4,256,128]{2,1,0:T(8,128)S(1)} %get-tuple-element.41.nat, f32[4,128]{1,0:T(4,128)} %cosz_in.1, f32[4,128]{1,0:T(4,128)} %albedo_in.1, f32[14]{0:T(128)} %ext_in.1, f32[14]{0:T(128)} %single_in.1, f32[14]{0:T(128)} %weight_in.1, s32[4,1,128]{2,1,0:T(1,128)} %order_in.1, s32[4]{0:T(128)} %bitcast.8, ...), custom_call_target="tpu_custom_call" | custom-call | flops 16000000 | bytes 16000000 | tf_op jit(solution)/shard_map/radiation/pallas_call | solution.py:570
  26.9 0.0 collective-permute-done.4.ra
  26.9 1.5 %second_stage_early.1 = (f32[8,256,128]{2,1,0:T(8,128)}, f32[256,128]{1,0:T(8,128)}, f32[4,256,128]{2,1,0:T(8,128)S(1)}, f32[4,64,128]{2,1,0:T(8,128)S(1)}) custom-call(f32[8,128,128]{2,1,0:T(8,128)S(1)} %get-tuple-element.27.tiles_first.q, f32[8,128,128]{2,1,0:T(8,128)S(1)} %get-tuple-element.36.s, f32[4,128,128]{2,1,0:T(8,128)S(1)} %get-tuple-element.30.ce, ...), custom_call_target="tpu_custom_call" | custom-call | flops 1000 | bytes 1000 | tf_op jit(solution)/shard_map/second_stage_early/pallas_call | solution.py:570
  28.5 0.9 %collective-permute-done.8.ra = f32[512,128]{1,0:T(8,128)S(1)} collective-permute-done((f32[512,128]{1,0:T(8,128)S(1)}, f32[512,128]{1,0:T(8,128)S(1)}, u32[]{:S(2)}, u32[]{:S(2)}) %collective-permute-start.8) | collective-permute-done | bytes 262176 | tf_op jit(solution)/shard_map/ppermute | solution.py:44
  29.3 0.0 collective-permute-done.9.rb
  29.3 0.8 %second_stage_late.1 = f32[8,256,128]{2,1,0:T(8,128)} custom-call(f32[4,256,128]{2,1,0:T(8,128)S(1)} %get-tuple-element.46.part, f32[4,64,128]{2,1,0:T(8,128)S(1)} %get-tuple-element.47.winds, f32[512,128]{1,0:T(8,128)S(1)} %collective-permute-done.8.ra, f32[512,128]{1,0:T(8,128)S(1)} %collective-permute-done.9.rb, ...), custom_call_target="tpu_custom_call", output_to_operand_aliasing={{}: (4, {})} | custom-call | flops 1000 | bytes 1000 | tf_op jit(solution)/shard_map/second_stage_late/pallas_call | solution.py:570
  (3 shorter events, 0.0 us)
Async XLA Ops:
  1.9 12.8 %collective-permute-start.2 = (f32[576,128]{1,0:T(8,128)S(1)}, f32[576,128]{1,0:T(8,128)S(1)}, u32[]{:S(2)}, u32[]{:S(2)}) collective-permute-start(f32[576,128]{1,0:T(8,128)S(1)} %get-tuple-element.34), channel_id=1, source_target_pairs={{0,1},{1,0},{2,3},{3,2},{4,5},{5,4},{6,7},{7,6},{8,9},{9,8},{10,11... | collective-permute-start | bytes 884744 | tf_op jit(solution)/shard_map/ppermute | solution.py:44
  5.0 9.7 %collective-permute-start.3 = (f32[576,128]{1,0:T(8,128)S(1)}, f32[576,128]{1,0:T(8,128)S(1)}, u32[]{:S(2)}, u32[]{:S(2)}) collective-permute-start(f32[576,128]{1,0:T(8,128)S(1)} %get-tuple-element.35), channel_id=1, source_target_pairs={{0,4},{1,2},{2,1},{3,7},{4,0},{5,6},{6,5},{7,3},{8,12},{9,10},{10,... | collective-permute-start | bytes 884744 | tf_op jit(solution)/shard_map/ppermute | solution.py:43
  5.4 12.6 %collective-permute-start.6 = (f32[512,128]{1,0:T(8,128)S(1)}, f32[512,128]{1,0:T(8,128)S(1)}, u32[]{:S(2)}, u32[]{:S(2)}) collective-permute-start(f32[512,128]{1,0:T(8,128)S(1)} %get-tuple-element.43), channel_id=1, source_target_pairs={{0,1},{1,0},{2,3},{3,2},{4,5},{5,4},{6,7},{7,6},{8,9},{9,8},{10,11... | collective-permute-start | bytes 786440 | tf_op jit(solution)/shard_map/ppermute | solution.py:44
  8.6 9.4 %collective-permute-start.7 = (f32[512,128]{1,0:T(8,128)S(1)}, f32[512,128]{1,0:T(8,128)S(1)}, u32[]{:S(2)}, u32[]{:S(2)}) collective-permute-start(f32[512,128]{1,0:T(8,128)S(1)} %get-tuple-element.44), channel_id=1, source_target_pairs={{0,4},{1,2},{2,1},{3,7},{4,0},{5,6},{6,5},{7,3},{8,12},{9,10},{10,... | collective-permute-start | bytes 786440 | tf_op jit(solution)/shard_map/ppermute | solution.py:43
  8.6 1.6 %collective-permute-start = (f32[80,128]{1,0:T(8,128)S(1)}, f32[80,128]{1,0:T(8,128)S(1)}, u32[]{:S(2)}, u32[]{:S(2)}) collective-permute-start(f32[80,128]{1,0:T(8,128)S(1)} %get-tuple-element.32), channel_id=1, source_target_pairs={{0,4},{4,0},{8,12},{12,8},{16,20},{20,16},{24,28},{28,24},{1,5},{5... | collective-permute-start | bytes 122888 | tf_op jit(solution)/shard_map/ppermute | solution.py:32
  10.2 4.5 %collective-permute-start.1 = (f32[80,128]{1,0:T(8,128)S(1)}, f32[80,128]{1,0:T(8,128)S(1)}, u32[]{:S(2)}, u32[]{:S(2)}) collective-permute-start(f32[80,128]{1,0:T(8,128)S(1)} %get-tuple-element.33), channel_id=1, source_target_pairs={{0,28},{4,8},{8,4},{12,16},{16,12},{20,24},{24,20},{28,0},{1,29},{... | collective-permute-start | bytes 122888 | tf_op jit(solution)/shard_map/ppermute | solution.py:32
  15.3 11.6 %collective-permute-start.4 = (f32[552,128]{1,0:T(8,128)S(1)}, f32[552,128]{1,0:T(8,128)S(1)}, u32[]{:S(2)}, u32[]{:S(2)}) collective-permute-start(f32[552,128]{1,0:T(8,128)S(1)} %get-tuple-element.38), channel_id=1, source_target_pairs={{0,1},{1,0},{2,3},{3,2},{4,5},{5,4},{6,7},{7,6},{8,9},{9,8},{10,11... | collective-permute-start | bytes 847880 | tf_op jit(solution)/shard_map/ppermute | solution.py:44
  16.7 10.2 %collective-permute-start.5 = (f32[552,128]{1,0:T(8,128)S(1)}, f32[552,128]{1,0:T(8,128)S(1)}, u32[]{:S(2)}, u32[]{:S(2)}) collective-permute-start(f32[552,128]{1,0:T(8,128)S(1)} %get-tuple-element.39), channel_id=1, source_target_pairs={{0,4},{1,2},{2,1},{3,7},{4,0},{5,6},{6,5},{7,3},{8,12},{9,10},{10,... | collective-permute-start | bytes 847880 | tf_op jit(solution)/shard_map/ppermute | solution.py:43
  18.7 10.6 %collective-permute-start.8 = (f32[512,128]{1,0:T(8,128)S(1)}, f32[512,128]{1,0:T(8,128)S(1)}, u32[]{:S(2)}, u32[]{:S(2)}) collective-permute-start(f32[512,128]{1,0:T(8,128)S(1)} %get-tuple-element.48), channel_id=1, source_target_pairs={{0,1},{1,0},{2,3},{3,2},{4,5},{5,4},{6,7},{7,6},{8,9},{9,8},{10,11... | collective-permute-start | bytes 786440 | tf_op jit(solution)/shard_map/ppermute | solution.py:44
  22.4 7.0 %collective-permute-start.9 = (f32[512,128]{1,0:T(8,128)S(1)}, f32[512,128]{1,0:T(8,128)S(1)}, u32[]{:S(2)}, u32[]{:S(2)}) collective-permute-start(f32[512,128]{1,0:T(8,128)S(1)} %get-tuple-element.49), channel_id=1, source_target_pairs={{0,4},{1,2},{2,1},{3,7},{4,0},{5,6},{6,5},{7,3},{8,12},{9,10},{10,... | collective-permute-start | bytes 786440 | tf_op jit(solution)/shard_map/ppermute | solution.py:43

commit v13 on v12

--- a/solution.py
+++ b/solution.py
@@ -82,7 +82,7 @@
     return jnp.where(head, tile[pl.ds(0, SUB), :], tile[pl.ds(LANES - SUB, SUB), :])
 
 
-def pack_first(pairs, nrows, fields, courant, tiles, za, zb, nat, nat_late, nat_wind, sems):
+def pack_first(pairs, nrows, fields, courant, za, zb, nat, nat_late, nat_wind, sems):
     n = 2 * pairs
     first = [
         pltpu.make_async_copy(fields.at[pl.ds(2 * p, 2)], nat.at[pl.ds(2 * p, 2)], sems.at[p]) for p in range(pairs)
@@ -97,15 +97,12 @@
 
     def body(p, up, down):
         for r in range(nrows):
-            tile = tile_of(native(nat, 2 * p, r, nrows), native(nat, 2 * p + 1, r, nrows))
-            tiles[nrows * p + r] = tile
-            (up if r >= 2 else down)[pl.ds((2 * p + r % 2) * LANES, LANES), :] = tile
+            for h in range(2):
+                span = pl.ds((2 * p + r % 2) * LANES + half * h, half)
+                (up if r >= 2 else down)[span, :] = native(nat, 2 * p + h, r, nrows)
         if p < pairs - 1:
             return
-        lane = lax.broadcasted_iota(jnp.int32, (half, LANES), 1)
         top = native(nat_wind, 1, nrows - 1, nrows) * (1.0 / 12.0)
-        top = tile_of(top, top)
-        top = jnp.where(lane < half, top[:half], top[half:])
         for ref in (up, down):
             ref[pl.ds(2 * pairs * LANES, half), :] = top
 
@@ -119,11 +116,12 @@
     east.wait()
 
 
-def pack_middle(pairs, nrows, nat, nat_wind, tiles_first, tiles, ce, cn, la, lb, za, zb):
+def pack_middle(pairs, nrows, nat, nat_late, nat_wind, tiles_first, tiles, ce, cn, la, lb, za, zb):
     up = jnp.where(is_even("lat"), 2, 0)
-    for p in range(pairs):
-        for r in range(nrows):
-            tiles[nrows * p + r] = tile_of(native(nat, 2 * p, r, nrows), native(nat, 2 * p + 1, r, nrows))
+    for source, ref in ((nat, tiles_first), (nat_late, tiles)):
+        for t in range(ref.shape[0]):
+            p, r = divmod(t, nrows)
+            ref[t] = tile_of(native(source, 2 * p, r, nrows), native(source, 2 * p + 1, r, nrows))
     for r in range(nrows):
         east = native(nat_wind, 0, r, nrows) * (1.0 / 12.0)
         north = native(nat_wind, 1, r, nrows) * (1.0 / 12.0)
@@ -280,22 +278,25 @@
 
 
 def first_stage_early(pairs, ntiles, nrows, q, ce, cn, la, lb, ra, rb, section, za, zb, below, side, *edges):
-    edge_w, edge_e, edge_c, edge_d, flux = edges
+    edge_w, edge_e, edge_c, edge_d, flux, beyond = edges
     lat_even, where = is_even("lat"), sources()
     half = LANES // 2
-    a = partners(where, ra, rb, pl.ds(2 * pairs * LANES, half))[0]
-    turned = pltpu.roll(a, half, 1)
-    low = lax.broadcasted_iota(jnp.int32, (half, LANES), 1) < half
-    below[pl.ds(0, half), :] = jnp.where(low, a, turned)
-    below[pl.ds(half, half), :] = jnp.where(low, turned, a)
+    wind = partners(where, ra, rb, pl.ds(2 * pairs * LANES, half))[0]
+    below[...] = tile_of(wind, wind)
     put_side(la, lb, ntiles, side)
     put_corners(lat_even, ntiles, nrows, 2 * pairs * LANES, side, za, zb)
     put_edges(ce, 0, side, side.shape[0] // SUB - 2 * nrows, nrows, edge_c, edge_d)
 
     def one(p, _):
+        for k in range(2):
+            span = pl.ds(pl.multiple_of((2 * p + k) * LANES, LANES), LANES)
+            south, north = partners(where, ra, rb, span)
+            beyond[k] = jnp.transpose(south)
+            beyond[2 + k] = jnp.transpose(north)
+
         def halo(k, shift):
-            start = pl.multiple_of((2 * p + k) * LANES, LANES)
-            return partners(where, ra, rb, pl.ds(start + shift, SUB))
+            here = pl.ds(shift, SUB)
+            return beyond[k, here, :], beyond[2 + k, here, :]
 
         put_edges(q, nrows * p, side, nrows * p, nrows, edge_w, edge_e)
         put_fluxes(q, nrows * p, nrows, ce, edge_w, edge_e, edge_c, flux)
@@ -590,16 +591,16 @@
     early, late = SPLIT, npairs - SPLIT
 
     z0 = shape(2 * early * ncols + ncols // 2, LANES)
-    tiles0, za, zb, nat, nat_late, nat_wind = call(
+    za, zb, nat, nat_late, nat_wind = call(
         functools.partial(pack_first, early, nrows),
         "pack_first",
         (
-            shape(nrows * early, ncols, LANES), z0, z0,
+            z0, z0,
             shape(2 * early, levels * nrows, ncols), shape(2 * late, levels * nrows, ncols),
             shape(2, levels * nrows, ncols),
         ),
         [HBM, HBM],
-        (VMEM,) * 6,
+        (VMEM,) * 5,
         (in_hbm(flat), in_hbm(wind)),
         [pltpu.SemaphoreType.DMA((early + 3,))],
     )
@@ -609,13 +610,16 @@
     sides = shape(SUB * (ntiles + 2 * nrows), LANES)
     edge = shape(SUB * (ntiles + nrows) // 2, LANES)
     z1 = shape(2 * late * ncols, LANES)
-    tiles1, ce, cn, la, lb, za, zb = call(
+    tiles0, tiles1, ce, cn, la, lb, za, zb = call(
         functools.partial(pack_middle, late, nrows),
         "pack_middle",
-        (shape(nrows * late, ncols, LANES), winds, winds, edge, edge, z1, z1),
+        (
+            shape(nrows * early, ncols, LANES), shape(nrows * late, ncols, LANES),
+            winds, winds, edge, edge, z1, z1,
+        ),
         [VMEM] * 3,
-        (VMEM,) * 7,
-        (nat_late, nat_wind, tiles0),
+        (VMEM,) * 8,
+        (nat, nat_late, nat_wind),
         [],
     )
     lat1 = lat_swaps(za, zb)
@@ -630,7 +634,7 @@
         [VMEM] * 7,
         (VMEM,) * 5,
         (tiles0, ce, cn, *lon, *lat0),
-        edges,
+        [*edges, scratch(nrows, ncols, LANES)],
         moved=1000_000_000,
     )
     lat2 = lat_swaps(za, zb)

time: 30.4 us -> 30.4 us (level)
  transfers between devices with their start and end apart: 10 -> 10, of which waited for: 4 -> 4; matrix products, arithmetic and copies ran while one was open for 0% -> 0% of each run, Pallas kernels for 25% -> 26%
where the time goes in v13:
time: 30.4 us; the launch traced here: 30.2 us
  starting transfers between devices  14 us (46%)
  Pallas kernels  10 us (33%)
  waiting for transfers between devices  5.48 us (18%)
  between operations  0.7 us (2%)
    ppermute x4, starting transfers between devices, lat_swaps(): lax.ppermute(first_block, 'lat', [(j, j ^ 1) for j in range(nlat)])  11.2 us
    pallas_call x7, Pallas kernels, call(): pl.pallas_call(kernel, out_shape=out_shape, in_specs=specs, out_specs=out...  10 us
    ppermute x1, waiting for transfers between devices, lon_swaps(): lax.ppermute(second_block, 'lon', second)  2.29 us
    ppermute x1, starting transfers between devices, lon_swaps(): lax.ppermute(second_block, 'lon', second)  2.19 us
    ppermute x4, waiting for transfers between devices, lat_swaps(): lax.ppermute(first_block, 'lat', [(j, j ^ 1) for j in range(nlat)])  2.1 us
    ppermute x1, waiting for transfers between devices, lon_swaps(): lax.ppermute(first_block, 'lon', first)  1.08 us
  transfers between devices with their start and end apart: 10, of which 4 were waited for; matrix products, arithmetic and copies ran while one was open for 0% of the time, Pallas kernels for 26%

profile of v13, /device:TPU:0, one launch (start us, length us, event | category | flops | bytes accessed | tf_op | source)
XLA Modules:
  0.0 30.2 jit_solution(4235488220968387670)
XLA Ops:
  0.6 1.3 %pack_first.1 = (f32[576,128]{1,0:T(8,128)S(1)}, f32[576,128]{1,0:T(8,128)S(1)}, f32[4,256,128]{2,1,0:T(8,128)S(1)}, f32[4,256,128]{2,1,0:T(8,128)S(1)}, f32[2,256,128]{2,1,0:T(8,128)S(1)}) custom-call(f32[8,256,128]{2,1,0:T(8,128)} %bitcast.6, f32[2,256,128]{2,1,0:T(8,128)} %bitcast.7), custom_call_target="tpu_custom_call" | custom-call | flops 1000 | bytes 1000 | tf_op jit(solution)/shard_map/pack_first/pallas_call | solution.py:571
  1.9 3.1 %collective-permute-start.2 = (f32[576,128]{1,0:T(8,128)S(1)}, f32[576,128]{1,0:T(8,128)S(1)}, u32[]{:S(2)}, u32[]{:S(2)}) collective-permute-start(f32[576,128]{1,0:T(8,128)S(1)} %get-tuple-element.35), channel_id=1, source_target_pairs={{0,1},{1,0},{2,3},{3,2},{4,5},{5,4},{6,7},{7,6},{8,9},{9,8},{10,11... | collective-permute-start | bytes 884744 | tf_op jit(solution)/shard_map/ppermute | solution.py:44
  5.0 0.0 collective-permute-start.3
  5.0 0.5 %pack_middle.1 = (f32[8,128,128]{2,1,0:T(8,128)S(1)}, f32[8,128,128]{2,1,0:T(8,128)S(1)}, f32[4,128,128]{2,1,0:T(8,128)S(1)}, f32[4,128,128]{2,1,0:T(8,128)S(1)}...) custom-call(f32[4,256,128]{2,1,0:T(8,128)S(1)} %get-tuple-element.27.nat, ...), custom_call_target="tpu_custom_call" | custom-call | flops 1000 | bytes 1000 | tf_op jit(solution)/shard_map/pack_middle/pallas_call | solution.py:571
  5.6 3.2 %collective-permute-start.6 = (f32[512,128]{1,0:T(8,128)S(1)}, f32[512,128]{1,0:T(8,128)S(1)}, u32[]{:S(2)}, u32[]{:S(2)}) collective-permute-start(f32[512,128]{1,0:T(8,128)S(1)} %get-tuple-element.43), channel_id=1, source_target_pairs={{0,1},{1,0},{2,3},{3,2},{4,5},{5,4},{6,7},{7,6},{8,9},{9,8},{10,11... | collective-permute-start | bytes 786440 | tf_op jit(solution)/shard_map/ppermute | solution.py:44
  8.8 0.0 collective-permute-start.7
  8.8 0.5 %collective-permute-start = (f32[80,128]{1,0:T(8,128)S(1)}, f32[80,128]{1,0:T(8,128)S(1)}, u32[]{:S(2)}, u32[]{:S(2)}) collective-permute-start(f32[80,128]{1,0:T(8,128)S(1)} %get-tuple-element.33), channel_id=1, source_target_pairs={{0,4},{4,0},{8,12},{12,8},{16,20},{20,16},{24,28},{28,24},{1,5},{5... | collective-permute-start | bytes 122888 | tf_op jit(solution)/shard_map/ppermute | solution.py:32
  9.3 1.1 %collective-permute-done.la = f32[80,128]{1,0:T(8,128)S(1)} collective-permute-done((f32[80,128]{1,0:T(8,128)S(1)}, f32[80,128]{1,0:T(8,128)S(1)}, u32[]{:S(2)}, u32[]{:S(2)}) %collective-permute-start) | collective-permute-done | bytes 40992 | tf_op jit(solution)/shard_map/ppermute | solution.py:32
  10.4 2.2 %collective-permute-start.1 = (f32[80,128]{1,0:T(8,128)S(1)}, f32[80,128]{1,0:T(8,128)S(1)}, u32[]{:S(2)}, u32[]{:S(2)}) collective-permute-start(f32[80,128]{1,0:T(8,128)S(1)} %get-tuple-element.34), channel_id=1, source_target_pairs={{0,28},{4,8},{8,4},{12,16},{16,12},{20,24},{24,20},{28,0},{1,29},{... | collective-permute-start | bytes 122888 | tf_op jit(solution)/shard_map/ppermute | solution.py:32
  12.6 2.3 %collective-permute-done.1.lb = f32[80,128]{1,0:T(8,128)S(1)} collective-permute-done((f32[80,128]{1,0:T(8,128)S(1)}, f32[80,128]{1,0:T(8,128)S(1)}, u32[]{:S(2)}, u32[]{:S(2)}) %collective-permute-start.1) | collective-permute-done | bytes 40992 | tf_op jit(solution)/shard_map/ppermute | solution.py:32
  14.8 0.0 collective-permute-done.2.ra
  14.8 0.0 collective-permute-done.3.rb
  14.8 0.7 %first_stage_early.1 = (f32[8,128,128]{2,1,0:T(8,128)S(1)}, f32[552,128]{1,0:T(8,128)S(1)}, f32[552,128]{1,0:T(8,128)S(1)}, f32[128,128]{1,0:T(8,128)S(1)}, f32[192,128]{1,0:T(8,128)S(1)}) custom-call(f32[8,128,128]{2,1,0:T(8,128)S(1)} %get-tuple-element.30.q, f32[4,128,128]{2,1,0:T(8,128)S(1)} %get-tuple-element.31.ce, ...), custom_call_target="tpu_custom_call" | custom-call | flops 1000000000 | bytes 1000000000 | tf_op jit(solution)/shard_map/first_stage_early/pallas_call | solution.py:571
  15.6 1.3 %collective-permute-start.4 = (f32[552,128]{1,0:T(8,128)S(1)}, f32[552,128]{1,0:T(8,128)S(1)}, u32[]{:S(2)}, u32[]{:S(2)}) collective-permute-start(f32[552,128]{1,0:T(8,128)S(1)} %get-tuple-element.39), channel_id=1, source_target_pairs={{0,1},{1,0},{2,3},{3,2},{4,5},{5,4},{6,7},{7,6},{8,9},{9,8},{10,11... | collective-permute-start | bytes 847880 | tf_op jit(solution)/shard_map/ppermute | solution.py:44
  16.8 0.0 collective-permute-start.5
  16.8 1.2 %collective-permute-done.6.ra = f32[512,128]{1,0:T(8,128)S(1)} collective-permute-done((f32[512,128]{1,0:T(8,128)S(1)}, f32[512,128]{1,0:T(8,128)S(1)}, u32[]{:S(2)}, u32[]{:S(2)}) %collective-permute-start.6) | collective-permute-done | bytes 262176 | tf_op jit(solution)/shard_map/ppermute | solution.py:44
  18.1 0.0 collective-permute-done.7.rb
  18.1 0.6 %first_stage_late.1 = (f32[8,128,128]{2,1,0:T(8,128)S(1)}, f32[512,128]{1,0:T(8,128)S(1)}, f32[512,128]{1,0:T(8,128)S(1)}) custom-call(f32[8,128,128]{2,1,0:T(8,128)S(1)} %get-tuple-element.42.q.q_late, f32[4,128,128]{2,1,0:T(8,128)S(1)} %get-tuple-element.31.ce, f32[4,128,128]{2,1,0:T(8,128)S(1)} %get-tuple-element.32.cn, ...), custom_call_target="tpu_custom_call" | custom-call | flops 12000000 | bytes 12000000 | tf_op jit(solution)/shard_map/first_stage_late/pallas_call | solution.py:571
  18.7 3.7 %collective-permute-start.8 = (f32[512,128]{1,0:T(8,128)S(1)}, f32[512,128]{1,0:T(8,128)S(1)}, u32[]{:S(2)}, u32[]{:S(2)}) collective-permute-start(f32[512,128]{1,0:T(8,128)S(1)} %get-tuple-element.48), channel_id=1, source_target_pairs={{0,1},{1,0},{2,3},{3,2},{4,5},{5,4},{6,7},{7,6},{8,9},{9,8},{10,11... | collective-permute-start | bytes 786440 | tf_op jit(solution)/shard_map/ppermute | solution.py:44
  22.4 4.5 %radiation.1.heating = f32[256,128]{1,0:T(8,128)S(1)} custom-call(f32[4,256,128]{2,1,0:T(8,128)S(1)} %get-tuple-element.27.nat, f32[4,128]{1,0:T(4,128)} %cosz_in.1, f32[4,128]{1,0:T(4,128)} %albedo_in.1, f32[14]{0:T(128)} %ext_in.1, f32[14]{0:T(128)} %single_in.1, f32[14]{0:T(128)} %weight_in.1, s32[4,1,128]{2,1,0:T(1,128)} %order_in.1, s32[4]{0:T(128)} %bitcast.8, ...), custom_call_target="tpu_custom_call" | custom-call | flops 16000000 | bytes 16000000 | tf_op jit(solution)/shard_map/radiation/pallas_call | solution.py:571
  26.9 0.0 collective-permute-done.4.ra
  26.9 1.5 %second_stage_early.1 = (f32[8,256,128]{2,1,0:T(8,128)}, f32[256,128]{1,0:T(8,128)}, f32[4,256,128]{2,1,0:T(8,128)S(1)}, f32[4,64,128]{2,1,0:T(8,128)S(1)}) custom-call(f32[8,128,128]{2,1,0:T(8,128)S(1)} %get-tuple-element.30.q, f32[8,128,128]{2,1,0:T(8,128)S(1)} %get-tuple-element.37.s, f32[4,128,128]{2,1,0:T(8,128)S(1)} %get-tuple-element.31.ce, ...), custom_call_target="tpu_custom_call" | custom-call | flops 1000 | bytes 1000 | tf_op jit(solution)/shard_map/second_stage_early/pallas_call | solution.py:571
  28.5 0.9 %collective-permute-done.8.ra = f32[512,128]{1,0:T(8,128)S(1)} collective-permute-done((f32[512,128]{1,0:T(8,128)S(1)}, f32[512,128]{1,0:T(8,128)S(1)}, u32[]{:S(2)}, u32[]{:S(2)}) %collective-permute-start.8) | collective-permute-done | bytes 262176 | tf_op jit(solution)/shard_map/ppermute | solution.py:44
  29.3 0.8 %second_stage_late.1 = f32[8,256,128]{2,1,0:T(8,128)} custom-call(f32[4,256,128]{2,1,0:T(8,128)S(1)} %get-tuple-element.46.part, f32[4,64,128]{2,1,0:T(8,128)S(1)} %get-tuple-element.47.winds, f32[512,128]{1,0:T(8,128)S(1)} %collective-permute-done.8.ra, f32[512,128]{1,0:T(8,128)S(1)} %collective-permute-done.9.rb, ...), custom_call_target="tpu_custom_call", output_to_operand_aliasing={{}: (4, {})} | custom-call | flops 1000 | bytes 1000 | tf_op jit(solution)/shard_map/second_stage_late/pallas_call | solution.py:571
  (3 shorter events, 0.0 us)
Async XLA Ops:
  1.9 12.9 %collective-permute-start.2 = (f32[576,128]{1,0:T(8,128)S(1)}, f32[576,128]{1,0:T(8,128)S(1)}, u32[]{:S(2)}, u32[]{:S(2)}) collective-permute-start(f32[576,128]{1,0:T(8,128)S(1)} %get-tuple-element.35), channel_id=1, source_target_pairs={{0,1},{1,0},{2,3},{3,2},{4,5},{5,4},{6,7},{7,6},{8,9},{9,8},{10,11... | collective-permute-start | bytes 884744 | tf_op jit(solution)/shard_map/ppermute | solution.py:44
  5.0 9.8 %collective-permute-start.3 = (f32[576,128]{1,0:T(8,128)S(1)}, f32[576,128]{1,0:T(8,128)S(1)}, u32[]{:S(2)}, u32[]{:S(2)}) collective-permute-start(f32[576,128]{1,0:T(8,128)S(1)} %get-tuple-element.36), channel_id=1, source_target_pairs={{0,4},{1,2},{2,1},{3,7},{4,0},{5,6},{6,5},{7,3},{8,12},{9,10},{10,... | collective-permute-start | bytes 884744 | tf_op jit(solution)/shard_map/ppermute | solution.py:43
  5.6 12.5 %collective-permute-start.6 = (f32[512,128]{1,0:T(8,128)S(1)}, f32[512,128]{1,0:T(8,128)S(1)}, u32[]{:S(2)}, u32[]{:S(2)}) collective-permute-start(f32[512,128]{1,0:T(8,128)S(1)} %get-tuple-element.43), channel_id=1, source_target_pairs={{0,1},{1,0},{2,3},{3,2},{4,5},{5,4},{6,7},{7,6},{8,9},{9,8},{10,11... | collective-permute-start | bytes 786440 | tf_op jit(solution)/shard_map/ppermute | solution.py:44
  8.8 9.3 %collective-permute-start.7 = (f32[512,128]{1,0:T(8,128)S(1)}, f32[512,128]{1,0:T(8,128)S(1)}, u32[]{:S(2)}, u32[]{:S(2)}) collective-permute-start(f32[512,128]{1,0:T(8,128)S(1)} %get-tuple-element.44), channel_id=1, source_target_pairs={{0,4},{1,2},{2,1},{3,7},{4,0},{5,6},{6,5},{7,3},{8,12},{9,10},{10,... | collective-permute-start | bytes 786440 | tf_op jit(solution)/shard_map/ppermute | solution.py:43
  8.8 1.6 %collective-permute-start = (f32[80,128]{1,0:T(8,128)S(1)}, f32[80,128]{1,0:T(8,128)S(1)}, u32[]{:S(2)}, u32[]{:S(2)}) collective-permute-start(f32[80,128]{1,0:T(8,128)S(1)} %get-tuple-element.33), channel_id=1, source_target_pairs={{0,4},{4,0},{8,12},{12,8},{16,20},{20,16},{24,28},{28,24},{1,5},{5... | collective-permute-start | bytes 122888 | tf_op jit(solution)/shard_map/ppermute | solution.py:32
  10.4 4.5 %collective-permute-start.1 = (f32[80,128]{1,0:T(8,128)S(1)}, f32[80,128]{1,0:T(8,128)S(1)}, u32[]{:S(2)}, u32[]{:S(2)}) collective-permute-start(f32[80,128]{1,0:T(8,128)S(1)} %get-tuple-element.34), channel_id=1, source_target_pairs={{0,28},{4,8},{8,4},{12,16},{16,12},{20,24},{24,20},{28,0},{1,29},{... | collective-permute-start | bytes 122888 | tf_op jit(solution)/shard_map/ppermute | solution.py:32
  15.6 11.3 %collective-permute-start.4 = (f32[552,128]{1,0:T(8,128)S(1)}, f32[552,128]{1,0:T(8,128)S(1)}, u32[]{:S(2)}, u32[]{:S(2)}) collective-permute-start(f32[552,128]{1,0:T(8,128)S(1)} %get-tuple-element.39), channel_id=1, source_target_pairs={{0,1},{1,0},{2,3},{3,2},{4,5},{5,4},{6,7},{7,6},{8,9},{9,8},{10,11... | collective-permute-start | bytes 847880 | tf_op jit(solution)/shard_map/ppermute | solution.py:44
  16.8 10.1 %collective-permute-start.5 = (f32[552,128]{1,0:T(8,128)S(1)}, f32[552,128]{1,0:T(8,128)S(1)}, u32[]{:S(2)}, u32[]{:S(2)}) collective-permute-start(f32[552,128]{1,0:T(8,128)S(1)} %get-tuple-element.40), channel_id=1, source_target_pairs={{0,4},{1,2},{2,1},{3,7},{4,0},{5,6},{6,5},{7,3},{8,12},{9,10},{10,... | collective-permute-start | bytes 847880 | tf_op jit(solution)/shard_map/ppermute | solution.py:43
  18.7 10.6 %collective-permute-start.8 = (f32[512,128]{1,0:T(8,128)S(1)}, f32[512,128]{1,0:T(8,128)S(1)}, u32[]{:S(2)}, u32[]{:S(2)}) collective-permute-start(f32[512,128]{1,0:T(8,128)S(1)} %get-tuple-element.48), channel_id=1, source_target_pairs={{0,1},{1,0},{2,3},{3,2},{4,5},{5,4},{6,7},{7,6},{8,9},{9,8},{10,11... | collective-permute-start | bytes 786440 | tf_op jit(solution)/shard_map/ppermute | solution.py:44
  22.4 6.9 %collective-permute-start.9 = (f32[512,128]{1,0:T(8,128)S(1)}, f32[512,128]{1,0:T(8,128)S(1)}, u32[]{:S(2)}, u32[]{:S(2)}) collective-permute-start(f32[512,128]{1,0:T(8,128)S(1)} %get-tuple-element.49), channel_id=1, source_target_pairs={{0,4},{1,2},{2,1},{3,7},{4,0},{5,6},{6,5},{7,3},{8,12},{9,10},{10,... | collective-permute-start | bytes 786440 | tf_op jit(solution)/shard_map/ppermute | solution.py:43
